TPU v7x, 32 devices: a whole 2x2x4 slice. The times are simulated.
32 devices in a mesh: gx: 8 (over z, y), ta: 4 (over x, core).
Axes of the slice: x: 2, y: 2, z: 4, core: 2. Of those that a mesh axis runs over, the one named last changes fastest.
Arguments:
- features: bfloat16 [1, 128, 16, 8, 4096], P(None, 'gx', 'ta'), may hold values from -6 to 6
- cotangent: bfloat16 [1, 128, 16, 8, 4096], P(None, 'gx', 'ta'), may hold values from -6 to 6
- spec_weight: float32 [32, 16, 8, 8, 1024], P(None, None, None, None, ('gx', 'ta')), may hold values from -2 to 2
- point_weight: bfloat16 [8, 8], replicated, may hold values from -2 to 2
- bias_vector: float32 [8], replicated, may hold values from -1 to 1
Outputs:
- output: bfloat16 [1, 128, 16, 8, 4096], P(None, 'gx', 'ta')
- grad_field: bfloat16 [1, 128, 16, 8, 4096], P(None, 'gx', 'ta')
- grad_spec: float32 [32, 16, 8, 8, 1024], P(None, None, None, None, ('gx', 'ta'))
- grad_point: float32 [8, 8], replicated
- grad_bias: float32 [8], replicated
All inputs are finite; a program needn't handle non-finite values.
Results may differ from a plain program's by a relative error of at most 0.014.
Values may be sent and summed in bfloat16 or wider, within the bound.
No kernel may reach another device: no remote copies, remote signals or barrier semaphores. Data moves between devices by JAX's collectives and lax.ppermute only.
A program may use at most 320 MiB of HBM per device.

v0:
```python
import math

import jax
import jax.numpy as jnp
from jax import lax
from jax.sharding import PartitionSpec as P

NX = 128
NY = 128
NZ = 32
NT = 16
MX = 16
MY = 16
MZ = 16
MT = 8
BATCH = 1
KX = 32
KT = 16


def basis(length, modes):
    frequency = jnp.concatenate([jnp.arange(modes + 1), jnp.arange(1, modes)])
    samples_at = jnp.arange(length)
    phases = (
        2.0
        * math.pi
        / length
        * (frequency[:, None] * samples_at[None, :] % length).astype(jnp.float32)
    )
    cosine_row = jnp.arange(2 * modes) <= modes
    waves = jnp.where(cosine_row[:, None], jnp.cos(phases), jnp.sin(phases))
    at_edge = cosine_row & ((frequency == 0) | (2 * frequency == length))
    scales = jnp.where(at_edge, math.sqrt(1.0 / length), math.sqrt(2.0 / length)).astype(
        jnp.float32
    )
    return waves * scales[:, None]


def joint_table(first_table, second_table):
    first_rows, first_len = first_table.shape
    second_rows, second_len = second_table.shape
    joined = first_table[:, None, :, None] * second_table[None, :, None, :]
    return joined.reshape(first_rows * second_rows, first_len * second_len)


def analyse_yz(spatial, yz_table):
    return jnp.einsum(
        "qp,bxtcp->bxtcq", yz_table, spatial.astype(jnp.float32), precision=lax.Precision.HIGHEST
    )


def build_yz(modes_in, yz_table):
    return jnp.einsum(
        "qp,bxtcq->bxtcp", yz_table, modes_in.astype(jnp.float32), precision=lax.Precision.HIGHEST
    )


def analyse_xt(spread, table):
    sizes = spread.shape
    flattened = spread.reshape(sizes[0], sizes[1] * sizes[2], sizes[3] * sizes[4]).astype(
        jnp.float32
    )
    spectral = jnp.einsum("mp,bpr->bmr", table, flattened, precision=lax.Precision.HIGHEST)
    return spectral.reshape(sizes[0], KX, KT, sizes[3], sizes[4])


def synthesise_xt(modes_in, table):
    sizes = modes_in.shape
    flattened = modes_in.reshape(sizes[0], sizes[1] * sizes[2], sizes[3] * sizes[4])
    spatial = jnp.einsum("mp,bmr->bpr", table, flattened, precision=lax.Precision.HIGHEST)
    return spatial.reshape(sizes[0], NX, NT, sizes[3], sizes[4])


def gelu_value(values):
    return 0.5 * values * (1.0 + jax.scipy.special.erf(values * 0.7071067811865476))


def gelu_slope(values):
    return (
        0.5 * (1.0 + jax.scipy.special.erf(values * 0.7071067811865476))
        + values * jnp.exp(-0.5 * values * values) * 0.3989422804014327
    )


def body(features, cotangent, spec_weight, point_weight, bias_vector):
    batches, x_local, t_local, chans, cells = features.shape
    by_table = basis(NY, MY).astype(jnp.bfloat16).astype(jnp.float32)
    bz_table = basis(NZ, MZ).astype(jnp.bfloat16).astype(jnp.float32)
    yz_table = joint_table(by_table, bz_table)
    xt_table = joint_table(basis(NX, MX), basis(NT, MT))
    norm_scale = float(BATCH * NX * NT * NY * NZ) ** (-0.5)
    yz_in = analyse_yz(features, yz_table).astype(jnp.bfloat16)
    spread_in = lax.all_to_all(
        lax.all_to_all(yz_in, "gx", split_axis=4, concat_axis=1, tiled=True),
        "ta",
        split_axis=4,
        concat_axis=2,
        tiled=True,
    )
    spectrum = analyse_xt(spread_in, xt_table)
    mixed = jnp.einsum("bklip,kliop->bklop", spectrum, spec_weight, precision=lax.Precision.HIGHEST)
    xt_out = synthesise_xt(mixed, xt_table).astype(jnp.bfloat16)
    returned = lax.all_to_all(
        lax.all_to_all(
            xt_out[:, :, :, :, None, None, :], "gx", split_axis=1, concat_axis=4, tiled=True
        ),
        "ta",
        split_axis=2,
        concat_axis=5,
        tiled=True,
    )
    returned = returned.reshape(batches, x_local, t_local, chans, -1)
    spatial = build_yz(returned, yz_table)
    pointwise = jnp.einsum(
        "oi,bxtip->bxtop", point_weight, features, preferred_element_type=jnp.float32
    )
    pre = spatial + pointwise + bias_vector[:, None]
    output = gelu_value(pre).astype(jnp.bfloat16)
    grad_pre = (cotangent.astype(jnp.float32) * gelu_slope(pre)).astype(jnp.bfloat16)
    local_point = jnp.einsum(
        "bxtop,bxtip->oi", grad_pre, features, preferred_element_type=jnp.float32
    )
    local_bias = jnp.sum(grad_pre.astype(jnp.float32), axis=(0, 1, 2, 4))
    total_point, total_bias = lax.psum((local_point, local_bias), ("gx", "ta"))
    yz_grad = analyse_yz(grad_pre, yz_table).astype(jnp.bfloat16)
    spread_grad = lax.all_to_all(
        lax.all_to_all(yz_grad, "gx", split_axis=4, concat_axis=1, tiled=True),
        "ta",
        split_axis=4,
        concat_axis=2,
        tiled=True,
    )
    grad_modes = analyse_xt(spread_grad, xt_table)
    yz_again = analyse_yz(features, yz_table).astype(jnp.bfloat16)
    spread_again = lax.all_to_all(
        lax.all_to_all(yz_again, "gx", split_axis=4, concat_axis=1, tiled=True),
        "ta",
        split_axis=4,
        concat_axis=2,
        tiled=True,
    )
    input_spec = analyse_xt(spread_again, xt_table)
    grad_spec = jnp.einsum(
        "bklip,bklop->kliop", input_spec, grad_modes, precision=lax.Precision.HIGHEST
    )
    grad_in_modes = jnp.einsum(
        "kliop,bklop->bklip", spec_weight, grad_modes, precision=lax.Precision.HIGHEST
    )
    xt_grad = synthesise_xt(grad_in_modes, xt_table).astype(jnp.bfloat16)
    grad_back = lax.all_to_all(
        lax.all_to_all(
            xt_grad[:, :, :, :, None, None, :], "gx", split_axis=1, concat_axis=4, tiled=True
        ),
        "ta",
        split_axis=2,
        concat_axis=5,
        tiled=True,
    )
    grad_back = grad_back.reshape(batches, x_local, t_local, chans, -1)
    grad_spatial = build_yz(grad_back, yz_table)
    grad_point_term = jnp.einsum(
        "oi,bxtop->bxtip", point_weight, grad_pre, preferred_element_type=jnp.float32
    )
    grad_field = (grad_spatial + grad_point_term).astype(jnp.bfloat16)
    return (output, grad_field, grad_spec, total_point * norm_scale, total_bias * norm_scale)


def solution(mesh):
    in_specs = (
        P(None, "gx", "ta", None, None),
        P(None, "gx", "ta", None, None),
        P(None, None, None, None, ("gx", "ta")),
        P(),
        P(),
    )
    out_specs = (
        P(None, "gx", "ta", None, None),
        P(None, "gx", "ta", None, None),
        P(None, None, None, None, ("gx", "ta")),
        P(),
        P(),
    )
    return jax.shard_map(body, mesh=mesh, in_specs=in_specs, out_specs=out_specs, check_vma=False)
```

profile of v0, /device:TPU:0, one launch (start us, length us, event | category | flops | bytes accessed | tf_op | source)
XLA Modules:
  0.0 691.5 jit_solution(5212247404187456889)
XLA Ops:
  1.1 21.4 %broadcast_multiply_fusion = f32[32,32,128,32]{3,2,1,0:T(8,128)} fusion(f32[32,32]{1,0:T(8,128)S(1)} %fusion.59, f32[32,128]{1,0:T(8,128)S(1)} %get-tuple-element.17), kind=kLoop, calls=%fused_computation | loop fusion | flops 4194304 | bytes 16797696 | tf_op jit(solution)/shard_map/mul | solution.py:42
  22.5 47.4 %reshape.480 = f32[1024,4096,1,1]{1,0,2,3:T(8,128)} reshape(f32[32,32,128,32]{3,2,1,0:T(8,128)} %broadcast_multiply_fusion) | data formatting | bytes 33554432 | tf_op jit(solution)/shard_map/mul | solution.py:42
  69.9 26.1 %fusion.37 = bf16[1,16,4,8,1024]{4,1,3,2,0:T(8,128)(2,1)S(1)} fusion(bf16[16,4,8,4096]{3,2,1,0:T(8,128)(2,1)} %bitcast.206, f32[1024,4096,1,1]{1,0,2,3:T(8,128)} %reshape.480), kind=kOutput, calls=%fused_computation.40 | convolution fusion | flops 25770328064 | bytes 22020096 | tf_op jit(solution)/shard_map/qp,bxtcp->bxtcq/dot_general | solution.py:47
  96.0 12.0 %copy.87 = bf16[1,16,4,8,1024]{1,3,2,0,4:T(8,128)(2,1)} copy(bf16[1,16,4,8,1024]{4,1,3,2,0:T(8,128)(2,1)S(1)} %fusion.37) | data formatting | bytes 2097152 | tf_op jit(solution)/shard_map/convert_element_type | solution.py:92
  107.9 11.2 %reshape.489 = bf16[8,2,32768]{2,1,0:T(2,128)(2,1)} reshape(bf16[1024,1,4,8,16]{4,3,2,1,0:T(8,128)(2,1)} %bitcast.185) | data formatting | bytes 2097152
  119.2 7.5 %all-to-all-start = ((bf16[8,2,32768]{2,1,0:T(2,128)(2,1)}), bf16[8,2,32768]{2,1,0:T(2,128)(2,1)S(1)}, u32[]{:S(2)}, u32[]{:S(2)}) async-start(bf16[8,2,32768]{2,1,0:T(2,128)(2,1)} %reshape.489), calls=%async_computation | async-start | bytes 2097152 | tf_op jit(solution)/shard_map/all_to_all | solution.py:94
  126.9 25.5 %all-to-all-done = bf16[8,2,32768]{2,1,0:T(2,128)(2,1)S(1)} async-done(((bf16[8,2,32768]{2,1,0:T(2,128)(2,1)}), bf16[8,2,32768]{2,1,0:T(2,128)(2,1)S(1)}, u32[]{:S(2)}, u32[]{:S(2)}) %all-to-all-start) | async-done | bytes 1048608 | tf_op jit(solution)/shard_map/all_to_all | solution.py:94
  152.4 7.4 %reshape.490 = bf16[1024,1,4,8,16]{4,3,2,1,0:T(8,128)(2,1)} reshape(bf16[8,2,32768]{2,1,0:T(2,128)(2,1)S(1)} %all-to-all-done) | data formatting | bytes 2097152
  159.8 8.1 %copy.132 = bf16[1,16,4,8,8,128]{5,4,3,2,1,0:T(8,128)(2,1)S(1)} copy(bf16[1,16,4,8,8,128]{1,3,2,5,4,0:T(8,128)(2,1)} %bitcast.186) | data formatting | bytes 2097152 | tf_op jit(solution)/shard_map/all_to_all | solution.py:94
  173.9 11.4 %broadcast_multiply_fusion.1 = f32[32,16,128,16]{3,2,1,0:T(8,128)} fusion(f32[16,16]{1,0:T(8,128)S(1)} %select_multiply_fusion.1, f32[32,128]{1,0:T(8,128)S(1)} %get-tuple-element.16), kind=kLoop, calls=%fused_computation.12 | loop fusion | flops 1048576 | bytes 4211712 | tf_op jit(solution)/shard_map/mul | solution.py:42
  185.2 28.3 %mul.296 = f32[512,2048]{1,0:T(8,128)} reshape(f32[32,16,128,16]{3,2,1,0:T(8,128)} %broadcast_multiply_fusion.1) | data formatting | bytes 8388608 | tf_op jit(solution)/shard_map/mul | solution.py:42
  231.0 9.3 %multiply_reduce_fusion.1 = f32[32,16,32,8]{2,3,1,0:T(8,128)} fusion(f32[32,16,8,8,32]{4,3,2,1,0:T(8,128)} %param.7, f32[32,16,32,8]{2,3,1,0:T(8,128)S(1)} %bitcast.189), kind=kLoop, calls=%fused_computation.10 | loop fusion | flops 1966080 | bytes 5242880 | tf_op jit(solution)/shard_map/bklip,kliop->bklop/dot_general | solution.py:101
  266.1 29.8 %all_to_all.142 = bf16[8,2,32768]{2,1,0:T(2,128)(2,1)} all-to-all(bf16[8,2,32768]{2,1,0:T(2,128)(2,1)S(1)} %reshape.491), channel_id=1, replica_groups=mesh['gx'=8,'ta'=4] {'gx'}, dimensions={0} | all-to-all | bytes 2097152 | tf_op jit(solution)/shard_map/all_to_all | solution.py:104
  302.9 9.1 %copy.157 = bf16[1,8,16,16,8,1,1,32]{7,1,4,2,3,6,5,0:T(8,128)(2,1)} copy(bf16[1,8,16,16,8,1,1,32]{7,4,3,2,1,6,5,0:T(8,128)(2,1)} %bitcast.191) | data formatting | bytes 2097152 | tf_op jit(solution)/shard_map/all_to_all | solution.py:104
  329.4 7.3 %all-to-all-done.3 = bf16[4,2,65536]{2,1,0:T(2,128)(2,1)S(1)} async-done(((bf16[4,2,65536]{2,1,0:T(2,128)(2,1)}), bf16[4,2,65536]{2,1,0:T(2,128)(2,1)S(1)}, u32[]{:S(2)}, u32[]{:S(2)}) %all-to-all-start.3) | async-done | bytes 1048608 | tf_op jit(solution)/shard_map/all_to_all | solution.py:103
  343.3 10.0 %copy.98 = bf16[1,16,4,8,8,4,1,32]{7,5,4,3,2,1,6,0:T(4,128)(2,1)} copy(bf16[1,16,4,8,8,4,1,32]{7,4,3,2,5,1,6,0:T(8,128)(2,1)S(1)} %bitcast.197) | data formatting | bytes 2097152 | tf_op jit(solution)/shard_map/all_to_all | solution.py:103
  353.3 8.7 %reshape.474 = bf16[16,4,8,1024]{3,2,1,0:T(8,128)(2,1)S(1)} reshape(bf16[1,16,4,8,8,4,1,32]{7,5,4,3,2,1,6,0:T(4,128)(2,1)} %copy.98) | data formatting | bytes 2097152 | tf_op jit(solution)/shard_map/reshape.10
  362.0 25.9 %convert_reduce_fusion = (f32[8]{0:T(128)S(1)}, bf16[1,16,4,8,4096]{4,3,2,1,0:T(8,128)(2,1)}, bf16[1,16,4,8,4096]{4,3,2,1,0:T(8,128)(2,1)}) fusion(bf16[1,16,4,8,4096]{4,3,2,1,0:T(8,128)(2,1)} %param.6, f32[8]{0:T(128)S(1)} %copy-done.1, f32[16,4,4096,8]{2,3,1,0:T(8,128)} %fusion.68, bf16[16,4,8,1024]{3,2,1,0:T(8,128)(2,1)S(1)} %reshape.474, ...), kind=kOutput, calls=%fused_computation.24 | convolution fusion | flops 25807552512 | bytes 38797376 | tf_op jit(solution)/shard_map/qp,bxtcq->bxtcp/dot_general | solution.py:53
  387.9 18.1 %fusion.34 = bf16[1,16,4,8,1024]{4,3,2,1,0:T(8,128)(2,1)S(1)} fusion(f32[1024,4096,1,1]{1,0,2,3:T(8,128)} %reshape.480, bf16[1,16,4,8,4096]{4,3,2,1,0:T(8,128)(2,1)} %get-tuple-element.8), kind=kOutput, calls=%fused_computation.39 | convolution fusion | flops 25770328064 | bytes 22020096 | tf_op jit(solution)/shard_map/qp,bxtcp->bxtcq/dot_general | solution.py:47
  406.0 12.2 %copy.99 = bf16[1,16,4,8,1024]{1,3,2,0,4:T(8,128)(2,1)} copy(bf16[1,16,4,8,1024]{4,3,2,1,0:T(8,128)(2,1)S(1)} %fusion.34) | data formatting | bytes 2097152 | tf_op jit(solution)/shard_map/convert_element_type | solution.py:125
  418.2 10.4 %reshape.495 = bf16[8,2,32768]{2,1,0:T(2,128)(2,1)S(1)} reshape(bf16[1024,1,4,8,16]{4,3,2,1,0:T(8,128)(2,1)} %bitcast.187) | data formatting | bytes 2097152
  428.6 29.1 %all_to_all.143 = bf16[8,2,32768]{2,1,0:T(2,128)(2,1)} all-to-all(bf16[8,2,32768]{2,1,0:T(2,128)(2,1)S(1)} %reshape.495), channel_id=1, replica_groups=mesh['gx'=8,'ta'=4] {'gx'}, dimensions={0} | all-to-all | bytes 2097152 | tf_op jit(solution)/shard_map/all_to_all | solution.py:127
  457.8 8.9 %reshape.496 = bf16[1024,1,4,8,16]{4,3,2,1,0:T(8,128)(2,1)} reshape(bf16[8,2,32768]{2,1,0:T(2,128)(2,1)} %all_to_all.143) | data formatting | bytes 2097152
  466.6 8.1 %copy.133 = bf16[1,16,4,8,8,128]{5,4,3,2,1,0:T(8,128)(2,1)S(1)} copy(bf16[1,16,4,8,8,128]{1,3,2,5,4,0:T(8,128)(2,1)} %bitcast.188) | data formatting | bytes 2097152 | tf_op jit(solution)/shard_map/all_to_all | solution.py:127
  478.4 17.3 %all_to_all.144 = bf16[1,128,4,8,128]{1,3,2,0,4:T(8,128)(2,1)S(1)} all-to-all(bf16[1,128,4,8,128]{1,3,2,0,4:T(8,128)(2,1)S(1)} %copy.102), channel_id=1, replica_groups=mesh['gx'=8,'ta'=4] {'ta'}, dimensions={4} | all-to-all | bytes 2097152 | tf_op jit(solution)/shard_map/all_to_all | solution.py:126
  516.3 15.9 %multiply_bitcast_fusion = (f32[32,16,8,8,32]{4,3,2,1,0:T(8,128)}, f32[32,16,32,8]{2,3,1,0:T(8,128)}) fusion(f32[32,16,32,8]{2,3,1,0:T(8,128)} %bitcast.199, f32[32,16,32,8]{2,3,1,0:T(8,128)S(1)} %bitcast.190, f32[32,16,8,8,32]{4,3,2,1,0:T(8,128)} %param.7), kind=kLoop, calls=%fused_computation.11 | loop fusion | flops 3014656 | bytes 9961472 | tf_op jit(solution)/shard_map/bklip,bklop->kliop/transpose | solution.py:143
  549.0 7.8 %reshape.497 = bf16[8,2,32768]{2,1,0:T(2,128)(2,1)} reshape(bf16[128,1,1,1,16,8,32]{6,5,4,3,2,1,0:T(8,128)(2,1)} %bitcast_bitcast_fusion) | data formatting | bytes 2097152
  566.6 41.0 %all-reduce = (f32[8,8]{1,0:T(8,128)S(1)}, f32[8]{0:T(128)S(1)}) all-reduce(f32[8,8]{1,0:T(8,128)S(1)} %fusion.42, f32[8]{0:T(128)S(1)} %get-tuple-element.7), channel_id=1, replica_groups=mesh['gx'=8,'ta'=4] {'gx','ta'}, use_global_device_ids=true, to_apply=%region_0.1 | all-reduce | flops 72 | bytes 576 | tf_op jit(solution)/shard_map/psum | solution.py:124
  612.1 9.0 %copy.158 = bf16[1,8,16,16,8,1,1,32]{7,1,4,2,3,6,5,0:T(8,128)(2,1)} copy(bf16[1,8,16,16,8,1,1,32]{7,4,3,2,1,6,5,0:T(8,128)(2,1)} %bitcast.194) | data formatting | bytes 2097152 | tf_op jit(solution)/shard_map/all_to_all | solution.py:151
  652.4 10.0 %copy.110 = bf16[1,16,4,8,8,4,1,32]{7,5,4,3,2,1,6,0:T(4,128)(2,1)} copy(bf16[1,16,4,8,8,4,1,32]{7,4,3,2,5,1,6,0:T(8,128)(2,1)S(1)} %bitcast.198) | data formatting | bytes 2097152 | tf_op jit(solution)/shard_map/all_to_all | solution.py:150
  662.4 8.8 %reshape.479 = bf16[16,4,8,1024]{3,2,1,0:T(8,128)(2,1)S(1)} reshape(bf16[1,16,4,8,8,4,1,32]{7,5,4,3,2,1,6,0:T(4,128)(2,1)} %copy.110) | data formatting | bytes 2097152 | tf_op jit(solution)/shard_map/reshape.44
  671.2 19.7 %fusion.14 = bf16[1,16,4,8,4096]{4,3,2,1,0:T(8,128)(2,1)} fusion(f32[16,4,4096,8]{2,3,1,0:T(8,128)} %fusion.66, bf16[16,4,8,1024]{3,2,1,0:T(8,128)(2,1)S(1)} %reshape.479, f32[1024,4096,1,1]{1,0,2,3:T(8,128)} %reshape.480), kind=kOutput, calls=%fused_computation.21 | convolution fusion | flops 25773998080 | bytes 30408704 | tf_op jit(solution)/shard_map/qp,bxtcq->bxtcp/dot_general | solution.py:53
  (63 shorter events, 167.4 us)
Async XLA Ops:
  0.6 321.7 %copy-start = (bf16[8,8]{1,0:T(8,128)(2,1)S(1)}, bf16[8,8]{1,0:T(8,128)(2,1)}, u32[]{:S(2)}) copy-start(bf16[8,8]{1,0:T(8,128)(2,1)} %param.8) | copy-start | bytes 388
  119.2 33.2 %all-to-all-start = ((bf16[8,2,32768]{2,1,0:T(2,128)(2,1)}), bf16[8,2,32768]{2,1,0:T(2,128)(2,1)S(1)}, u32[]{:S(2)}, u32[]{:S(2)}) async-start(bf16[8,2,32768]{2,1,0:T(2,128)(2,1)} %reshape.489), calls=%async_computation | async-start | bytes 2097152 | tf_op jit(solution)/shard_map/all_to_all | solution.py:94
  170.3 43.2 %all-to-all-start.1 = ((bf16[1,128,4,8,128]{1,3,2,0,4:T(8,128)(2,1)}), bf16[1,128,4,8,128]{1,3,2,0,4:T(8,128)(2,1)S(1)}, u32[]{:S(2)}, u32[]{:S(2)}) async-start(bf16[1,128,4,8,128]{1,3,2,0,4:T(8,128)(2,1)} %copy.90), calls=%async_computation.1 | async-start | bytes 2097152 | tf_op jit(solution)/shard_map/all_to_all | solution.py:93
  318.4 18.3 %all-to-all-start.3 = ((bf16[4,2,65536]{2,1,0:T(2,128)(2,1)}), bf16[4,2,65536]{2,1,0:T(2,128)(2,1)S(1)}, u32[]{:S(2)}, u32[]{:S(2)}) async-start(bf16[4,2,65536]{2,1,0:T(2,128)(2,1)} %reshape.493), calls=%async_computation.3 | async-start | bytes 2097152 | tf_op jit(solution)/shard_map/all_to_all | solution.py:103
  353.3 8.7 %copy-start.1 = (f32[8]{0:T(128)S(1)}, f32[8]{0:T(128)}, u32[]{:S(2)}) copy-start(f32[8]{0:T(128)} %param.9) | copy-start | bytes 100
  556.8 50.8 %all-to-all-start.6 = ((bf16[8,2,32768]{2,1,0:T(2,128)(2,1)}), bf16[8,2,32768]{2,1,0:T(2,128)(2,1)S(1)}, u32[]{:S(2)}, u32[]{:S(2)}) async-start(bf16[8,2,32768]{2,1,0:T(2,128)(2,1)} %reshape.497), calls=%async_computation.6 | async-start | bytes 2097152 | tf_op jit(solution)/shard_map/all_to_all | solution.py:151
  627.6 18.2 %all-to-all-start.7 = ((bf16[4,2,65536]{2,1,0:T(2,128)(2,1)}), bf16[4,2,65536]{2,1,0:T(2,128)(2,1)S(1)}, u32[]{:S(2)}, u32[]{:S(2)}) async-start(bf16[4,2,65536]{2,1,0:T(2,128)(2,1)} %reshape.499), calls=%async_computation.7 | async-start | bytes 2097152 | tf_op jit(solution)/shard_map/all_to_all | solution.py:150
where the time goes:
time: 702 us; the launch traced here: 691 us
  local copies, waits for them, and re-layouts  319 us (45%)
  matrix products  133 us (19%)
  blocking collectives  117 us (17%)
  other arithmetic  59.7 us (9%)
  waiting for transfers between devices  39.2 us (6%)
  starting transfers between devices  22.3 us (3%)
    unnamed x18, local copies, waits for them, and re-layouts  93.6 us
    mul x2, local copies, waits for them, and re-layouts, joint_table(): joined = first_table[:, None, :, None] * second_table[None, :, None, :]  75.7 us
    dot_general x2, matrix products, build_yz(): jnp.einsum('qp,bxtcq->bxtcp', yz_table, modes_in.astype(jnp.float32), pre...  45.6 us
    dot_general x2, matrix products, analyse_yz(): jnp.einsum('qp,bxtcp->bxtcq', yz_table, spatial.astype(jnp.float32), prec...  44.2 us
    psum x1, blocking collectives, body(): total_point, total_bias = lax.psum((local_point, local_bias), ('gx', 'ta'))  41 us
    another operation x8, local copies, waits for them, and re-layouts  35.1 us
    mul x2, other arithmetic, joint_table(): joined = first_table[:, None, :, None] * second_table[None, :, None, :]  32.8 us
    all_to_all x1, blocking collectives, body(): lax.all_to_all(xt_out[:, :, :, :, None, None, :], 'gx', split_axis=1, con...  29.8 us
  transfers between devices with their start and end apart: 5, of which 3 were waited for; matrix products, arithmetic and copies ran while one was open for 9% of the time, Pallas kernels for 0%

commit v1 on v0

v1 whole, which is shorter than its diff:
```python
import functools
import math

import jax
import jax.numpy as jnp
import ml_dtypes
import numpy as np
from jax import lax
from jax.experimental import pallas as pl
from jax.experimental.pallas import tpu as pltpu
from jax.sharding import PartitionSpec as P

NX = 128
NY = 128
NZ = 32
NT = 16
MX = 16
MY = 16
MZ = 16
MT = 8
BATCH = 1
KX = 32
KT = 16
CHANS = 8
CELLS = NY * NZ
KQ = 1024
LANES = 128
F32 = jnp.float32
BF16 = jnp.bfloat16


def basis(length, modes):
    frequency = np.concatenate([np.arange(modes + 1), np.arange(1, modes)])
    samples_at = np.arange(length)
    phases = (2.0 * math.pi / length) * (frequency[:, None] * samples_at[None, :] % length)
    cosine_row = np.arange(2 * modes) <= modes
    waves = np.where(cosine_row[:, None], np.cos(phases), np.sin(phases))
    at_edge = cosine_row & ((frequency == 0) | (2 * frequency == length))
    scales = np.where(at_edge, math.sqrt(1.0 / length), math.sqrt(2.0 / length))
    return (waves * scales[:, None]).astype(np.float32)


def narrow(table):
    return np.asarray(table, np.float32).astype(ml_dtypes.bfloat16)


def vmem_params(mebibytes):
    return pltpu.CompilerParams(vmem_limit_bytes=mebibytes * 1024 * 1024)


def matmul(left, right):
    return jnp.dot(left, right, preferred_element_type=F32)


def swap_groups(tiles):
    rows = tiles[0].shape[0]
    lane = lax.broadcasted_iota(jnp.int32, (rows, LANES), 1)
    low_half = lane < 64
    even = (lane // 32) % 2 == 0
    first, second, third, fourth = tiles
    b0 = jnp.where(low_half, first, pltpu.roll(third, 64, 1))
    b2 = jnp.where(low_half, pltpu.roll(first, 64, 1), third)
    b1 = jnp.where(low_half, second, pltpu.roll(fourth, 64, 1))
    b3 = jnp.where(low_half, pltpu.roll(second, 64, 1), fourth)
    return (
        jnp.where(even, b0, pltpu.roll(b1, 32, 1)),
        jnp.where(even, pltpu.roll(b0, 96, 1), b1),
        jnp.where(even, b2, pltpu.roll(b3, 32, 1)),
        jnp.where(even, pltpu.roll(b2, 96, 1), b3),
    )


def pack_modes(modes, packed_ref, xl, tl):
    width = modes.shape[1]
    split = modes.reshape(xl, tl, CHANS, width)
    for tile in range(width // LANES):
        at = slice(tile * LANES, (tile + 1) * LANES)
        tiles = [split[:, step, :, at].reshape(xl * CHANS, LANES) for step in range(tl)]
        for owner, block in enumerate(swap_groups(tiles)):
            packed_ref[tile * tl + owner] = block.astype(BF16)


def unpack_modes(packed_ref, wide_ref, xl, tl):
    for tile in range(KQ // LANES):
        tiles = [packed_ref[tile * tl + owner].astype(F32) for owner in range(tl)]
        for step, block in enumerate(swap_groups(tiles)):
            wide_ref[:, step, :, tile * LANES : (tile + 1) * LANES] = block.reshape(
                xl, CHANS, LANES
            )


def analyse_kernel(xl, tl, field_ref, table_ref, packed_ref):
    pack_modes(matmul(field_ref[...], table_ref[...]), packed_ref, xl, tl)


def analyse(field, table, xl, tl, devices):
    rows = field.shape[0]
    steps = 4
    width = KQ // steps
    return pl.pallas_call(
        functools.partial(analyse_kernel, xl, tl),
        grid=(steps,),
        in_specs=[
            pl.BlockSpec((rows, CELLS), lambda n: (0, 0)),
            pl.BlockSpec((CELLS, width), lambda n: (0, n)),
        ],
        out_specs=pl.BlockSpec((devices // steps, LANES, LANES), lambda n: (n, 0, 0)),
        out_shape=jax.ShapeDtypeStruct((devices, LANES, LANES), BF16),
        compiler_params=vmem_params(48),
        cost_estimate=pl.CostEstimate(
            flops=2 * rows * CELLS * KQ, bytes_accessed=13 << 20, transcendentals=0
        ),
        name="analyse",
    )(field, table)


def weight_kernel(weight_ref, packed_ref):
    for kx in range(weight_ref.shape[0]):
        for group in range(KT // 4):
            parts = [weight_ref[kx, 4 * group + k] for k in range(4)]
            packed_ref[kx, :, :, group * LANES : (group + 1) * LANES] = jnp.concatenate(
                parts, axis=-1
            )


def pack_weight(weight):
    per = 4
    own = weight.shape[4]
    return pl.pallas_call(
        weight_kernel,
        grid=(KX // per,),
        in_specs=[pl.BlockSpec((per, KT, CHANS, CHANS, own), lambda n: (n, 0, 0, 0, 0))],
        out_specs=pl.BlockSpec((per, CHANS, CHANS, KT * own), lambda n: (n, 0, 0, 0)),
        out_shape=jax.ShapeDtypeStruct((KX, CHANS, CHANS, KT * own), F32),
        compiler_params=vmem_params(24),
        cost_estimate=pl.CostEstimate(flops=1 << 20, bytes_accessed=20 << 20, transcendentals=0),
        name="pack_weight",
    )(weight)


def to_modes(spread_ref, x_table_ref, t_table_ref):
    gx, ta = spread_ref.shape[:2]
    beside = jnp.concatenate(
        [spread_ref[:, at].reshape(gx * LANES, LANES) for at in range(ta)], axis=1
    )
    half = matmul(x_table_ref[...], beside).astype(BF16)
    return matmul(half, t_table_ref[...])


def from_modes(modes, x_table_ref, t_table_ref, spread_ref):
    gx, ta = spread_ref.shape[:2]
    half = matmul(modes.astype(BF16), t_table_ref[...]).astype(BF16)
    full = matmul(x_table_ref[...], half).astype(BF16)
    for at in range(ta):
        spread_ref[:, at] = full[:, at * LANES : (at + 1) * LANES].reshape(gx, LANES, LANES)


def mix_kernel(
    spread_ref, weight_ref, x_in_ref, t_in_ref, x_out_ref, t_out_ref, spectrum_ref, back_ref, mixed
):
    spectrum_ref[...] = to_modes(spread_ref, x_in_ref, t_in_ref)
    for kx in range(KX):
        rows = slice(kx * CHANS, (kx + 1) * CHANS)
        own = spectrum_ref[rows, :]
        total = own[0:1, :] * weight_ref[kx, 0]
        for i in range(1, CHANS):
            total = total + own[i : i + 1, :] * weight_ref[kx, i]
        mixed[rows, :] = total
    from_modes(mixed[...], x_out_ref, t_out_ref, back_ref)


def mix_back_kernel(
    spread_ref, weight_ref, x_in_ref, t_in_ref, x_out_ref, t_out_ref, grad_ref, back_ref, mixed
):
    grad_ref[...] = to_modes(spread_ref, x_in_ref, t_in_ref)
    for kx in range(KX):
        rows = slice(kx * CHANS, (kx + 1) * CHANS)
        own = grad_ref[rows, :]
        sums = [
            jnp.sum(own * weight_ref[kx, i], axis=0, keepdims=True) for i in range(CHANS)
        ]
        mixed[rows, :] = jnp.concatenate(sums, axis=0)
    from_modes(mixed[...], x_out_ref, t_out_ref, back_ref)


def mix(kernel, spread, weight, tables, name):
    modes = (KX * CHANS, weight.shape[3])
    return pl.pallas_call(
        kernel,
        out_shape=(
            jax.ShapeDtypeStruct(modes, F32),
            jax.ShapeDtypeStruct(spread.shape, BF16),
        ),
        in_specs=[pl.BlockSpec(memory_space=pltpu.VMEM)] * 6,
        out_specs=[pl.BlockSpec(memory_space=pltpu.VMEM)] * 2,
        scratch_shapes=[pltpu.VMEM(modes, F32)],
        compiler_params=vmem_params(32),
        cost_estimate=pl.CostEstimate(flops=1 << 30, bytes_accessed=9 << 20, transcendentals=0),
        name=name,
    )(spread, weight, *tables)


def outer_kernel(spectrum_ref, grad_ref, result_ref):
    own = result_ref.shape[4]
    for kx in range(result_ref.shape[0]):
        rows = slice(kx * CHANS, (kx + 1) * CHANS)
        for group in range(KT // 4):
            at = slice(group * LANES, (group + 1) * LANES)
            inputs = spectrum_ref[rows, at]
            grads = grad_ref[rows, at]
            for i in range(CHANS):
                product = inputs[i : i + 1, :] * grads
                for k in range(4):
                    result_ref[kx, 4 * group + k, i] = product[:, k * own : (k + 1) * own]


def outer(spectrum, grad, own):
    per = 4
    width = KT * own
    return pl.pallas_call(
        outer_kernel,
        grid=(KX // per,),
        in_specs=[pl.BlockSpec((per * CHANS, width), lambda n: (n, 0))] * 2,
        out_specs=pl.BlockSpec((per, KT, CHANS, CHANS, own), lambda n: (n, 0, 0, 0, 0)),
        out_shape=jax.ShapeDtypeStruct((KX, KT, CHANS, CHANS, own), F32),
        compiler_params=vmem_params(24),
        cost_estimate=pl.CostEstimate(flops=1 << 20, bytes_accessed=17 << 20, transcendentals=0),
        name="outer",
    )(spectrum, grad)


def normal_parts(values):
    t = 1.0 / (1.0 + 0.2316419 * jnp.abs(values))
    density = jnp.exp(-0.5 * values * values) * 0.3989422804014327
    series = 1.330274429 * t - 1.821255978
    series = series * t + 1.781477937
    series = series * t - 0.356563782
    series = series * t + 0.319381530
    tail = density * (series * t)
    return jnp.where(values >= 0.0, 1.0 - tail, tail), density


def middle_kernel(
    xl,
    tl,
    packed_ref,
    field_ref,
    cotangent_ref,
    build_ref,
    analyse_ref,
    mixer_ref,
    bias_ref,
    output_ref,
    grad_ref,
    sent_ref,
    sums_ref,
    wide,
    modes,
    pre,
    total,
    gram,
    row_sums,
):
    step = pl.program_id(0)
    rows = field_ref.shape[0]
    half = mixer_ref.shape[0]

    @pl.when(step == 0)
    def _():
        unpack_modes(packed_ref, wide, xl, tl)
        modes[...] = wide[...].reshape(rows, KQ).astype(BF16)
        total[...] = jnp.zeros_like(total)
        gram[...] = jnp.zeros_like(gram)
        row_sums[...] = jnp.zeros_like(row_sums)

    pre[...] = matmul(modes[...], build_ref[...])
    for at in range(rows // half):
        part = slice(at * half, (at + 1) * half)
        pre[part, :] += matmul(mixer_ref[...], field_ref[part, :])

    chunk = 16

    def pointwise(index, carry):
        part = pl.ds(pl.multiple_of(index * chunk, chunk), chunk)
        values = pre[part, :] + bias_ref[part, 0:1]
        integral, density = normal_parts(values)
        output_ref[part, :] = (values * integral).astype(BF16)
        slope = integral + values * density
        grad = (cotangent_ref[part, :].astype(F32) * slope).astype(BF16)
        grad_ref[part, :] = grad
        wide_grad = grad.astype(F32)
        sums = row_sums[part, :]
        for tile in range(wide_grad.shape[1] // LANES):
            sums = sums + wide_grad[:, tile * LANES : (tile + 1) * LANES]
        row_sums[part, :] = sums
        return carry

    lax.fori_loop(0, rows // chunk, pointwise, 0)

    total[...] += matmul(grad_ref[...], analyse_ref[...])
    for at in range(rows // half):
        part = slice(at * half, (at + 1) * half)
        gram[...] += lax.dot_general(
            grad_ref[part, :],
            field_ref[part, :],
            (((1,), (1,)), ((), ())),
            preferred_element_type=F32,
        )

    @pl.when(step == pl.num_programs(0) - 1)
    def _():
        pack_modes(total[...], sent_ref, xl, tl)
        row = lax.broadcasted_iota(jnp.int32, (half, half), 0)
        column = lax.broadcasted_iota(jnp.int32, (half, half), 1)
        same = jnp.where(row // CHANS == column // CHANS, gram[...], 0.0)
        folded = jnp.sum(same.reshape(half // CHANS, CHANS, half), axis=0)
        source = lax.broadcasted_iota(jnp.int32, (half, LANES), 0)
        target = lax.broadcasted_iota(jnp.int32, (half, LANES), 1)
        select = jnp.where(source % CHANS == target, 1.0, 0.0)
        point = jnp.dot(
            folded, select, precision=lax.Precision.HIGHEST, preferred_element_type=F32
        )
        bias = jnp.sum(
            jnp.sum(row_sums[...].reshape(rows // CHANS, CHANS, LANES), axis=0),
            axis=1,
            keepdims=True,
        )
        lane = lax.broadcasted_iota(jnp.int32, (CHANS, LANES), 1)
        sums_ref[...] = jnp.where(lane == CHANS, bias, point)


def middle(packed, field, cotangent, build_table, analyse_table, mixer, bias, xl, tl):
    rows = field.shape[0]
    width = 512
    steps = CELLS // width
    half = mixer.shape[0]
    whole = lambda *shape: pl.BlockSpec(shape, lambda n: (0,) * len(shape))
    tile = pl.BlockSpec((rows, width), lambda n: (0, n))
    return pl.pallas_call(
        functools.partial(middle_kernel, xl, tl),
        grid=(steps,),
        in_specs=[
            whole(*packed.shape),
            tile,
            tile,
            pl.BlockSpec((KQ, width), lambda n: (0, n)),
            pl.BlockSpec((width, KQ), lambda n: (n, 0)),
            whole(half, half),
            whole(rows, LANES),
        ],
        out_specs=[tile, tile, whole(*packed.shape), whole(CHANS, LANES)],
        out_shape=(
            jax.ShapeDtypeStruct((rows, CELLS), BF16),
            jax.ShapeDtypeStruct((rows, CELLS), BF16),
            jax.ShapeDtypeStruct(packed.shape, BF16),
            jax.ShapeDtypeStruct((CHANS, LANES), F32),
        ),
        scratch_shapes=[
            pltpu.VMEM((xl, tl, CHANS, KQ), F32),
            pltpu.VMEM((rows, KQ), BF16),
            pltpu.VMEM((rows, width), F32),
            pltpu.VMEM((rows, KQ), F32),
            pltpu.VMEM((half, half), F32),
            pltpu.VMEM((rows, LANES), F32),
        ],
        compiler_params=vmem_params(48),
        cost_estimate=pl.CostEstimate(
            flops=5 * rows * CELLS * KQ, bytes_accessed=34 << 20, transcendentals=rows * CELLS
        ),
        name="middle",
    )(packed, field, cotangent, build_table, analyse_table, mixer, bias)


def last_kernel(xl, tl, packed_ref, grad_ref, build_ref, mixer_ref, field_ref, wide, modes):
    rows = grad_ref.shape[0]
    half = mixer_ref.shape[0]

    @pl.when(pl.program_id(0) == 0)
    def _():
        unpack_modes(packed_ref, wide, xl, tl)
        modes[...] = wide[...].reshape(rows, KQ).astype(BF16)

    for at in range(rows // half):
        part = slice(at * half, (at + 1) * half)
        field_ref[part, :] = (
            matmul(modes[part, :], build_ref[...]) + matmul(mixer_ref[...], grad_ref[part, :])
        ).astype(BF16)


def last(packed, grad, build_table, mixer, xl, tl):
    rows = grad.shape[0]
    width = 512
    half = mixer.shape[0]
    tile = pl.BlockSpec((rows, width), lambda n: (0, n))
    return pl.pallas_call(
        functools.partial(last_kernel, xl, tl),
        grid=(CELLS // width,),
        in_specs=[
            pl.BlockSpec(packed.shape, lambda n: (0, 0, 0)),
            tile,
            pl.BlockSpec((KQ, width), lambda n: (0, n)),
            pl.BlockSpec((half, half), lambda n: (0, 0)),
        ],
        out_specs=tile,
        out_shape=jax.ShapeDtypeStruct((rows, CELLS), BF16),
        scratch_shapes=[
            pltpu.VMEM((xl, tl, CHANS, KQ), F32),
            pltpu.VMEM((rows, KQ), BF16),
        ],
        compiler_params=vmem_params(32),
        cost_estimate=pl.CostEstimate(
            flops=2 * rows * CELLS * KQ, bytes_accessed=18 << 20, transcendentals=0
        ),
        name="last",
    )(packed, grad, build_table, mixer)


def swap(blocks):
    return lax.all_to_all(blocks, ("gx", "ta"), split_axis=0, concat_axis=0, tiled=True)


def fast_body(gx, ta, features, cotangent, spec_weight, point_weight, bias_vector):
    _, xl, tl, _, cells = features.shape
    own = spec_weight.shape[4]
    devices = gx * ta
    rows = xl * tl * CHANS
    yz = np.kron(
        narrow(basis(NY, MY)).astype(np.float32), narrow(basis(NZ, MZ)).astype(np.float32)
    )
    build_table = jnp.asarray(narrow(yz))
    analyse_table = jnp.asarray(narrow(yz.T))
    x_wide = np.kron(basis(NX, MX), np.eye(CHANS))
    t_wide = np.kron(basis(NT, MT), np.eye(own))
    x_in, x_out = jnp.asarray(narrow(x_wide)), jnp.asarray(narrow(x_wide.T))
    t_in, t_out = jnp.asarray(narrow(t_wide.T)), jnp.asarray(narrow(t_wide))
    tables = (x_in, t_in, x_out, t_out)
    norm_scale = float(BATCH * NX * NT * NY * NZ) ** (-0.5)

    field = features.reshape(rows, cells)
    packed_weight = pack_weight(spec_weight)
    group = rows // 2
    eye = jnp.asarray(np.eye(group // CHANS), BF16)
    mixer = jnp.kron(eye, point_weight)
    mixer_back = jnp.kron(eye, point_weight.T)
    bias = jnp.broadcast_to(jnp.tile(bias_vector, xl * tl)[:, None], (rows, LANES))

    spread_shape = (gx, ta, LANES, LANES)
    spread_in = swap(analyse(field, analyse_table, xl, tl, devices)).reshape(spread_shape)
    spectrum, mixed = mix(mix_kernel, spread_in, packed_weight, tables, "mix")
    returned = swap(mixed.reshape(devices, LANES, LANES))
    output, grad_pre, sent, sums = middle(
        returned,
        field,
        cotangent.reshape(rows, cells),
        build_table,
        analyse_table,
        mixer,
        bias,
        xl,
        tl,
    )
    gathered = lax.all_gather(sums, ("gx", "ta"))
    spread_grad = swap(sent).reshape(spread_shape)
    grad_modes, mixed_back = mix(mix_back_kernel, spread_grad, packed_weight, tables, "mix_back")
    grad_back = swap(mixed_back.reshape(devices, LANES, LANES))
    grad_spec = outer(spectrum, grad_modes, own)
    grad_field = last(grad_back, grad_pre, build_table, mixer_back, xl, tl)
    summed = jnp.sum(gathered, axis=0) * norm_scale
    return (
        output.reshape(features.shape),
        grad_field.reshape(features.shape),
        grad_spec,
        summed[:, :CHANS],
        summed[:, CHANS],
    )


def analyse_yz(spatial, yz_table):
    return jnp.einsum(
        "qp,bxtcp->bxtcq", yz_table, spatial.astype(F32), precision=lax.Precision.HIGHEST
    )


def build_yz(modes_in, yz_table):
    return jnp.einsum(
        "qp,bxtcq->bxtcp", yz_table, modes_in.astype(F32), precision=lax.Precision.HIGHEST
    )


def analyse_xt(spread, table):
    sizes = spread.shape
    flattened = spread.reshape(sizes[0], sizes[1] * sizes[2], sizes[3] * sizes[4]).astype(F32)
    spectral = jnp.einsum("mp,bpr->bmr", table, flattened, precision=lax.Precision.HIGHEST)
    return spectral.reshape(sizes[0], KX, KT, sizes[3], sizes[4])


def synthesise_xt(modes_in, table):
    sizes = modes_in.shape
    flattened = modes_in.reshape(sizes[0], sizes[1] * sizes[2], sizes[3] * sizes[4])
    spatial = jnp.einsum("mp,bmr->bpr", table, flattened, precision=lax.Precision.HIGHEST)
    return spatial.reshape(sizes[0], NX, NT, sizes[3], sizes[4])


def to_owners(modes_in):
    first = lax.all_to_all(modes_in, "gx", split_axis=4, concat_axis=1, tiled=True)
    return lax.all_to_all(first, "ta", split_axis=4, concat_axis=2, tiled=True)


def to_cells(spread, shape):
    first = lax.all_to_all(
        spread[:, :, :, :, None, None, :], "gx", split_axis=1, concat_axis=4, tiled=True
    )
    second = lax.all_to_all(first, "ta", split_axis=2, concat_axis=5, tiled=True)
    return second.reshape(shape[:4] + (-1,))


def general_body(features, cotangent, spec_weight, point_weight, bias_vector):
    shape = features.shape
    yz_table = jnp.asarray(
        np.kron(narrow(basis(NY, MY)).astype(np.float32), narrow(basis(NZ, MZ)).astype(np.float32))
    )
    xt_table = jnp.asarray(np.kron(basis(NX, MX), basis(NT, MT)))
    norm_scale = float(BATCH * NX * NT * NY * NZ) ** (-0.5)
    highest = lax.Precision.HIGHEST
    spectrum = analyse_xt(to_owners(analyse_yz(features, yz_table).astype(BF16)), xt_table)
    mixed = jnp.einsum("bklip,kliop->bklop", spectrum, spec_weight, precision=highest)
    returned = to_cells(synthesise_xt(mixed, xt_table).astype(BF16), shape)
    pointwise = jnp.einsum("oi,bxtip->bxtop", point_weight, features, preferred_element_type=F32)
    pre = build_yz(returned, yz_table) + pointwise + bias_vector[:, None]
    integral = 0.5 * (1.0 + jax.scipy.special.erf(pre * 0.7071067811865476))
    output = (pre * integral).astype(BF16)
    slope = integral + pre * jnp.exp(-0.5 * pre * pre) * 0.3989422804014327
    grad_pre = (cotangent.astype(F32) * slope).astype(BF16)
    local_point = jnp.einsum("bxtop,bxtip->oi", grad_pre, features, preferred_element_type=F32)
    local_bias = jnp.sum(grad_pre.astype(F32), axis=(0, 1, 2, 4))
    total_point, total_bias = lax.psum((local_point, local_bias), ("gx", "ta"))
    grad_modes = analyse_xt(to_owners(analyse_yz(grad_pre, yz_table).astype(BF16)), xt_table)
    grad_spec = jnp.einsum("bklip,bklop->kliop", spectrum, grad_modes, precision=highest)
    grad_in = jnp.einsum("kliop,bklop->bklip", spec_weight, grad_modes, precision=highest)
    grad_back = to_cells(synthesise_xt(grad_in, xt_table).astype(BF16), shape)
    point_term = jnp.einsum("oi,bxtop->bxtip", point_weight, grad_pre, preferred_element_type=F32)
    grad_field = (build_yz(grad_back, yz_table) + point_term).astype(BF16)
    return (output, grad_field, grad_spec, total_point * norm_scale, total_bias * norm_scale)


def solution(mesh):
    split_field = P(None, "gx", "ta", None, None)
    split_weight = P(None, None, None, None, ("gx", "ta"))
    in_specs = (split_field, split_field, split_weight, P(), P())
    out_specs = (split_field, split_field, split_weight, P(), P())
    gx, ta = mesh.shape["gx"], mesh.shape["ta"]
    own, xl, tl = KQ // (gx * ta), NX // gx, NT // ta
    if own == 32 and xl * CHANS == LANES and tl == 4:
        body = functools.partial(fast_body, gx, ta)
    else:
        body = general_body
    return jax.shard_map(body, mesh=mesh, in_specs=in_specs, out_specs=out_specs, check_vma=False)
```

time: 702 us -> 243 us (0.35); the launches traced: 691 us -> 242 us
  local copies, waits for them, and re-layouts: 319 us -> 28.6 us
  matrix products: 133 us -> 0 us
  Pallas kernels: 0 us -> 83.3 us
  other arithmetic: 59.7 us -> 2.39 us
  blocking collectives: 117 us -> 78.1 us
  starting transfers between devices: 22.3 us -> 14.7 us
    dot_general x11 -> x0, matrix products: 133 us -> none  [the longest x2 45.6 us: build_yz(): jnp.einsum('qp,bxtcq->bxtcp', yz_table, modes_in.astype(jnp.float32), pre...]
    pallas_call x0 -> x7, Pallas kernels: none -> 83.3 us  [the longest x1 49 us: middle(): pl.pallas_call(functools.partial(middle_kernel, xl, tl), grid=(steps,), i...]
    all_to_all x16 -> x0, local copies, waits for them, and re-layouts: 80 us -> none  [the longest x2 13.1 us: body(): lax.all_to_all(lax.all_to_all(xt_out[:, :, :, :, None, None, :], 'gx', sp...]
    unnamed x18 -> x36, local copies, waits for them, and re-layouts: 93.6 us -> 19.5 us
    mul x2, local copies, waits for them, and re-layouts: 75.7 us -> 8.11 us  [the longest x1 4.06 us: fast_body(): mixer_back = jnp.kron(eye, point_weight.T)]
    all_gather x0 -> x1, blocking collectives: none -> 48.4 us  [fast_body(): gathered = lax.all_gather(sums, ('gx', 'ta'))]
    all_to_all x3 -> x1, blocking collectives: 76.3 us -> 29.7 us  [swap(): lax.all_to_all(blocks, ('gx', 'ta'), split_axis=0, concat_axis=0, tiled=T...]
    psum x1 -> x0, blocking collectives: 41 us -> none  [body(): total_point, total_bias = lax.psum((local_point, local_bias), ('gx', 'ta'))]
  transfers between devices with their start and end apart: 5 -> 3, of which waited for: 3 -> 2; matrix products, arithmetic and copies ran while one was open for 9% -> 5% of each run, Pallas kernels for 0% -> 5%
where the time goes in v1:
time: 243 us; the launch traced here: 242 us
  Pallas kernels  83.3 us (34%)
  blocking collectives  78.1 us (32%)
  waiting for transfers between devices  34.2 us (14%)
  local copies, waits for them, and re-layouts  28.6 us (12%)
  starting transfers between devices  14.7 us (6%)
    pallas_call x1, Pallas kernels, middle(): pl.pallas_call(functools.partial(middle_kernel, xl, tl), grid=(steps,), i...  49 us
    all_gather x1, blocking collectives, fast_body(): gathered = lax.all_gather(sums, ('gx', 'ta'))  48.4 us
    all_to_all x3, waiting for transfers between devices, swap(): lax.all_to_all(blocks, ('gx', 'ta'), split_axis=0, concat_axis=0, tiled=T...  34.2 us
    all_to_all x1, blocking collectives, swap(): lax.all_to_all(blocks, ('gx', 'ta'), split_axis=0, concat_axis=0, tiled=T...  29.7 us
    unnamed x36, local copies, waits for them, and re-layouts  19.5 us
    all_to_all x3, starting transfers between devices, swap(): lax.all_to_all(blocks, ('gx', 'ta'), split_axis=0, concat_axis=0, tiled=T...  14.7 us
    pallas_call x1, Pallas kernels, last(): pl.pallas_call(functools.partial(last_kernel, xl, tl), grid=(CELLS // wid...  9.68 us
    pallas_call x1, Pallas kernels, analyse(): pl.pallas_call(functools.partial(analyse_kernel, xl, tl), grid=(steps,),...  8.31 us
  transfers between devices with their start and end apart: 3, of which 2 were waited for; matrix products, arithmetic and copies ran while one was open for 5% of the time, Pallas kernels for 5%

profile of v1, /device:TPU:0, one launch (start us, length us, event | category | flops | bytes accessed | tf_op | source)
XLA Modules:
  0.0 242.2 jit_solution(6560688183616684408)
XLA Ops:
  0.6 0.0 copy-start.13
  0.6 2.2 copy-done.13
  2.8 8.3 %analyse.1 = bf16[32,128,128]{2,1,0:T(8,128)(2,1)} custom-call(bf16[512,4096]{1,0:T(8,128)(2,1)S(1)} %bitcast.20, bf16[4096,1024]{1,0:T(8,128)(2,1)} %constant.19.clone.table_ref.analyse_ref), custom_call_target="tpu_custom_call" | custom-call | flops 4294967296 | bytes 13631488 | tf_op jit(solution)/shard_map/analyse/pallas_call | solution.py:100
  11.1 7.3 %all-to-all-start = ((bf16[32,128,128]{2,1,0:T(8,128)(2,1)}), bf16[32,128,128]{2,1,0:T(8,128)(2,1)S(1)}, u32[]{:S(2)}, u32[]{:S(2)}) async-start(bf16[32,128,128]{2,1,0:T(8,128)(2,1)} %analyse.1), calls=%async_computation | async-start | bytes 2097152 | tf_op jit(solution)/shard_map/all_to_all | solution.py:419
  18.4 0.0 copy-start.3
  18.5 5.8 %copy-done.3 = f32[32,16,8,8,32]{4,3,2,1,0:T(8,128)S(1)} copy-done((f32[32,16,8,8,32]{4,3,2,1,0:T(8,128)S(1)}, f32[32,16,8,8,32]{4,3,2,1,0:T(8,128)}, u32[]{:S(2)}) %copy-start.3) | copy-done | bytes 4194328
  24.2 3.8 %pack_weight.1.weight_ref = f32[32,8,8,512]{3,2,1,0:T(8,128)S(1)} custom-call(f32[32,16,8,8,32]{4,3,2,1,0:T(8,128)S(1)} %copy-done.3), custom_call_target="tpu_custom_call" | custom-call | flops 1048576 | bytes 20971520 | tf_op jit(solution)/shard_map/pack_weight/pallas_call | solution.py:129
  28.1 0.0 copy-start
  28.1 2.0 copy-done
  30.1 14.6 %all-to-all-done = bf16[32,128,128]{2,1,0:T(8,128)(2,1)S(1)} async-done(((bf16[32,128,128]{2,1,0:T(8,128)(2,1)}), bf16[32,128,128]{2,1,0:T(8,128)(2,1)S(1)}, u32[]{:S(2)}, u32[]{:S(2)}) %all-to-all-start) | async-done | bytes 1048608 | tf_op jit(solution)/shard_map/all_to_all | solution.py:419
  44.7 2.2 copy-done.1
  46.9 1.5 mix.1
  48.5 1.0 copy-done.10
  49.4 0.8 copy-done.11
  50.3 3.6 %all-to-all-start.1 = ((bf16[32,128,128]{2,1,0:T(8,128)(2,1)}), bf16[32,128,128]{2,1,0:T(8,128)(2,1)S(1)}, u32[]{:S(2)}, u32[]{:S(2)}) async-start(bf16[32,128,128]{2,1,0:T(8,128)(2,1)} %bitcast.18), calls=%async_computation.1 | async-start | bytes 2097152 | tf_op jit(solution)/shard_map/all_to_all | solution.py:419
  53.9 0.1 copy.18
  54.0 2.4 broadcast_multiply_fusion
  56.3 4.1 %mul.48.mixer_ref = bf16[256,256]{1,0:T(8,128)(2,1)S(1)} reshape(bf16[32,8,32,8]{3,2,1,0:T(8,128)(2,1)} %get-tuple-element.22) | data formatting | bytes 262144 | tf_op jit(solution)/shard_map/jit(kron)/mul | solution.py:443
  60.4 0.1 broadcast_in_dim.13
  60.5 19.6 %all-to-all-done.1.packed_ref = bf16[32,128,128]{2,1,0:T(8,128)(2,1)S(1)} async-done(((bf16[32,128,128]{2,1,0:T(8,128)(2,1)}), bf16[32,128,128]{2,1,0:T(8,128)(2,1)S(1)}, u32[]{:S(2)}, u32[]{:S(2)}) %all-to-all-start.1) | async-done | bytes 1048608 | tf_op jit(solution)/shard_map/all_to_all | solution.py:419
  80.1 0.1 broadcast_in_dim.14.bias_ref
  80.2 49.0 %middle.1 = (bf16[512,4096]{1,0:T(8,128)(2,1)}, bf16[512,4096]{1,0:T(8,128)(2,1)}, bf16[32,128,128]{2,1,0:T(8,128)(2,1)S(1)}, f32[8,128]{1,0:T(8,128)S(1)}) custom-call(bf16[32,128,128]{2,1,0:T(8,128)(2,1)S(1)} %all-to-all-done.1.packed_ref, bf16[512,4096]{1,0:T(8,128)(2,1)} %bitcast.19, bf16[512,4096]{1,0:T(8,128)(2,1)} %bitcast.24, ...), custom_call_target="tpu_custom_call" | custom-call | flops 10737418240 | bytes 35651584 | tf_op jit(solution)/shard_map/middle/pallas_call | solution.py:339
  129.2 29.7 %all_to_all.20 = bf16[32,128,128]{2,1,0:T(8,128)(2,1)S(1)} all-to-all(bf16[32,128,128]{2,1,0:T(8,128)(2,1)S(1)} %get-tuple-element.15), channel_id=1, replica_groups=mesh['gx'=8,'ta'=4] {'gx','ta'}, dimensions={0} | all-to-all | bytes 2097152 | tf_op jit(solution)/shard_map/all_to_all | solution.py:419
  158.9 3.2 %mix_back.1 = (f32[256,512]{1,0:T(8,128)S(1)}, bf16[8,4,128,128]{3,2,1,0:T(8,128)(2,1)}) custom-call(bf16[8,4,128,128]{3,2,1,0:T(8,128)(2,1)S(1)} %bitcast.17, f32[32,8,8,512]{3,2,1,0:T(8,128)S(1)} %copy-done.2, bf16[256,1024]{1,0:T(8,128)(2,1)S(1)} %copy-done.6, bf16[512,512]{1,0:T(8,128)(2,1)S(1)} %copy-done.8, bf16[1024,256]{1,0:T(8,128)(2,1)S(1)} %copy-done.7, ...), custom_call_target="tpu_custom_call" | custom-call | flops 1073741824 | bytes 9437184 | tf_op jit(solution)/shard_map/mix_back/pallas_call | solution.py:188
  162.0 3.8 %all-to-all-start.3 = ((bf16[32,128,128]{2,1,0:T(8,128)(2,1)}), bf16[32,128,128]{2,1,0:T(8,128)(2,1)S(1)}, u32[]{:S(2)}, u32[]{:S(2)}) async-start(bf16[32,128,128]{2,1,0:T(8,128)(2,1)} %bitcast.6), calls=%async_computation.3 | async-start | bytes 2097152 | tf_op jit(solution)/shard_map/all_to_all | solution.py:419
  165.8 4.1 %mul.51.mixer_ref = bf16[256,256]{1,0:T(8,128)(2,1)S(1)} reshape(bf16[32,8,32,8]{3,2,1,0:T(8,128)(2,1)} %get-tuple-element.21) | data formatting | bytes 262144 | tf_op jit(solution)/shard_map/jit(kron)/mul | solution.py:444
  169.9 48.4 %all-gather = f32[256,128]{1,0:T(8,128)S(1)} all-gather(f32[8,128]{1,0:T(8,128)S(1)} %get-tuple-element.20), channel_id=2, replica_groups=mesh['gx'=8,'ta'=4] {'gx','ta'}, dimensions={0}, use_global_device_ids=true | all-gather | bytes 135168 | tf_op jit(solution)/shard_map/all_gather | solution.py:462
  218.4 0.7 slice_reduce_fusion
  219.1 7.9 %outer.1 = f32[32,16,8,8,32]{4,3,2,1,0:T(8,128)} custom-call(f32[256,512]{1,0:T(8,128)S(1)} %copy-done.12, f32[256,512]{1,0:T(8,128)S(1)} %get-tuple-element.19.grad_ref), custom_call_target="tpu_custom_call" | custom-call | flops 1048576 | bytes 17825792 | tf_op jit(solution)/shard_map/outer/pallas_call | solution.py:220
  227.0 3.4 %copy-done.4 = bf16[1024,4096]{1,0:T(8,128)(2,1)S(1)} copy-done((bf16[1024,4096]{1,0:T(8,128)(2,1)S(1)}, bf16[1024,4096]{1,0:T(8,128)(2,1)}, u32[]{:S(2)}) %copy-start.4) | copy-done | bytes 8388632
  230.3 2.2 copy-done.5
  232.5 9.7 %last.1 = bf16[512,4096]{1,0:T(8,128)(2,1)} custom-call(bf16[32,128,128]{2,1,0:T(8,128)(2,1)S(1)} %all-to-all-done.3.packed_ref, bf16[512,4096]{1,0:T(8,128)(2,1)S(1)} %copy-done.5, bf16[1024,4096]{1,0:T(8,128)(2,1)S(1)} %copy-done.4, bf16[256,256]{1,0:T(8,128)(2,1)S(1)} %mul.51.mixer_ref), custom_call_target="tpu_custom_call" | custom-call | flops 4294967296 | bytes 18874368 | tf_op jit(solution)/shard_map/last/pallas_call | solution.py:395
  (29 shorter events, 0.1 us)
Async XLA Ops:
  0.6 2.2 copy-start.13
  11.1 33.5 %all-to-all-start = ((bf16[32,128,128]{2,1,0:T(8,128)(2,1)}), bf16[32,128,128]{2,1,0:T(8,128)(2,1)S(1)}, u32[]{:S(2)}, u32[]{:S(2)}) async-start(bf16[32,128,128]{2,1,0:T(8,128)(2,1)} %analyse.1), calls=%async_computation | async-start | bytes 2097152 | tf_op jit(solution)/shard_map/all_to_all | solution.py:419
  18.4 5.8 %copy-start.3 = (f32[32,16,8,8,32]{4,3,2,1,0:T(8,128)S(1)}, f32[32,16,8,8,32]{4,3,2,1,0:T(8,128)}, u32[]{:S(2)}) copy-start(f32[32,16,8,8,32]{4,3,2,1,0:T(8,128)} %weight_ref.1) | copy-start | bytes 12582916
  24.2 20.5 %copy-start.6 = (bf16[256,1024]{1,0:T(8,128)(2,1)S(1)}, bf16[256,1024]{1,0:T(8,128)(2,1)}, u32[]{:S(2)}) copy-start(bf16[256,1024]{1,0:T(8,128)(2,1)} %constant.20.clone.x_in_ref) | copy-start | bytes 1572868
  24.2 20.5 %copy-start.7 = (bf16[1024,256]{1,0:T(8,128)(2,1)S(1)}, bf16[1024,256]{1,0:T(8,128)(2,1)}, u32[]{:S(2)}) copy-start(bf16[1024,256]{1,0:T(8,128)(2,1)} %constant.21.clone.x_out_ref) | copy-start | bytes 1572868
  24.2 20.5 %copy-start.8 = (bf16[512,512]{1,0:T(8,128)(2,1)S(1)}, bf16[512,512]{1,0:T(8,128)(2,1)}, u32[]{:S(2)}) copy-start(bf16[512,512]{1,0:T(8,128)(2,1)} %constant.22.clone.t_in_ref) | copy-start | bytes 1572868
  24.2 20.5 %copy-start.9 = (bf16[512,512]{1,0:T(8,128)(2,1)S(1)}, bf16[512,512]{1,0:T(8,128)(2,1)}, u32[]{:S(2)}) copy-start(bf16[512,512]{1,0:T(8,128)(2,1)} %constant.23.clone.t_out_ref) | copy-start | bytes 1572868
  28.1 2.0 copy-start
  44.7 2.2 copy-start.1
  46.9 7.0 %copy-start.15 = (bf16[8,8]{1,0:T(8,128)(2,1)S(1)}, bf16[8,8]{1,0:T(8,128)(2,1)}, u32[]{:S(2)}) copy-start(bf16[8,8]{1,0:T(8,128)(2,1)} %param.15) | copy-start | bytes 388
  46.9 7.1 %copy-start.16 = (bf16[32,32]{1,0:T(8,128)(2,1)S(1)}, bf16[32,32]{1,0:T(8,128)(2,1)}, u32[]{:S(2)}) copy-start(bf16[32,32]{1,0:T(8,128)(2,1)} %constant.24.clone) | copy-start | bytes 6148
  48.4 1.0 copy-start.10
  49.4 0.8 copy-start.11
  50.2 10.1 %copy-start.17 = (f32[8]{0:T(128)S(1)}, f32[8]{0:T(128)}, u32[]{:S(2)}) copy-start(f32[8]{0:T(128)} %param.16) | copy-start | bytes 100
  50.3 29.9 %all-to-all-start.1 = ((bf16[32,128,128]{2,1,0:T(8,128)(2,1)}), bf16[32,128,128]{2,1,0:T(8,128)(2,1)S(1)}, u32[]{:S(2)}, u32[]{:S(2)}) async-start(bf16[32,128,128]{2,1,0:T(8,128)(2,1)} %bitcast.18), calls=%async_computation.1 | async-start | bytes 2097152 | tf_op jit(solution)/shard_map/all_to_all | solution.py:419
  80.2 78.6 %copy-start.2 = (f32[32,8,8,512]{3,2,1,0:T(8,128)S(1)}, f32[32,8,8,512]{3,2,1,0:T(8,128)}, u32[]{:S(2)}) copy-start(f32[32,8,8,512]{3,2,1,0:T(8,128)} %copy-done) | copy-start | bytes 12582916
  158.9 60.2 %copy-start.12 = (f32[256,512]{1,0:T(8,128)S(1)}, f32[256,512]{1,0:T(8,128)}, u32[]{:S(2)}) copy-start(f32[256,512]{1,0:T(8,128)} %copy-done.11) | copy-start | bytes 1572868
  162.0 64.9 %all-to-all-start.3 = ((bf16[32,128,128]{2,1,0:T(8,128)(2,1)}), bf16[32,128,128]{2,1,0:T(8,128)(2,1)S(1)}, u32[]{:S(2)}, u32[]{:S(2)}) async-start(bf16[32,128,128]{2,1,0:T(8,128)(2,1)} %bitcast.6), calls=%async_computation.3 | async-start | bytes 2097152 | tf_op jit(solution)/shard_map/all_to_all | solution.py:419
  218.4 8.6 %copy-start.14 = (f32[8,128]{1,0:T(8,128)}, f32[8,128]{1,0:T(8,128)S(1)}, u32[]{:S(2)}) copy-start(f32[8,128]{1,0:T(8,128)S(1)} %broadcast_multiply_fusion.2) | copy-start | bytes 12292
  227.0 3.4 %copy-start.4 = (bf16[1024,4096]{1,0:T(8,128)(2,1)S(1)}, bf16[1024,4096]{1,0:T(8,128)(2,1)}, u32[]{:S(2)}) copy-start(bf16[1024,4096]{1,0:T(8,128)(2,1)} %constant.18.clone.build_ref) | copy-start | bytes 25165828
  230.3 2.2 copy-start.5

commit v2 on v1

v2 whole, which is shorter than its diff:
```python
import functools
import math

import jax
import jax.numpy as jnp
import ml_dtypes
import numpy as np
from jax import lax
from jax.experimental import pallas as pl
from jax.experimental.pallas import tpu as pltpu
from jax.sharding import PartitionSpec as P

NX = 128
NY = 128
NZ = 32
NT = 16
MX = 16
MY = 16
MZ = 16
MT = 8
BATCH = 1
KX = 32
KT = 16
CHANS = 8
CELLS = NY * NZ
KQ = 1024
LANES = 128
PARTS = 2
LOG2_E = math.log2(math.e)
DENSITY = 1.0 / math.sqrt(2.0 * math.pi)
F32 = jnp.float32
BF16 = jnp.bfloat16


def basis(length, modes):
    frequency = np.concatenate([np.arange(modes + 1), np.arange(1, modes)])
    samples_at = np.arange(length)
    phases = (2.0 * math.pi / length) * (frequency[:, None] * samples_at[None, :] % length)
    cosine_row = np.arange(2 * modes) <= modes
    waves = np.where(cosine_row[:, None], np.cos(phases), np.sin(phases))
    at_edge = cosine_row & ((frequency == 0) | (2 * frequency == length))
    scales = np.where(at_edge, math.sqrt(1.0 / length), math.sqrt(2.0 / length))
    return (waves * scales[:, None]).astype(np.float32)


def narrow(table):
    return np.asarray(table, np.float32).astype(ml_dtypes.bfloat16)


def vmem_params(mebibytes):
    return pltpu.CompilerParams(vmem_limit_bytes=mebibytes * 1024 * 1024)


def matmul(left, right):
    return jnp.dot(left, right, preferred_element_type=F32)


def swap_groups(tiles):
    rows = tiles[0].shape[0]
    lane = lax.broadcasted_iota(jnp.int32, (rows, LANES), 1)
    low_half = lane < 64
    even = (lane // 32) % 2 == 0
    first, second, third, fourth = tiles
    b0 = jnp.where(low_half, first, pltpu.roll(third, 64, 1))
    b2 = jnp.where(low_half, pltpu.roll(first, 64, 1), third)
    b1 = jnp.where(low_half, second, pltpu.roll(fourth, 64, 1))
    b3 = jnp.where(low_half, pltpu.roll(second, 64, 1), fourth)
    return (
        jnp.where(even, b0, pltpu.roll(b1, 32, 1)),
        jnp.where(even, pltpu.roll(b0, 96, 1), b1),
        jnp.where(even, b2, pltpu.roll(b3, 32, 1)),
        jnp.where(even, pltpu.roll(b2, 96, 1), b3),
    )


def pack_modes(modes, packed_ref, xl, tl):
    width = modes.shape[1]
    split = modes.reshape(xl, tl, CHANS, width)
    for tile in range(width // LANES):
        at = slice(tile * LANES, (tile + 1) * LANES)
        tiles = [split[:, step, :, at].reshape(xl * CHANS, LANES) for step in range(tl)]
        for owner, block in enumerate(swap_groups(tiles)):
            packed_ref[tile * tl + owner] = block.astype(BF16)


def unpack_modes(packed_ref, wide_ref, xl, tl):
    for tile in range(KQ // LANES):
        tiles = [packed_ref[tile * tl + owner].astype(F32) for owner in range(tl)]
        for step, block in enumerate(swap_groups(tiles)):
            wide_ref[:, step, :, tile * LANES : (tile + 1) * LANES] = block.reshape(
                xl, CHANS, LANES
            )


def analyse_kernel(xl, tl, field_ref, table_ref, packed_ref):
    pack_modes(matmul(field_ref[...], table_ref[...]), packed_ref, xl, tl)


def analyse(field, table, part, xl, tl, devices):
    rows = xl * tl * CHANS
    steps = 4
    width = KQ // steps
    return pl.pallas_call(
        functools.partial(analyse_kernel, xl, tl),
        grid=(steps,),
        in_specs=[
            pl.BlockSpec((rows, CELLS), lambda n: (part, 0)),
            pl.BlockSpec((CELLS, width), lambda n: (0, n)),
        ],
        out_specs=pl.BlockSpec((devices // steps, xl * CHANS, LANES), lambda n: (n, 0, 0)),
        out_shape=jax.ShapeDtypeStruct((devices, xl * CHANS, LANES), BF16),
        compiler_params=vmem_params(56),
        cost_estimate=pl.CostEstimate(
            flops=2 * rows * CELLS * KQ, bytes_accessed=10 << 20, transcendentals=0
        ),
        name="analyse",
    )(field, table)


def weight_kernel(weight_ref, packed_ref):
    for kx in range(weight_ref.shape[0]):
        for group in range(KT // 4):
            parts = [weight_ref[kx, 4 * group + k] for k in range(4)]
            packed_ref[kx, :, :, group * LANES : (group + 1) * LANES] = jnp.concatenate(
                parts, axis=-1
            )


def pack_weight(weight):
    per = 4
    own = weight.shape[4]
    return pl.pallas_call(
        weight_kernel,
        grid=(KX // per,),
        in_specs=[pl.BlockSpec((per, KT, CHANS, CHANS, own), lambda n: (n, 0, 0, 0, 0))],
        out_specs=pl.BlockSpec((per, CHANS, CHANS, KT * own), lambda n: (n, 0, 0, 0)),
        out_shape=jax.ShapeDtypeStruct((KX, CHANS, CHANS, KT * own), F32),
        compiler_params=vmem_params(56),
        cost_estimate=pl.CostEstimate(flops=1 << 20, bytes_accessed=20 << 20, transcendentals=0),
        name="pack_weight",
    )(weight)


def to_modes(spread_refs, x_table_refs, t_table_ref):
    total = 0.0
    for spread_ref, x_table_ref in zip(spread_refs, x_table_refs):
        gx, ta, rows, _ = spread_ref.shape
        beside = jnp.concatenate(
            [spread_ref[:, at].reshape(gx * rows, LANES) for at in range(ta)], axis=1
        )
        total = total + matmul(x_table_ref[...], beside)
    return matmul(total.astype(BF16), t_table_ref[...])


def from_modes(modes, x_table_ref, t_table_ref, held_ref):
    gx, ta, rows, _ = held_ref.shape[1:]
    half = matmul(modes.astype(BF16), t_table_ref[...]).astype(BF16)
    for part in range(PARTS):
        full = matmul(x_table_ref[part], half).astype(BF16)
        for at in range(ta):
            held_ref[part, :, at] = full[:, at * LANES : (at + 1) * LANES].reshape(gx, rows, LANES)


def mix_kernel(
    backward,
    spread_a_ref,
    spread_b_ref,
    weight_ref,
    x_in_ref,
    t_in_ref,
    x_out_ref,
    t_out_ref,
    modes_ref,
    back_a_ref,
    back_b_ref,
    weight,
    modes,
    mixed,
    held,
    weight_sem,
    modes_sem,
    back_sems,
):
    fetch = pltpu.make_async_copy(weight_ref, weight, weight_sem)
    fetch.start()
    modes[...] = to_modes(
        (spread_a_ref, spread_b_ref), (x_in_ref.at[0], x_in_ref.at[1]), t_in_ref
    )
    keep = pltpu.make_async_copy(modes, modes_ref, modes_sem)
    keep.start()
    fetch.wait()
    for kx in range(KX):
        rows = slice(kx * CHANS, (kx + 1) * CHANS)
        own = modes[rows, :]
        if backward:
            sums = [jnp.sum(own * weight[kx, i], axis=0, keepdims=True) for i in range(CHANS)]
            mixed[rows, :] = jnp.concatenate(sums, axis=0)
        else:
            total = own[0:1, :] * weight[kx, 0]
            for i in range(1, CHANS):
                total = total + own[i : i + 1, :] * weight[kx, i]
            mixed[rows, :] = total
    from_modes(mixed[...], x_out_ref, t_out_ref, held)
    sends = [
        pltpu.make_async_copy(held.at[part], ref, back_sems.at[part])
        for part, ref in enumerate((back_a_ref, back_b_ref))
    ]
    for send in sends:
        send.start()
    for send in sends:
        send.wait()
    keep.wait()


def mix(spreads, weight, tables, backward):
    modes = (KX * CHANS, weight.shape[3])
    shape = spreads[0].shape
    anywhere = pl.BlockSpec(memory_space=pl.ANY)
    on_chip = pl.BlockSpec(memory_space=pltpu.VMEM)
    return pl.pallas_call(
        functools.partial(mix_kernel, backward),
        out_shape=(
            jax.ShapeDtypeStruct(modes, F32),
            jax.ShapeDtypeStruct(shape, BF16),
            jax.ShapeDtypeStruct(shape, BF16),
        ),
        in_specs=[on_chip] * 2 + [anywhere] + [on_chip] * 4,
        out_specs=[anywhere] * 3,
        scratch_shapes=[
            pltpu.VMEM(weight.shape, F32),
            pltpu.VMEM(modes, F32),
            pltpu.VMEM(modes, F32),
            pltpu.VMEM((PARTS,) + shape, BF16),
            pltpu.SemaphoreType.DMA,
            pltpu.SemaphoreType.DMA,
            pltpu.SemaphoreType.DMA((PARTS,)),
        ],
        compiler_params=vmem_params(32),
        cost_estimate=pl.CostEstimate(flops=1 << 30, bytes_accessed=9 << 20, transcendentals=0),
        name="mix_back" if backward else "mix",
    )(*spreads, weight, *tables)


def outer_kernel(spectrum_ref, grad_ref, result_ref):
    own = result_ref.shape[4]
    for kx in range(result_ref.shape[0]):
        rows = slice(kx * CHANS, (kx + 1) * CHANS)
        for group in range(KT // 4):
            at = slice(group * LANES, (group + 1) * LANES)
            inputs = spectrum_ref[rows, at]
            grads = grad_ref[rows, at]
            for i in range(CHANS):
                product = inputs[i : i + 1, :] * grads
                for k in range(4):
                    result_ref[kx, 4 * group + k, i] = product[:, k * own : (k + 1) * own]


def outer(spectrum, grad, own):
    per = 4
    width = KT * own
    return pl.pallas_call(
        outer_kernel,
        grid=(KX // per,),
        in_specs=[pl.BlockSpec((per * CHANS, width), lambda n: (n, 0))] * 2,
        out_specs=pl.BlockSpec((per, KT, CHANS, CHANS, own), lambda n: (n, 0, 0, 0, 0)),
        out_shape=jax.ShapeDtypeStruct((KX, KT, CHANS, CHANS, own), F32),
        compiler_params=vmem_params(56),
        cost_estimate=pl.CostEstimate(flops=1 << 20, bytes_accessed=17 << 20, transcendentals=0),
        name="outer",
    )(spectrum, grad)


def normal_parts(values):
    scaled = 1.0 + 0.2316419 * jnp.abs(values)
    guess = pl.reciprocal(scaled, approx=True)
    t = guess * (2.0 - scaled * guess)
    decay = jnp.exp2(values * values * (-0.5 * LOG2_E))
    series = (1.330274429 * DENSITY) * t - 1.821255978 * DENSITY
    series = series * t + 1.781477937 * DENSITY
    series = series * t - 0.356563782 * DENSITY
    series = series * t + 0.319381530 * DENSITY
    tail = decay * (series * t)
    return jnp.where(values >= 0.0, 1.0 - tail, tail), decay


def middle_kernel(
    xl,
    tl,
    packed_ref,
    field_ref,
    cotangent_ref,
    build_ref,
    analyse_ref,
    mixer_ref,
    bias_ref,
    sums_in_ref,
    _,
    output_ref,
    grad_ref,
    sent_ref,
    sums_ref,
    wide,
    modes,
    total,
    gram,
    row_sums,
):
    step = pl.program_id(0)
    rows, width = field_ref.shape
    tile = 256
    chunk = 32

    @pl.when(step == 0)
    def _():
        unpack_modes(packed_ref, wide, xl, tl)
        modes[...] = wide[...].reshape(rows, KQ).astype(BF16)
        total[...] = jnp.zeros_like(total)
        gram[...] = jnp.zeros_like(gram)
        row_sums[...] = jnp.zeros_like(row_sums)

    def build(at):
        return matmul(modes[...], build_ref[:, at]) + matmul(mixer_ref[...], field_ref[:, at])

    def pointwise(pre, at):
        for first in range(0, rows, chunk):
            part = slice(first, first + chunk)
            bias = bias_ref[part, :]
            values = pre[part, :] + jnp.concatenate([bias] * (tile // LANES), axis=1)
            integral, decay = normal_parts(values)
            output_ref[part, at] = (values * integral).astype(BF16)
            slope = integral + (values * DENSITY) * decay
            grad = (cotangent_ref[part, at].astype(F32) * slope).astype(BF16)
            grad_ref[part, at] = grad
            wide_grad = grad.astype(F32)
            sums = row_sums[part, :]
            for lanes in range(0, tile, LANES):
                sums = sums + wide_grad[:, lanes : lanes + LANES]
            row_sums[part, :] = sums

    def gather(at):
        total[...] += matmul(grad_ref[:, at], analyse_ref[at, :])
        gram[...] += lax.dot_general(
            grad_ref[:, at],
            field_ref[:, at],
            (((1,), (1,)), ((), ())),
            preferred_element_type=F32,
        )

    tiles = [slice(first, first + tile) for first in range(0, width, tile)]
    ready = build(tiles[0])
    for index, at in enumerate(tiles):
        pre = ready
        if index + 1 < len(tiles):
            ready = build(tiles[index + 1])
        pointwise(pre, at)
        if index % 2 == 1:
            gather(slice(tiles[index - 1].start, at.stop))

    @pl.when(step == pl.num_programs(0) - 1)
    def _():
        pack_modes(total[...], sent_ref, xl, tl)
        row = lax.broadcasted_iota(jnp.int32, (rows, rows), 0)
        column = lax.broadcasted_iota(jnp.int32, (rows, rows), 1)
        same = jnp.where(row // CHANS == column // CHANS, gram[...], 0.0)
        folded = jnp.sum(same.reshape(rows // CHANS, CHANS, rows), axis=0)
        source = lax.broadcasted_iota(jnp.int32, (rows, LANES), 0)
        target = lax.broadcasted_iota(jnp.int32, (rows, LANES), 1)
        select = jnp.where(source % CHANS == target, 1.0, 0.0)
        point = jnp.dot(
            folded, select, precision=lax.Precision.HIGHEST, preferred_element_type=F32
        )
        bias = jnp.sum(
            jnp.sum(row_sums[...].reshape(rows // CHANS, CHANS, LANES), axis=0),
            axis=1,
            keepdims=True,
        )
        lane = lax.broadcasted_iota(jnp.int32, (CHANS, LANES), 1)
        sums_ref[...] = sums_in_ref[...] + jnp.where(lane == CHANS, bias, point)


def middle(packed, field, cotangent, tables, mixer, bias, sums, output, part, xl, tl):
    build_table, analyse_table = tables
    rows = xl * tl * CHANS
    width = 512
    whole = lambda *shape: pl.BlockSpec(shape, lambda n: (0,) * len(shape))
    tile = pl.BlockSpec((rows, width), lambda n: (part, n))
    kernel = functools.partial(middle_kernel, xl, tl)
    operands = (packed, field, cotangent, build_table, analyse_table, mixer, bias, sums)
    specs = [
        whole(*packed.shape),
        tile,
        tile,
        pl.BlockSpec((KQ, width), lambda n: (0, n)),
        pl.BlockSpec((width, KQ), lambda n: (n, 0)),
        whole(rows, rows),
        whole(rows, LANES),
        whole(CHANS, LANES),
    ]
    aliases = {}
    if output is None:
        inner = kernel
        kernel = lambda *refs: inner(*refs[:8], None, *refs[8:])
    else:
        aliases = {len(operands): 0}
        operands += (output,)
        specs.append(pl.BlockSpec(memory_space=pl.ANY))
    return pl.pallas_call(
        kernel,
        grid=(CELLS // width,),
        in_specs=specs,
        out_specs=[
            tile,
            pl.BlockSpec((rows, width), lambda n: (0, n)),
            whole(*packed.shape),
            whole(CHANS, LANES),
        ],
        out_shape=(
            jax.ShapeDtypeStruct(field.shape, BF16),
            jax.ShapeDtypeStruct((rows, CELLS), BF16),
            jax.ShapeDtypeStruct(packed.shape, BF16),
            jax.ShapeDtypeStruct((CHANS, LANES), F32),
        ),
        scratch_shapes=[
            pltpu.VMEM((xl, tl, CHANS, KQ), F32),
            pltpu.VMEM((rows, KQ), BF16),
            pltpu.VMEM((rows, KQ), F32),
            pltpu.VMEM((rows, rows), F32),
            pltpu.VMEM((rows, LANES), F32),
        ],
        input_output_aliases=aliases,
        compiler_params=vmem_params(56),
        cost_estimate=pl.CostEstimate(
            flops=5 * rows * CELLS * KQ, bytes_accessed=26 << 20, transcendentals=rows * CELLS
        ),
        name="middle",
    )(*operands)


def last_kernel(xl, tl, packed_ref, grad_ref, build_ref, mixer_ref, _, field_ref, wide, modes):
    rows = grad_ref.shape[0]

    @pl.when(pl.program_id(0) == 0)
    def _():
        unpack_modes(packed_ref, wide, xl, tl)
        modes[...] = wide[...].reshape(rows, KQ).astype(BF16)

    field_ref[...] = (
        matmul(modes[...], build_ref[...]) + matmul(mixer_ref[...], grad_ref[...])
    ).astype(BF16)


def last(packed, grad, build_table, mixer, result, part, xl, tl):
    rows = grad.shape[0]
    width = 512
    kernel = functools.partial(last_kernel, xl, tl)
    operands = (packed, grad, build_table, mixer)
    specs = [
        pl.BlockSpec(packed.shape, lambda n: (0, 0, 0)),
        pl.BlockSpec((rows, width), lambda n: (0, n)),
        pl.BlockSpec((KQ, width), lambda n: (0, n)),
        pl.BlockSpec((rows, rows), lambda n: (0, 0)),
    ]
    aliases = {}
    if result is None:
        inner = kernel
        kernel = lambda *refs: inner(*refs[:4], None, *refs[4:])
    else:
        aliases = {len(operands): 0}
        operands += (result,)
        specs.append(pl.BlockSpec(memory_space=pl.ANY))
    return pl.pallas_call(
        kernel,
        grid=(CELLS // width,),
        in_specs=specs,
        out_specs=pl.BlockSpec((rows, width), lambda n: (part, n)),
        out_shape=jax.ShapeDtypeStruct((rows * PARTS, CELLS), BF16),
        scratch_shapes=[
            pltpu.VMEM((xl, tl, CHANS, KQ), F32),
            pltpu.VMEM((rows, KQ), BF16),
        ],
        input_output_aliases=aliases,
        compiler_params=vmem_params(56),
        cost_estimate=pl.CostEstimate(
            flops=2 * rows * CELLS * KQ, bytes_accessed=12 << 20, transcendentals=0
        ),
        name="last",
    )(*operands)


def swap(blocks):
    return lax.all_to_all(blocks, ("gx", "ta"), split_axis=0, concat_axis=0, tiled=True)


def sum_everywhere(values, devices):
    step = 1
    while step < devices:
        pairs = [(at, at ^ step) for at in range(devices)]
        values = values + lax.ppermute(values, ("gx", "ta"), pairs)
        step *= 2
    return values


def fast_body(gx, ta, features, cotangent, spec_weight, point_weight, bias_vector):
    _, xl_all, tl, _, cells = features.shape
    own = spec_weight.shape[4]
    devices = gx * ta
    xl = xl_all // PARTS
    rows = xl * tl * CHANS
    yz = np.kron(
        narrow(basis(NY, MY)).astype(np.float32), narrow(basis(NZ, MZ)).astype(np.float32)
    )
    build_table = jnp.asarray(narrow(yz))
    analyse_table = jnp.asarray(narrow(yz.T))
    x_split = basis(NX, MX).reshape(KX, gx, PARTS, xl)
    x_wide = [
        np.kron(x_split[:, :, part].reshape(KX, gx * xl), np.eye(CHANS)) for part in range(PARTS)
    ]
    t_wide = np.kron(basis(NT, MT), np.eye(own))
    x_in = jnp.asarray(narrow(np.stack(x_wide)))
    x_out = jnp.asarray(narrow(np.stack([table.T for table in x_wide])))
    t_in, t_out = jnp.asarray(narrow(t_wide.T)), jnp.asarray(narrow(t_wide))
    tables = (x_in, t_in, x_out, t_out)
    norm_scale = float(BATCH * NX * NT * NY * NZ) ** (-0.5)

    field = features.reshape(PARTS * rows, cells)
    cot = cotangent.reshape(PARTS * rows, cells)
    pick = np.tile(np.eye(CHANS, dtype=np.float32), (rows // CHANS, 1))
    same = np.kron(np.eye(rows // CHANS, dtype=np.float32), np.ones((CHANS, CHANS), np.float32))
    picked = jnp.asarray(narrow(pick))
    spread_point = matmul(matmul(picked, point_weight).astype(BF16), picked.T)
    spread_back = matmul(matmul(picked, point_weight.T).astype(BF16), picked.T)
    mixer = (spread_point * jnp.asarray(same)).astype(BF16)
    mixer_back = (spread_back * jnp.asarray(same)).astype(BF16)
    bias = jnp.dot(
        jnp.asarray(pick),
        jnp.broadcast_to(bias_vector[:, None], (CHANS, LANES)),
        precision=lax.Precision.HIGHEST,
    )
    spread_shape = (gx, ta, xl * CHANS, LANES)
    block_shape = (devices, xl * CHANS, LANES)

    packed_weight = pack_weight(spec_weight)
    spread_in = [
        swap(analyse(field, analyse_table, part, xl, tl, devices)).reshape(spread_shape)
        for part in range(PARTS)
    ]
    spectrum, *mixed = mix(spread_in, packed_weight, tables, False)
    output, sums = None, jnp.zeros((CHANS, LANES), F32)
    grads, spread_grad = [], []
    for part in range(PARTS):
        returned = swap(mixed[part].reshape(block_shape))
        output, grad, sent, sums = middle(
            returned,
            field,
            cot,
            (build_table, analyse_table),
            mixer,
            bias,
            sums,
            output,
            part,
            xl,
            tl,
        )
        grads.append(grad)
        spread_grad.append(swap(sent).reshape(spread_shape))
    summed = sum_everywhere(sums, devices) * norm_scale
    grad_modes, *mixed_back = mix(spread_grad, packed_weight, tables, True)
    grad_field = None
    for part in range(PARTS):
        grad_back = swap(mixed_back[part].reshape(block_shape))
        grad_field = last(
            grad_back, grads[part], build_table, mixer_back, grad_field, part, xl, tl
        )
    grad_spec = outer(spectrum, grad_modes, own)
    return (
        output.reshape(features.shape),
        grad_field.reshape(features.shape),
        grad_spec,
        summed[:, :CHANS],
        summed[:, CHANS],
    )


def analyse_yz(spatial, yz_table):
    return jnp.einsum(
        "qp,bxtcp->bxtcq", yz_table, spatial.astype(F32), precision=lax.Precision.HIGHEST
    )


def build_yz(modes_in, yz_table):
    return jnp.einsum(
        "qp,bxtcq->bxtcp", yz_table, modes_in.astype(F32), precision=lax.Precision.HIGHEST
    )


def analyse_xt(spread, table):
    sizes = spread.shape
    flattened = spread.reshape(sizes[0], sizes[1] * sizes[2], sizes[3] * sizes[4]).astype(F32)
    spectral = jnp.einsum("mp,bpr->bmr", table, flattened, precision=lax.Precision.HIGHEST)
    return spectral.reshape(sizes[0], KX, KT, sizes[3], sizes[4])


def synthesise_xt(modes_in, table):
    sizes = modes_in.shape
    flattened = modes_in.reshape(sizes[0], sizes[1] * sizes[2], sizes[3] * sizes[4])
    spatial = jnp.einsum("mp,bmr->bpr", table, flattened, precision=lax.Precision.HIGHEST)
    return spatial.reshape(sizes[0], NX, NT, sizes[3], sizes[4])


def to_owners(modes_in):
    first = lax.all_to_all(modes_in, "gx", split_axis=4, concat_axis=1, tiled=True)
    return lax.all_to_all(first, "ta", split_axis=4, concat_axis=2, tiled=True)


def to_cells(spread, shape):
    first = lax.all_to_all(
        spread[:, :, :, :, None, None, :], "gx", split_axis=1, concat_axis=4, tiled=True
    )
    second = lax.all_to_all(first, "ta", split_axis=2, concat_axis=5, tiled=True)
    return second.reshape(shape[:4] + (-1,))


def general_body(features, cotangent, spec_weight, point_weight, bias_vector):
    shape = features.shape
    yz_table = jnp.asarray(
        np.kron(narrow(basis(NY, MY)).astype(np.float32), narrow(basis(NZ, MZ)).astype(np.float32))
    )
    xt_table = jnp.asarray(np.kron(basis(NX, MX), basis(NT, MT)))
    norm_scale = float(BATCH * NX * NT * NY * NZ) ** (-0.5)
    highest = lax.Precision.HIGHEST
    spectrum = analyse_xt(to_owners(analyse_yz(features, yz_table).astype(BF16)), xt_table)
    mixed = jnp.einsum("bklip,kliop->bklop", spectrum, spec_weight, precision=highest)
    returned = to_cells(synthesise_xt(mixed, xt_table).astype(BF16), shape)
    pointwise = jnp.einsum("oi,bxtip->bxtop", point_weight, features, preferred_element_type=F32)
    pre = build_yz(returned, yz_table) + pointwise + bias_vector[:, None]
    integral = 0.5 * (1.0 + jax.scipy.special.erf(pre * 0.7071067811865476))
    output = (pre * integral).astype(BF16)
    slope = integral + pre * jnp.exp(-0.5 * pre * pre) * 0.3989422804014327
    grad_pre = (cotangent.astype(F32) * slope).astype(BF16)
    local_point = jnp.einsum("bxtop,bxtip->oi", grad_pre, features, preferred_element_type=F32)
    local_bias = jnp.sum(grad_pre.astype(F32), axis=(0, 1, 2, 4))
    total_point, total_bias = lax.psum((local_point, local_bias), ("gx", "ta"))
    grad_modes = analyse_xt(to_owners(analyse_yz(grad_pre, yz_table).astype(BF16)), xt_table)
    grad_spec = jnp.einsum("bklip,bklop->kliop", spectrum, grad_modes, precision=highest)
    grad_in = jnp.einsum("kliop,bklop->bklip", spec_weight, grad_modes, precision=highest)
    grad_back = to_cells(synthesise_xt(grad_in, xt_table).astype(BF16), shape)
    point_term = jnp.einsum("oi,bxtop->bxtip", point_weight, grad_pre, preferred_element_type=F32)
    grad_field = (build_yz(grad_back, yz_table) + point_term).astype(BF16)
    return (output, grad_field, grad_spec, total_point * norm_scale, total_bias * norm_scale)


def solution(mesh):
    split_field = P(None, "gx", "ta", None, None)
    split_weight = P(None, None, None, None, ("gx", "ta"))
    in_specs = (split_field, split_field, split_weight, P(), P())
    out_specs = (split_field, split_field, split_weight, P(), P())
    gx, ta = mesh.shape["gx"], mesh.shape["ta"]
    own, xl, tl = KQ // (gx * ta), NX // gx, NT // ta
    if own == 32 and xl * CHANS == LANES and tl == 4:
        body = functools.partial(fast_body, gx, ta)
    else:
        body = general_body
    return jax.shard_map(body, mesh=mesh, in_specs=in_specs, out_specs=out_specs, check_vma=False)
```

time: 243 us -> 220 us (0.905)
  local copies, waits for them, and re-layouts: 28.6 us -> 8.11 us
  blocking collectives: 78.1 us -> 58.4 us
  starting transfers between devices: 14.7 us -> 30.2 us
  waiting for transfers between devices: 34.2 us -> 20.7 us
  Pallas kernels: 83.3 us -> 96.3 us
  matrix products: 0 us -> 3.75 us
    all_gather x1 -> x0, blocking collectives: 48.4 us -> none  [fast_body(): gathered = lax.all_gather(sums, ('gx', 'ta'))]
    all_to_all x1 -> x3, blocking collectives: 29.7 us -> 58.4 us  [swap(): lax.all_to_all(blocks, ('gx', 'ta'), split_axis=0, concat_axis=0, tiled=T...]
    all_to_all x3 -> x5, waiting for transfers between devices: 34.2 us -> 12.6 us  [swap(): lax.all_to_all(blocks, ('gx', 'ta'), split_axis=0, concat_axis=0, tiled=T...]
    unnamed x36 -> x34, local copies, waits for them, and re-layouts: 19.5 us -> 6.83 us
    mul x2 -> x0, local copies, waits for them, and re-layouts: 8.11 us -> none  [the longest x1 4.06 us: fast_body(): mixer_back = jnp.kron(eye, point_weight.T)]
    ppermute x0 -> x5, waiting for transfers between devices: none -> 8.1 us  [sum_everywhere(): values = values + lax.ppermute(values, ('gx', 'ta'), pairs)]
    all_to_all x3 -> x5, starting transfers between devices: 14.7 us -> 22.5 us  [swap(): lax.all_to_all(blocks, ('gx', 'ta'), split_axis=0, concat_axis=0, tiled=T...]
    ppermute x0 -> x5, starting transfers between devices: none -> 7.69 us  [sum_everywhere(): values = values + lax.ppermute(values, ('gx', 'ta'), pairs)]
  transfers between devices with their start and end apart: 3 -> 10, of which waited for: 2 -> 7; matrix products, arithmetic and copies ran while one was open for 5% -> 2% of each run, Pallas kernels for 5% -> 34%
where the time goes in v2:
time: 220 us; the launch traced here: 218 us
  Pallas kernels  96.3 us (44%)
  blocking collectives  58.4 us (27%)
  starting transfers between devices  30.2 us (14%)
  waiting for transfers between devices  20.7 us (9%)
  local copies, waits for them, and re-layouts  8.11 us (4%)
  matrix products  3.75 us (2%)
    all_to_all x3, blocking collectives, swap(): lax.all_to_all(blocks, ('gx', 'ta'), split_axis=0, concat_axis=0, tiled=T...  58.4 us
    pallas_call x2, Pallas kernels, middle(): pl.pallas_call(kernel, grid=(CELLS // width,), in_specs=specs, out_specs=...  35.6 us
    all_to_all x5, starting transfers between devices, swap(): lax.all_to_all(blocks, ('gx', 'ta'), split_axis=0, concat_axis=0, tiled=T...  22.5 us
    pallas_call x2, Pallas kernels, last(): pl.pallas_call(kernel, grid=(CELLS // width,), in_specs=specs, out_specs=...  20.2 us
    pallas_call x2, Pallas kernels, analyse(): pl.pallas_call(functools.partial(analyse_kernel, xl, tl), grid=(steps,),...  14.7 us
    all_to_all x5, waiting for transfers between devices, swap(): lax.all_to_all(blocks, ('gx', 'ta'), split_axis=0, concat_axis=0, tiled=T...  12.6 us
    pallas_call x1, Pallas kernels, pack_weight(): pl.pallas_call(weight_kernel, grid=(KX // per,), in_specs=[pl.BlockSpec((...  11.2 us
    pallas_call x1, Pallas kernels, outer(): pl.pallas_call(outer_kernel, grid=(KX // per,), in_specs=[pl.BlockSpec((p...  9.06 us
  transfers between devices with their start and end apart: 10, of which 7 were waited for; matrix products, arithmetic and copies ran while one was open for 2% of the time, Pallas kernels for 34%

profile of v2, /device:TPU:0, one launch (start us, length us, event | category | flops | bytes accessed | tf_op | source)
XLA Modules:
  0.0 218.3 jit_solution(7158224475650056532)
XLA Ops:
  0.6 7.3 %analyse.2 = bf16[32,64,128]{2,1,0:T(8,128)(2,1)} custom-call(bf16[512,4096]{1,0:T(8,128)(2,1)} %bitcast.27, bf16[4096,1024]{1,0:T(8,128)(2,1)} %constant.23.clone.table_ref.refs_4_.analyse_ref), custom_call_target="tpu_custom_call" | custom-call | flops 2147483648 | bytes 10485760 | tf_op jit(solution)/shard_map/analyse/pallas_call | solution.py:103
  8.0 7.3 %all-to-all-start = ((bf16[32,64,128]{2,1,0:T(8,128)(2,1)}), bf16[32,64,128]{2,1,0:T(8,128)(2,1)S(1)}, u32[]{:S(2)}, u32[]{:S(2)}) async-start(bf16[32,64,128]{2,1,0:T(8,128)(2,1)} %analyse.2), calls=%async_computation | async-start | bytes 1048576 | tf_op jit(solution)/shard_map/all_to_all | solution.py:491
  15.3 7.3 %analyse.3 = bf16[32,64,128]{2,1,0:T(8,128)(2,1)} custom-call(bf16[512,4096]{1,0:T(8,128)(2,1)} %bitcast.28, bf16[4096,1024]{1,0:T(8,128)(2,1)} %constant.23.clone.table_ref.refs_4_.analyse_ref), custom_call_target="tpu_custom_call" | custom-call | flops 2147483648 | bytes 10485760 | tf_op jit(solution)/shard_map/analyse/pallas_call | solution.py:103
  22.6 8.2 %all-to-all-done = bf16[32,64,128]{2,1,0:T(8,128)(2,1)S(1)} async-done(((bf16[32,64,128]{2,1,0:T(8,128)(2,1)}), bf16[32,64,128]{2,1,0:T(8,128)(2,1)S(1)}, u32[]{:S(2)}, u32[]{:S(2)}) %all-to-all-start) | async-done | bytes 524320 | tf_op jit(solution)/shard_map/all_to_all | solution.py:491
  30.8 3.1 %all-to-all-start.1 = ((bf16[32,64,128]{2,1,0:T(8,128)(2,1)}), bf16[32,64,128]{2,1,0:T(8,128)(2,1)S(1)}, u32[]{:S(2)}, u32[]{:S(2)}) async-start(bf16[32,64,128]{2,1,0:T(8,128)(2,1)} %analyse.3), calls=%async_computation.1 | async-start | bytes 1048576 | tf_op jit(solution)/shard_map/all_to_all | solution.py:491
  34.0 11.2 %pack_weight.1.weight_ref = f32[32,8,8,512]{3,2,1,0:T(8,128)} custom-call(f32[32,16,8,8,32]{4,3,2,1,0:T(8,128)} %weight_ref.1), custom_call_target="tpu_custom_call" | custom-call | flops 1048576 | bytes 20971520 | tf_op jit(solution)/shard_map/pack_weight/pallas_call | solution.py:132
  45.1 4.3 %all-to-all-done.1 = bf16[32,64,128]{2,1,0:T(8,128)(2,1)S(1)} async-done(((bf16[32,64,128]{2,1,0:T(8,128)(2,1)}), bf16[32,64,128]{2,1,0:T(8,128)(2,1)S(1)}, u32[]{:S(2)}, u32[]{:S(2)}) %all-to-all-start.1) | async-done | bytes 524320 | tf_op jit(solution)/shard_map/all_to_all | solution.py:491
  49.5 2.2 copy-done.1
  51.7 2.1 mix.1
  54.6 18.5 %all_to_all.40.refs_0_ = bf16[32,64,128]{2,1,0:T(8,128)(2,1)} all-to-all(bf16[32,64,128]{2,1,0:T(8,128)(2,1)S(1)} %bitcast.26), channel_id=1, replica_groups=mesh['gx'=8,'ta'=4] {'gx','ta'}, dimensions={0} | all-to-all | bytes 1048576 | tf_op jit(solution)/shard_map/all_to_all | solution.py:491
  73.1 3.1 %all-to-all-start.2 = ((bf16[32,64,128]{2,1,0:T(8,128)(2,1)}), bf16[32,64,128]{2,1,0:T(8,128)(2,1)S(1)}, u32[]{:S(2)}, u32[]{:S(2)}) async-start(bf16[32,64,128]{2,1,0:T(8,128)(2,1)} %bitcast.24), calls=%async_computation.2 | async-start | bytes 1048576 | tf_op jit(solution)/shard_map/all_to_all | solution.py:491
  76.2 1.9 fusion.2.refs_6_.bias_ref
  78.1 0.9 fusion.refs_5_.mixer_ref
  79.6 17.8 %middle.2 = (bf16[512,4096]{1,0:T(8,128)(2,1)}, bf16[256,4096]{1,0:T(8,128)(2,1)}, bf16[32,64,128]{2,1,0:T(8,128)(2,1)}, f32[8,128]{1,0:T(8,128)}) custom-call(bf16[32,64,128]{2,1,0:T(8,128)(2,1)} %all_to_all.40.refs_0_, bf16[512,4096]{1,0:T(8,128)(2,1)} %bitcast.29, bf16[512,4096]{1,0:T(8,128)(2,1)} %bitcast.32, ...), custom_call_target="tpu_custom_call" | custom-call | flops 5368709120 | bytes 27262976 | tf_op jit(solution)/shard_map/middle/pallas_call | solution.py:407
  97.4 5.8 %all-to-all-start.4 = ((bf16[32,64,128]{2,1,0:T(8,128)(2,1)}), bf16[32,64,128]{2,1,0:T(8,128)(2,1)S(1)}, u32[]{:S(2)}, u32[]{:S(2)}) async-start(bf16[32,64,128]{2,1,0:T(8,128)(2,1)} %get-tuple-element.24), calls=%async_computation.4 | async-start | bytes 1048576 | tf_op jit(solution)/shard_map/all_to_all | solution.py:491
  103.3 17.8 %middle.3 = (bf16[512,4096]{1,0:T(8,128)(2,1)}, bf16[256,4096]{1,0:T(8,128)(2,1)}, bf16[32,64,128]{2,1,0:T(8,128)(2,1)}, f32[8,128]{1,0:T(8,128)}) custom-call(bf16[32,64,128]{2,1,0:T(8,128)(2,1)} %copy-done.10, bf16[512,4096]{1,0:T(8,128)(2,1)} %bitcast.30, bf16[512,4096]{1,0:T(8,128)(2,1)} %bitcast.33, ...), custom_call_target="tpu_custom_call", output_to_operand_aliasing={{0}: (8, {})} | custom-call | flops 5368709120 | bytes 27262976 | tf_op jit(solution)/shard_map/middle/pallas_call | solution.py:407
  121.1 21.4 %all_to_all.41 = bf16[32,64,128]{2,1,0:T(8,128)(2,1)S(1)} all-to-all(bf16[32,64,128]{2,1,0:T(8,128)(2,1)} %get-tuple-element.25), channel_id=1, replica_groups=mesh['gx'=8,'ta'=4] {'gx','ta'}, dimensions={0} | all-to-all | bytes 1048576 | tf_op jit(solution)/shard_map/all_to_all | solution.py:491
  142.5 2.2 %copy-done.2 = f32[32,8,8,512]{3,2,1,0:T(8,128)S(1)} copy-done((f32[32,8,8,512]{3,2,1,0:T(8,128)S(1)}, f32[32,8,8,512]{3,2,1,0:T(8,128)}, u32[]{:S(2)}) %copy-start.2) | copy-done | bytes 4194328
  144.7 3.5 %mix_back.1 = (f32[256,512]{1,0:T(8,128)S(1)}, bf16[8,4,64,128]{3,2,1,0:T(8,128)(2,1)S(1)}, bf16[8,4,64,128]{3,2,1,0:T(8,128)(2,1)}) custom-call(bf16[8,4,64,128]{3,2,1,0:T(8,128)(2,1)S(1)} %bitcast.20, bf16[8,4,64,128]{3,2,1,0:T(8,128)(2,1)S(1)} %bitcast.23, f32[32,8,8,512]{3,2,1,0:T(8,128)S(1)} %copy-done.2, bf16[2,256,512]{2,1,0:T(8,128)(2,1)S(1)} %copy-done.3, ...), custom_call_target="tpu_custom_call" | custom-call | flops 1073741824 | bytes 9437184 | tf_op jit(solution)/shard_map/mix_back/pallas_call | solution.py:220
  149.0 18.5 %all_to_all.42.refs_0_ = bf16[32,64,128]{2,1,0:T(8,128)(2,1)} all-to-all(bf16[32,64,128]{2,1,0:T(8,128)(2,1)S(1)} %bitcast.25), channel_id=1, replica_groups=mesh['gx'=8,'ta'=4] {'gx','ta'}, dimensions={0} | all-to-all | bytes 1048576 | tf_op jit(solution)/shard_map/all_to_all | solution.py:491
  167.5 3.3 %all-to-all-start.6 = ((bf16[32,64,128]{2,1,0:T(8,128)(2,1)}), bf16[32,64,128]{2,1,0:T(8,128)(2,1)S(1)}, u32[]{:S(2)}, u32[]{:S(2)}) async-start(bf16[32,64,128]{2,1,0:T(8,128)(2,1)} %bitcast.9), calls=%async_computation.6 | async-start | bytes 1048576 | tf_op jit(solution)/shard_map/all_to_all | solution.py:491
  170.9 1.1 collective-permute-done
  172.0 1.6 collective-permute-start.1
  173.6 2.0 collective-permute-done.1
  175.6 1.6 collective-permute-start.2
  177.3 2.1 collective-permute-done.2
  179.4 1.4 collective-permute-start.3
  180.9 2.2 collective-permute-done.3
  183.0 2.9 %collective-permute-start.4 = (f32[8,128]{1,0:T(8,128)S(1)}, f32[8,128]{1,0:T(8,128)S(1)}, u32[]{:S(2)}, u32[]{:S(2)}) collective-permute-start(f32[8,128]{1,0:T(8,128)S(1)} %add.18), channel_id=1, source_target_pairs={{0,16},{1,17},{2,18},{3,19},{4,20},{5,21},{6,22},{7,23},{8,24},{9,... | collective-permute-start | bytes 12296 | tf_op jit(solution)/shard_map/ppermute | solution.py:498
  188.2 9.1 %outer.1 = f32[32,16,8,8,32]{4,3,2,1,0:T(8,128)} custom-call(f32[256,512]{1,0:T(8,128)} %copy-done.7, f32[256,512]{1,0:T(8,128)} %copy-done.8), custom_call_target="tpu_custom_call" | custom-call | flops 1048576 | bytes 17825792 | tf_op jit(solution)/shard_map/outer/pallas_call | solution.py:261
  197.3 10.1 %last.2._ = bf16[512,4096]{1,0:T(8,128)(2,1)} custom-call(bf16[32,64,128]{2,1,0:T(8,128)(2,1)} %all_to_all.42.refs_0_, bf16[256,4096]{1,0:T(8,128)(2,1)} %get-tuple-element.29.refs_1_, bf16[1024,4096]{1,0:T(8,128)(2,1)} %constant.22.clone.refs_3_.build_ref.refs_2_, bf16[256,256]{1,0:T(8,128)(2,1)} %fusion.1.refs_3_.mixer_ref), custom_call_target="tpu_custom_call" | custom-call | flops 2147483648 | bytes 12582912 | tf_op jit(solution)/shard_map/last/pallas_call | solution.py:471
  208.2 10.1 %last.3 = bf16[512,4096]{1,0:T(8,128)(2,1)} custom-call(bf16[32,64,128]{2,1,0:T(8,128)(2,1)} %copy-done.11, bf16[256,4096]{1,0:T(8,128)(2,1)} %get-tuple-element.27.grad_ref, bf16[1024,4096]{1,0:T(8,128)(2,1)} %constant.22.clone.refs_3_.build_ref.refs_2_, bf16[256,256]{1,0:T(8,128)(2,1)} %fusion.1.refs_3_.mixer_ref, ...), custom_call_target="tpu_custom_call", output_to_operand_aliasing={{}: (4, {})} | custom-call | flops 2147483648 | bytes 12582912 | tf_op jit(solution)/shard_map/last/pallas_call | solution.py:471
  (45 shorter events, 5.6 us)
Async XLA Ops:
  0.6 77.5 %copy-start = (bf16[8,8]{1,0:T(8,128)(2,1)S(1)}, bf16[8,8]{1,0:T(8,128)(2,1)}, u32[]{:S(2)}) copy-start(bf16[8,8]{1,0:T(8,128)(2,1)} %param.17) | copy-start | bytes 388
  8.0 22.9 %all-to-all-start = ((bf16[32,64,128]{2,1,0:T(8,128)(2,1)}), bf16[32,64,128]{2,1,0:T(8,128)(2,1)S(1)}, u32[]{:S(2)}, u32[]{:S(2)}) async-start(bf16[32,64,128]{2,1,0:T(8,128)(2,1)} %analyse.2), calls=%async_computation | async-start | bytes 1048576 | tf_op jit(solution)/shard_map/all_to_all | solution.py:491
  30.8 18.6 %all-to-all-start.1 = ((bf16[32,64,128]{2,1,0:T(8,128)(2,1)}), bf16[32,64,128]{2,1,0:T(8,128)(2,1)S(1)}, u32[]{:S(2)}, u32[]{:S(2)}) async-start(bf16[32,64,128]{2,1,0:T(8,128)(2,1)} %analyse.3), calls=%async_computation.1 | async-start | bytes 1048576 | tf_op jit(solution)/shard_map/all_to_all | solution.py:491
  33.9 15.5 %copy-start.3 = (bf16[2,256,512]{2,1,0:T(8,128)(2,1)S(1)}, bf16[2,256,512]{2,1,0:T(8,128)(2,1)}, u32[]{:S(2)}) copy-start(bf16[2,256,512]{2,1,0:T(8,128)(2,1)} %constant.24.clone.x_in_ref) | copy-start | bytes 1572868
  33.9 15.5 %copy-start.4 = (bf16[512,512]{1,0:T(8,128)(2,1)S(1)}, bf16[512,512]{1,0:T(8,128)(2,1)}, u32[]{:S(2)}) copy-start(bf16[512,512]{1,0:T(8,128)(2,1)} %constant.26.clone.t_in_ref) | copy-start | bytes 1572868
  33.9 15.5 %copy-start.5 = (bf16[2,512,256]{2,1,0:T(8,128)(2,1)S(1)}, bf16[2,512,256]{2,1,0:T(8,128)(2,1)}, u32[]{:S(2)}) copy-start(bf16[2,512,256]{2,1,0:T(8,128)(2,1)} %constant.25.clone.x_out_ref) | copy-start | bytes 1572868
  34.0 15.5 %copy-start.6 = (bf16[512,512]{1,0:T(8,128)(2,1)S(1)}, bf16[512,512]{1,0:T(8,128)(2,1)}, u32[]{:S(2)}) copy-start(bf16[512,512]{1,0:T(8,128)(2,1)} %constant.27.clone.t_out_ref) | copy-start | bytes 1572868
  49.5 2.2 %copy-start.1 = (f32[32,8,8,512]{3,2,1,0:T(8,128)S(1)}, f32[32,8,8,512]{3,2,1,0:T(8,128)}, u32[]{:S(2)}) copy-start(f32[32,8,8,512]{3,2,1,0:T(8,128)} %pack_weight.1.weight_ref) | copy-start | bytes 12582916
  51.7 24.5 %copy-start.16 = (f32[8]{0:T(128)S(1)}, f32[8]{0:T(128)}, u32[]{:S(2)}) copy-start(f32[8]{0:T(128)} %param.18) | copy-start | bytes 100
  51.7 26.4 %copy-start.12 = (f32[256,256]{1,0:T(8,128)S(1)}, f32[256,256]{1,0:T(8,128)}, u32[]{:S(2)}) copy-start(f32[256,256]{1,0:T(8,128)} %constant.29.clone) | copy-start | bytes 786436
  51.7 26.4 %copy-start.13 = (bf16[256,8]{1,0:T(8,128)(2,1)S(1)}, bf16[256,8]{1,0:T(8,128)(2,1)}, u32[]{:S(2)}) copy-start(bf16[256,8]{1,0:T(8,128)(2,1)} %constant.28.clone) | copy-start | bytes 12292
  53.8 0.8 copy-start.7
  54.6 18.5 %copy-start.9 = (bf16[8,4,64,128]{3,2,1,0:T(8,128)(2,1)}, bf16[8,4,64,128]{3,2,1,0:T(8,128)(2,1)S(1)}, u32[]{:S(2)}) copy-start(bf16[8,4,64,128]{3,2,1,0:T(8,128)(2,1)S(1)} %get-tuple-element.19) | copy-start | bytes 1572868
  73.1 24.3 %all-to-all-start.2 = ((bf16[32,64,128]{2,1,0:T(8,128)(2,1)}), bf16[32,64,128]{2,1,0:T(8,128)(2,1)S(1)}, u32[]{:S(2)}, u32[]{:S(2)}) async-start(bf16[32,64,128]{2,1,0:T(8,128)(2,1)} %bitcast.24), calls=%async_computation.2 | async-start | bytes 1048576 | tf_op jit(solution)/shard_map/all_to_all | solution.py:491
  97.4 5.9 %copy-start.10 = (bf16[32,64,128]{2,1,0:T(8,128)(2,1)}, bf16[32,64,128]{2,1,0:T(8,128)(2,1)S(1)}, u32[]{:S(2)}) copy-start(bf16[32,64,128]{2,1,0:T(8,128)(2,1)S(1)} %all-to-all-done.2.packed_ref) | copy-start | bytes 1572868
  97.4 23.7 %all-to-all-start.4 = ((bf16[32,64,128]{2,1,0:T(8,128)(2,1)}), bf16[32,64,128]{2,1,0:T(8,128)(2,1)S(1)}, u32[]{:S(2)}, u32[]{:S(2)}) async-start(bf16[32,64,128]{2,1,0:T(8,128)(2,1)} %get-tuple-element.24), calls=%async_computation.4 | async-start | bytes 1048576 | tf_op jit(solution)/shard_map/all_to_all | solution.py:491
  142.5 2.2 %copy-start.2 = (f32[32,8,8,512]{3,2,1,0:T(8,128)S(1)}, f32[32,8,8,512]{3,2,1,0:T(8,128)}, u32[]{:S(2)}) copy-start(f32[32,8,8,512]{3,2,1,0:T(8,128)} %pack_weight.1.weight_ref) | copy-start | bytes 12582916
  144.7 26.1 %copy-start.15 = (f32[8,128]{1,0:T(8,128)S(1)}, f32[8,128]{1,0:T(8,128)}, u32[]{:S(2)}) copy-start(f32[8,128]{1,0:T(8,128)} %get-tuple-element.32) | copy-start | bytes 12292
  148.2 0.8 copy-start.8
  167.5 39.9 %all-to-all-start.6 = ((bf16[32,64,128]{2,1,0:T(8,128)(2,1)}), bf16[32,64,128]{2,1,0:T(8,128)(2,1)S(1)}, u32[]{:S(2)}, u32[]{:S(2)}) async-start(bf16[32,64,128]{2,1,0:T(8,128)(2,1)} %bitcast.9), calls=%async_computation.6 | async-start | bytes 1048576 | tf_op jit(solution)/shard_map/all_to_all | solution.py:491
  170.8 1.2 collective-permute-start
  172.0 3.6 %collective-permute-start.1 = (f32[8,128]{1,0:T(8,128)S(1)}, f32[8,128]{1,0:T(8,128)S(1)}, u32[]{:S(2)}, u32[]{:S(2)}) collective-permute-start(f32[8,128]{1,0:T(8,128)S(1)} %add.15), channel_id=1, source_target_pairs={{0,2},{1,3},{2,0},{3,1},{4,6},{5,7},{6,4},{7,5},{8,10},{9,11},{10,... | collective-permute-start | bytes 12296 | tf_op jit(solution)/shard_map/ppermute | solution.py:498
  175.6 3.8 %collective-permute-start.2 = (f32[8,128]{1,0:T(8,128)S(1)}, f32[8,128]{1,0:T(8,128)S(1)}, u32[]{:S(2)}, u32[]{:S(2)}) collective-permute-start(f32[8,128]{1,0:T(8,128)S(1)} %add.16), channel_id=1, source_target_pairs={{0,4},{1,5},{2,6},{3,7},{4,0},{5,1},{6,2},{7,3},{8,12},{9,13},{10,... | collective-permute-start | bytes 12296 | tf_op jit(solution)/shard_map/ppermute | solution.py:498
  179.4 3.6 %collective-permute-start.3 = (f32[8,128]{1,0:T(8,128)S(1)}, f32[8,128]{1,0:T(8,128)S(1)}, u32[]{:S(2)}, u32[]{:S(2)}) collective-permute-start(f32[8,128]{1,0:T(8,128)S(1)} %add.17), channel_id=1, source_target_pairs={{0,8},{1,9},{2,10},{3,11},{4,12},{5,13},{6,14},{7,15},{8,0},{9,1},... | collective-permute-start | bytes 12296 | tf_op jit(solution)/shard_map/ppermute | solution.py:498
  183.0 4.5 %collective-permute-start.4 = (f32[8,128]{1,0:T(8,128)S(1)}, f32[8,128]{1,0:T(8,128)S(1)}, u32[]{:S(2)}, u32[]{:S(2)}) collective-permute-start(f32[8,128]{1,0:T(8,128)S(1)} %add.18), channel_id=1, source_target_pairs={{0,16},{1,17},{2,18},{3,19},{4,20},{5,21},{6,22},{7,23},{8,24},{9,... | collective-permute-start | bytes 12296 | tf_op jit(solution)/shard_map/ppermute | solution.py:498
  187.5 9.8 %copy-start.14 = (f32[8,128]{1,0:T(8,128)}, f32[8,128]{1,0:T(8,128)S(1)}, u32[]{:S(2)}) copy-start(f32[8,128]{1,0:T(8,128)S(1)} %add_multiply_fusion) | copy-start | bytes 12292
  207.4 0.8 copy-start.11

commit v3 on v2

--- a/solution.py
+++ b/solution.py
@@ -26,6 +26,7 @@
 KQ = 1024
 LANES = 128
 PARTS = 2
+WIDTH = 512
 LOG2_E = math.log2(math.e)
 DENSITY = 1.0 / math.sqrt(2.0 * math.pi)
 F32 = jnp.float32
@@ -53,6 +54,12 @@
 
 def matmul(left, right):
     return jnp.dot(left, right, preferred_element_type=F32)
+
+
+def matmul_turned(left, right):
+    return lax.dot_general(
+        left, right, (((1,), (1,)), ((), ())), preferred_element_type=F32
+    )
 
 
 def swap_groups(tiles):
@@ -73,12 +80,11 @@
     )
 
 
-def pack_modes(modes, packed_ref, xl, tl):
-    width = modes.shape[1]
-    split = modes.reshape(xl, tl, CHANS, width)
-    for tile in range(width // LANES):
-        at = slice(tile * LANES, (tile + 1) * LANES)
-        tiles = [split[:, step, :, at].reshape(xl * CHANS, LANES) for step in range(tl)]
+def pack_modes(modes_ref, packed_ref, xl, tl):
+    for tile in range(KQ // LANES):
+        modes = modes_ref[tile * LANES : (tile + 1) * LANES, :].T
+        split = modes.reshape(xl, tl, CHANS, LANES)
+        tiles = [split[:, step].reshape(xl * CHANS, LANES) for step in range(tl)]
         for owner, block in enumerate(swap_groups(tiles)):
             packed_ref[tile * tl + owner] = block.astype(BF16)
 
@@ -92,26 +98,43 @@
             )
 
 
-def analyse_kernel(xl, tl, field_ref, table_ref, packed_ref):
-    pack_modes(matmul(field_ref[...], table_ref[...]), packed_ref, xl, tl)
-
-
-def analyse(field, table, part, xl, tl, devices):
+def analyse_kernel(xl, tl, field_ref, table_ref, packed_ref, total):
+    step = pl.program_id(0)
+    part = 0.0
+    for at in range(table_ref.shape[0]):
+        part = part + matmul_turned(
+            table_ref[at], field_ref[:, at * WIDTH : (at + 1) * WIDTH]
+        )
+
+    @pl.when(step == 0)
+    def _():
+        total[...] = part
+
+    @pl.when(step > 0)
+    def _():
+        total[...] += part
+
+    @pl.when(step == pl.num_programs(0) - 1)
+    def _():
+        pack_modes(total, packed_ref, xl, tl)
+
+
+def analyse(field, table, xl, tl, devices):
     rows = xl * tl * CHANS
-    steps = 4
-    width = KQ // steps
+    per = 2
     return pl.pallas_call(
         functools.partial(analyse_kernel, xl, tl),
-        grid=(steps,),
+        grid=(CELLS // (per * WIDTH),),
         in_specs=[
-            pl.BlockSpec((rows, CELLS), lambda n: (part, 0)),
-            pl.BlockSpec((CELLS, width), lambda n: (0, n)),
+            pl.BlockSpec((rows, per * WIDTH), lambda n: (0, n)),
+            pl.BlockSpec((per, KQ, WIDTH), lambda n: (n, 0, 0)),
         ],
-        out_specs=pl.BlockSpec((devices // steps, xl * CHANS, LANES), lambda n: (n, 0, 0)),
+        out_specs=pl.BlockSpec((devices, xl * CHANS, LANES), lambda n: (0, 0, 0)),
         out_shape=jax.ShapeDtypeStruct((devices, xl * CHANS, LANES), BF16),
+        scratch_shapes=[pltpu.VMEM((KQ, rows), F32)],
         compiler_params=vmem_params(56),
         cost_estimate=pl.CostEstimate(
-            flops=2 * rows * CELLS * KQ, bytes_accessed=10 << 20, transcendentals=0
+            flops=2 * rows * CELLS * KQ, bytes_accessed=13 << 20, transcendentals=0
         ),
         name="analyse",
     )(field, table)
@@ -141,21 +164,21 @@
     )(weight)
 
 
-def to_modes(spread_refs, x_table_refs, t_table_ref):
+def to_modes(spread_refs, x_table_ref, t_table_ref):
     total = 0.0
-    for spread_ref, x_table_ref in zip(spread_refs, x_table_refs):
+    for part, spread_ref in enumerate(spread_refs):
         gx, ta, rows, _ = spread_ref.shape
         beside = jnp.concatenate(
             [spread_ref[:, at].reshape(gx * rows, LANES) for at in range(ta)], axis=1
         )
-        total = total + matmul(x_table_ref[...], beside)
+        total = total + matmul(x_table_ref[part], beside)
     return matmul(total.astype(BF16), t_table_ref[...])
 
 
 def from_modes(modes, x_table_ref, t_table_ref, held_ref):
-    gx, ta, rows, _ = held_ref.shape[1:]
+    parts, gx, ta, rows, _ = held_ref.shape
     half = matmul(modes.astype(BF16), t_table_ref[...]).astype(BF16)
-    for part in range(PARTS):
+    for part in range(parts):
         full = matmul(x_table_ref[part], half).astype(BF16)
         for at in range(ta):
             held_ref[part, :, at] = full[:, at * LANES : (at + 1) * LANES].reshape(gx, rows, LANES)
@@ -163,29 +186,20 @@
 
 def mix_kernel(
     backward,
-    spread_a_ref,
-    spread_b_ref,
     weight_ref,
+    _,
     x_in_ref,
     t_in_ref,
     x_out_ref,
     t_out_ref,
-    modes_ref,
-    back_a_ref,
-    back_b_ref,
-    weight,
-    modes,
-    mixed,
-    held,
-    weight_sem,
-    modes_sem,
-    back_sems,
+    *refs,
 ):
+    ins, outs = x_in_ref.shape[0], x_out_ref.shape[0]
+    spread_refs, modes_ref, back_refs = refs[:ins], refs[ins], refs[ins + 1 : ins + 1 + outs]
+    weight, modes, mixed, held, weight_sem, modes_sem, back_sems = refs[ins + 1 + outs :]
     fetch = pltpu.make_async_copy(weight_ref, weight, weight_sem)
     fetch.start()
-    modes[...] = to_modes(
-        (spread_a_ref, spread_b_ref), (x_in_ref.at[0], x_in_ref.at[1]), t_in_ref
-    )
+    modes[...] = to_modes(spread_refs, x_in_ref, t_in_ref)
     keep = pltpu.make_async_copy(modes, modes_ref, modes_sem)
     keep.start()
     fetch.wait()
@@ -203,7 +217,7 @@
     from_modes(mixed[...], x_out_ref, t_out_ref, held)
     sends = [
         pltpu.make_async_copy(held.at[part], ref, back_sems.at[part])
-        for part, ref in enumerate((back_a_ref, back_b_ref))
+        for part, ref in enumerate(back_refs)
     ]
     for send in sends:
         send.start()
@@ -212,33 +226,31 @@
     keep.wait()
 
 
-def mix(spreads, weight, tables, backward):
+def mix(spreads, weight, after, tables, backward):
     modes = (KX * CHANS, weight.shape[3])
-    shape = spreads[0].shape
+    gx, ta, _, lanes = spreads[0].shape
+    outs = tables[2].shape[0]
+    back = (gx, ta, tables[2].shape[1] // gx, lanes)
     anywhere = pl.BlockSpec(memory_space=pl.ANY)
     on_chip = pl.BlockSpec(memory_space=pltpu.VMEM)
     return pl.pallas_call(
         functools.partial(mix_kernel, backward),
-        out_shape=(
-            jax.ShapeDtypeStruct(modes, F32),
-            jax.ShapeDtypeStruct(shape, BF16),
-            jax.ShapeDtypeStruct(shape, BF16),
-        ),
-        in_specs=[on_chip] * 2 + [anywhere] + [on_chip] * 4,
-        out_specs=[anywhere] * 3,
+        out_shape=[jax.ShapeDtypeStruct(modes, F32)] + [jax.ShapeDtypeStruct(back, BF16)] * outs,
+        in_specs=[anywhere] * 2 + [on_chip] * (4 + len(spreads)),
+        out_specs=[anywhere] * (1 + outs),
         scratch_shapes=[
             pltpu.VMEM(weight.shape, F32),
             pltpu.VMEM(modes, F32),
             pltpu.VMEM(modes, F32),
-            pltpu.VMEM((PARTS,) + shape, BF16),
+            pltpu.VMEM((outs,) + back, BF16),
             pltpu.SemaphoreType.DMA,
             pltpu.SemaphoreType.DMA,
-            pltpu.SemaphoreType.DMA((PARTS,)),
+            pltpu.SemaphoreType.DMA((outs,)),
         ],
-        compiler_params=vmem_params(32),
+        compiler_params=vmem_params(52),
         cost_estimate=pl.CostEstimate(flops=1 << 30, bytes_accessed=9 << 20, transcendentals=0),
         name="mix_back" if backward else "mix",
-    )(*spreads, weight, *tables)
+    )(weight, after, *tables, *spreads)
 
 
 def outer_kernel(spectrum_ref, grad_ref, result_ref):
@@ -289,8 +301,7 @@
     packed_ref,
     field_ref,
     cotangent_ref,
-    build_ref,
-    analyse_ref,
+    table_ref,
     mixer_ref,
     bias_ref,
     sums_in_ref,
@@ -302,7 +313,6 @@
     wide,
     modes,
     total,
-    gram,
     row_sums,
 ):
     step = pl.program_id(0)
@@ -315,11 +325,10 @@
         unpack_modes(packed_ref, wide, xl, tl)
         modes[...] = wide[...].reshape(rows, KQ).astype(BF16)
         total[...] = jnp.zeros_like(total)
-        gram[...] = jnp.zeros_like(gram)
         row_sums[...] = jnp.zeros_like(row_sums)
 
     def build(at):
-        return matmul(modes[...], build_ref[:, at]) + matmul(mixer_ref[...], field_ref[:, at])
+        return matmul(modes[...], table_ref[0, :, at]) + matmul(mixer_ref[...], field_ref[:, at])
 
     def pointwise(pre, at):
         for first in range(0, rows, chunk):
@@ -338,13 +347,8 @@
             row_sums[part, :] = sums
 
     def gather(at):
-        total[...] += matmul(grad_ref[:, at], analyse_ref[at, :])
-        gram[...] += lax.dot_general(
-            grad_ref[:, at],
-            field_ref[:, at],
-            (((1,), (1,)), ((), ())),
-            preferred_element_type=F32,
-        )
+        passing = jnp.concatenate([table_ref[0, :, at], field_ref[:, at]], axis=0)
+        total[...] += matmul_turned(passing, grad_ref[:, at])
 
     tiles = [slice(first, first + tile) for first in range(0, width, tile)]
     ready = build(tiles[0])
@@ -358,10 +362,10 @@
 
     @pl.when(step == pl.num_programs(0) - 1)
     def _():
-        pack_modes(total[...], sent_ref, xl, tl)
+        pack_modes(total, sent_ref, xl, tl)
         row = lax.broadcasted_iota(jnp.int32, (rows, rows), 0)
         column = lax.broadcasted_iota(jnp.int32, (rows, rows), 1)
-        same = jnp.where(row // CHANS == column // CHANS, gram[...], 0.0)
+        same = jnp.where(row // CHANS == column // CHANS, total[KQ:, :].T, 0.0)
         folded = jnp.sum(same.reshape(rows // CHANS, CHANS, rows), axis=0)
         source = lax.broadcasted_iota(jnp.int32, (rows, LANES), 0)
         target = lax.broadcasted_iota(jnp.int32, (rows, LANES), 1)
@@ -378,20 +382,18 @@
         sums_ref[...] = sums_in_ref[...] + jnp.where(lane == CHANS, bias, point)
 
 
-def middle(packed, field, cotangent, tables, mixer, bias, sums, output, part, xl, tl):
-    build_table, analyse_table = tables
+def middle(packed, field, cotangent, table, mixer, bias, sums, output, part, xl, tl):
     rows = xl * tl * CHANS
-    width = 512
+    width = WIDTH
     whole = lambda *shape: pl.BlockSpec(shape, lambda n: (0,) * len(shape))
     tile = pl.BlockSpec((rows, width), lambda n: (part, n))
     kernel = functools.partial(middle_kernel, xl, tl)
-    operands = (packed, field, cotangent, build_table, analyse_table, mixer, bias, sums)
+    operands = (packed, field, cotangent, table, mixer, bias, sums)
     specs = [
         whole(*packed.shape),
         tile,
         tile,
-        pl.BlockSpec((KQ, width), lambda n: (0, n)),
-        pl.BlockSpec((width, KQ), lambda n: (n, 0)),
+        pl.BlockSpec((1, KQ, width), lambda n: (n, 0, 0)),
         whole(rows, rows),
         whole(rows, LANES),
         whole(CHANS, LANES),
@@ -399,7 +401,7 @@
     aliases = {}
     if output is None:
         inner = kernel
-        kernel = lambda *refs: inner(*refs[:8], None, *refs[8:])
+        kernel = lambda *refs: inner(*refs[:7], None, *refs[7:])
     else:
         aliases = {len(operands): 0}
         operands += (output,)
@@ -423,8 +425,7 @@
         scratch_shapes=[
             pltpu.VMEM((xl, tl, CHANS, KQ), F32),
             pltpu.VMEM((rows, KQ), BF16),
-            pltpu.VMEM((rows, KQ), F32),
-            pltpu.VMEM((rows, rows), F32),
+            pltpu.VMEM((KQ + rows, rows), F32),
             pltpu.VMEM((rows, LANES), F32),
         ],
         input_output_aliases=aliases,
@@ -436,55 +437,43 @@
     )(*operands)
 
 
-def last_kernel(xl, tl, packed_ref, grad_ref, build_ref, mixer_ref, _, field_ref, wide, modes):
-    rows = grad_ref.shape[0]
+def last_kernel(xl, tl, packed_ref, table_ref, mixer_ref, *refs):
+    grad_refs, (field_ref, wide, modes) = refs[:PARTS], refs[PARTS:]
 
     @pl.when(pl.program_id(0) == 0)
     def _():
         unpack_modes(packed_ref, wide, xl, tl)
-        modes[...] = wide[...].reshape(rows, KQ).astype(BF16)
-
-    field_ref[...] = (
-        matmul(modes[...], build_ref[...]) + matmul(mixer_ref[...], grad_ref[...])
-    ).astype(BF16)
-
-
-def last(packed, grad, build_table, mixer, result, part, xl, tl):
-    rows = grad.shape[0]
-    width = 512
-    kernel = functools.partial(last_kernel, xl, tl)
-    operands = (packed, grad, build_table, mixer)
-    specs = [
-        pl.BlockSpec(packed.shape, lambda n: (0, 0, 0)),
-        pl.BlockSpec((rows, width), lambda n: (0, n)),
-        pl.BlockSpec((KQ, width), lambda n: (0, n)),
-        pl.BlockSpec((rows, rows), lambda n: (0, 0)),
-    ]
-    aliases = {}
-    if result is None:
-        inner = kernel
-        kernel = lambda *refs: inner(*refs[:4], None, *refs[4:])
-    else:
-        aliases = {len(operands): 0}
-        operands += (result,)
-        specs.append(pl.BlockSpec(memory_space=pl.ANY))
+        modes[...] = wide[...].reshape(modes.shape).astype(BF16)
+
+    spatial = matmul(modes[...], table_ref[0])
+    point = [matmul(mixer_ref[...], grad_ref[...]) for grad_ref in grad_refs]
+    field_ref[...] = (spatial + jnp.concatenate(point, axis=0)).astype(BF16)
+
+
+def last(packed, grads, table, mixer, xl, tl):
+    rows = xl * tl * CHANS
+    part = rows // PARTS
     return pl.pallas_call(
-        kernel,
-        grid=(CELLS // width,),
-        in_specs=specs,
-        out_specs=pl.BlockSpec((rows, width), lambda n: (part, n)),
-        out_shape=jax.ShapeDtypeStruct((rows * PARTS, CELLS), BF16),
+        functools.partial(last_kernel, xl, tl),
+        grid=(CELLS // WIDTH,),
+        in_specs=[
+            pl.BlockSpec(packed.shape, lambda n: (0, 0, 0)),
+            pl.BlockSpec((1, KQ, WIDTH), lambda n: (n, 0, 0)),
+            pl.BlockSpec((part, part), lambda n: (0, 0)),
+        ]
+        + [pl.BlockSpec((part, WIDTH), lambda n: (0, n))] * PARTS,
+        out_specs=pl.BlockSpec((rows, WIDTH), lambda n: (0, n)),
+        out_shape=jax.ShapeDtypeStruct((rows, CELLS), BF16),
         scratch_shapes=[
             pltpu.VMEM((xl, tl, CHANS, KQ), F32),
             pltpu.VMEM((rows, KQ), BF16),
         ],
-        input_output_aliases=aliases,
         compiler_params=vmem_params(56),
         cost_estimate=pl.CostEstimate(
-            flops=2 * rows * CELLS * KQ, bytes_accessed=12 << 20, transcendentals=0
+            flops=2 * rows * CELLS * KQ, bytes_accessed=18 << 20, transcendentals=0
         ),
         name="last",
-    )(*operands)
+    )(packed, table, mixer, *grads)
 
 
 def swap(blocks):
@@ -509,17 +498,23 @@
     yz = np.kron(
         narrow(basis(NY, MY)).astype(np.float32), narrow(basis(NZ, MZ)).astype(np.float32)
     )
-    build_table = jnp.asarray(narrow(yz))
-    analyse_table = jnp.asarray(narrow(yz.T))
+    blocks = yz.reshape(KQ, CELLS // WIDTH, WIDTH).transpose(1, 0, 2)
+    table = jnp.asarray(narrow(blocks))
+    x_whole = basis(NX, MX).reshape(KX, gx, 1, xl_all)
     x_split = basis(NX, MX).reshape(KX, gx, PARTS, xl)
-    x_wide = [
-        np.kron(x_split[:, :, part].reshape(KX, gx * xl), np.eye(CHANS)) for part in range(PARTS)
+    x_tables = [
+        np.stack(
+            [
+                np.kron(split[:, :, part].reshape(KX, -1), np.eye(CHANS))
+                for part in range(split.shape[2])
+            ]
+        )
+        for split in (x_whole, x_split)
     ]
+    x_in = [jnp.asarray(narrow(x_table)) for x_table in x_tables]
+    x_out = [jnp.asarray(narrow(x_table.transpose(0, 2, 1))) for x_table in x_tables]
     t_wide = np.kron(basis(NT, MT), np.eye(own))
-    x_in = jnp.asarray(narrow(np.stack(x_wide)))
-    x_out = jnp.asarray(narrow(np.stack([table.T for table in x_wide])))
     t_in, t_out = jnp.asarray(narrow(t_wide.T)), jnp.asarray(narrow(t_wide))
-    tables = (x_in, t_in, x_out, t_out)
     norm_scale = float(BATCH * NX * NT * NY * NZ) ** (-0.5)
 
     field = features.reshape(PARTS * rows, cells)
@@ -536,43 +531,32 @@
         jnp.broadcast_to(bias_vector[:, None], (CHANS, LANES)),
         precision=lax.Precision.HIGHEST,
     )
-    spread_shape = (gx, ta, xl * CHANS, LANES)
-    block_shape = (devices, xl * CHANS, LANES)
-
+    part_shape = (gx, ta, xl * CHANS, LANES)
+    whole_shape = (gx, ta, xl_all * CHANS, LANES)
     packed_weight = pack_weight(spec_weight)
-    spread_in = [
-        swap(analyse(field, analyse_table, part, xl, tl, devices)).reshape(spread_shape)
-        for part in range(PARTS)
-    ]
-    spectrum, *mixed = mix(spread_in, packed_weight, tables, False)
-    output, sums = None, jnp.zeros((CHANS, LANES), F32)
+    sums = jnp.zeros((CHANS, LANES), F32)
+
+    spread_in = swap(analyse(field, table, xl_all, tl, devices)).reshape(whole_shape)
+    spectrum, *mixed = mix(
+        [spread_in], packed_weight, sums, (x_in[0], t_in, x_out[1], t_out), False
+    )
+    output = None
     grads, spread_grad = [], []
     for part in range(PARTS):
-        returned = swap(mixed[part].reshape(block_shape))
+        returned = swap(mixed[part].reshape(devices, xl * CHANS, LANES))
         output, grad, sent, sums = middle(
-            returned,
-            field,
-            cot,
-            (build_table, analyse_table),
-            mixer,
-            bias,
-            sums,
-            output,
-            part,
-            xl,
-            tl,
+            returned, field, cot, table, mixer, bias, sums, output, part, xl, tl
         )
         grads.append(grad)
-        spread_grad.append(swap(sent).reshape(spread_shape))
-    summed = sum_everywhere(sums, devices) * norm_scale
-    grad_modes, *mixed_back = mix(spread_grad, packed_weight, tables, True)
-    grad_field = None
-    for part in range(PARTS):
-        grad_back = swap(mixed_back[part].reshape(block_shape))
-        grad_field = last(
-            grad_back, grads[part], build_table, mixer_back, grad_field, part, xl, tl
-        )
+        spread_grad.append(swap(sent).reshape(part_shape))
+    summed = sum_everywhere(sums, devices)
+    grad_modes, mixed_back = mix(
+        spread_grad, packed_weight, summed, (x_in[1], t_in, x_out[0], t_out), True
+    )
+    grad_back = swap(mixed_back.reshape(devices, xl_all * CHANS, LANES))
     grad_spec = outer(spectrum, grad_modes, own)
+    grad_field = last(grad_back, grads, table, mixer_back, xl_all, tl)
+    summed = summed * norm_scale
     return (
         output.reshape(features.shape),
         grad_field.reshape(features.shape),

time: 220 us -> 196 us (0.89)
  blocking collectives: 58.4 us -> 19.1 us
  waiting for transfers between devices: 20.7 us -> 39.7 us
  Pallas kernels: 96.3 us -> 90.4 us
  starting transfers between devices: 30.2 us -> 35.7 us
  local copies, waits for them, and re-layouts: 8.11 us -> 5.11 us
    all_to_all x3 -> x1, blocking collectives: 58.4 us -> 19.1 us  [swap(): lax.all_to_all(blocks, ('gx', 'ta'), split_axis=0, concat_axis=0, tiled=T...]
    all_to_all x5, waiting for transfers between devices: 12.6 us -> 30.8 us  [swap(): lax.all_to_all(blocks, ('gx', 'ta'), split_axis=0, concat_axis=0, tiled=T...]
    all_to_all x5, starting transfers between devices: 22.5 us -> 27.9 us  [swap(): lax.all_to_all(blocks, ('gx', 'ta'), split_axis=0, concat_axis=0, tiled=T...]
    pallas_call x6 -> x4, Pallas kernels: 40.5 us -> 36.5 us  [the longest x1 12.9 us: last(): pl.pallas_call(functools.partial(last_kernel, xl, tl), grid=(CELLS // WID...]
    unnamed x34 -> x32, local copies, waits for them, and re-layouts: 6.83 us -> 4.42 us
  transfers between devices with their start and end apart: 10 -> 10, of which waited for: 7 -> 7; matrix products, arithmetic and copies ran while one was open for 2% -> 2% of each run, Pallas kernels for 34% -> 28%
where the time goes in v3:
time: 196 us; the launch traced here: 194 us
  Pallas kernels  90.4 us (46%)
  waiting for transfers between devices  39.7 us (20%)
  starting transfers between devices  35.7 us (18%)
  blocking collectives  19.1 us (10%)
  local copies, waits for them, and re-layouts  5.11 us (3%)
  matrix products  2.84 us (1%)
    pallas_call x2, Pallas kernels, middle(): pl.pallas_call(kernel, grid=(CELLS // width,), in_specs=specs, out_specs=...  33.8 us
    all_to_all x5, waiting for transfers between devices, swap(): lax.all_to_all(blocks, ('gx', 'ta'), split_axis=0, concat_axis=0, tiled=T...  30.8 us
    all_to_all x5, starting transfers between devices, swap(): lax.all_to_all(blocks, ('gx', 'ta'), split_axis=0, concat_axis=0, tiled=T...  27.9 us
    all_to_all x1, blocking collectives, swap(): lax.all_to_all(blocks, ('gx', 'ta'), split_axis=0, concat_axis=0, tiled=T...  19.1 us
    pallas_call x1, Pallas kernels, last(): pl.pallas_call(functools.partial(last_kernel, xl, tl), grid=(CELLS // WID...  12.9 us
    pallas_call x2, Pallas kernels, mix(): pl.pallas_call(functools.partial(mix_kernel, backward), out_shape=[jax.Sh...  12.7 us
    pallas_call x1, Pallas kernels, pack_weight(): pl.pallas_call(weight_kernel, grid=(KX // per,), in_specs=[pl.BlockSpec((...  11 us
    pallas_call x1, Pallas kernels, analyse(): pl.pallas_call(functools.partial(analyse_kernel, xl, tl), grid=(CELLS //...  10.8 us
  transfers between devices with their start and end apart: 10, of which 7 were waited for; matrix products, arithmetic and copies ran while one was open for 2% of the time, Pallas kernels for 28%

profile of v3, /device:TPU:0, one launch (start us, length us, event | category | flops | bytes accessed | tf_op | source)
XLA Modules:
  0.0 194.4 jit_solution(8180533492682195173)
XLA Ops:
  0.6 10.8 %analyse.1 = bf16[32,128,128]{2,1,0:T(8,128)(2,1)} custom-call(bf16[512,4096]{1,0:T(8,128)(2,1)} %bitcast.21, bf16[8,1024,512]{2,1,0:T(8,128)(2,1)} %constant.24.clone.table_ref.refs_3_), custom_call_target="tpu_custom_call" | custom-call | flops 4294967296 | bytes 13631488 | tf_op jit(solution)/shard_map/analyse/pallas_call | solution.py:125
  11.5 7.3 %all-to-all-start = ((bf16[32,128,128]{2,1,0:T(8,128)(2,1)}), bf16[32,128,128]{2,1,0:T(8,128)(2,1)S(1)}, u32[]{:S(2)}, u32[]{:S(2)}) async-start(bf16[32,128,128]{2,1,0:T(8,128)(2,1)} %analyse.1), calls=%async_computation | async-start | bytes 2097152 | tf_op jit(solution)/shard_map/all_to_all | solution.py:480
  18.8 11.0 %pack_weight.1.weight_ref = f32[32,8,8,512]{3,2,1,0:T(8,128)} custom-call(f32[32,16,8,8,32]{4,3,2,1,0:T(8,128)} %weight_ref.1), custom_call_target="tpu_custom_call" | custom-call | flops 1048576 | bytes 20971520 | tf_op jit(solution)/shard_map/pack_weight/pallas_call | solution.py:155
  29.8 15.2 %all-to-all-done = bf16[32,128,128]{2,1,0:T(8,128)(2,1)S(1)} async-done(((bf16[32,128,128]{2,1,0:T(8,128)(2,1)}), bf16[32,128,128]{2,1,0:T(8,128)(2,1)S(1)}, u32[]{:S(2)}, u32[]{:S(2)}) %all-to-all-start) | async-done | bytes 1048608 | tf_op jit(solution)/shard_map/all_to_all | solution.py:480
  45.0 1.0 copy-done.7
  46.0 6.0 %mix.1 = (f32[256,512]{1,0:T(8,128)S(1)}, bf16[8,4,64,128]{3,2,1,0:T(8,128)(2,1)S(1)}, bf16[8,4,64,128]{3,2,1,0:T(8,128)(2,1)}) custom-call(f32[32,8,8,512]{3,2,1,0:T(8,128)} %pack_weight.1.weight_ref, f32[8,128]{1,0:T(8,128)S(1)} %broadcast_in_dim.4._.refs_6_, bf16[1,256,1024]{2,1,0:T(8,128)(2,1)} %constant.25.clone.x_in_ref, ...), custom_call_target="tpu_custom_call" | custom-call | flops 1073741824 | bytes 9437184 | tf_op jit(solution)/shard_map/mix/pallas_call | solution.py:236
  52.0 0.8 copy-done.3
  52.8 19.1 %all_to_all.30.refs_0_ = bf16[32,64,128]{2,1,0:T(8,128)(2,1)} all-to-all(bf16[32,64,128]{2,1,0:T(8,128)(2,1)S(1)} %bitcast.18), channel_id=1, replica_groups=mesh['gx'=8,'ta'=4] {'gx','ta'}, dimensions={0} | all-to-all | bytes 1048576 | tf_op jit(solution)/shard_map/all_to_all | solution.py:480
  71.8 3.1 %all-to-all-start.1 = ((bf16[32,64,128]{2,1,0:T(8,128)(2,1)}), bf16[32,64,128]{2,1,0:T(8,128)(2,1)S(1)}, u32[]{:S(2)}, u32[]{:S(2)}) async-start(bf16[32,64,128]{2,1,0:T(8,128)(2,1)} %bitcast.2), calls=%async_computation.1 | async-start | bytes 1048576 | tf_op jit(solution)/shard_map/all_to_all | solution.py:480
  74.9 1.0 fusion.2.refs_5_.bias_ref
  75.9 0.9 fusion.refs_4_.mixer_ref
  76.9 16.9 %middle.2 = (bf16[512,4096]{1,0:T(8,128)(2,1)}, bf16[256,4096]{1,0:T(8,128)(2,1)}, bf16[32,64,128]{2,1,0:T(8,128)(2,1)}, f32[8,128]{1,0:T(8,128)}) custom-call(bf16[32,64,128]{2,1,0:T(8,128)(2,1)} %all_to_all.30.refs_0_, bf16[512,4096]{1,0:T(8,128)(2,1)} %bitcast.22, bf16[512,4096]{1,0:T(8,128)(2,1)} %bitcast.24, ...), custom_call_target="tpu_custom_call" | custom-call | flops 5368709120 | bytes 27262976 | tf_op jit(solution)/shard_map/middle/pallas_call | solution.py:409
  93.8 5.8 %all-to-all-start.3 = ((bf16[32,64,128]{2,1,0:T(8,128)(2,1)}), bf16[32,64,128]{2,1,0:T(8,128)(2,1)S(1)}, u32[]{:S(2)}, u32[]{:S(2)}) async-start(bf16[32,64,128]{2,1,0:T(8,128)(2,1)} %get-tuple-element.24), calls=%async_computation.3 | async-start | bytes 1048576 | tf_op jit(solution)/shard_map/all_to_all | solution.py:480
  99.7 16.9 %middle.3 = (bf16[512,4096]{1,0:T(8,128)(2,1)}, bf16[256,4096]{1,0:T(8,128)(2,1)}, bf16[32,64,128]{2,1,0:T(8,128)(2,1)}, f32[8,128]{1,0:T(8,128)}) custom-call(bf16[32,64,128]{2,1,0:T(8,128)(2,1)} %copy-done.10, bf16[512,4096]{1,0:T(8,128)(2,1)} %bitcast.23, bf16[512,4096]{1,0:T(8,128)(2,1)} %bitcast.25, ...), custom_call_target="tpu_custom_call", output_to_operand_aliasing={{0}: (7, {})} | custom-call | flops 5368709120 | bytes 27262976 | tf_op jit(solution)/shard_map/middle/pallas_call | solution.py:409
  116.6 6.0 %all-to-all-start.4 = ((bf16[32,64,128]{2,1,0:T(8,128)(2,1)}), bf16[32,64,128]{2,1,0:T(8,128)(2,1)S(1)}, u32[]{:S(2)}, u32[]{:S(2)}) async-start(bf16[32,64,128]{2,1,0:T(8,128)(2,1)} %get-tuple-element.25), calls=%async_computation.4 | async-start | bytes 1048576 | tf_op jit(solution)/shard_map/all_to_all | solution.py:480
  122.8 1.3 collective-permute-done
  124.8 1.6 collective-permute-start.1
  126.4 2.0 %collective-permute-done.1 = f32[8,128]{1,0:T(8,128)S(1)} collective-permute-done((f32[8,128]{1,0:T(8,128)S(1)}, f32[8,128]{1,0:T(8,128)S(1)}, u32[]{:S(2)}, u32[]{:S(2)}) %collective-permute-start.1) | collective-permute-done | bytes 4128 | tf_op jit(solution)/shard_map/ppermute | solution.py:487
  128.4 1.8 collective-permute-start.2
  130.2 1.8 collective-permute-done.2
  132.0 1.6 collective-permute-start.3
  133.7 2.0 %collective-permute-done.3 = f32[8,128]{1,0:T(8,128)S(1)} collective-permute-done((f32[8,128]{1,0:T(8,128)S(1)}, f32[8,128]{1,0:T(8,128)S(1)}, u32[]{:S(2)}, u32[]{:S(2)}) %collective-permute-start.3) | collective-permute-done | bytes 4128 | tf_op jit(solution)/shard_map/ppermute | solution.py:487
  135.6 2.6 %collective-permute-start.4 = (f32[8,128]{1,0:T(8,128)S(1)}, f32[8,128]{1,0:T(8,128)S(1)}, u32[]{:S(2)}, u32[]{:S(2)}) collective-permute-start(f32[8,128]{1,0:T(8,128)S(1)} %add.18), channel_id=1, source_target_pairs={{0,16},{1,17},{2,18},{3,19},{4,20},{5,21},{6,22},{7,23},{8,24},{9,... | collective-permute-start | bytes 12296 | tf_op jit(solution)/shard_map/ppermute | solution.py:487
  138.3 1.9 collective-permute-done.4
  141.0 6.8 %mix_back.1 = (f32[256,512]{1,0:T(8,128)S(1)}, bf16[8,4,128,128]{3,2,1,0:T(8,128)(2,1)}) custom-call(f32[32,8,8,512]{3,2,1,0:T(8,128)} %pack_weight.1.weight_ref, f32[8,128]{1,0:T(8,128)S(1)} %get-tuple-element.32._, bf16[2,256,512]{2,1,0:T(8,128)(2,1)S(1)} %copy-done.2, bf16[512,512]{1,0:T(8,128)(2,1)S(1)} %copy-done.1, ...), custom_call_target="tpu_custom_call" | custom-call | flops 1073741824 | bytes 9437184 | tf_op jit(solution)/shard_map/mix_back/pallas_call | solution.py:236
  147.8 0.8 copy-done.4
  148.5 5.7 %all-to-all-start.5 = ((bf16[32,128,128]{2,1,0:T(8,128)(2,1)}), bf16[32,128,128]{2,1,0:T(8,128)(2,1)S(1)}, u32[]{:S(2)}, u32[]{:S(2)}) async-start(bf16[32,128,128]{2,1,0:T(8,128)(2,1)} %bitcast.29), calls=%async_computation.5 | async-start | bytes 2097152 | tf_op jit(solution)/shard_map/all_to_all | solution.py:480
  154.2 0.9 fusion.1.mixer_ref
  155.9 9.1 %outer.1 = f32[32,16,8,8,32]{4,3,2,1,0:T(8,128)} custom-call(f32[256,512]{1,0:T(8,128)} %copy-done.3, f32[256,512]{1,0:T(8,128)} %copy-done.4), custom_call_target="tpu_custom_call" | custom-call | flops 1048576 | bytes 17825792 | tf_op jit(solution)/shard_map/outer/pallas_call | solution.py:273
  164.9 15.5 %all-to-all-done.5.packed_ref = bf16[32,128,128]{2,1,0:T(8,128)(2,1)S(1)} async-done(((bf16[32,128,128]{2,1,0:T(8,128)(2,1)}), bf16[32,128,128]{2,1,0:T(8,128)(2,1)S(1)}, u32[]{:S(2)}, u32[]{:S(2)}) %all-to-all-start.5) | async-done | bytes 1048608 | tf_op jit(solution)/shard_map/all_to_all | solution.py:480
  180.5 1.0 copy-done.6
  181.5 12.9 %last.1 = bf16[512,4096]{1,0:T(8,128)(2,1)} custom-call(bf16[32,128,128]{2,1,0:T(8,128)(2,1)} %copy-done.6, bf16[8,1024,512]{2,1,0:T(8,128)(2,1)} %constant.24.clone.table_ref.refs_3_, bf16[256,256]{1,0:T(8,128)(2,1)} %fusion.1.mixer_ref, bf16[256,4096]{1,0:T(8,128)(2,1)} %get-tuple-element.27.refs_0_, bf16[256,4096]{1,0:T(8,128)(2,1)} %get-tuple-element.28.refs_1_), custom_call_target="tpu_custom_call" | custom-call | flops 4294967296 | bytes 18874368 | tf_op jit(solution)/shard_map/last/pallas_call | solution.py:456
  (39 shorter events, 2.4 us)
Async XLA Ops:
  0.6 75.3 %copy-start = (bf16[8,8]{1,0:T(8,128)(2,1)S(1)}, bf16[8,8]{1,0:T(8,128)(2,1)}, u32[]{:S(2)}) copy-start(bf16[8,8]{1,0:T(8,128)(2,1)} %param.18) | copy-start | bytes 388
  11.5 33.5 %all-to-all-start = ((bf16[32,128,128]{2,1,0:T(8,128)(2,1)}), bf16[32,128,128]{2,1,0:T(8,128)(2,1)S(1)}, u32[]{:S(2)}, u32[]{:S(2)}) async-start(bf16[32,128,128]{2,1,0:T(8,128)(2,1)} %analyse.1), calls=%async_computation | async-start | bytes 2097152 | tf_op jit(solution)/shard_map/all_to_all | solution.py:480
  45.0 1.0 copy-start.7
  46.0 25.9 %copy-start.5 = (f32[8,128]{1,0:T(8,128)}, f32[8,128]{1,0:T(8,128)S(1)}, u32[]{:S(2)}) copy-start(f32[8,128]{1,0:T(8,128)S(1)} %broadcast_in_dim.4._.refs_6_) | copy-start | bytes 12292
  46.0 28.9 %copy-start.13 = (f32[256,8]{1,0:T(8,128)S(1)}, f32[256,8]{1,0:T(8,128)}, u32[]{:S(2)}) copy-start(f32[256,8]{1,0:T(8,128)} %constant.33.clone) | copy-start | bytes 24580
  46.0 29.0 %copy-start.15 = (f32[8]{0:T(128)S(1)}, f32[8]{0:T(128)}, u32[]{:S(2)}) copy-start(f32[8]{0:T(128)} %param.19) | copy-start | bytes 100
  46.0 29.9 %copy-start.11 = (f32[256,256]{1,0:T(8,128)S(1)}, f32[256,256]{1,0:T(8,128)}, u32[]{:S(2)}) copy-start(f32[256,256]{1,0:T(8,128)} %constant.32.clone) | copy-start | bytes 786436
  46.0 29.9 %copy-start.12 = (bf16[256,8]{1,0:T(8,128)(2,1)S(1)}, bf16[256,8]{1,0:T(8,128)(2,1)}, u32[]{:S(2)}) copy-start(bf16[256,8]{1,0:T(8,128)(2,1)} %constant.31.clone) | copy-start | bytes 12292
  52.0 0.8 copy-start.3
  71.8 21.9 %all-to-all-start.1 = ((bf16[32,64,128]{2,1,0:T(8,128)(2,1)}), bf16[32,64,128]{2,1,0:T(8,128)(2,1)S(1)}, u32[]{:S(2)}, u32[]{:S(2)}) async-start(bf16[32,64,128]{2,1,0:T(8,128)(2,1)} %bitcast.2), calls=%async_computation.1 | async-start | bytes 1048576 | tf_op jit(solution)/shard_map/all_to_all | solution.py:480
  93.8 5.9 %copy-start.10 = (bf16[32,64,128]{2,1,0:T(8,128)(2,1)}, bf16[32,64,128]{2,1,0:T(8,128)(2,1)S(1)}, u32[]{:S(2)}) copy-start(bf16[32,64,128]{2,1,0:T(8,128)(2,1)S(1)} %all-to-all-done.1.packed_ref) | copy-start | bytes 1572868
  93.8 22.8 %all-to-all-start.3 = ((bf16[32,64,128]{2,1,0:T(8,128)(2,1)}), bf16[32,64,128]{2,1,0:T(8,128)(2,1)S(1)}, u32[]{:S(2)}, u32[]{:S(2)}) async-start(bf16[32,64,128]{2,1,0:T(8,128)(2,1)} %get-tuple-element.24), calls=%async_computation.3 | async-start | bytes 1048576 | tf_op jit(solution)/shard_map/all_to_all | solution.py:480
  99.6 41.3 %copy-start.1 = (bf16[512,512]{1,0:T(8,128)(2,1)S(1)}, bf16[512,512]{1,0:T(8,128)(2,1)}, u32[]{:S(2)}) copy-start(bf16[512,512]{1,0:T(8,128)(2,1)} %constant.29.clone.t_in_ref) | copy-start | bytes 1572868
  99.6 41.3 %copy-start.2 = (bf16[2,256,512]{2,1,0:T(8,128)(2,1)S(1)}, bf16[2,256,512]{2,1,0:T(8,128)(2,1)}, u32[]{:S(2)}) copy-start(bf16[2,256,512]{2,1,0:T(8,128)(2,1)} %constant.26.clone.x_in_ref) | copy-start | bytes 1572868
  116.6 23.5 %copy-start.8 = (bf16[32,64,128]{2,1,0:T(8,128)(2,1)}, bf16[32,64,128]{2,1,0:T(8,128)(2,1)S(1)}, u32[]{:S(2)}) copy-start(bf16[32,64,128]{2,1,0:T(8,128)(2,1)S(1)} %all-to-all-done.3) | copy-start | bytes 1572868
  116.6 23.5 %all-to-all-start.4 = ((bf16[32,64,128]{2,1,0:T(8,128)(2,1)}), bf16[32,64,128]{2,1,0:T(8,128)(2,1)S(1)}, u32[]{:S(2)}, u32[]{:S(2)}) async-start(bf16[32,64,128]{2,1,0:T(8,128)(2,1)} %get-tuple-element.25), calls=%async_computation.4 | async-start | bytes 1048576 | tf_op jit(solution)/shard_map/all_to_all | solution.py:480
  122.7 1.4 collective-permute-start
  124.8 3.6 %collective-permute-start.1 = (f32[8,128]{1,0:T(8,128)S(1)}, f32[8,128]{1,0:T(8,128)S(1)}, u32[]{:S(2)}, u32[]{:S(2)}) collective-permute-start(f32[8,128]{1,0:T(8,128)S(1)} %add.15), channel_id=1, source_target_pairs={{0,2},{1,3},{2,0},{3,1},{4,6},{5,7},{6,4},{7,5},{8,10},{9,11},{10,... | collective-permute-start | bytes 12296 | tf_op jit(solution)/shard_map/ppermute | solution.py:487
  128.4 3.6 %collective-permute-start.2 = (f32[8,128]{1,0:T(8,128)S(1)}, f32[8,128]{1,0:T(8,128)S(1)}, u32[]{:S(2)}, u32[]{:S(2)}) collective-permute-start(f32[8,128]{1,0:T(8,128)S(1)} %add.16), channel_id=1, source_target_pairs={{0,4},{1,5},{2,6},{3,7},{4,0},{5,1},{6,2},{7,3},{8,12},{9,13},{10,... | collective-permute-start | bytes 12296 | tf_op jit(solution)/shard_map/ppermute | solution.py:487
  132.0 3.6 %collective-permute-start.3 = (f32[8,128]{1,0:T(8,128)S(1)}, f32[8,128]{1,0:T(8,128)S(1)}, u32[]{:S(2)}, u32[]{:S(2)}) collective-permute-start(f32[8,128]{1,0:T(8,128)S(1)} %add.17), channel_id=1, source_target_pairs={{0,8},{1,9},{2,10},{3,11},{4,12},{5,13},{6,14},{7,15},{8,0},{9,1},... | collective-permute-start | bytes 12296 | tf_op jit(solution)/shard_map/ppermute | solution.py:487
  135.6 4.5 %collective-permute-start.4 = (f32[8,128]{1,0:T(8,128)S(1)}, f32[8,128]{1,0:T(8,128)S(1)}, u32[]{:S(2)}, u32[]{:S(2)}) collective-permute-start(f32[8,128]{1,0:T(8,128)S(1)} %add.18), channel_id=1, source_target_pairs={{0,16},{1,17},{2,18},{3,19},{4,20},{5,21},{6,22},{7,23},{8,24},{9,... | collective-permute-start | bytes 12296 | tf_op jit(solution)/shard_map/ppermute | solution.py:487
  140.1 15.0 %copy-start.14 = (f32[8,128]{1,0:T(8,128)}, f32[8,128]{1,0:T(8,128)S(1)}, u32[]{:S(2)}) copy-start(f32[8,128]{1,0:T(8,128)S(1)} %get-tuple-element.31) | copy-start | bytes 12292
  140.2 0.8 copy-start.9
  147.7 0.8 copy-start.4
  148.5 31.9 %all-to-all-start.5 = ((bf16[32,128,128]{2,1,0:T(8,128)(2,1)}), bf16[32,128,128]{2,1,0:T(8,128)(2,1)S(1)}, u32[]{:S(2)}, u32[]{:S(2)}) async-start(bf16[32,128,128]{2,1,0:T(8,128)(2,1)} %bitcast.29), calls=%async_computation.5 | async-start | bytes 2097152 | tf_op jit(solution)/shard_map/all_to_all | solution.py:480
  180.5 1.0 copy-start.6

commit v4 on v3

--- a/solution.py
+++ b/solution.py
@@ -80,13 +80,19 @@
     )
 
 
-def pack_modes(modes_ref, packed_ref, xl, tl):
+def pack_modes(modes_ref, held_ref, packed_ref, sems, xl, tl):
+    sends = []
     for tile in range(KQ // LANES):
         modes = modes_ref[tile * LANES : (tile + 1) * LANES, :].T
         split = modes.reshape(xl, tl, CHANS, LANES)
         tiles = [split[:, step].reshape(xl * CHANS, LANES) for step in range(tl)]
-        for owner, block in enumerate(swap_groups(tiles)):
-            packed_ref[tile * tl + owner] = block.astype(BF16)
+        owners = slice(tile * tl, (tile + 1) * tl)
+        held_ref[owners] = jnp.stack([block.astype(BF16) for block in swap_groups(tiles)])
+        send = pltpu.make_async_copy(held_ref.at[owners], packed_ref.at[owners], sems.at[tile])
+        send.start()
+        sends.append(send)
+    for send in sends:
+        send.wait()
 
 
 def unpack_modes(packed_ref, wide_ref, xl, tl):
@@ -98,41 +104,60 @@
             )
 
 
-def analyse_kernel(xl, tl, field_ref, table_ref, packed_ref, total):
-    step = pl.program_id(0)
-    part = 0.0
-    for at in range(table_ref.shape[0]):
-        part = part + matmul_turned(
-            table_ref[at], field_ref[:, at * WIDTH : (at + 1) * WIDTH]
-        )
-
-    @pl.when(step == 0)
-    def _():
-        total[...] = part
-
-    @pl.when(step > 0)
-    def _():
-        total[...] += part
-
-    @pl.when(step == pl.num_programs(0) - 1)
-    def _():
-        pack_modes(total, packed_ref, xl, tl)
+def analyse_kernel(
+    xl, tl, field_ref, table_ref, packed_ref, field, table, total, held, field_sems, table_sems, sems
+):
+    chunks = table.shape[0]
+    ahead = 4
+    fetches = []
+    for at in range(chunks):
+        lanes = slice(at * WIDTH, (at + 1) * WIDTH)
+        fetches.append(
+            (
+                pltpu.make_async_copy(field_ref.at[:, lanes], field.at[at], field_sems.at[at]),
+                pltpu.make_async_copy(table_ref.at[at], table.at[at], table_sems.at[at]),
+            )
+        )
+
+    def start(at):
+        for fetch in fetches[at]:
+            fetch.start()
+
+    for at in range(ahead):
+        start(at)
+    for at in range(0, chunks, 2):
+        for now in (at, at + 1):
+            for fetch in fetches[now]:
+                fetch.wait()
+            if now + ahead < chunks:
+                start(now + ahead)
+        part = matmul_turned(
+            jnp.concatenate([table[at], table[at + 1]], axis=1),
+            jnp.concatenate([field[at], field[at + 1]], axis=1),
+        )
+        total[...] = part if at == 0 else total[...] + part
+    pack_modes(total, held, packed_ref, sems, xl, tl)
 
 
 def analyse(field, table, xl, tl, devices):
     rows = xl * tl * CHANS
-    per = 2
+    chunks = CELLS // WIDTH
+    packed = (devices, xl * CHANS, LANES)
     return pl.pallas_call(
         functools.partial(analyse_kernel, xl, tl),
-        grid=(CELLS // (per * WIDTH),),
-        in_specs=[
-            pl.BlockSpec((rows, per * WIDTH), lambda n: (0, n)),
-            pl.BlockSpec((per, KQ, WIDTH), lambda n: (n, 0, 0)),
+        in_specs=[pl.BlockSpec(memory_space=pltpu.HBM)] * 2,
+        out_specs=pl.BlockSpec(memory_space=pl.ANY),
+        out_shape=jax.ShapeDtypeStruct(packed, BF16),
+        scratch_shapes=[
+            pltpu.VMEM((chunks, rows, WIDTH), BF16),
+            pltpu.VMEM((chunks, KQ, WIDTH), BF16),
+            pltpu.VMEM((KQ, rows), F32),
+            pltpu.VMEM(packed, BF16),
+            pltpu.SemaphoreType.DMA((chunks,)),
+            pltpu.SemaphoreType.DMA((chunks,)),
+            pltpu.SemaphoreType.DMA((KQ // LANES,)),
         ],
-        out_specs=pl.BlockSpec((devices, xl * CHANS, LANES), lambda n: (0, 0, 0)),
-        out_shape=jax.ShapeDtypeStruct((devices, xl * CHANS, LANES), BF16),
-        scratch_shapes=[pltpu.VMEM((KQ, rows), F32)],
-        compiler_params=vmem_params(56),
+        compiler_params=vmem_params(44),
         cost_estimate=pl.CostEstimate(
             flops=2 * rows * CELLS * KQ, bytes_accessed=13 << 20, transcendentals=0
         ),
@@ -158,7 +183,7 @@
         in_specs=[pl.BlockSpec((per, KT, CHANS, CHANS, own), lambda n: (n, 0, 0, 0, 0))],
         out_specs=pl.BlockSpec((per, CHANS, CHANS, KT * own), lambda n: (n, 0, 0, 0)),
         out_shape=jax.ShapeDtypeStruct((KX, CHANS, CHANS, KT * own), F32),
-        compiler_params=vmem_params(56),
+        compiler_params=vmem_params(44),
         cost_estimate=pl.CostEstimate(flops=1 << 20, bytes_accessed=20 << 20, transcendentals=0),
         name="pack_weight",
     )(weight)
@@ -196,13 +221,31 @@
 ):
     ins, outs = x_in_ref.shape[0], x_out_ref.shape[0]
     spread_refs, modes_ref, back_refs = refs[:ins], refs[ins], refs[ins + 1 : ins + 1 + outs]
-    weight, modes, mixed, held, weight_sem, modes_sem, back_sems = refs[ins + 1 + outs :]
-    fetch = pltpu.make_async_copy(weight_ref, weight, weight_sem)
-    fetch.start()
-    modes[...] = to_modes(spread_refs, x_in_ref, t_in_ref)
-    keep = pltpu.make_async_copy(modes, modes_ref, modes_sem)
+    weight, modes, mixed, held, x_in, t_in, x_out, t_out, sems, weight_sems, back_sems = refs[
+        ins + 1 + outs :
+    ]
+    pieces = weight_sems.shape[0]
+    per = KX // pieces
+    sources = (x_in_ref, t_in_ref, t_out_ref, x_out_ref)
+    tables = [
+        pltpu.make_async_copy(source, target, sems.at[at])
+        for at, (source, target) in enumerate(zip(sources, (x_in, t_in, t_out, x_out)))
+    ]
+    fetches = []
+    for at in range(pieces):
+        part = slice(at * per, (at + 1) * per)
+        fetches.append(
+            pltpu.make_async_copy(weight_ref.at[part], weight.at[part], weight_sems.at[at])
+        )
+    for copy in tables[:2] + fetches + tables[2:]:
+        copy.start()
+    tables[0].wait()
+    tables[1].wait()
+    modes[...] = to_modes(spread_refs, x_in, t_in)
+    keep = pltpu.make_async_copy(modes, modes_ref, sems.at[4])
     keep.start()
-    fetch.wait()
+    for fetch in fetches:
+        fetch.wait()
     for kx in range(KX):
         rows = slice(kx * CHANS, (kx + 1) * CHANS)
         own = modes[rows, :]
@@ -214,7 +257,9 @@
             for i in range(1, CHANS):
                 total = total + own[i : i + 1, :] * weight[kx, i]
             mixed[rows, :] = total
-    from_modes(mixed[...], x_out_ref, t_out_ref, held)
+    tables[2].wait()
+    tables[3].wait()
+    from_modes(mixed[...], x_out, t_out, held)
     sends = [
         pltpu.make_async_copy(held.at[part], ref, back_sems.at[part])
         for part, ref in enumerate(back_refs)
@@ -233,21 +278,23 @@
     back = (gx, ta, tables[2].shape[1] // gx, lanes)
     anywhere = pl.BlockSpec(memory_space=pl.ANY)
     on_chip = pl.BlockSpec(memory_space=pltpu.VMEM)
+    apart = pl.BlockSpec(memory_space=pltpu.HBM)
     return pl.pallas_call(
         functools.partial(mix_kernel, backward),
         out_shape=[jax.ShapeDtypeStruct(modes, F32)] + [jax.ShapeDtypeStruct(back, BF16)] * outs,
-        in_specs=[anywhere] * 2 + [on_chip] * (4 + len(spreads)),
-        out_specs=[anywhere] * (1 + outs),
+        in_specs=[apart] + [anywhere] + [apart] * 4 + [on_chip] * len(spreads),
+        out_specs=[apart] + [anywhere] * outs,
         scratch_shapes=[
             pltpu.VMEM(weight.shape, F32),
             pltpu.VMEM(modes, F32),
             pltpu.VMEM(modes, F32),
             pltpu.VMEM((outs,) + back, BF16),
-            pltpu.SemaphoreType.DMA,
-            pltpu.SemaphoreType.DMA,
+            *[pltpu.VMEM(table.shape, BF16) for table in tables],
+            pltpu.SemaphoreType.DMA((5,)),
+            pltpu.SemaphoreType.DMA((8,)),
             pltpu.SemaphoreType.DMA((outs,)),
         ],
-        compiler_params=vmem_params(52),
+        compiler_params=vmem_params(40),
         cost_estimate=pl.CostEstimate(flops=1 << 30, bytes_accessed=9 << 20, transcendentals=0),
         name="mix_back" if backward else "mix",
     )(weight, after, *tables, *spreads)
@@ -276,7 +323,7 @@
         in_specs=[pl.BlockSpec((per * CHANS, width), lambda n: (n, 0))] * 2,
         out_specs=pl.BlockSpec((per, KT, CHANS, CHANS, own), lambda n: (n, 0, 0, 0, 0)),
         out_shape=jax.ShapeDtypeStruct((KX, KT, CHANS, CHANS, own), F32),
-        compiler_params=vmem_params(56),
+        compiler_params=vmem_params(44),
         cost_estimate=pl.CostEstimate(flops=1 << 20, bytes_accessed=17 << 20, transcendentals=0),
         name="outer",
     )(spectrum, grad)
@@ -313,87 +360,102 @@
     wide,
     modes,
     total,
-    row_sums,
+    table,
+    held,
+    table_sems,
+    sems,
 ):
     step = pl.program_id(0)
     rows, width = field_ref.shape
     tile = 256
     chunk = 32
+    chunks = table.shape[0]
+    ahead = 3
+    ones = 16
+
+    def fetch(at):
+        return pltpu.make_async_copy(table_ref.at[at], table.at[at], table_sems.at[at])
 
     @pl.when(step == 0)
     def _():
+        for at in range(ahead):
+            fetch(at).start()
         unpack_modes(packed_ref, wide, xl, tl)
         modes[...] = wide[...].reshape(rows, KQ).astype(BF16)
         total[...] = jnp.zeros_like(total)
-        row_sums[...] = jnp.zeros_like(row_sums)
-
-    def build(at):
-        return matmul(modes[...], table_ref[0, :, at]) + matmul(mixer_ref[...], field_ref[:, at])
-
-    def pointwise(pre, at):
+
+    @pl.when(step + ahead < chunks)
+    def _():
+        fetch(step + ahead).start()
+
+    fetch(step).wait()
+
+    passing = jnp.concatenate(
+        [table[step], field_ref[...], jnp.ones((ones, width), BF16)], axis=0
+    )
+    cotangent = cotangent_ref[...]
+    biases = jnp.concatenate([bias_ref[...]] * (tile // LANES), axis=1)
+    pre = [
+        matmul(modes[...], table[step, :, at : at + tile])
+        + matmul(mixer_ref[...], field_ref[:, at : at + tile])
+        for at in range(0, width, tile)
+    ]
+    results, grads = [], []
+    for index, at in enumerate(range(0, width, tile)):
+        results.append([])
+        grads.append([])
         for first in range(0, rows, chunk):
             part = slice(first, first + chunk)
-            bias = bias_ref[part, :]
-            values = pre[part, :] + jnp.concatenate([bias] * (tile // LANES), axis=1)
+            values = pre[index][part] + biases[part]
             integral, decay = normal_parts(values)
-            output_ref[part, at] = (values * integral).astype(BF16)
+            results[-1].append((values * integral).astype(BF16))
             slope = integral + (values * DENSITY) * decay
-            grad = (cotangent_ref[part, at].astype(F32) * slope).astype(BF16)
-            grad_ref[part, at] = grad
-            wide_grad = grad.astype(F32)
-            sums = row_sums[part, :]
-            for lanes in range(0, tile, LANES):
-                sums = sums + wide_grad[:, lanes : lanes + LANES]
-            row_sums[part, :] = sums
-
-    def gather(at):
-        passing = jnp.concatenate([table_ref[0, :, at], field_ref[:, at]], axis=0)
-        total[...] += matmul_turned(passing, grad_ref[:, at])
-
-    tiles = [slice(first, first + tile) for first in range(0, width, tile)]
-    ready = build(tiles[0])
-    for index, at in enumerate(tiles):
-        pre = ready
-        if index + 1 < len(tiles):
-            ready = build(tiles[index + 1])
-        pointwise(pre, at)
-        if index % 2 == 1:
-            gather(slice(tiles[index - 1].start, at.stop))
+            wide_cotangent = cotangent[part, at : at + tile].astype(F32)
+            grads[-1].append((wide_cotangent * slope).astype(BF16))
+    grad = jnp.concatenate([jnp.concatenate(column, axis=0) for column in grads], axis=1)
+    output_ref[...] = jnp.concatenate(
+        [jnp.concatenate(column, axis=0) for column in results], axis=1
+    )
+    grad_ref[...] = grad
+    total[...] += matmul_turned(passing, grad)
 
     @pl.when(step == pl.num_programs(0) - 1)
     def _():
-        pack_modes(total, sent_ref, xl, tl)
+        pack_modes(total, held, sent_ref, sems, xl, tl)
         row = lax.broadcasted_iota(jnp.int32, (rows, rows), 0)
         column = lax.broadcasted_iota(jnp.int32, (rows, rows), 1)
-        same = jnp.where(row // CHANS == column // CHANS, total[KQ:, :].T, 0.0)
+        gram = total[KQ : KQ + rows, :].T
+        bias = total[KQ + rows : KQ + rows + CHANS, :]
+        same = jnp.where(row // CHANS == column // CHANS, gram, 0.0)
         folded = jnp.sum(same.reshape(rows // CHANS, CHANS, rows), axis=0)
         source = lax.broadcasted_iota(jnp.int32, (rows, LANES), 0)
         target = lax.broadcasted_iota(jnp.int32, (rows, LANES), 1)
         select = jnp.where(source % CHANS == target, 1.0, 0.0)
+        chan = lax.broadcasted_iota(jnp.int32, (CHANS, rows), 0)
+        place = lax.broadcasted_iota(jnp.int32, (CHANS, rows), 1)
+        own_bias = jnp.sum(
+            jnp.where(place % CHANS == chan, bias, 0.0), axis=1, keepdims=True
+        )
         point = jnp.dot(
             folded, select, precision=lax.Precision.HIGHEST, preferred_element_type=F32
         )
-        bias = jnp.sum(
-            jnp.sum(row_sums[...].reshape(rows // CHANS, CHANS, LANES), axis=0),
-            axis=1,
-            keepdims=True,
-        )
         lane = lax.broadcasted_iota(jnp.int32, (CHANS, LANES), 1)
-        sums_ref[...] = sums_in_ref[...] + jnp.where(lane == CHANS, bias, point)
+        sums_ref[...] = sums_in_ref[...] + jnp.where(lane == CHANS, own_bias, point)
 
 
 def middle(packed, field, cotangent, table, mixer, bias, sums, output, part, xl, tl):
     rows = xl * tl * CHANS
     width = WIDTH
+    chunks = CELLS // width
     whole = lambda *shape: pl.BlockSpec(shape, lambda n: (0,) * len(shape))
     tile = pl.BlockSpec((rows, width), lambda n: (part, n))
     kernel = functools.partial(middle_kernel, xl, tl)
     operands = (packed, field, cotangent, table, mixer, bias, sums)
     specs = [
-        whole(*packed.shape),
+        pl.BlockSpec(memory_space=pltpu.VMEM),
         tile,
         tile,
-        pl.BlockSpec((1, KQ, width), lambda n: (n, 0, 0)),
+        pl.BlockSpec(memory_space=pltpu.HBM),
         whole(rows, rows),
         whole(rows, LANES),
         whole(CHANS, LANES),
@@ -405,15 +467,15 @@
     else:
         aliases = {len(operands): 0}
         operands += (output,)
-        specs.append(pl.BlockSpec(memory_space=pl.ANY))
+        specs.append(pl.BlockSpec(memory_space=pltpu.HBM))
     return pl.pallas_call(
         kernel,
-        grid=(CELLS // width,),
+        grid=(chunks,),
         in_specs=specs,
         out_specs=[
             tile,
             pl.BlockSpec((rows, width), lambda n: (0, n)),
-            whole(*packed.shape),
+            pl.BlockSpec(memory_space=pl.ANY),
             whole(CHANS, LANES),
         ],
         out_shape=(
@@ -425,55 +487,96 @@
         scratch_shapes=[
             pltpu.VMEM((xl, tl, CHANS, KQ), F32),
             pltpu.VMEM((rows, KQ), BF16),
-            pltpu.VMEM((KQ + rows, rows), F32),
-            pltpu.VMEM((rows, LANES), F32),
+            pltpu.VMEM((KQ + rows + 16, rows), F32),
+            pltpu.VMEM((chunks, KQ, width), BF16),
+            pltpu.VMEM(packed.shape, BF16),
+            pltpu.SemaphoreType.DMA((chunks,)),
+            pltpu.SemaphoreType.DMA((KQ // LANES,)),
         ],
         input_output_aliases=aliases,
-        compiler_params=vmem_params(56),
+        compiler_params=vmem_params(44),
         cost_estimate=pl.CostEstimate(
-            flops=5 * rows * CELLS * KQ, bytes_accessed=26 << 20, transcendentals=rows * CELLS
+            flops=5 * rows * CELLS * KQ, bytes_accessed=18 << 20, transcendentals=rows * CELLS
         ),
         name="middle",
     )(*operands)
 
 
-def last_kernel(xl, tl, packed_ref, table_ref, mixer_ref, *refs):
-    grad_refs, (field_ref, wide, modes) = refs[:PARTS], refs[PARTS:]
-
-    @pl.when(pl.program_id(0) == 0)
-    def _():
-        unpack_modes(packed_ref, wide, xl, tl)
-        modes[...] = wide[...].reshape(modes.shape).astype(BF16)
-
-    spatial = matmul(modes[...], table_ref[0])
-    point = [matmul(mixer_ref[...], grad_ref[...]) for grad_ref in grad_refs]
-    field_ref[...] = (spatial + jnp.concatenate(point, axis=0)).astype(BF16)
+def last_kernel(
+    xl,
+    tl,
+    packed_ref,
+    mixer_ref,
+    table_ref,
+    *refs,
+):
+    grad_refs, field_ref = refs[:PARTS], refs[PARTS]
+    wide, modes, table, grads, field, table_sems, grad_sems, field_sems = refs[PARTS + 1 :]
+    chunks = table.shape[0]
+    ahead = 4
+    fetches, sends = [], []
+    for at in range(chunks):
+        lanes = slice(at * WIDTH, (at + 1) * WIDTH)
+        fetches.append([pltpu.make_async_copy(table_ref.at[at], table.at[at], table_sems.at[at])])
+        for part, grad_ref in enumerate(grad_refs):
+            fetches[at].append(
+                pltpu.make_async_copy(
+                    grad_ref.at[:, lanes], grads.at[at, part], grad_sems.at[at, part]
+                )
+            )
+        sends.append(
+            pltpu.make_async_copy(field.at[at], field_ref.at[:, lanes], field_sems.at[at])
+        )
+
+    def start(at):
+        for fetch in fetches[at]:
+            fetch.start()
+
+    for at in range(ahead):
+        start(at)
+    unpack_modes(packed_ref, wide, xl, tl)
+    modes[...] = wide[...].reshape(modes.shape).astype(BF16)
+    for at in range(chunks):
+        for fetch in fetches[at]:
+            fetch.wait()
+        if at + ahead < chunks:
+            start(at + ahead)
+        point = [matmul(mixer_ref[...], grads[at, part]) for part in range(PARTS)]
+        field[at] = (
+            matmul(modes[...], table[at]) + jnp.concatenate(point, axis=0)
+        ).astype(BF16)
+        sends[at].start()
+    for send in sends:
+        send.wait()
 
 
 def last(packed, grads, table, mixer, xl, tl):
     rows = xl * tl * CHANS
     part = rows // PARTS
+    chunks = CELLS // WIDTH
+    apart = pl.BlockSpec(memory_space=pltpu.HBM)
+    on_chip = pl.BlockSpec(memory_space=pltpu.VMEM)
     return pl.pallas_call(
         functools.partial(last_kernel, xl, tl),
-        grid=(CELLS // WIDTH,),
-        in_specs=[
-            pl.BlockSpec(packed.shape, lambda n: (0, 0, 0)),
-            pl.BlockSpec((1, KQ, WIDTH), lambda n: (n, 0, 0)),
-            pl.BlockSpec((part, part), lambda n: (0, 0)),
-        ]
-        + [pl.BlockSpec((part, WIDTH), lambda n: (0, n))] * PARTS,
-        out_specs=pl.BlockSpec((rows, WIDTH), lambda n: (0, n)),
+        in_specs=[on_chip] * 2 + [apart] * (1 + PARTS),
+        out_specs=apart,
         out_shape=jax.ShapeDtypeStruct((rows, CELLS), BF16),
         scratch_shapes=[
             pltpu.VMEM((xl, tl, CHANS, KQ), F32),
             pltpu.VMEM((rows, KQ), BF16),
+            pltpu.VMEM((chunks, KQ, WIDTH), BF16),
+            pltpu.VMEM((chunks, PARTS, part, WIDTH), BF16),
+            pltpu.VMEM((chunks, rows, WIDTH), BF16),
+            pltpu.SemaphoreType.DMA((chunks,)),
+            pltpu.SemaphoreType.DMA((chunks, PARTS)),
+            pltpu.SemaphoreType.DMA((chunks,)),
         ],
-        compiler_params=vmem_params(56),
+        compiler_params=vmem_params(44),
         cost_estimate=pl.CostEstimate(
             flops=2 * rows * CELLS * KQ, bytes_accessed=18 << 20, transcendentals=0
         ),
         name="last",
-    )(packed, table, mixer, *grads)
+    )(packed, mixer, table, *grads)
 
 
 def swap(blocks):

time: 196 us -> 205 us (1.046)
  local copies, waits for them, and re-layouts: 5.11 us -> 26 us
  Pallas kernels: 90.4 us -> 80.4 us
    unnamed x32 -> x64, local copies, waits for them, and re-layouts: 4.42 us -> 25.3 us
    pallas_call x2, Pallas kernels: 12.7 us -> 6.77 us  [mix(): pl.pallas_call(functools.partial(mix_kernel, backward), out_shape=[jax.Sh...]
where the time goes in v4:
time: 205 us; the launch traced here: 203 us
  Pallas kernels  80.4 us (39%)
  waiting for transfers between devices  37.7 us (18%)
  starting transfers between devices  36.5 us (18%)
  local copies, waits for them, and re-layouts  26 us (13%)
  blocking collectives  19 us (9%)
  matrix products  2.74 us (1%)
    pallas_call x2, Pallas kernels, middle(): pl.pallas_call(kernel, grid=(chunks,), in_specs=specs, out_specs=[tile, p...  38.6 us
    all_to_all x5, waiting for transfers between devices, swap(): lax.all_to_all(blocks, ('gx', 'ta'), split_axis=0, concat_axis=0, tiled=T...  29 us
    all_to_all x5, starting transfers between devices, swap(): lax.all_to_all(blocks, ('gx', 'ta'), split_axis=0, concat_axis=0, tiled=T...  28.4 us
    unnamed x64, local copies, waits for them, and re-layouts  25.3 us
    all_to_all x1, blocking collectives, swap(): lax.all_to_all(blocks, ('gx', 'ta'), split_axis=0, concat_axis=0, tiled=T...  19 us
    pallas_call x1, Pallas kernels, pack_weight(): pl.pallas_call(weight_kernel, grid=(KX // per,), in_specs=[pl.BlockSpec((...  9.51 us
    pallas_call x1, Pallas kernels, last(): pl.pallas_call(functools.partial(last_kernel, xl, tl), in_specs=[on_chip]...  9.26 us
    ppermute x5, waiting for transfers between devices, sum_everywhere(): values = values + lax.ppermute(values, ('gx', 'ta'), pairs)  8.69 us
  transfers between devices with their start and end apart: 10, of which 7 were waited for; matrix products, arithmetic and copies ran while one was open for 2% of the time, Pallas kernels for 28%

profile of v4, /device:TPU:0, one launch (start us, length us, event | category | flops | bytes accessed | tf_op | source)
XLA Modules:
  0.0 203.4 jit_solution(455453872738729704)
XLA Ops:
  0.7 2.2 %copy-done.4 = bf16[1,16,4,8,4096]{4,3,2,1,0:T(8,128)(2,1)S(1)} copy-done((bf16[1,16,4,8,4096]{4,3,2,1,0:T(8,128)(2,1)S(1)}, bf16[1,16,4,8,4096]{4,3,2,1,0:T(8,128)(2,1)}, u32[]{:S(2)}) %copy-start.4) | copy-done | bytes 4194328
  2.8 8.4 %analyse.1 = bf16[32,128,128]{2,1,0:T(8,128)(2,1)} custom-call(bf16[512,4096]{1,0:T(8,128)(2,1)S(1)} %bitcast.19, bf16[8,1024,512]{2,1,0:T(8,128)(2,1)} %constant.24.clone.table_ref.refs_3_), custom_call_target="tpu_custom_call" | custom-call | flops 4294967296 | bytes 13631488 | tf_op jit(solution)/shard_map/analyse/pallas_call | solution.py:146
  11.2 7.3 %all-to-all-start = ((bf16[32,128,128]{2,1,0:T(8,128)(2,1)}), bf16[32,128,128]{2,1,0:T(8,128)(2,1)S(1)}, u32[]{:S(2)}, u32[]{:S(2)}) async-start(bf16[32,128,128]{2,1,0:T(8,128)(2,1)} %analyse.1), calls=%async_computation | async-start | bytes 2097152 | tf_op jit(solution)/shard_map/all_to_all | solution.py:583
  18.6 9.5 %pack_weight.1.weight_ref = f32[32,8,8,512]{3,2,1,0:T(8,128)S(1)} custom-call(f32[32,16,8,8,32]{4,3,2,1,0:T(8,128)} %weight_ref.1), custom_call_target="tpu_custom_call" | custom-call | flops 1048576 | bytes 20971520 | tf_op jit(solution)/shard_map/pack_weight/pallas_call | solution.py:180
  28.1 2.0 copy-done.1
  30.1 14.6 %all-to-all-done = bf16[32,128,128]{2,1,0:T(8,128)(2,1)S(1)} async-done(((bf16[32,128,128]{2,1,0:T(8,128)(2,1)}), bf16[32,128,128]{2,1,0:T(8,128)(2,1)S(1)}, u32[]{:S(2)}, u32[]{:S(2)}) %all-to-all-start) | async-done | bytes 1048608 | tf_op jit(solution)/shard_map/all_to_all | solution.py:583
  44.8 2.2 %copy-done.2 = f32[32,8,8,512]{3,2,1,0:T(8,128)S(1)} copy-done((f32[32,8,8,512]{3,2,1,0:T(8,128)S(1)}, f32[32,8,8,512]{3,2,1,0:T(8,128)}, u32[]{:S(2)}) %copy-start.2) | copy-done | bytes 4194328
  47.0 2.4 %mix.1 = (f32[256,512]{1,0:T(8,128)S(1)}, bf16[8,4,64,128]{3,2,1,0:T(8,128)(2,1)S(1)}, bf16[8,4,64,128]{3,2,1,0:T(8,128)(2,1)S(1)}) custom-call(f32[32,8,8,512]{3,2,1,0:T(8,128)S(1)} %copy-done.2, f32[8,128]{1,0:T(8,128)S(1)} %broadcast_in_dim.4._.refs_6_, bf16[1,256,1024]{2,1,0:T(8,128)(2,1)S(1)} %copy-done.20, bf16[512,512]{1,0:T(8,128)(2,1)S(1)} %copy-done.9, ...), custom_call_target="tpu_custom_call" | custom-call | flops 1073741824 | bytes 9437184 | tf_op jit(solution)/shard_map/mix/pallas_call | solution.py:282
  50.3 19.0 %all_to_all.30.refs_0_ = bf16[32,64,128]{2,1,0:T(8,128)(2,1)S(1)} all-to-all(bf16[32,64,128]{2,1,0:T(8,128)(2,1)S(1)} %bitcast.24), channel_id=1, replica_groups=mesh['gx'=8,'ta'=4] {'gx','ta'}, dimensions={0} | all-to-all | bytes 1048576 | tf_op jit(solution)/shard_map/all_to_all | solution.py:583
  69.2 3.1 %all-to-all-start.1 = ((bf16[32,64,128]{2,1,0:T(8,128)(2,1)}), bf16[32,64,128]{2,1,0:T(8,128)(2,1)S(1)}, u32[]{:S(2)}, u32[]{:S(2)}) async-start(bf16[32,64,128]{2,1,0:T(8,128)(2,1)} %bitcast.23), calls=%async_computation.1 | async-start | bytes 1048576 | tf_op jit(solution)/shard_map/all_to_all | solution.py:583
  73.9 2.2 %copy-done.5 = bf16[1,16,4,8,4096]{4,3,2,1,0:T(8,128)(2,1)S(1)} copy-done((bf16[1,16,4,8,4096]{4,3,2,1,0:T(8,128)(2,1)S(1)}, bf16[1,16,4,8,4096]{4,3,2,1,0:T(8,128)(2,1)}, u32[]{:S(2)}) %copy-start.5) | copy-done | bytes 4194328
  76.1 19.3 %middle.2 = (bf16[512,4096]{1,0:T(8,128)(2,1)}, bf16[256,4096]{1,0:T(8,128)(2,1)S(1)}, bf16[32,64,128]{2,1,0:T(8,128)(2,1)S(1)}, f32[8,128]{1,0:T(8,128)S(1)}) custom-call(bf16[32,64,128]{2,1,0:T(8,128)(2,1)S(1)} %all_to_all.30.refs_0_, bf16[512,4096]{1,0:T(8,128)(2,1)S(1)} %bitcast.20, bf16[512,4096]{1,0:T(8,128)(2,1)} %bitcast.26, ...), custom_call_target="tpu_custom_call" | custom-call | flops 5368709120 | bytes 18874368 | tf_op jit(solution)/shard_map/middle/pallas_call | solution.py:471
  96.2 6.1 %all-to-all-start.3 = ((bf16[32,64,128]{2,1,0:T(8,128)(2,1)}), bf16[32,64,128]{2,1,0:T(8,128)(2,1)}, u32[]{:S(2)}, u32[]{:S(2)}) async-start(bf16[32,64,128]{2,1,0:T(8,128)(2,1)} %copy-done.25), calls=%async_computation.3 | async-start | bytes 1048576 | tf_op jit(solution)/shard_map/all_to_all | solution.py:583
  102.4 2.2 %copy-done.6 = bf16[1,16,4,8,4096]{4,3,2,1,0:T(8,128)(2,1)S(1)} copy-done((bf16[1,16,4,8,4096]{4,3,2,1,0:T(8,128)(2,1)S(1)}, bf16[1,16,4,8,4096]{4,3,2,1,0:T(8,128)(2,1)}, u32[]{:S(2)}) %copy-start.6) | copy-done | bytes 4194328
  105.6 19.4 %middle.3 = (bf16[512,4096]{1,0:T(8,128)(2,1)}, bf16[256,4096]{1,0:T(8,128)(2,1)S(1)}, bf16[32,64,128]{2,1,0:T(8,128)(2,1)S(1)}, f32[8,128]{1,0:T(8,128)S(1)}) custom-call(bf16[32,64,128]{2,1,0:T(8,128)(2,1)S(1)} %copy-done.14, bf16[512,4096]{1,0:T(8,128)(2,1)S(1)} %bitcast.21, bf16[512,4096]{1,0:T(8,128)(2,1)} %bitcast.27, ...), custom_call_target="tpu_custom_call", output_to_operand_aliasing={{0}: (7, {})} | custom-call | flops 5368709120 | bytes 18874368 | tf_op jit(solution)/shard_map/middle/pallas_call | solution.py:471
  125.0 1.3 copy-done.7
  127.1 5.7 %all-to-all-start.4 = ((bf16[32,64,128]{2,1,0:T(8,128)(2,1)}), bf16[32,64,128]{2,1,0:T(8,128)(2,1)}, u32[]{:S(2)}, u32[]{:S(2)}) async-start(bf16[32,64,128]{2,1,0:T(8,128)(2,1)} %copy-done.24), calls=%async_computation.4 | async-start | bytes 1048576 | tf_op jit(solution)/shard_map/all_to_all | solution.py:583
  134.1 1.7 collective-permute-start.1
  135.8 1.9 collective-permute-done.1
  137.7 1.8 collective-permute-start.2
  139.5 2.0 collective-permute-done.2
  141.5 1.5 collective-permute-start.3
  143.0 2.1 %collective-permute-done.3 = f32[8,128]{1,0:T(8,128)S(1)} collective-permute-done((f32[8,128]{1,0:T(8,128)S(1)}, f32[8,128]{1,0:T(8,128)S(1)}, u32[]{:S(2)}, u32[]{:S(2)}) %collective-permute-start.3) | collective-permute-done | bytes 4128 | tf_op jit(solution)/shard_map/ppermute | solution.py:590
  145.1 2.9 %collective-permute-start.4 = (f32[8,128]{1,0:T(8,128)S(1)}, f32[8,128]{1,0:T(8,128)S(1)}, u32[]{:S(2)}, u32[]{:S(2)}) collective-permute-start(f32[8,128]{1,0:T(8,128)S(1)} %add.18), channel_id=1, source_target_pairs={{0,16},{1,17},{2,18},{3,19},{4,20},{5,21},{6,22},{7,23},{8,24},{9,... | collective-permute-start | bytes 12296 | tf_op jit(solution)/shard_map/ppermute | solution.py:590
  148.0 1.6 collective-permute-done.4
  149.7 2.2 %copy-done.3 = f32[32,8,8,512]{3,2,1,0:T(8,128)S(1)} copy-done((f32[32,8,8,512]{3,2,1,0:T(8,128)S(1)}, f32[32,8,8,512]{3,2,1,0:T(8,128)}, u32[]{:S(2)}) %copy-start.3) | copy-done | bytes 4194328
  153.9 4.3 %mix_back.1 = (f32[256,512]{1,0:T(8,128)S(1)}, bf16[8,4,128,128]{3,2,1,0:T(8,128)(2,1)S(1)}) custom-call(f32[32,8,8,512]{3,2,1,0:T(8,128)S(1)} %copy-done.3, f32[8,128]{1,0:T(8,128)S(1)} %get-tuple-element.32._, bf16[2,256,512]{2,1,0:T(8,128)(2,1)S(1)} %copy-done.16, bf16[512,512]{1,0:T(8,128)(2,1)S(1)} %copy-done.10, bf16[1,1024,256]{2,1,0:T(8,128)(2,1)S(1)} %copy-done.17, ...), custom_call_target="tpu_custom_call" | custom-call | flops 1073741824 | bytes 9437184 | tf_op jit(solution)/shard_map/mix_back/pallas_call | solution.py:282
  160.1 6.1 %all-to-all-start.5 = ((bf16[32,128,128]{2,1,0:T(8,128)(2,1)}), bf16[32,128,128]{2,1,0:T(8,128)(2,1)S(1)}, u32[]{:S(2)}, u32[]{:S(2)}) async-start(bf16[32,128,128]{2,1,0:T(8,128)(2,1)} %bitcast.22), calls=%async_computation.5 | async-start | bytes 2097152 | tf_op jit(solution)/shard_map/all_to_all | solution.py:583
  170.2 7.9 %outer.1 = f32[32,16,8,8,32]{4,3,2,1,0:T(8,128)} custom-call(f32[256,512]{1,0:T(8,128)S(1)} %copy-done.19, f32[256,512]{1,0:T(8,128)S(1)} %copy-done.23), custom_call_target="tpu_custom_call" | custom-call | flops 1048576 | bytes 17825792 | tf_op jit(solution)/shard_map/outer/pallas_call | solution.py:320
  178.1 14.4 %all-to-all-done.5.packed_ref = bf16[32,128,128]{2,1,0:T(8,128)(2,1)S(1)} async-done(((bf16[32,128,128]{2,1,0:T(8,128)(2,1)}), bf16[32,128,128]{2,1,0:T(8,128)(2,1)S(1)}, u32[]{:S(2)}, u32[]{:S(2)}) %all-to-all-start.5) | async-done | bytes 1048608 | tf_op jit(solution)/shard_map/all_to_all | solution.py:583
  192.4 1.6 copy-done.8
  194.0 9.3 %last.1 = bf16[512,4096]{1,0:T(8,128)(2,1)} custom-call(bf16[32,128,128]{2,1,0:T(8,128)(2,1)S(1)} %all-to-all-done.5.packed_ref, bf16[256,256]{1,0:T(8,128)(2,1)S(1)} %fusion.1.mixer_ref, bf16[8,1024,512]{2,1,0:T(8,128)(2,1)} %constant.24.clone.table_ref.refs_3_, bf16[256,4096]{1,0:T(8,128)(2,1)S(1)} %get-tuple-element.27.refs_0_, ...), custom_call_target="tpu_custom_call" | custom-call | flops 4294967296 | bytes 18874368 | tf_op jit(solution)/shard_map/last/pallas_call | solution.py:559
  (71 shorter events, 14.1 us)
Async XLA Ops:
  0.6 72.0 %copy-start = (bf16[8,8]{1,0:T(8,128)(2,1)S(1)}, bf16[8,8]{1,0:T(8,128)(2,1)}, u32[]{:S(2)}) copy-start(bf16[8,8]{1,0:T(8,128)(2,1)} %param.18) | copy-start | bytes 388
  0.6 2.2 %copy-start.4 = (bf16[1,16,4,8,4096]{4,3,2,1,0:T(8,128)(2,1)S(1)}, bf16[1,16,4,8,4096]{4,3,2,1,0:T(8,128)(2,1)}, u32[]{:S(2)}) copy-start(bf16[1,16,4,8,4096]{4,3,2,1,0:T(8,128)(2,1)} %param.15) | copy-start | bytes 12582916
  11.2 33.6 %all-to-all-start = ((bf16[32,128,128]{2,1,0:T(8,128)(2,1)}), bf16[32,128,128]{2,1,0:T(8,128)(2,1)S(1)}, u32[]{:S(2)}, u32[]{:S(2)}) async-start(bf16[32,128,128]{2,1,0:T(8,128)(2,1)} %analyse.1), calls=%async_computation | async-start | bytes 2097152 | tf_op jit(solution)/shard_map/all_to_all | solution.py:583
  18.6 26.2 %copy-start.9 = (bf16[512,512]{1,0:T(8,128)(2,1)S(1)}, bf16[512,512]{1,0:T(8,128)(2,1)}, u32[]{:S(2)}) copy-start(bf16[512,512]{1,0:T(8,128)(2,1)} %constant.29.clone.t_in_ref) | copy-start | bytes 1572868
  18.6 26.2 %copy-start.11 = (bf16[512,512]{1,0:T(8,128)(2,1)S(1)}, bf16[512,512]{1,0:T(8,128)(2,1)}, u32[]{:S(2)}) copy-start(bf16[512,512]{1,0:T(8,128)(2,1)} %constant.30.clone.t_out_ref) | copy-start | bytes 1572868
  18.6 26.2 %copy-start.20 = (bf16[1,256,1024]{2,1,0:T(8,128)(2,1)S(1)}, bf16[1,256,1024]{2,1,0:T(8,128)(2,1)}, u32[]{:S(2)}) copy-start(bf16[1,256,1024]{2,1,0:T(8,128)(2,1)} %constant.25.clone.x_in_ref) | copy-start | bytes 1572868
  18.6 26.2 %copy-start.21 = (bf16[2,512,256]{2,1,0:T(8,128)(2,1)S(1)}, bf16[2,512,256]{2,1,0:T(8,128)(2,1)}, u32[]{:S(2)}) copy-start(bf16[2,512,256]{2,1,0:T(8,128)(2,1)} %constant.28.clone.x_out_ref) | copy-start | bytes 1572868
  28.1 2.0 copy-start.1
  44.8 2.2 %copy-start.2 = (f32[32,8,8,512]{3,2,1,0:T(8,128)S(1)}, f32[32,8,8,512]{3,2,1,0:T(8,128)}, u32[]{:S(2)}) copy-start(f32[32,8,8,512]{3,2,1,0:T(8,128)} %copy-done.1) | copy-start | bytes 12582916
  47.0 25.3 %copy-start.29 = (f32[256,8]{1,0:T(8,128)S(1)}, f32[256,8]{1,0:T(8,128)}, u32[]{:S(2)}) copy-start(f32[256,8]{1,0:T(8,128)} %constant.33.clone) | copy-start | bytes 24580
  47.0 25.3 %copy-start.31 = (f32[8]{0:T(128)S(1)}, f32[8]{0:T(128)}, u32[]{:S(2)}) copy-start(f32[8]{0:T(128)} %param.19) | copy-start | bytes 100
  47.0 25.6 %copy-start.28 = (bf16[256,8]{1,0:T(8,128)(2,1)S(1)}, bf16[256,8]{1,0:T(8,128)(2,1)}, u32[]{:S(2)}) copy-start(bf16[256,8]{1,0:T(8,128)(2,1)} %constant.31.clone) | copy-start | bytes 12292
  50.2 19.0 %copy-start.26 = (bf16[8,4,64,128]{3,2,1,0:T(8,128)(2,1)}, bf16[8,4,64,128]{3,2,1,0:T(8,128)(2,1)S(1)}, u32[]{:S(2)}) copy-start(bf16[8,4,64,128]{3,2,1,0:T(8,128)(2,1)S(1)} %get-tuple-element.18) | copy-start | bytes 1572868
  69.2 27.0 %all-to-all-start.1 = ((bf16[32,64,128]{2,1,0:T(8,128)(2,1)}), bf16[32,64,128]{2,1,0:T(8,128)(2,1)S(1)}, u32[]{:S(2)}, u32[]{:S(2)}) async-start(bf16[32,64,128]{2,1,0:T(8,128)(2,1)} %bitcast.23), calls=%async_computation.1 | async-start | bytes 1048576 | tf_op jit(solution)/shard_map/all_to_all | solution.py:583
  73.9 2.2 %copy-start.5 = (bf16[1,16,4,8,4096]{4,3,2,1,0:T(8,128)(2,1)S(1)}, bf16[1,16,4,8,4096]{4,3,2,1,0:T(8,128)(2,1)}, u32[]{:S(2)}) copy-start(bf16[1,16,4,8,4096]{4,3,2,1,0:T(8,128)(2,1)} %param.15) | copy-start | bytes 12582916
  96.2 6.2 %copy-start.13 = (bf16[32,64,128]{2,1,0:T(8,128)(2,1)}, bf16[32,64,128]{2,1,0:T(8,128)(2,1)S(1)}, u32[]{:S(2)}) copy-start(bf16[32,64,128]{2,1,0:T(8,128)(2,1)S(1)} %all-to-all-done.1.packed_ref) | copy-start | bytes 1572868
  96.2 30.9 %all-to-all-start.3 = ((bf16[32,64,128]{2,1,0:T(8,128)(2,1)}), bf16[32,64,128]{2,1,0:T(8,128)(2,1)}, u32[]{:S(2)}, u32[]{:S(2)}) async-start(bf16[32,64,128]{2,1,0:T(8,128)(2,1)} %copy-done.25), calls=%async_computation.3 | async-start | bytes 1048576 | tf_op jit(solution)/shard_map/all_to_all | solution.py:583
  102.3 2.2 %copy-start.6 = (bf16[1,16,4,8,4096]{4,3,2,1,0:T(8,128)(2,1)S(1)}, bf16[1,16,4,8,4096]{4,3,2,1,0:T(8,128)(2,1)}, u32[]{:S(2)}) copy-start(bf16[1,16,4,8,4096]{4,3,2,1,0:T(8,128)(2,1)} %param.15) | copy-start | bytes 12582916
  105.6 44.1 %copy-start.10 = (bf16[512,512]{1,0:T(8,128)(2,1)S(1)}, bf16[512,512]{1,0:T(8,128)(2,1)}, u32[]{:S(2)}) copy-start(bf16[512,512]{1,0:T(8,128)(2,1)} %constant.29.clone.t_in_ref) | copy-start | bytes 1572868
  105.6 44.1 %copy-start.12 = (bf16[512,512]{1,0:T(8,128)(2,1)S(1)}, bf16[512,512]{1,0:T(8,128)(2,1)}, u32[]{:S(2)}) copy-start(bf16[512,512]{1,0:T(8,128)(2,1)} %constant.30.clone.t_out_ref) | copy-start | bytes 1572868
  125.0 1.3 copy-start.7
  127.1 22.5 %all-to-all-start.4 = ((bf16[32,64,128]{2,1,0:T(8,128)(2,1)}), bf16[32,64,128]{2,1,0:T(8,128)(2,1)}, u32[]{:S(2)}, u32[]{:S(2)}) async-start(bf16[32,64,128]{2,1,0:T(8,128)(2,1)} %copy-done.24), calls=%async_computation.4 | async-start | bytes 1048576 | tf_op jit(solution)/shard_map/all_to_all | solution.py:583
  132.8 1.2 collective-permute-start
  134.1 3.6 %collective-permute-start.1 = (f32[8,128]{1,0:T(8,128)S(1)}, f32[8,128]{1,0:T(8,128)S(1)}, u32[]{:S(2)}, u32[]{:S(2)}) collective-permute-start(f32[8,128]{1,0:T(8,128)S(1)} %add.15), channel_id=1, source_target_pairs={{0,2},{1,3},{2,0},{3,1},{4,6},{5,7},{6,4},{7,5},{8,10},{9,11},{10,... | collective-permute-start | bytes 12296 | tf_op jit(solution)/shard_map/ppermute | solution.py:590
  137.7 3.8 %collective-permute-start.2 = (f32[8,128]{1,0:T(8,128)S(1)}, f32[8,128]{1,0:T(8,128)S(1)}, u32[]{:S(2)}, u32[]{:S(2)}) collective-permute-start(f32[8,128]{1,0:T(8,128)S(1)} %add.16), channel_id=1, source_target_pairs={{0,4},{1,5},{2,6},{3,7},{4,0},{5,1},{6,2},{7,3},{8,12},{9,13},{10,... | collective-permute-start | bytes 12296 | tf_op jit(solution)/shard_map/ppermute | solution.py:590
  141.5 3.6 %collective-permute-start.3 = (f32[8,128]{1,0:T(8,128)S(1)}, f32[8,128]{1,0:T(8,128)S(1)}, u32[]{:S(2)}, u32[]{:S(2)}) collective-permute-start(f32[8,128]{1,0:T(8,128)S(1)} %add.17), channel_id=1, source_target_pairs={{0,8},{1,9},{2,10},{3,11},{4,12},{5,13},{6,14},{7,15},{8,0},{9,1},... | collective-permute-start | bytes 12296 | tf_op jit(solution)/shard_map/ppermute | solution.py:590
  145.1 4.5 %collective-permute-start.4 = (f32[8,128]{1,0:T(8,128)S(1)}, f32[8,128]{1,0:T(8,128)S(1)}, u32[]{:S(2)}, u32[]{:S(2)}) collective-permute-start(f32[8,128]{1,0:T(8,128)S(1)} %add.18), channel_id=1, source_target_pairs={{0,16},{1,17},{2,18},{3,19},{4,20},{5,21},{6,22},{7,23},{8,24},{9,... | collective-permute-start | bytes 12296 | tf_op jit(solution)/shard_map/ppermute | solution.py:590
  149.6 17.8 %copy-start.30 = (f32[8,128]{1,0:T(8,128)}, f32[8,128]{1,0:T(8,128)S(1)}, u32[]{:S(2)}) copy-start(f32[8,128]{1,0:T(8,128)S(1)} %get-tuple-element.31) | copy-start | bytes 12292
  149.7 2.2 %copy-start.3 = (f32[32,8,8,512]{3,2,1,0:T(8,128)S(1)}, f32[32,8,8,512]{3,2,1,0:T(8,128)}, u32[]{:S(2)}) copy-start(f32[32,8,8,512]{3,2,1,0:T(8,128)} %copy-done.1) | copy-start | bytes 12582916
  153.9 12.3 %copy-start.27 = (f32[256,256]{1,0:T(8,128)S(1)}, f32[256,256]{1,0:T(8,128)}, u32[]{:S(2)}) copy-start(f32[256,256]{1,0:T(8,128)} %constant.32.clone) | copy-start | bytes 786436
  160.1 32.4 %all-to-all-start.5 = ((bf16[32,128,128]{2,1,0:T(8,128)(2,1)}), bf16[32,128,128]{2,1,0:T(8,128)(2,1)S(1)}, u32[]{:S(2)}, u32[]{:S(2)}) async-start(bf16[32,128,128]{2,1,0:T(8,128)(2,1)} %bitcast.22), calls=%async_computation.5 | async-start | bytes 2097152 | tf_op jit(solution)/shard_map/all_to_all | solution.py:583
  192.4 1.6 copy-start.8
  (10 other events, 9.4 us)

commit v5 on v4

--- a/solution.py
+++ b/solution.py
@@ -157,7 +157,7 @@
             pltpu.SemaphoreType.DMA((chunks,)),
             pltpu.SemaphoreType.DMA((KQ // LANES,)),
         ],
-        compiler_params=vmem_params(44),
+        compiler_params=vmem_params(60),
         cost_estimate=pl.CostEstimate(
             flops=2 * rows * CELLS * KQ, bytes_accessed=13 << 20, transcendentals=0
         ),
@@ -183,7 +183,7 @@
         in_specs=[pl.BlockSpec((per, KT, CHANS, CHANS, own), lambda n: (n, 0, 0, 0, 0))],
         out_specs=pl.BlockSpec((per, CHANS, CHANS, KT * own), lambda n: (n, 0, 0, 0)),
         out_shape=jax.ShapeDtypeStruct((KX, CHANS, CHANS, KT * own), F32),
-        compiler_params=vmem_params(44),
+        compiler_params=vmem_params(60),
         cost_estimate=pl.CostEstimate(flops=1 << 20, bytes_accessed=20 << 20, transcendentals=0),
         name="pack_weight",
     )(weight)
@@ -221,8 +221,12 @@
 ):
     ins, outs = x_in_ref.shape[0], x_out_ref.shape[0]
     spread_refs, modes_ref, back_refs = refs[:ins], refs[ins], refs[ins + 1 : ins + 1 + outs]
-    weight, modes, mixed, held, x_in, t_in, x_out, t_out, sems, weight_sems, back_sems = refs[
-        ins + 1 + outs :
+    scratch = refs[ins + 1 + outs :]
+    weight, modes, mixed, held, x_in, t_in, x_out, t_out = scratch[:8]
+    spreads, (sems, weight_sems, spread_sems, back_sems) = scratch[8:-4], scratch[-4:]
+    arrivals = [
+        pltpu.make_async_copy(source, target, spread_sems.at[at])
+        for at, (source, target) in enumerate(zip(spread_refs, spreads))
     ]
     pieces = weight_sems.shape[0]
     per = KX // pieces
@@ -237,11 +241,11 @@
         fetches.append(
             pltpu.make_async_copy(weight_ref.at[part], weight.at[part], weight_sems.at[at])
         )
-    for copy in tables[:2] + fetches + tables[2:]:
+    for copy in arrivals + tables[:2] + fetches + tables[2:]:
         copy.start()
-    tables[0].wait()
-    tables[1].wait()
-    modes[...] = to_modes(spread_refs, x_in, t_in)
+    for copy in arrivals + tables[:2]:
+        copy.wait()
+    modes[...] = to_modes(spreads, x_in, t_in)
     keep = pltpu.make_async_copy(modes, modes_ref, sems.at[4])
     keep.start()
     for fetch in fetches:
@@ -277,12 +281,11 @@
     outs = tables[2].shape[0]
     back = (gx, ta, tables[2].shape[1] // gx, lanes)
     anywhere = pl.BlockSpec(memory_space=pl.ANY)
-    on_chip = pl.BlockSpec(memory_space=pltpu.VMEM)
     apart = pl.BlockSpec(memory_space=pltpu.HBM)
     return pl.pallas_call(
         functools.partial(mix_kernel, backward),
         out_shape=[jax.ShapeDtypeStruct(modes, F32)] + [jax.ShapeDtypeStruct(back, BF16)] * outs,
-        in_specs=[apart] + [anywhere] + [apart] * 4 + [on_chip] * len(spreads),
+        in_specs=[apart] + [anywhere] + [apart] * 4 + [anywhere] * len(spreads),
         out_specs=[apart] + [anywhere] * outs,
         scratch_shapes=[
             pltpu.VMEM(weight.shape, F32),
@@ -290,11 +293,13 @@
             pltpu.VMEM(modes, F32),
             pltpu.VMEM((outs,) + back, BF16),
             *[pltpu.VMEM(table.shape, BF16) for table in tables],
+            *[pltpu.VMEM(spread.shape, BF16) for spread in spreads],
             pltpu.SemaphoreType.DMA((5,)),
             pltpu.SemaphoreType.DMA((8,)),
+            pltpu.SemaphoreType.DMA((len(spreads),)),
             pltpu.SemaphoreType.DMA((outs,)),
         ],
-        compiler_params=vmem_params(40),
+        compiler_params=vmem_params(60),
         cost_estimate=pl.CostEstimate(flops=1 << 30, bytes_accessed=9 << 20, transcendentals=0),
         name="mix_back" if backward else "mix",
     )(weight, after, *tables, *spreads)
@@ -323,7 +328,7 @@
         in_specs=[pl.BlockSpec((per * CHANS, width), lambda n: (n, 0))] * 2,
         out_specs=pl.BlockSpec((per, KT, CHANS, CHANS, own), lambda n: (n, 0, 0, 0, 0)),
         out_shape=jax.ShapeDtypeStruct((KX, KT, CHANS, CHANS, own), F32),
-        compiler_params=vmem_params(44),
+        compiler_params=vmem_params(60),
         cost_estimate=pl.CostEstimate(flops=1 << 20, bytes_accessed=17 << 20, transcendentals=0),
         name="outer",
     )(spectrum, grad)
@@ -342,15 +347,44 @@
     return jnp.where(values >= 0.0, 1.0 - tail, tail), decay
 
 
+def point_kernel(mixer_ref, bias_ref, *refs):
+    field_refs, mixed_ref = refs[:PARTS], refs[PARTS]
+    rows, width = field_refs[0].shape
+    bias = jnp.concatenate([bias_ref[...]] * (width // LANES), axis=1)
+    for part, field_ref in enumerate(field_refs):
+        mixed = matmul(mixer_ref[...], field_ref[...]) + bias
+        mixed_ref[part * rows : (part + 1) * rows, :] = mixed.astype(mixed_ref.dtype)
+
+
+def point(fields, parts, mixer, bias, dtype, name):
+    rows = mixer.shape[0]
+    tiles = [pl.BlockSpec((rows, WIDTH), lambda n, part=part: (part, n)) for part in parts]
+    return pl.pallas_call(
+        point_kernel,
+        grid=(CELLS // WIDTH,),
+        in_specs=[
+            pl.BlockSpec((rows, rows), lambda n: (0, 0)),
+            pl.BlockSpec((rows, LANES), lambda n: (0, 0)),
+        ]
+        + tiles,
+        out_specs=pl.BlockSpec((PARTS * rows, WIDTH), lambda n: (0, n)),
+        out_shape=jax.ShapeDtypeStruct((PARTS * rows, CELLS), dtype),
+        compiler_params=vmem_params(60),
+        cost_estimate=pl.CostEstimate(
+            flops=2 * PARTS * rows * CELLS * rows, bytes_accessed=12 << 20, transcendentals=0
+        ),
+        name=name,
+    )(mixer, bias, *fields)
+
+
 def middle_kernel(
     xl,
     tl,
     packed_ref,
     field_ref,
     cotangent_ref,
+    mixed_ref,
     table_ref,
-    mixer_ref,
-    bias_ref,
     sums_in_ref,
     _,
     output_ref,
@@ -360,64 +394,44 @@
     wide,
     modes,
     total,
-    table,
     held,
-    table_sems,
     sems,
 ):
     step = pl.program_id(0)
     rows, width = field_ref.shape
     tile = 256
     chunk = 32
-    chunks = table.shape[0]
-    ahead = 3
     ones = 16
-
-    def fetch(at):
-        return pltpu.make_async_copy(table_ref.at[at], table.at[at], table_sems.at[at])
 
     @pl.when(step == 0)
     def _():
-        for at in range(ahead):
-            fetch(at).start()
         unpack_modes(packed_ref, wide, xl, tl)
         modes[...] = wide[...].reshape(rows, KQ).astype(BF16)
         total[...] = jnp.zeros_like(total)
 
-    @pl.when(step + ahead < chunks)
-    def _():
-        fetch(step + ahead).start()
-
-    fetch(step).wait()
-
-    passing = jnp.concatenate(
-        [table[step], field_ref[...], jnp.ones((ones, width), BF16)], axis=0
-    )
-    cotangent = cotangent_ref[...]
-    biases = jnp.concatenate([bias_ref[...]] * (tile // LANES), axis=1)
-    pre = [
-        matmul(modes[...], table[step, :, at : at + tile])
-        + matmul(mixer_ref[...], field_ref[:, at : at + tile])
-        for at in range(0, width, tile)
-    ]
-    results, grads = [], []
-    for index, at in enumerate(range(0, width, tile)):
-        results.append([])
-        grads.append([])
+    def build(at):
+        return matmul(modes[...], table_ref[0, :, at])
+
+    def pointwise(pre, at):
         for first in range(0, rows, chunk):
             part = slice(first, first + chunk)
-            values = pre[index][part] + biases[part]
+            values = pre[part, :] + mixed_ref[part, at]
             integral, decay = normal_parts(values)
-            results[-1].append((values * integral).astype(BF16))
+            output_ref[part, at] = (values * integral).astype(BF16)
             slope = integral + (values * DENSITY) * decay
-            wide_cotangent = cotangent[part, at : at + tile].astype(F32)
-            grads[-1].append((wide_cotangent * slope).astype(BF16))
-    grad = jnp.concatenate([jnp.concatenate(column, axis=0) for column in grads], axis=1)
-    output_ref[...] = jnp.concatenate(
-        [jnp.concatenate(column, axis=0) for column in results], axis=1
-    )
-    grad_ref[...] = grad
-    total[...] += matmul_turned(passing, grad)
+            grad_ref[part, at] = (cotangent_ref[part, at].astype(F32) * slope).astype(BF16)
+
+    tiles = [slice(first, first + tile) for first in range(0, width, tile)]
+    ready = build(tiles[0])
+    for index, at in enumerate(tiles):
+        pre = ready
+        if index + 1 < len(tiles):
+            ready = build(tiles[index + 1])
+        pointwise(pre, at)
+    passing = jnp.concatenate(
+        [table_ref[0], field_ref[...], jnp.ones((ones, width), BF16)], axis=0
+    )
+    total[...] += matmul_turned(passing, grad_ref[...])
 
     @pl.when(step == pl.num_programs(0) - 1)
     def _():
@@ -436,34 +450,33 @@
         own_bias = jnp.sum(
             jnp.where(place % CHANS == chan, bias, 0.0), axis=1, keepdims=True
         )
-        point = jnp.dot(
+        sums = jnp.dot(
             folded, select, precision=lax.Precision.HIGHEST, preferred_element_type=F32
         )
         lane = lax.broadcasted_iota(jnp.int32, (CHANS, LANES), 1)
-        sums_ref[...] = sums_in_ref[...] + jnp.where(lane == CHANS, own_bias, point)
-
-
-def middle(packed, field, cotangent, table, mixer, bias, sums, output, part, xl, tl):
+        sums_ref[...] = sums_in_ref[...] + jnp.where(lane == CHANS, own_bias, sums)
+
+
+def middle(packed, field, cotangent, mixed, table, sums, output, part, xl, tl):
     rows = xl * tl * CHANS
     width = WIDTH
     chunks = CELLS // width
     whole = lambda *shape: pl.BlockSpec(shape, lambda n: (0,) * len(shape))
     tile = pl.BlockSpec((rows, width), lambda n: (part, n))
     kernel = functools.partial(middle_kernel, xl, tl)
-    operands = (packed, field, cotangent, table, mixer, bias, sums)
+    operands = (packed, field, cotangent, mixed, table, sums)
     specs = [
-        pl.BlockSpec(memory_space=pltpu.VMEM),
+        whole(*packed.shape),
         tile,
         tile,
-        pl.BlockSpec(memory_space=pltpu.HBM),
-        whole(rows, rows),
-        whole(rows, LANES),
+        tile,
+        pl.BlockSpec((1, KQ, width), lambda n: (n, 0, 0)),
         whole(CHANS, LANES),
     ]
     aliases = {}
     if output is None:
         inner = kernel
-        kernel = lambda *refs: inner(*refs[:7], None, *refs[7:])
+        kernel = lambda *refs: inner(*refs[:6], None, *refs[6:])
     else:
         aliases = {len(operands): 0}
         operands += (output,)
@@ -488,13 +501,11 @@
             pltpu.VMEM((xl, tl, CHANS, KQ), F32),
             pltpu.VMEM((rows, KQ), BF16),
             pltpu.VMEM((KQ + rows + 16, rows), F32),
-            pltpu.VMEM((chunks, KQ, width), BF16),
             pltpu.VMEM(packed.shape, BF16),
-            pltpu.SemaphoreType.DMA((chunks,)),
             pltpu.SemaphoreType.DMA((KQ // LANES,)),
         ],
         input_output_aliases=aliases,
-        compiler_params=vmem_params(44),
+        compiler_params=vmem_params(60),
         cost_estimate=pl.CostEstimate(
             flops=5 * rows * CELLS * KQ, bytes_accessed=18 << 20, transcendentals=rows * CELLS
         ),
@@ -502,28 +513,21 @@
     )(*operands)
 
 
-def last_kernel(
-    xl,
-    tl,
-    packed_ref,
-    mixer_ref,
-    table_ref,
-    *refs,
-):
-    grad_refs, field_ref = refs[:PARTS], refs[PARTS]
-    wide, modes, table, grads, field, table_sems, grad_sems, field_sems = refs[PARTS + 1 :]
+def last_kernel(xl, tl, packed_ref, table_ref, mixed_ref, field_ref, *scratch):
+    packed, wide, modes, table, mixed, field, packed_sem, table_sems, mixed_sems, field_sems = (
+        scratch
+    )
     chunks = table.shape[0]
     ahead = 4
     fetches, sends = [], []
     for at in range(chunks):
         lanes = slice(at * WIDTH, (at + 1) * WIDTH)
-        fetches.append([pltpu.make_async_copy(table_ref.at[at], table.at[at], table_sems.at[at])])
-        for part, grad_ref in enumerate(grad_refs):
-            fetches[at].append(
-                pltpu.make_async_copy(
-                    grad_ref.at[:, lanes], grads.at[at, part], grad_sems.at[at, part]
-                )
+        fetches.append(
+            (
+                pltpu.make_async_copy(table_ref.at[at], table.at[at], table_sems.at[at]),
+                pltpu.make_async_copy(mixed_ref.at[:, lanes], mixed.at[at], mixed_sems.at[at]),
             )
+        )
         sends.append(
             pltpu.make_async_copy(field.at[at], field_ref.at[:, lanes], field_sems.at[at])
         )
@@ -532,51 +536,50 @@
         for fetch in fetches[at]:
             fetch.start()
 
+    own = pltpu.make_async_copy(packed_ref, packed, packed_sem)
+    own.start()
     for at in range(ahead):
         start(at)
-    unpack_modes(packed_ref, wide, xl, tl)
+    own.wait()
+    unpack_modes(packed, wide, xl, tl)
     modes[...] = wide[...].reshape(modes.shape).astype(BF16)
     for at in range(chunks):
         for fetch in fetches[at]:
             fetch.wait()
         if at + ahead < chunks:
             start(at + ahead)
-        point = [matmul(mixer_ref[...], grads[at, part]) for part in range(PARTS)]
-        field[at] = (
-            matmul(modes[...], table[at]) + jnp.concatenate(point, axis=0)
-        ).astype(BF16)
+        field[at] = (matmul(modes[...], table[at]) + mixed[at].astype(F32)).astype(BF16)
         sends[at].start()
     for send in sends:
         send.wait()
 
 
-def last(packed, grads, table, mixer, xl, tl):
+def last(packed, mixed, table, xl, tl):
     rows = xl * tl * CHANS
-    part = rows // PARTS
     chunks = CELLS // WIDTH
-    apart = pl.BlockSpec(memory_space=pltpu.HBM)
-    on_chip = pl.BlockSpec(memory_space=pltpu.VMEM)
     return pl.pallas_call(
         functools.partial(last_kernel, xl, tl),
-        in_specs=[on_chip] * 2 + [apart] * (1 + PARTS),
-        out_specs=apart,
+        in_specs=[pl.BlockSpec(memory_space=pl.ANY)] + [pl.BlockSpec(memory_space=pltpu.HBM)] * 2,
+        out_specs=pl.BlockSpec(memory_space=pltpu.HBM),
         out_shape=jax.ShapeDtypeStruct((rows, CELLS), BF16),
         scratch_shapes=[
+            pltpu.VMEM(packed.shape, BF16),
             pltpu.VMEM((xl, tl, CHANS, KQ), F32),
             pltpu.VMEM((rows, KQ), BF16),
             pltpu.VMEM((chunks, KQ, WIDTH), BF16),
-            pltpu.VMEM((chunks, PARTS, part, WIDTH), BF16),
             pltpu.VMEM((chunks, rows, WIDTH), BF16),
+            pltpu.VMEM((chunks, rows, WIDTH), BF16),
+            pltpu.SemaphoreType.DMA,
             pltpu.SemaphoreType.DMA((chunks,)),
-            pltpu.SemaphoreType.DMA((chunks, PARTS)),
+            pltpu.SemaphoreType.DMA((chunks,)),
             pltpu.SemaphoreType.DMA((chunks,)),
         ],
-        compiler_params=vmem_params(44),
+        compiler_params=vmem_params(60),
         cost_estimate=pl.CostEstimate(
             flops=2 * rows * CELLS * KQ, bytes_accessed=18 << 20, transcendentals=0
         ),
         name="last",
-    )(packed, mixer, table, *grads)
+    )(packed, table, mixed)
 
 
 def swap(blocks):
@@ -643,12 +646,14 @@
     spectrum, *mixed = mix(
         [spread_in], packed_weight, sums, (x_in[0], t_in, x_out[1], t_out), False
     )
+    halves = range(PARTS)
+    mixed_field = point([field] * PARTS, halves, mixer, bias, F32, "point")
     output = None
     grads, spread_grad = [], []
     for part in range(PARTS):
         returned = swap(mixed[part].reshape(devices, xl * CHANS, LANES))
         output, grad, sent, sums = middle(
-            returned, field, cot, table, mixer, bias, sums, output, part, xl, tl
+            returned, field, cot, mixed_field, table, sums, output, part, xl, tl
         )
         grads.append(grad)
         spread_grad.append(swap(sent).reshape(part_shape))
@@ -658,7 +663,8 @@
     )
     grad_back = swap(mixed_back.reshape(devices, xl_all * CHANS, LANES))
     grad_spec = outer(spectrum, grad_modes, own)
-    grad_field = last(grad_back, grads, table, mixer_back, xl_all, tl)
+    mixed_grad = point(grads, [0] * PARTS, mixer_back, jnp.zeros_like(bias), BF16, "point_back")
+    grad_field = last(grad_back, mixed_grad, table, xl_all, tl)
     summed = summed * norm_scale
     return (
         output.reshape(features.shape),

time: 205 us -> 200 us (0.976)
  Pallas kernels: 80.4 us -> 103 us
  local copies, waits for them, and re-layouts: 26 us -> 4.19 us
  waiting for transfers between devices: 37.7 us -> 31.4 us
    unnamed x64 -> x22, local copies, waits for them, and re-layouts: 25.3 us -> 2.22 us
    pallas_call x1 -> x3, Pallas kernels: 9.26 us -> 26.3 us  [the longest x2 15.9 us: point(): pl.pallas_call(point_kernel, grid=(CELLS // WIDTH,), in_specs=[pl.BlockSp...]
    all_to_all x5, waiting for transfers between devices: 29 us -> 22.5 us  [swap(): lax.all_to_all(blocks, ('gx', 'ta'), split_axis=0, concat_axis=0, tiled=T...]
    pallas_call x2, Pallas kernels: 6.77 us -> 12.2 us  [mix(): pl.pallas_call(functools.partial(mix_kernel, backward), out_shape=[jax.Sh...]
    pallas_call x2, Pallas kernels: 38.6 us -> 35.8 us  [middle(): pl.pallas_call(kernel, grid=(chunks,), in_specs=specs, out_specs=[tile, p...]
  transfers between devices with their start and end apart: 10 -> 10, of which waited for: 7 -> 7; matrix products, arithmetic and copies ran while one was open for 2% -> 3% of each run, Pallas kernels for 28% -> 36%
where the time goes in v5:
time: 200 us; the launch traced here: 198 us
  Pallas kernels  103 us (52%)
  starting transfers between devices  35.7 us (18%)
  waiting for transfers between devices  31.4 us (16%)
  blocking collectives  19.3 us (10%)
  local copies, waits for them, and re-layouts  4.19 us (2%)
  matrix products  2.86 us (1%)
    pallas_call x2, Pallas kernels, middle(): pl.pallas_call(kernel, grid=(chunks,), in_specs=specs, out_specs=[tile, p...  35.8 us
    all_to_all x5, starting transfers between devices, swap(): lax.all_to_all(blocks, ('gx', 'ta'), split_axis=0, concat_axis=0, tiled=T...  27.9 us
    all_to_all x5, waiting for transfers between devices, swap(): lax.all_to_all(blocks, ('gx', 'ta'), split_axis=0, concat_axis=0, tiled=T...  22.5 us
    all_to_all x1, blocking collectives, swap(): lax.all_to_all(blocks, ('gx', 'ta'), split_axis=0, concat_axis=0, tiled=T...  19.3 us
    pallas_call x2, Pallas kernels, point(): pl.pallas_call(point_kernel, grid=(CELLS // WIDTH,), in_specs=[pl.BlockSp...  15.9 us
    pallas_call x2, Pallas kernels, mix(): pl.pallas_call(functools.partial(mix_kernel, backward), out_shape=[jax.Sh...  12.2 us
    pallas_call x1, Pallas kernels, pack_weight(): pl.pallas_call(weight_kernel, grid=(KX // per,), in_specs=[pl.BlockSpec((...  11 us
    pallas_call x1, Pallas kernels, last(): pl.pallas_call(functools.partial(last_kernel, xl, tl), in_specs=[pl.Block...  10.4 us
  transfers between devices with their start and end apart: 10, of which 7 were waited for; matrix products, arithmetic and copies ran while one was open for 3% of the time, Pallas kernels for 36%

profile of v5, /device:TPU:0, one launch (start us, length us, event | category | flops | bytes accessed | tf_op | source)
XLA Modules:
  0.0 198.4 jit_solution(12619144376251043479)
XLA Ops:
  0.6 8.4 %analyse.1 = bf16[32,128,128]{2,1,0:T(8,128)(2,1)} custom-call(bf16[512,4096]{1,0:T(8,128)(2,1)} %bitcast.18, bf16[8,1024,512]{2,1,0:T(8,128)(2,1)} %constant.11.clone.table_ref.refs_4_), custom_call_target="tpu_custom_call" | custom-call | flops 4294967296 | bytes 13631488 | tf_op jit(solution)/shard_map/analyse/pallas_call | solution.py:146
  9.0 7.3 %all-to-all-start = ((bf16[32,128,128]{2,1,0:T(8,128)(2,1)}), bf16[32,128,128]{2,1,0:T(8,128)(2,1)S(1)}, u32[]{:S(2)}, u32[]{:S(2)}) async-start(bf16[32,128,128]{2,1,0:T(8,128)(2,1)} %analyse.1), calls=%async_computation | async-start | bytes 2097152 | tf_op jit(solution)/shard_map/all_to_all | solution.py:586
  16.4 11.0 %pack_weight.1.weight_ref = f32[32,8,8,512]{3,2,1,0:T(8,128)} custom-call(f32[32,16,8,8,32]{4,3,2,1,0:T(8,128)} %weight_ref.1), custom_call_target="tpu_custom_call" | custom-call | flops 1048576 | bytes 20971520 | tf_op jit(solution)/shard_map/pack_weight/pallas_call | solution.py:180
  27.4 15.2 %all-to-all-done = bf16[32,128,128]{2,1,0:T(8,128)(2,1)S(1)} async-done(((bf16[32,128,128]{2,1,0:T(8,128)(2,1)}), bf16[32,128,128]{2,1,0:T(8,128)(2,1)S(1)}, u32[]{:S(2)}, u32[]{:S(2)}) %all-to-all-start) | async-done | bytes 1048608 | tf_op jit(solution)/shard_map/all_to_all | solution.py:586
  43.6 5.7 %mix.1 = (f32[256,512]{1,0:T(8,128)}, bf16[8,4,64,128]{3,2,1,0:T(8,128)(2,1)}, bf16[8,4,64,128]{3,2,1,0:T(8,128)(2,1)}) custom-call(f32[32,8,8,512]{3,2,1,0:T(8,128)} %pack_weight.1.weight_ref, f32[8,128]{1,0:T(8,128)} %broadcast_in_dim.12._.refs_5_, bf16[1,256,1024]{2,1,0:T(8,128)(2,1)} %constant.26.clone.x_in_ref, ...), custom_call_target="tpu_custom_call" | custom-call | flops 1073741824 | bytes 9437184 | tf_op jit(solution)/shard_map/mix/pallas_call | solution.py:285
  49.3 19.3 %all_to_all.30.refs_0_ = bf16[32,64,128]{2,1,0:T(8,128)(2,1)} all-to-all(bf16[32,64,128]{2,1,0:T(8,128)(2,1)} %bitcast.32), channel_id=1, replica_groups=mesh['gx'=8,'ta'=4] {'gx','ta'}, dimensions={0} | all-to-all | bytes 1048576 | tf_op jit(solution)/shard_map/all_to_all | solution.py:586
  68.6 3.1 %all-to-all-start.1 = ((bf16[32,64,128]{2,1,0:T(8,128)(2,1)}), bf16[32,64,128]{2,1,0:T(8,128)(2,1)S(1)}, u32[]{:S(2)}, u32[]{:S(2)}) async-start(bf16[32,64,128]{2,1,0:T(8,128)(2,1)} %bitcast.31), calls=%async_computation.1 | async-start | bytes 1048576 | tf_op jit(solution)/shard_map/all_to_all | solution.py:586
  71.7 1.0 fusion.2.bias_ref
  72.7 0.9 fusion.mixer_ref
  73.6 8.2 %point.1.refs_3_.mixed_ref = f32[512,4096]{1,0:T(8,128)} custom-call(bf16[256,256]{1,0:T(8,128)(2,1)} %fusion.mixer_ref, f32[256,128]{1,0:T(8,128)} %fusion.2.bias_ref, bf16[512,4096]{1,0:T(8,128)(2,1)} %bitcast.19, bf16[512,4096]{1,0:T(8,128)(2,1)} %bitcast.20), custom_call_target="tpu_custom_call" | custom-call | flops 1073741824 | bytes 12582912 | tf_op jit(solution)/shard_map/point/pallas_call | solution.py:362
  81.9 17.9 %middle.2 = (bf16[512,4096]{1,0:T(8,128)(2,1)}, bf16[256,4096]{1,0:T(8,128)(2,1)}, bf16[32,64,128]{2,1,0:T(8,128)(2,1)}, f32[8,128]{1,0:T(8,128)}) custom-call(bf16[32,64,128]{2,1,0:T(8,128)(2,1)} %all_to_all.30.refs_0_, bf16[512,4096]{1,0:T(8,128)(2,1)} %bitcast.21, bf16[512,4096]{1,0:T(8,128)(2,1)} %bitcast.23, f32[512,4096]{1,0:T(8,128)} %point.1.refs_3_.mixed_ref, ...), custom_call_target="tpu_custom_call" | custom-call | flops 5368709120 | bytes 18874368 | tf_op jit(solution)/shard_map/middle/pallas_call | solution.py:484
  99.8 5.8 %all-to-all-start.3 = ((bf16[32,64,128]{2,1,0:T(8,128)(2,1)}), bf16[32,64,128]{2,1,0:T(8,128)(2,1)S(1)}, u32[]{:S(2)}, u32[]{:S(2)}) async-start(bf16[32,64,128]{2,1,0:T(8,128)(2,1)} %get-tuple-element.24), calls=%async_computation.3 | async-start | bytes 1048576 | tf_op jit(solution)/shard_map/all_to_all | solution.py:586
  105.6 17.9 %middle.3 = (bf16[512,4096]{1,0:T(8,128)(2,1)}, bf16[256,4096]{1,0:T(8,128)(2,1)}, bf16[32,64,128]{2,1,0:T(8,128)(2,1)}, f32[8,128]{1,0:T(8,128)}) custom-call(bf16[32,64,128]{2,1,0:T(8,128)(2,1)} %copy-done.3, bf16[512,4096]{1,0:T(8,128)(2,1)} %bitcast.22, bf16[512,4096]{1,0:T(8,128)(2,1)} %bitcast.24, ...), custom_call_target="tpu_custom_call", output_to_operand_aliasing={{0}: (6, {})} | custom-call | flops 5368709120 | bytes 18874368 | tf_op jit(solution)/shard_map/middle/pallas_call | solution.py:484
  123.6 6.0 %all-to-all-start.4 = ((bf16[32,64,128]{2,1,0:T(8,128)(2,1)}), bf16[32,64,128]{2,1,0:T(8,128)(2,1)S(1)}, u32[]{:S(2)}, u32[]{:S(2)}) async-start(bf16[32,64,128]{2,1,0:T(8,128)(2,1)} %get-tuple-element.25), calls=%async_computation.4 | async-start | bytes 1048576 | tf_op jit(solution)/shard_map/all_to_all | solution.py:586
  129.8 1.3 collective-permute-done
  131.7 1.6 collective-permute-start.1
  133.3 2.0 %collective-permute-done.1 = f32[8,128]{1,0:T(8,128)S(1)} collective-permute-done((f32[8,128]{1,0:T(8,128)S(1)}, f32[8,128]{1,0:T(8,128)S(1)}, u32[]{:S(2)}, u32[]{:S(2)}) %collective-permute-start.1) | collective-permute-done | bytes 4128 | tf_op jit(solution)/shard_map/ppermute | solution.py:593
  135.4 1.8 collective-permute-start.2
  137.2 1.8 collective-permute-done.2
  139.0 1.6 collective-permute-start.3
  140.6 2.0 collective-permute-done.3
  142.6 2.6 %collective-permute-start.4 = (f32[8,128]{1,0:T(8,128)S(1)}, f32[8,128]{1,0:T(8,128)S(1)}, u32[]{:S(2)}, u32[]{:S(2)}) collective-permute-start(f32[8,128]{1,0:T(8,128)S(1)} %add.18), channel_id=1, source_target_pairs={{0,16},{1,17},{2,18},{3,19},{4,20},{5,21},{6,22},{7,23},{8,24},{9,... | collective-permute-start | bytes 12296 | tf_op jit(solution)/shard_map/ppermute | solution.py:593
  145.2 1.9 collective-permute-done.4
  147.7 0.8 copy-done.5
  148.5 6.4 %mix_back.1 = (f32[256,512]{1,0:T(8,128)}, bf16[8,4,128,128]{3,2,1,0:T(8,128)(2,1)}) custom-call(f32[32,8,8,512]{3,2,1,0:T(8,128)} %pack_weight.1.weight_ref, f32[8,128]{1,0:T(8,128)} %get-tuple-element.32._, bf16[2,256,512]{2,1,0:T(8,128)(2,1)} %constant.27.clone.x_in_ref, bf16[512,512]{1,0:T(8,128)(2,1)} %constant.30.clone.t_in_ref, ...), custom_call_target="tpu_custom_call" | custom-call | flops 1073741824 | bytes 9437184 | tf_op jit(solution)/shard_map/mix_back/pallas_call | solution.py:285
  154.9 5.7 %all-to-all-start.5 = ((bf16[32,128,128]{2,1,0:T(8,128)(2,1)}), bf16[32,128,128]{2,1,0:T(8,128)(2,1)S(1)}, u32[]{:S(2)}, u32[]{:S(2)}) async-start(bf16[32,128,128]{2,1,0:T(8,128)(2,1)} %bitcast.30), calls=%async_computation.5 | async-start | bytes 2097152 | tf_op jit(solution)/shard_map/all_to_all | solution.py:586
  160.6 0.9 fusion.1.mixer_ref
  162.2 7.6 %point_back.1.mixed_ref = bf16[512,4096]{1,0:T(8,128)(2,1)} custom-call(bf16[256,256]{1,0:T(8,128)(2,1)} %fusion.1.mixer_ref, f32[256,128]{1,0:T(8,128)} %broadcast_in_dim.14.bias_ref, bf16[256,4096]{1,0:T(8,128)(2,1)} %get-tuple-element.27.refs_0_, bf16[256,4096]{1,0:T(8,128)(2,1)} %get-tuple-element.28.refs_1_), custom_call_target="tpu_custom_call" | custom-call | flops 1073741824 | bytes 12582912 | tf_op jit(solution)/shard_map/point_back/pallas_call | solution.py:362
  170.6 9.1 %outer.1 = f32[32,16,8,8,32]{4,3,2,1,0:T(8,128)} custom-call(f32[256,512]{1,0:T(8,128)} %get-tuple-element.29.spectrum_ref, f32[256,512]{1,0:T(8,128)} %get-tuple-element.30.grad_ref), custom_call_target="tpu_custom_call" | custom-call | flops 1048576 | bytes 17825792 | tf_op jit(solution)/shard_map/outer/pallas_call | solution.py:325
  179.6 7.2 %all-to-all-done.5.packed_ref = bf16[32,128,128]{2,1,0:T(8,128)(2,1)S(1)} async-done(((bf16[32,128,128]{2,1,0:T(8,128)(2,1)}), bf16[32,128,128]{2,1,0:T(8,128)(2,1)S(1)}, u32[]{:S(2)}, u32[]{:S(2)}) %all-to-all-start.5) | async-done | bytes 1048608 | tf_op jit(solution)/shard_map/all_to_all | solution.py:586
  186.9 1.0 copy-done.1
  187.9 10.4 %last.1 = bf16[512,4096]{1,0:T(8,128)(2,1)} custom-call(bf16[32,128,128]{2,1,0:T(8,128)(2,1)} %copy-done.1, bf16[8,1024,512]{2,1,0:T(8,128)(2,1)} %constant.11.clone.table_ref.refs_4_, bf16[512,4096]{1,0:T(8,128)(2,1)} %point_back.1.mixed_ref), custom_call_target="tpu_custom_call" | custom-call | flops 4294967296 | bytes 18874368 | tf_op jit(solution)/shard_map/last/pallas_call | solution.py:560
  (32 shorter events, 3.8 us)
Async XLA Ops:
  0.6 72.1 %copy-start = (bf16[8,8]{1,0:T(8,128)(2,1)S(1)}, bf16[8,8]{1,0:T(8,128)(2,1)}, u32[]{:S(2)}) copy-start(bf16[8,8]{1,0:T(8,128)(2,1)} %param.18) | copy-start | bytes 388
  9.0 33.5 %all-to-all-start = ((bf16[32,128,128]{2,1,0:T(8,128)(2,1)}), bf16[32,128,128]{2,1,0:T(8,128)(2,1)S(1)}, u32[]{:S(2)}, u32[]{:S(2)}) async-start(bf16[32,128,128]{2,1,0:T(8,128)(2,1)} %analyse.1), calls=%async_computation | async-start | bytes 2097152 | tf_op jit(solution)/shard_map/all_to_all | solution.py:586
  42.6 1.0 copy-start.2
  43.6 28.1 %copy-start.8 = (f32[256,8]{1,0:T(8,128)S(1)}, f32[256,8]{1,0:T(8,128)}, u32[]{:S(2)}) copy-start(f32[256,8]{1,0:T(8,128)} %constant.34.clone) | copy-start | bytes 24580
  43.6 28.1 %copy-start.10 = (f32[8]{0:T(128)S(1)}, f32[8]{0:T(128)}, u32[]{:S(2)}) copy-start(f32[8]{0:T(128)} %param.19) | copy-start | bytes 100
  43.6 29.1 %copy-start.6 = (f32[256,256]{1,0:T(8,128)S(1)}, f32[256,256]{1,0:T(8,128)}, u32[]{:S(2)}) copy-start(f32[256,256]{1,0:T(8,128)} %constant.33.clone) | copy-start | bytes 786436
  43.6 29.1 %copy-start.7 = (bf16[256,8]{1,0:T(8,128)(2,1)S(1)}, bf16[256,8]{1,0:T(8,128)(2,1)}, u32[]{:S(2)}) copy-start(bf16[256,8]{1,0:T(8,128)(2,1)} %constant.32.clone) | copy-start | bytes 12292
  68.6 31.2 %all-to-all-start.1 = ((bf16[32,64,128]{2,1,0:T(8,128)(2,1)}), bf16[32,64,128]{2,1,0:T(8,128)(2,1)S(1)}, u32[]{:S(2)}, u32[]{:S(2)}) async-start(bf16[32,64,128]{2,1,0:T(8,128)(2,1)} %bitcast.31), calls=%async_computation.1 | async-start | bytes 1048576 | tf_op jit(solution)/shard_map/all_to_all | solution.py:586
  99.8 5.9 %copy-start.3 = (bf16[32,64,128]{2,1,0:T(8,128)(2,1)}, bf16[32,64,128]{2,1,0:T(8,128)(2,1)S(1)}, u32[]{:S(2)}) copy-start(bf16[32,64,128]{2,1,0:T(8,128)(2,1)S(1)} %all-to-all-done.1.packed_ref) | copy-start | bytes 1572868
  99.8 23.8 %all-to-all-start.3 = ((bf16[32,64,128]{2,1,0:T(8,128)(2,1)}), bf16[32,64,128]{2,1,0:T(8,128)(2,1)S(1)}, u32[]{:S(2)}, u32[]{:S(2)}) async-start(bf16[32,64,128]{2,1,0:T(8,128)(2,1)} %get-tuple-element.24), calls=%async_computation.3 | async-start | bytes 1048576 | tf_op jit(solution)/shard_map/all_to_all | solution.py:586
  123.6 24.1 %copy-start.4 = (bf16[32,64,128]{2,1,0:T(8,128)(2,1)}, bf16[32,64,128]{2,1,0:T(8,128)(2,1)S(1)}, u32[]{:S(2)}) copy-start(bf16[32,64,128]{2,1,0:T(8,128)(2,1)S(1)} %all-to-all-done.3) | copy-start | bytes 1572868
  123.6 24.1 %all-to-all-start.4 = ((bf16[32,64,128]{2,1,0:T(8,128)(2,1)}), bf16[32,64,128]{2,1,0:T(8,128)(2,1)S(1)}, u32[]{:S(2)}, u32[]{:S(2)}) async-start(bf16[32,64,128]{2,1,0:T(8,128)(2,1)} %get-tuple-element.25), calls=%async_computation.4 | async-start | bytes 1048576 | tf_op jit(solution)/shard_map/all_to_all | solution.py:586
  129.6 1.4 collective-permute-start
  131.7 3.6 %collective-permute-start.1 = (f32[8,128]{1,0:T(8,128)S(1)}, f32[8,128]{1,0:T(8,128)S(1)}, u32[]{:S(2)}, u32[]{:S(2)}) collective-permute-start(f32[8,128]{1,0:T(8,128)S(1)} %add.15), channel_id=1, source_target_pairs={{0,2},{1,3},{2,0},{3,1},{4,6},{5,7},{6,4},{7,5},{8,10},{9,11},{10,... | collective-permute-start | bytes 12296 | tf_op jit(solution)/shard_map/ppermute | solution.py:593
  135.4 3.6 %collective-permute-start.2 = (f32[8,128]{1,0:T(8,128)S(1)}, f32[8,128]{1,0:T(8,128)S(1)}, u32[]{:S(2)}, u32[]{:S(2)}) collective-permute-start(f32[8,128]{1,0:T(8,128)S(1)} %add.16), channel_id=1, source_target_pairs={{0,4},{1,5},{2,6},{3,7},{4,0},{5,1},{6,2},{7,3},{8,12},{9,13},{10,... | collective-permute-start | bytes 12296 | tf_op jit(solution)/shard_map/ppermute | solution.py:593
  139.0 3.6 %collective-permute-start.3 = (f32[8,128]{1,0:T(8,128)S(1)}, f32[8,128]{1,0:T(8,128)S(1)}, u32[]{:S(2)}, u32[]{:S(2)}) collective-permute-start(f32[8,128]{1,0:T(8,128)S(1)} %add.17), channel_id=1, source_target_pairs={{0,8},{1,9},{2,10},{3,11},{4,12},{5,13},{6,14},{7,15},{8,0},{9,1},... | collective-permute-start | bytes 12296 | tf_op jit(solution)/shard_map/ppermute | solution.py:593
  142.6 4.5 %collective-permute-start.4 = (f32[8,128]{1,0:T(8,128)S(1)}, f32[8,128]{1,0:T(8,128)S(1)}, u32[]{:S(2)}, u32[]{:S(2)}) collective-permute-start(f32[8,128]{1,0:T(8,128)S(1)} %add.18), channel_id=1, source_target_pairs={{0,16},{1,17},{2,18},{3,19},{4,20},{5,21},{6,22},{7,23},{8,24},{9,... | collective-permute-start | bytes 12296 | tf_op jit(solution)/shard_map/ppermute | solution.py:593
  147.7 22.2 %copy-start.9 = (f32[8,128]{1,0:T(8,128)}, f32[8,128]{1,0:T(8,128)S(1)}, u32[]{:S(2)}) copy-start(f32[8,128]{1,0:T(8,128)S(1)} %get-tuple-element.31) | copy-start | bytes 12292
  147.7 0.8 copy-start.5
  154.9 31.9 %all-to-all-start.5 = ((bf16[32,128,128]{2,1,0:T(8,128)(2,1)}), bf16[32,128,128]{2,1,0:T(8,128)(2,1)S(1)}, u32[]{:S(2)}, u32[]{:S(2)}) async-start(bf16[32,128,128]{2,1,0:T(8,128)(2,1)} %bitcast.30), calls=%async_computation.5 | async-start | bytes 2097152 | tf_op jit(solution)/shard_map/all_to_all | solution.py:586
  186.9 1.0 copy-start.1

commit v6 on v5

--- a/solution.py
+++ b/solution.py
@@ -27,7 +27,6 @@
 LANES = 128
 PARTS = 2
 WIDTH = 512
-LOG2_E = math.log2(math.e)
 DENSITY = 1.0 / math.sqrt(2.0 * math.pi)
 F32 = jnp.float32
 BF16 = jnp.bfloat16
@@ -169,9 +168,8 @@
     for kx in range(weight_ref.shape[0]):
         for group in range(KT // 4):
             parts = [weight_ref[kx, 4 * group + k] for k in range(4)]
-            packed_ref[kx, :, :, group * LANES : (group + 1) * LANES] = jnp.concatenate(
-                parts, axis=-1
-            )
+            joined = jnp.concatenate(parts, axis=-1).reshape(CHANS * CHANS, LANES)
+            packed_ref[kx, :, group * LANES : (group + 1) * LANES] = joined.astype(BF16)
 
 
 def pack_weight(weight):
@@ -181,8 +179,8 @@
         weight_kernel,
         grid=(KX // per,),
         in_specs=[pl.BlockSpec((per, KT, CHANS, CHANS, own), lambda n: (n, 0, 0, 0, 0))],
-        out_specs=pl.BlockSpec((per, CHANS, CHANS, KT * own), lambda n: (n, 0, 0, 0)),
-        out_shape=jax.ShapeDtypeStruct((KX, CHANS, CHANS, KT * own), F32),
+        out_specs=pl.BlockSpec((per, CHANS * CHANS, KT * own), lambda n: (n, 0, 0)),
+        out_shape=jax.ShapeDtypeStruct((KX, CHANS * CHANS, KT * own), BF16),
         compiler_params=vmem_params(60),
         cost_estimate=pl.CostEstimate(flops=1 << 20, bytes_accessed=20 << 20, transcendentals=0),
         name="pack_weight",
@@ -211,14 +209,12 @@
 
 def mix_kernel(
     backward,
+    afters,
     weight_ref,
-    _,
-    x_in_ref,
-    t_in_ref,
-    x_out_ref,
-    t_out_ref,
     *refs,
 ):
+    x_in_ref, t_in_ref, x_out_ref, t_out_ref = refs[afters : afters + 4]
+    refs = refs[afters + 4 :]
     ins, outs = x_in_ref.shape[0], x_out_ref.shape[0]
     spread_refs, modes_ref, back_refs = refs[:ins], refs[ins], refs[ins + 1 : ins + 1 + outs]
     scratch = refs[ins + 1 + outs :]
@@ -253,13 +249,14 @@
     for kx in range(KX):
         rows = slice(kx * CHANS, (kx + 1) * CHANS)
         own = modes[rows, :]
+        weights = weight[kx].astype(F32).reshape(CHANS, CHANS, own.shape[1])
         if backward:
-            sums = [jnp.sum(own * weight[kx, i], axis=0, keepdims=True) for i in range(CHANS)]
+            sums = [jnp.sum(own * weights[i], axis=0, keepdims=True) for i in range(CHANS)]
             mixed[rows, :] = jnp.concatenate(sums, axis=0)
         else:
-            total = own[0:1, :] * weight[kx, 0]
+            total = own[0:1, :] * weights[0]
             for i in range(1, CHANS):
-                total = total + own[i : i + 1, :] * weight[kx, i]
+                total = total + own[i : i + 1, :] * weights[i]
             mixed[rows, :] = total
     tables[2].wait()
     tables[3].wait()
@@ -276,19 +273,19 @@
 
 
 def mix(spreads, weight, after, tables, backward):
-    modes = (KX * CHANS, weight.shape[3])
+    modes = (KX * CHANS, weight.shape[2])
     gx, ta, _, lanes = spreads[0].shape
     outs = tables[2].shape[0]
     back = (gx, ta, tables[2].shape[1] // gx, lanes)
     anywhere = pl.BlockSpec(memory_space=pl.ANY)
     apart = pl.BlockSpec(memory_space=pltpu.HBM)
     return pl.pallas_call(
-        functools.partial(mix_kernel, backward),
+        functools.partial(mix_kernel, backward, len(after)),
         out_shape=[jax.ShapeDtypeStruct(modes, F32)] + [jax.ShapeDtypeStruct(back, BF16)] * outs,
-        in_specs=[apart] + [anywhere] + [apart] * 4 + [anywhere] * len(spreads),
+        in_specs=[apart] + [anywhere] * len(after) + [apart] * 4 + [anywhere] * len(spreads),
         out_specs=[apart] + [anywhere] * outs,
         scratch_shapes=[
-            pltpu.VMEM(weight.shape, F32),
+            pltpu.VMEM(weight.shape, BF16),
             pltpu.VMEM(modes, F32),
             pltpu.VMEM(modes, F32),
             pltpu.VMEM((outs,) + back, BF16),
@@ -302,7 +299,7 @@
         compiler_params=vmem_params(60),
         cost_estimate=pl.CostEstimate(flops=1 << 30, bytes_accessed=9 << 20, transcendentals=0),
         name="mix_back" if backward else "mix",
-    )(weight, after, *tables, *spreads)
+    )(weight, *after, *tables, *spreads)
 
 
 def outer_kernel(spectrum_ref, grad_ref, result_ref):
@@ -338,7 +335,7 @@
     scaled = 1.0 + 0.2316419 * jnp.abs(values)
     guess = pl.reciprocal(scaled, approx=True)
     t = guess * (2.0 - scaled * guess)
-    decay = jnp.exp2(values * values * (-0.5 * LOG2_E))
+    decay = jnp.exp(values * values * -0.5)
     series = (1.330274429 * DENSITY) * t - 1.821255978 * DENSITY
     series = series * t + 1.781477937 * DENSITY
     series = series * t - 0.356563782 * DENSITY
@@ -347,44 +344,15 @@
     return jnp.where(values >= 0.0, 1.0 - tail, tail), decay
 
 
-def point_kernel(mixer_ref, bias_ref, *refs):
-    field_refs, mixed_ref = refs[:PARTS], refs[PARTS]
-    rows, width = field_refs[0].shape
-    bias = jnp.concatenate([bias_ref[...]] * (width // LANES), axis=1)
-    for part, field_ref in enumerate(field_refs):
-        mixed = matmul(mixer_ref[...], field_ref[...]) + bias
-        mixed_ref[part * rows : (part + 1) * rows, :] = mixed.astype(mixed_ref.dtype)
-
-
-def point(fields, parts, mixer, bias, dtype, name):
-    rows = mixer.shape[0]
-    tiles = [pl.BlockSpec((rows, WIDTH), lambda n, part=part: (part, n)) for part in parts]
-    return pl.pallas_call(
-        point_kernel,
-        grid=(CELLS // WIDTH,),
-        in_specs=[
-            pl.BlockSpec((rows, rows), lambda n: (0, 0)),
-            pl.BlockSpec((rows, LANES), lambda n: (0, 0)),
-        ]
-        + tiles,
-        out_specs=pl.BlockSpec((PARTS * rows, WIDTH), lambda n: (0, n)),
-        out_shape=jax.ShapeDtypeStruct((PARTS * rows, CELLS), dtype),
-        compiler_params=vmem_params(60),
-        cost_estimate=pl.CostEstimate(
-            flops=2 * PARTS * rows * CELLS * rows, bytes_accessed=12 << 20, transcendentals=0
-        ),
-        name=name,
-    )(mixer, bias, *fields)
-
-
 def middle_kernel(
     xl,
     tl,
     packed_ref,
     field_ref,
     cotangent_ref,
-    mixed_ref,
     table_ref,
+    mixer_ref,
+    bias_ref,
     sums_in_ref,
     _,
     output_ref,
@@ -409,17 +377,22 @@
         modes[...] = wide[...].reshape(rows, KQ).astype(BF16)
         total[...] = jnp.zeros_like(total)
 
+    blocks = table_ref.shape[0]
+
     def build(at):
-        return matmul(modes[...], table_ref[0, :, at])
+        block, first = divmod(at.start, WIDTH)
+        spatial = matmul(modes[...], table_ref[block, :, first : first + tile])
+        return spatial + matmul(mixer_ref[...], field_ref[:, at])
 
     def pointwise(pre, at):
         for first in range(0, rows, chunk):
             part = slice(first, first + chunk)
-            values = pre[part, :] + mixed_ref[part, at]
+            values = pre[part, :] + jnp.concatenate([bias_ref[part, :]] * (tile // LANES), axis=1)
             integral, decay = normal_parts(values)
             output_ref[part, at] = (values * integral).astype(BF16)
             slope = integral + (values * DENSITY) * decay
-            grad_ref[part, at] = (cotangent_ref[part, at].astype(F32) * slope).astype(BF16)
+            grad = (cotangent_ref[part, at].astype(F32) * slope).astype(BF16)
+            grad_ref[at.start // WIDTH, part, at.start % WIDTH : at.start % WIDTH + tile] = grad
 
     tiles = [slice(first, first + tile) for first in range(0, width, tile)]
     ready = build(tiles[0])
@@ -428,10 +401,10 @@
         if index + 1 < len(tiles):
             ready = build(tiles[index + 1])
         pointwise(pre, at)
-    passing = jnp.concatenate(
-        [table_ref[0], field_ref[...], jnp.ones((ones, width), BF16)], axis=0
-    )
-    total[...] += matmul_turned(passing, grad_ref[...])
+    passing = jnp.concatenate([table_ref[at] for at in range(blocks)], axis=1)
+    passing = jnp.concatenate([passing, field_ref[...], jnp.ones((ones, width), BF16)], axis=0)
+    grads = jnp.concatenate([grad_ref[at] for at in range(blocks)], axis=1)
+    total[...] += matmul_turned(passing, grads)
 
     @pl.when(step == pl.num_programs(0) - 1)
     def _():
@@ -457,43 +430,44 @@
         sums_ref[...] = sums_in_ref[...] + jnp.where(lane == CHANS, own_bias, sums)
 
 
-def middle(packed, field, cotangent, mixed, table, sums, output, part, xl, tl):
+def middle(packed, field, cotangent, table, mixer, bias, sums, output, part, xl, tl):
     rows = xl * tl * CHANS
-    width = WIDTH
-    chunks = CELLS // width
+    per = 2
+    chunks = CELLS // WIDTH
     whole = lambda *shape: pl.BlockSpec(shape, lambda n: (0,) * len(shape))
-    tile = pl.BlockSpec((rows, width), lambda n: (part, n))
+    tile = pl.BlockSpec((rows, per * WIDTH), lambda n: (part, n))
     kernel = functools.partial(middle_kernel, xl, tl)
-    operands = (packed, field, cotangent, mixed, table, sums)
+    operands = (packed, field, cotangent, table, mixer, bias, sums)
     specs = [
         whole(*packed.shape),
         tile,
         tile,
-        tile,
-        pl.BlockSpec((1, KQ, width), lambda n: (n, 0, 0)),
+        pl.BlockSpec((per, KQ, WIDTH), lambda n: (n, 0, 0)),
+        whole(rows, rows),
+        whole(rows, LANES),
         whole(CHANS, LANES),
     ]
     aliases = {}
     if output is None:
         inner = kernel
-        kernel = lambda *refs: inner(*refs[:6], None, *refs[6:])
+        kernel = lambda *refs: inner(*refs[:7], None, *refs[7:])
     else:
         aliases = {len(operands): 0}
         operands += (output,)
         specs.append(pl.BlockSpec(memory_space=pltpu.HBM))
     return pl.pallas_call(
         kernel,
-        grid=(chunks,),
+        grid=(chunks // per,),
         in_specs=specs,
         out_specs=[
             tile,
-            pl.BlockSpec((rows, width), lambda n: (0, n)),
+            pl.BlockSpec((per, rows, WIDTH), lambda n: (n, 0, 0)),
             pl.BlockSpec(memory_space=pl.ANY),
             whole(CHANS, LANES),
         ],
         out_shape=(
             jax.ShapeDtypeStruct(field.shape, BF16),
-            jax.ShapeDtypeStruct((rows, CELLS), BF16),
+            jax.ShapeDtypeStruct((chunks, rows, WIDTH), BF16),
             jax.ShapeDtypeStruct(packed.shape, BF16),
             jax.ShapeDtypeStruct((CHANS, LANES), F32),
         ),
@@ -513,8 +487,10 @@
     )(*operands)
 
 
-def last_kernel(xl, tl, packed_ref, table_ref, mixed_ref, field_ref, *scratch):
-    packed, wide, modes, table, mixed, field, packed_sem, table_sems, mixed_sems, field_sems = (
+def last_kernel(xl, tl, mixer_ref, packed_ref, table_ref, *refs):
+    grad_refs, field_ref = refs[:PARTS], refs[PARTS]
+    scratch = refs[PARTS + 1 :]
+    packed, wide, modes, table, grads, field, packed_sem, table_sems, grad_sems, field_sems = (
         scratch
     )
     chunks = table.shape[0]
@@ -522,12 +498,13 @@
     fetches, sends = [], []
     for at in range(chunks):
         lanes = slice(at * WIDTH, (at + 1) * WIDTH)
-        fetches.append(
-            (
-                pltpu.make_async_copy(table_ref.at[at], table.at[at], table_sems.at[at]),
-                pltpu.make_async_copy(mixed_ref.at[:, lanes], mixed.at[at], mixed_sems.at[at]),
+        fetches.append([pltpu.make_async_copy(table_ref.at[at], table.at[at], table_sems.at[at])])
+        for part, grad_ref in enumerate(grad_refs):
+            fetches[at].append(
+                pltpu.make_async_copy(
+                    grad_ref.at[at], grads.at[at, part], grad_sems.at[at, part]
+                )
             )
-        )
         sends.append(
             pltpu.make_async_copy(field.at[at], field_ref.at[:, lanes], field_sems.at[at])
         )
@@ -548,30 +525,39 @@
             fetch.wait()
         if at + ahead < chunks:
             start(at + ahead)
-        field[at] = (matmul(modes[...], table[at]) + mixed[at].astype(F32)).astype(BF16)
+        point = [matmul(mixer_ref[...], grads[at, part]) for part in range(PARTS)]
+        field[at] = (
+            matmul(modes[...], table[at]) + jnp.concatenate(point, axis=0)
+        ).astype(BF16)
         sends[at].start()
     for send in sends:
         send.wait()
 
 
-def last(packed, mixed, table, xl, tl):
+def last(packed, grads, table, mixer, xl, tl):
     rows = xl * tl * CHANS
+    part = rows // PARTS
     chunks = CELLS // WIDTH
+    apart = pl.BlockSpec(memory_space=pltpu.HBM)
     return pl.pallas_call(
         functools.partial(last_kernel, xl, tl),
-        in_specs=[pl.BlockSpec(memory_space=pl.ANY)] + [pl.BlockSpec(memory_space=pltpu.HBM)] * 2,
-        out_specs=pl.BlockSpec(memory_space=pltpu.HBM),
+        in_specs=[
+            pl.BlockSpec(memory_space=pltpu.VMEM),
+            pl.BlockSpec(memory_space=pl.ANY),
+        ]
+        + [apart] * (1 + PARTS),
+        out_specs=apart,
         out_shape=jax.ShapeDtypeStruct((rows, CELLS), BF16),
         scratch_shapes=[
             pltpu.VMEM(packed.shape, BF16),
             pltpu.VMEM((xl, tl, CHANS, KQ), F32),
             pltpu.VMEM((rows, KQ), BF16),
             pltpu.VMEM((chunks, KQ, WIDTH), BF16),
-            pltpu.VMEM((chunks, rows, WIDTH), BF16),
+            pltpu.VMEM((chunks, PARTS, part, WIDTH), BF16),
             pltpu.VMEM((chunks, rows, WIDTH), BF16),
             pltpu.SemaphoreType.DMA,
             pltpu.SemaphoreType.DMA((chunks,)),
-            pltpu.SemaphoreType.DMA((chunks,)),
+            pltpu.SemaphoreType.DMA((chunks, PARTS)),
             pltpu.SemaphoreType.DMA((chunks,)),
         ],
         compiler_params=vmem_params(60),
@@ -579,16 +565,15 @@
             flops=2 * rows * CELLS * KQ, bytes_accessed=18 << 20, transcendentals=0
         ),
         name="last",
-    )(packed, table, mixed)
+    )(mixer, packed, table, *grads)
 
 
 def swap(blocks):
     return lax.all_to_all(blocks, ("gx", "ta"), split_axis=0, concat_axis=0, tiled=True)
 
 
-def sum_everywhere(values, devices):
-    step = 1
-    while step < devices:
+def sum_pairs(values, devices, step, end):
+    while step < end:
         pairs = [(at, at ^ step) for at in range(devices)]
         values = values + lax.ppermute(values, ("gx", "ta"), pairs)
         step *= 2
@@ -644,28 +629,25 @@
 
     spread_in = swap(analyse(field, table, xl_all, tl, devices)).reshape(whole_shape)
     spectrum, *mixed = mix(
-        [spread_in], packed_weight, sums, (x_in[0], t_in, x_out[1], t_out), False
-    )
-    halves = range(PARTS)
-    mixed_field = point([field] * PARTS, halves, mixer, bias, F32, "point")
+        [spread_in], packed_weight, (mixer, mixer_back, bias), (x_in[0], t_in, x_out[1], t_out), False
+    )
     output = None
     grads, spread_grad = [], []
     for part in range(PARTS):
         returned = swap(mixed[part].reshape(devices, xl * CHANS, LANES))
         output, grad, sent, sums = middle(
-            returned, field, cot, mixed_field, table, sums, output, part, xl, tl
+            returned, field, cot, table, mixer, bias, sums, output, part, xl, tl
         )
         grads.append(grad)
         spread_grad.append(swap(sent).reshape(part_shape))
-    summed = sum_everywhere(sums, devices)
+    partly = sum_pairs(sums, devices, 1, 8)
     grad_modes, mixed_back = mix(
-        spread_grad, packed_weight, summed, (x_in[1], t_in, x_out[0], t_out), True
+        spread_grad, packed_weight, (partly,), (x_in[1], t_in, x_out[0], t_out), True
     )
     grad_back = swap(mixed_back.reshape(devices, xl_all * CHANS, LANES))
     grad_spec = outer(spectrum, grad_modes, own)
-    mixed_grad = point(grads, [0] * PARTS, mixer_back, jnp.zeros_like(bias), BF16, "point_back")
-    grad_field = last(grad_back, mixed_grad, table, xl_all, tl)
-    summed = summed * norm_scale
+    grad_field = last(grad_back, grads, table, mixer_back, xl_all, tl)
+    summed = sum_pairs(partly, devices, 8, devices) * norm_scale
     return (
         output.reshape(features.shape),
         grad_field.reshape(features.shape),

time: 200 us -> 193 us (0.965)
  Pallas kernels: 103 us -> 84.4 us
  waiting for transfers between devices: 31.4 us -> 44 us
    pallas_call x6 -> x4, Pallas kernels: 63.8 us -> 44.7 us  [the longest x2 33.5 us: middle(): pl.pallas_call(kernel, grid=(chunks // per,), in_specs=specs, out_specs=[...]
    ppermute x5, waiting for transfers between devices: 8.96 us -> 24.8 us  [sum_pairs(): values = values + lax.ppermute(values, ('gx', 'ta'), pairs)]
    all_to_all x5, waiting for transfers between devices: 22.5 us -> 19.2 us  [swap(): lax.all_to_all(blocks, ('gx', 'ta'), split_axis=0, concat_axis=0, tiled=T...]
    all_to_all x5, starting transfers between devices: 27.9 us -> 25.1 us  [swap(): lax.all_to_all(blocks, ('gx', 'ta'), split_axis=0, concat_axis=0, tiled=T...]
    ppermute x5, starting transfers between devices: 7.81 us -> 10.3 us  [sum_pairs(): values = values + lax.ppermute(values, ('gx', 'ta'), pairs)]
    pallas_call x1, Pallas kernels: 10.4 us -> 12.6 us  [last(): pl.pallas_call(functools.partial(last_kernel, xl, tl), in_specs=[pl.Block...]
  transfers between devices with their start and end apart: 10 -> 10, of which waited for: 7 -> 7; matrix products, arithmetic and copies ran while one was open for 3% -> 3% of each run, Pallas kernels for 36% -> 27%
where the time goes in v6:
time: 193 us; the launch traced here: 192 us
  Pallas kernels  84.4 us (44%)
  waiting for transfers between devices  44 us (23%)
  starting transfers between devices  35.4 us (18%)
  blocking collectives  19.3 us (10%)
  local copies, waits for them, and re-layouts  4.13 us (2%)
  matrix products  2.83 us (1%)
    pallas_call x2, Pallas kernels, middle(): pl.pallas_call(kernel, grid=(chunks // per,), in_specs=specs, out_specs=[...  33.5 us
    all_to_all x5, starting transfers between devices, swap(): lax.all_to_all(blocks, ('gx', 'ta'), split_axis=0, concat_axis=0, tiled=T...  25.1 us
    ppermute x5, waiting for transfers between devices, sum_pairs(): values = values + lax.ppermute(values, ('gx', 'ta'), pairs)  24.8 us
    all_to_all x1, blocking collectives, swap(): lax.all_to_all(blocks, ('gx', 'ta'), split_axis=0, concat_axis=0, tiled=T...  19.3 us
    all_to_all x5, waiting for transfers between devices, swap(): lax.all_to_all(blocks, ('gx', 'ta'), split_axis=0, concat_axis=0, tiled=T...  19.2 us
    pallas_call x1, Pallas kernels, last(): pl.pallas_call(functools.partial(last_kernel, xl, tl), in_specs=[pl.Block...  12.6 us
    pallas_call x2, Pallas kernels, mix(): pl.pallas_call(functools.partial(mix_kernel, backward, len(after)), out_s...  11.1 us
    ppermute x5, starting transfers between devices, sum_pairs(): values = values + lax.ppermute(values, ('gx', 'ta'), pairs)  10.3 us
  transfers between devices with their start and end apart: 10, of which 7 were waited for; matrix products, arithmetic and copies ran while one was open for 3% of the time, Pallas kernels for 27%

profile of v6, /device:TPU:0, one launch (start us, length us, event | category | flops | bytes accessed | tf_op | source)
XLA Modules:
  0.0 192.4 jit_solution(14729685876593759571)
XLA Ops:
  0.6 8.4 %analyse.1 = bf16[32,128,128]{2,1,0:T(8,128)(2,1)} custom-call(bf16[512,4096]{1,0:T(8,128)(2,1)} %bitcast.20, bf16[8,1024,512]{2,1,0:T(8,128)(2,1)} %constant.24.clone.table_ref.refs_3_), custom_call_target="tpu_custom_call" | custom-call | flops 4294967296 | bytes 13631488 | tf_op jit(solution)/shard_map/analyse/pallas_call | solution.py:145
  9.0 7.3 %all-to-all-start = ((bf16[32,128,128]{2,1,0:T(8,128)(2,1)}), bf16[32,128,128]{2,1,0:T(8,128)(2,1)S(1)}, u32[]{:S(2)}, u32[]{:S(2)}) async-start(bf16[32,128,128]{2,1,0:T(8,128)(2,1)} %analyse.1), calls=%async_computation | async-start | bytes 2097152 | tf_op jit(solution)/shard_map/all_to_all | solution.py:572
  16.4 9.7 %pack_weight.1.weight_ref = bf16[32,64,512]{2,1,0:T(8,128)(2,1)} custom-call(f32[32,16,8,8,32]{4,3,2,1,0:T(8,128)} %weight_ref.1), custom_call_target="tpu_custom_call" | custom-call | flops 1048576 | bytes 20971520 | tf_op jit(solution)/shard_map/pack_weight/pallas_call | solution.py:178
  26.1 1.0 fusion.2.refs_2_.refs_5_.bias_ref
  27.1 0.9 fusion.refs_0_.refs_4_.mixer_ref
  28.0 0.9 fusion.1.refs_1_.mixer_ref
  29.0 13.6 %all-to-all-done = bf16[32,128,128]{2,1,0:T(8,128)(2,1)S(1)} async-done(((bf16[32,128,128]{2,1,0:T(8,128)(2,1)}), bf16[32,128,128]{2,1,0:T(8,128)(2,1)S(1)}, u32[]{:S(2)}, u32[]{:S(2)}) %all-to-all-start) | async-done | bytes 1048608 | tf_op jit(solution)/shard_map/all_to_all | solution.py:572
  42.6 1.0 copy-done.3
  43.6 5.1 %mix.1 = (f32[256,512]{1,0:T(8,128)}, bf16[8,4,64,128]{3,2,1,0:T(8,128)(2,1)}, bf16[8,4,64,128]{3,2,1,0:T(8,128)(2,1)}) custom-call(bf16[32,64,512]{2,1,0:T(8,128)(2,1)} %pack_weight.1.weight_ref, bf16[256,256]{1,0:T(8,128)(2,1)} %fusion.refs_0_.refs_4_.mixer_ref, bf16[256,256]{1,0:T(8,128)(2,1)} %fusion.1.refs_1_.mixer_ref, ...), custom_call_target="tpu_custom_call" | custom-call | flops 1073741824 | bytes 9437184 | tf_op jit(solution)/shard_map/mix/pallas_call | solution.py:282
  48.7 19.3 %all_to_all.30.refs_0_ = bf16[32,64,128]{2,1,0:T(8,128)(2,1)} all-to-all(bf16[32,64,128]{2,1,0:T(8,128)(2,1)} %bitcast.30), channel_id=1, replica_groups=mesh['gx'=8,'ta'=4] {'gx','ta'}, dimensions={0} | all-to-all | bytes 1048576 | tf_op jit(solution)/shard_map/all_to_all | solution.py:572
  68.0 3.1 %all-to-all-start.1 = ((bf16[32,64,128]{2,1,0:T(8,128)(2,1)}), bf16[32,64,128]{2,1,0:T(8,128)(2,1)S(1)}, u32[]{:S(2)}, u32[]{:S(2)}) async-start(bf16[32,64,128]{2,1,0:T(8,128)(2,1)} %bitcast.29), calls=%async_computation.1 | async-start | bytes 1048576 | tf_op jit(solution)/shard_map/all_to_all | solution.py:572
  71.7 16.8 %middle.2 = (bf16[512,4096]{1,0:T(8,128)(2,1)}, bf16[8,256,512]{2,1,0:T(8,128)(2,1)}, bf16[32,64,128]{2,1,0:T(8,128)(2,1)}, f32[8,128]{1,0:T(8,128)}) custom-call(bf16[32,64,128]{2,1,0:T(8,128)(2,1)} %all_to_all.30.refs_0_, bf16[512,4096]{1,0:T(8,128)(2,1)} %bitcast.21, bf16[512,4096]{1,0:T(8,128)(2,1)} %bitcast.23, ...), custom_call_target="tpu_custom_call" | custom-call | flops 5368709120 | bytes 18874368 | tf_op jit(solution)/shard_map/middle/pallas_call | solution.py:458
  88.5 6.0 %all-to-all-start.3 = ((bf16[32,64,128]{2,1,0:T(8,128)(2,1)}), bf16[32,64,128]{2,1,0:T(8,128)(2,1)S(1)}, u32[]{:S(2)}, u32[]{:S(2)}) async-start(bf16[32,64,128]{2,1,0:T(8,128)(2,1)} %get-tuple-element.24), calls=%async_computation.3 | async-start | bytes 1048576 | tf_op jit(solution)/shard_map/all_to_all | solution.py:572
  94.5 16.8 %middle.3 = (bf16[512,4096]{1,0:T(8,128)(2,1)}, bf16[8,256,512]{2,1,0:T(8,128)(2,1)}, bf16[32,64,128]{2,1,0:T(8,128)(2,1)}, f32[8,128]{1,0:T(8,128)}) custom-call(bf16[32,64,128]{2,1,0:T(8,128)(2,1)} %copy-done.6, bf16[512,4096]{1,0:T(8,128)(2,1)} %bitcast.22, bf16[512,4096]{1,0:T(8,128)(2,1)} %bitcast.24, ...), custom_call_target="tpu_custom_call", output_to_operand_aliasing={{0}: (7, {})} | custom-call | flops 5368709120 | bytes 18874368 | tf_op jit(solution)/shard_map/middle/pallas_call | solution.py:458
  111.3 5.7 %all-to-all-start.4 = ((bf16[32,64,128]{2,1,0:T(8,128)(2,1)}), bf16[32,64,128]{2,1,0:T(8,128)(2,1)S(1)}, u32[]{:S(2)}, u32[]{:S(2)}) async-start(bf16[32,64,128]{2,1,0:T(8,128)(2,1)} %get-tuple-element.25), calls=%async_computation.4 | async-start | bytes 1048576 | tf_op jit(solution)/shard_map/all_to_all | solution.py:572
  117.3 1.1 collective-permute-done
  119.1 1.8 collective-permute-start.1
  120.9 1.9 collective-permute-done.1
  122.8 2.0 %collective-permute-start.2 = (f32[8,128]{1,0:T(8,128)S(1)}, f32[8,128]{1,0:T(8,128)S(1)}, u32[]{:S(2)}, u32[]{:S(2)}) collective-permute-start(f32[8,128]{1,0:T(8,128)S(1)} %add.16), channel_id=1, source_target_pairs={{0,4},{1,5},{2,6},{3,7},{4,0},{5,1},{6,2},{7,3},{8,12},{9,13},{10,... | collective-permute-start | bytes 12296 | tf_op jit(solution)/shard_map/ppermute | solution.py:578
  124.7 1.7 collective-permute-done.2
  127.0 5.6 %all-to-all-done.4 = bf16[32,64,128]{2,1,0:T(8,128)(2,1)S(1)} async-done(((bf16[32,64,128]{2,1,0:T(8,128)(2,1)}), bf16[32,64,128]{2,1,0:T(8,128)(2,1)S(1)}, u32[]{:S(2)}, u32[]{:S(2)}) %all-to-all-start.4) | async-done | bytes 524320 | tf_op jit(solution)/shard_map/all_to_all | solution.py:572
  132.5 0.8 copy-done.5
  133.4 6.0 %mix_back.1 = (f32[256,512]{1,0:T(8,128)}, bf16[8,4,128,128]{3,2,1,0:T(8,128)(2,1)}) custom-call(bf16[32,64,512]{2,1,0:T(8,128)(2,1)} %pack_weight.1.weight_ref, f32[8,128]{1,0:T(8,128)} %add.17.refs_0_, bf16[2,256,512]{2,1,0:T(8,128)(2,1)} %constant.26.clone.refs_1_, bf16[512,512]{1,0:T(8,128)(2,1)} %constant.29.clone.refs_4_.refs_2_, ...), custom_call_target="tpu_custom_call" | custom-call | flops 1073741824 | bytes 9437184 | tf_op jit(solution)/shard_map/mix_back/pallas_call | solution.py:282
  139.4 3.1 %all-to-all-start.5 = ((bf16[32,128,128]{2,1,0:T(8,128)(2,1)}), bf16[32,128,128]{2,1,0:T(8,128)(2,1)S(1)}, u32[]{:S(2)}, u32[]{:S(2)}) async-start(bf16[32,128,128]{2,1,0:T(8,128)(2,1)} %bitcast.28), calls=%async_computation.5 | async-start | bytes 2097152 | tf_op jit(solution)/shard_map/all_to_all | solution.py:572
  142.4 1.8 collective-permute-start.3
  144.3 15.9 %collective-permute-done.3 = f32[8,128]{1,0:T(8,128)S(1)} collective-permute-done((f32[8,128]{1,0:T(8,128)S(1)}, f32[8,128]{1,0:T(8,128)S(1)}, u32[]{:S(2)}, u32[]{:S(2)}) %collective-permute-start.3) | collective-permute-done | bytes 4128 | tf_op jit(solution)/shard_map/ppermute | solution.py:578
  160.2 4.4 %collective-permute-start.4 = (f32[8,128]{1,0:T(8,128)S(1)}, f32[8,128]{1,0:T(8,128)S(1)}, u32[]{:S(2)}, u32[]{:S(2)}) collective-permute-start(f32[8,128]{1,0:T(8,128)S(1)} %add.18), channel_id=1, source_target_pairs={{0,16},{1,17},{2,18},{3,19},{4,20},{5,21},{6,22},{7,23},{8,24},{9,... | collective-permute-start | bytes 12296 | tf_op jit(solution)/shard_map/ppermute | solution.py:578
  164.7 4.2 %collective-permute-done.4 = f32[8,128]{1,0:T(8,128)S(1)} collective-permute-done((f32[8,128]{1,0:T(8,128)S(1)}, f32[8,128]{1,0:T(8,128)S(1)}, u32[]{:S(2)}, u32[]{:S(2)}) %collective-permute-start.4) | collective-permute-done | bytes 4128 | tf_op jit(solution)/shard_map/ppermute | solution.py:578
  168.9 0.7 slice_reduce_fusion
  169.6 9.1 %outer.1 = f32[32,16,8,8,32]{4,3,2,1,0:T(8,128)} custom-call(f32[256,512]{1,0:T(8,128)} %get-tuple-element.29.spectrum_ref, f32[256,512]{1,0:T(8,128)} %get-tuple-element.30.grad_ref), custom_call_target="tpu_custom_call" | custom-call | flops 1048576 | bytes 17825792 | tf_op jit(solution)/shard_map/outer/pallas_call | solution.py:322
  178.6 1.0 copy-done.2
  179.6 12.6 %last.1 = bf16[512,4096]{1,0:T(8,128)(2,1)} custom-call(bf16[256,256]{1,0:T(8,128)(2,1)} %fusion.1.refs_1_.mixer_ref, bf16[32,128,128]{2,1,0:T(8,128)(2,1)} %copy-done.2, bf16[8,1024,512]{2,1,0:T(8,128)(2,1)} %constant.24.clone.table_ref.refs_3_, bf16[8,256,512]{2,1,0:T(8,128)(2,1)} %get-tuple-element.27.refs_0_, bf16[8,256,512]{2,1,0:T(8,128)(2,1)} %get-tuple-element.28.refs_1_), custom_call_target="tpu_custom_call" | custom-call | flops 4294967296 | bytes 18874368 | tf_op jit(solution)/shard_map/last/pallas_call | solution.py:542
  (33 shorter events, 2.3 us)
Async XLA Ops:
  0.6 26.5 %copy-start = (bf16[8,8]{1,0:T(8,128)(2,1)S(1)}, bf16[8,8]{1,0:T(8,128)(2,1)}, u32[]{:S(2)}) copy-start(bf16[8,8]{1,0:T(8,128)(2,1)} %param.18) | copy-start | bytes 388
  9.0 33.5 %all-to-all-start = ((bf16[32,128,128]{2,1,0:T(8,128)(2,1)}), bf16[32,128,128]{2,1,0:T(8,128)(2,1)S(1)}, u32[]{:S(2)}, u32[]{:S(2)}) async-start(bf16[32,128,128]{2,1,0:T(8,128)(2,1)} %analyse.1), calls=%async_computation | async-start | bytes 2097152 | tf_op jit(solution)/shard_map/all_to_all | solution.py:572
  16.4 9.8 %copy-start.9 = (f32[256,8]{1,0:T(8,128)S(1)}, f32[256,8]{1,0:T(8,128)}, u32[]{:S(2)}) copy-start(f32[256,8]{1,0:T(8,128)} %constant.33.clone) | copy-start | bytes 24580
  16.4 9.8 %copy-start.12 = (f32[8]{0:T(128)S(1)}, f32[8]{0:T(128)}, u32[]{:S(2)}) copy-start(f32[8]{0:T(128)} %param.19) | copy-start | bytes 100
  16.4 10.7 %copy-start.7 = (f32[256,256]{1,0:T(8,128)S(1)}, f32[256,256]{1,0:T(8,128)}, u32[]{:S(2)}) copy-start(f32[256,256]{1,0:T(8,128)} %constant.32.clone) | copy-start | bytes 786436
  16.4 10.7 %copy-start.8 = (bf16[256,8]{1,0:T(8,128)(2,1)S(1)}, bf16[256,8]{1,0:T(8,128)(2,1)}, u32[]{:S(2)}) copy-start(bf16[256,8]{1,0:T(8,128)(2,1)} %constant.31.clone) | copy-start | bytes 12292
  42.6 1.0 copy-start.3
  68.0 20.5 %all-to-all-start.1 = ((bf16[32,64,128]{2,1,0:T(8,128)(2,1)}), bf16[32,64,128]{2,1,0:T(8,128)(2,1)S(1)}, u32[]{:S(2)}, u32[]{:S(2)}) async-start(bf16[32,64,128]{2,1,0:T(8,128)(2,1)} %bitcast.29), calls=%async_computation.1 | async-start | bytes 1048576 | tf_op jit(solution)/shard_map/all_to_all | solution.py:572
  88.5 6.0 %copy-start.6 = (bf16[32,64,128]{2,1,0:T(8,128)(2,1)}, bf16[32,64,128]{2,1,0:T(8,128)(2,1)S(1)}, u32[]{:S(2)}) copy-start(bf16[32,64,128]{2,1,0:T(8,128)(2,1)S(1)} %all-to-all-done.1.packed_ref) | copy-start | bytes 1572868
  88.5 22.8 %all-to-all-start.3 = ((bf16[32,64,128]{2,1,0:T(8,128)(2,1)}), bf16[32,64,128]{2,1,0:T(8,128)(2,1)S(1)}, u32[]{:S(2)}, u32[]{:S(2)}) async-start(bf16[32,64,128]{2,1,0:T(8,128)(2,1)} %get-tuple-element.24), calls=%async_computation.3 | async-start | bytes 1048576 | tf_op jit(solution)/shard_map/all_to_all | solution.py:572
  111.3 21.2 %copy-start.4 = (bf16[32,64,128]{2,1,0:T(8,128)(2,1)}, bf16[32,64,128]{2,1,0:T(8,128)(2,1)S(1)}, u32[]{:S(2)}) copy-start(bf16[32,64,128]{2,1,0:T(8,128)(2,1)S(1)} %all-to-all-done.3) | copy-start | bytes 1572868
  111.3 21.2 %all-to-all-start.4 = ((bf16[32,64,128]{2,1,0:T(8,128)(2,1)}), bf16[32,64,128]{2,1,0:T(8,128)(2,1)S(1)}, u32[]{:S(2)}, u32[]{:S(2)}) async-start(bf16[32,64,128]{2,1,0:T(8,128)(2,1)} %get-tuple-element.25), calls=%async_computation.4 | async-start | bytes 1048576 | tf_op jit(solution)/shard_map/all_to_all | solution.py:572
  117.0 1.4 collective-permute-start
  119.1 3.6 %collective-permute-start.1 = (f32[8,128]{1,0:T(8,128)S(1)}, f32[8,128]{1,0:T(8,128)S(1)}, u32[]{:S(2)}, u32[]{:S(2)}) collective-permute-start(f32[8,128]{1,0:T(8,128)S(1)} %add.15), channel_id=1, source_target_pairs={{0,2},{1,3},{2,0},{3,1},{4,6},{5,7},{6,4},{7,5},{8,10},{9,11},{10,... | collective-permute-start | bytes 12296 | tf_op jit(solution)/shard_map/ppermute | solution.py:578
  122.8 3.6 %collective-permute-start.2 = (f32[8,128]{1,0:T(8,128)S(1)}, f32[8,128]{1,0:T(8,128)S(1)}, u32[]{:S(2)}, u32[]{:S(2)}) collective-permute-start(f32[8,128]{1,0:T(8,128)S(1)} %add.16), channel_id=1, source_target_pairs={{0,4},{1,5},{2,6},{3,7},{4,0},{5,1},{6,2},{7,3},{8,12},{9,13},{10,... | collective-permute-start | bytes 12296 | tf_op jit(solution)/shard_map/ppermute | solution.py:578
  127.0 15.5 %copy-start.10 = (f32[8,128]{1,0:T(8,128)S(1)}, f32[8,128]{1,0:T(8,128)}, u32[]{:S(2)}) copy-start(f32[8,128]{1,0:T(8,128)} %add.17.refs_0_) | copy-start | bytes 12292
  132.5 0.8 copy-start.5
  139.4 39.3 %all-to-all-start.5 = ((bf16[32,128,128]{2,1,0:T(8,128)(2,1)}), bf16[32,128,128]{2,1,0:T(8,128)(2,1)S(1)}, u32[]{:S(2)}, u32[]{:S(2)}) async-start(bf16[32,128,128]{2,1,0:T(8,128)(2,1)} %bitcast.28), calls=%async_computation.5 | async-start | bytes 2097152 | tf_op jit(solution)/shard_map/all_to_all | solution.py:572
  142.4 17.8 %collective-permute-start.3 = (f32[8,128]{1,0:T(8,128)S(1)}, f32[8,128]{1,0:T(8,128)S(1)}, u32[]{:S(2)}, u32[]{:S(2)}) collective-permute-start(f32[8,128]{1,0:T(8,128)S(1)} %copy-done.10), channel_id=1, source_target_pairs={{0,8},{1,9},{2,10},{3,11},{4,12},{5,13},{6,14},{7,15},{8,0},{9,1},... | collective-permute-start | bytes 12296 | tf_op jit(solution)/shard_map/ppermute | solution.py:578
  160.2 8.6 %collective-permute-start.4 = (f32[8,128]{1,0:T(8,128)S(1)}, f32[8,128]{1,0:T(8,128)S(1)}, u32[]{:S(2)}, u32[]{:S(2)}) collective-permute-start(f32[8,128]{1,0:T(8,128)S(1)} %add.18), channel_id=1, source_target_pairs={{0,16},{1,17},{2,18},{3,19},{4,20},{5,21},{6,22},{7,23},{8,24},{9,... | collective-permute-start | bytes 12296 | tf_op jit(solution)/shard_map/ppermute | solution.py:578
  168.9 9.8 %copy-start.11 = (f32[8,128]{1,0:T(8,128)}, f32[8,128]{1,0:T(8,128)S(1)}, u32[]{:S(2)}) copy-start(f32[8,128]{1,0:T(8,128)S(1)} %add_multiply_fusion) | copy-start | bytes 12292
  178.6 1.0 copy-start.2
  179.6 12.6 %copy-start.1 = (bf16[8,8]{1,0:T(8,128)(2,1)S(1)}, bf16[8,8]{1,0:T(8,128)(2,1)}, u32[]{:S(2)}) copy-start(bf16[8,8]{1,0:T(8,128)(2,1)} %param.18) | copy-start | bytes 388

commit v7 on v6

--- a/solution.py
+++ b/solution.py
@@ -198,13 +198,28 @@
     return matmul(total.astype(BF16), t_table_ref[...])
 
 
-def from_modes(modes, x_table_ref, t_table_ref, held_ref):
+def from_modes(modes, x_table_ref, t_table_ref, held_ref, back_refs, sems):
     parts, gx, ta, rows, _ = held_ref.shape
     half = matmul(modes.astype(BF16), t_table_ref[...]).astype(BF16)
+    pieces = sems.shape[1]
+    per = gx // pieces
+    sends = []
     for part in range(parts):
-        full = matmul(x_table_ref[part], half).astype(BF16)
-        for at in range(ta):
-            held_ref[part, :, at] = full[:, at * LANES : (at + 1) * LANES].reshape(gx, rows, LANES)
+        for piece in range(pieces):
+            table = x_table_ref[part, piece * per * rows : (piece + 1) * per * rows, :]
+            full = matmul(table, half).astype(BF16)
+            owners = slice(piece * per, (piece + 1) * per)
+            for at in range(ta):
+                held_ref[part, owners, at] = full[:, at * LANES : (at + 1) * LANES].reshape(
+                    per, rows, LANES
+                )
+            send = pltpu.make_async_copy(
+                held_ref.at[part, owners], back_refs[part].at[owners], sems.at[part, piece]
+            )
+            send.start()
+            sends.append(send)
+    for send in sends:
+        send.wait()
 
 
 def mix_kernel(
@@ -260,15 +275,7 @@
             mixed[rows, :] = total
     tables[2].wait()
     tables[3].wait()
-    from_modes(mixed[...], x_out, t_out, held)
-    sends = [
-        pltpu.make_async_copy(held.at[part], ref, back_sems.at[part])
-        for part, ref in enumerate(back_refs)
-    ]
-    for send in sends:
-        send.start()
-    for send in sends:
-        send.wait()
+    from_modes(mixed[...], x_out, t_out, held, back_refs, back_sems)
     keep.wait()
 
 
@@ -294,7 +301,7 @@
             pltpu.SemaphoreType.DMA((5,)),
             pltpu.SemaphoreType.DMA((8,)),
             pltpu.SemaphoreType.DMA((len(spreads),)),
-            pltpu.SemaphoreType.DMA((outs,)),
+            pltpu.SemaphoreType.DMA((outs, 4 // outs)),
         ],
         compiler_params=vmem_params(60),
         cost_estimate=pl.CostEstimate(flops=1 << 30, bytes_accessed=9 << 20, transcendentals=0),
@@ -342,6 +349,33 @@
     series = series * t + 0.319381530 * DENSITY
     tail = decay * (series * t)
     return jnp.where(values >= 0.0, 1.0 - tail, tail), decay
+
+
+def point_kernel(mixer_ref, *refs):
+    grad_refs, mixed_ref = refs[:PARTS], refs[PARTS]
+    rows = mixer_ref.shape[0]
+    for at in range(mixed_ref.shape[0]):
+        for part, grad_ref in enumerate(grad_refs):
+            mixed = matmul(mixer_ref[...], grad_ref[at])
+            mixed_ref[at, part * rows : (part + 1) * rows, :] = mixed.astype(BF16)
+
+
+def point(grads, mixer):
+    chunks, rows, _ = grads[0].shape
+    per = 2
+    return pl.pallas_call(
+        point_kernel,
+        grid=(chunks // per,),
+        in_specs=[pl.BlockSpec((rows, rows), lambda n: (0, 0))]
+        + [pl.BlockSpec((per, rows, WIDTH), lambda n: (n, 0, 0))] * PARTS,
+        out_specs=pl.BlockSpec((per, PARTS * rows, WIDTH), lambda n: (n, 0, 0)),
+        out_shape=jax.ShapeDtypeStruct((chunks, PARTS * rows, WIDTH), BF16),
+        compiler_params=vmem_params(60),
+        cost_estimate=pl.CostEstimate(
+            flops=2 * PARTS * rows * CELLS * rows, bytes_accessed=8 << 20, transcendentals=0
+        ),
+        name="point",
+    )(mixer, *grads)
 
 
 def middle_kernel(
@@ -427,7 +461,8 @@
             folded, select, precision=lax.Precision.HIGHEST, preferred_element_type=F32
         )
         lane = lax.broadcasted_iota(jnp.int32, (CHANS, LANES), 1)
-        sums_ref[...] = sums_in_ref[...] + jnp.where(lane == CHANS, own_bias, sums)
+        sums = jnp.where(lane == CHANS, own_bias, sums)
+        sums_ref[...] = sums if sums_in_ref is None else sums_in_ref[...] + sums
 
 
 def middle(packed, field, cotangent, table, mixer, bias, sums, output, part, xl, tl):
@@ -437,7 +472,7 @@
     whole = lambda *shape: pl.BlockSpec(shape, lambda n: (0,) * len(shape))
     tile = pl.BlockSpec((rows, per * WIDTH), lambda n: (part, n))
     kernel = functools.partial(middle_kernel, xl, tl)
-    operands = (packed, field, cotangent, table, mixer, bias, sums)
+    operands = (packed, field, cotangent, table, mixer, bias)
     specs = [
         whole(*packed.shape),
         tile,
@@ -445,16 +480,15 @@
         pl.BlockSpec((per, KQ, WIDTH), lambda n: (n, 0, 0)),
         whole(rows, rows),
         whole(rows, LANES),
-        whole(CHANS, LANES),
     ]
     aliases = {}
     if output is None:
         inner = kernel
-        kernel = lambda *refs: inner(*refs[:7], None, *refs[7:])
+        kernel = lambda *refs: inner(*refs[:6], None, None, *refs[6:])
     else:
-        aliases = {len(operands): 0}
-        operands += (output,)
-        specs.append(pl.BlockSpec(memory_space=pltpu.HBM))
+        operands += (sums, output)
+        aliases = {len(operands) - 1: 0}
+        specs += [whole(CHANS, LANES), pl.BlockSpec(memory_space=pltpu.HBM)]
     return pl.pallas_call(
         kernel,
         grid=(chunks // per,),
@@ -487,24 +521,19 @@
     )(*operands)
 
 
-def last_kernel(xl, tl, mixer_ref, packed_ref, table_ref, *refs):
-    grad_refs, field_ref = refs[:PARTS], refs[PARTS]
-    scratch = refs[PARTS + 1 :]
-    packed, wide, modes, table, grads, field, packed_sem, table_sems, grad_sems, field_sems = (
-        scratch
-    )
+def last_kernel(xl, tl, packed_ref, table_ref, mixed_ref, field_ref, *scratch):
+    wide, modes, table, mixed, field, table_sems, mixed_sems, field_sems = scratch
     chunks = table.shape[0]
     ahead = 4
     fetches, sends = [], []
     for at in range(chunks):
         lanes = slice(at * WIDTH, (at + 1) * WIDTH)
-        fetches.append([pltpu.make_async_copy(table_ref.at[at], table.at[at], table_sems.at[at])])
-        for part, grad_ref in enumerate(grad_refs):
-            fetches[at].append(
-                pltpu.make_async_copy(
-                    grad_ref.at[at], grads.at[at, part], grad_sems.at[at, part]
-                )
+        fetches.append(
+            (
+                pltpu.make_async_copy(table_ref.at[at], table.at[at], table_sems.at[at]),
+                pltpu.make_async_copy(mixed_ref.at[at], mixed.at[at], mixed_sems.at[at]),
             )
+        )
         sends.append(
             pltpu.make_async_copy(field.at[at], field_ref.at[:, lanes], field_sems.at[at])
         )
@@ -513,67 +542,55 @@
         for fetch in fetches[at]:
             fetch.start()
 
-    own = pltpu.make_async_copy(packed_ref, packed, packed_sem)
-    own.start()
     for at in range(ahead):
         start(at)
-    own.wait()
-    unpack_modes(packed, wide, xl, tl)
+    unpack_modes(packed_ref, wide, xl, tl)
     modes[...] = wide[...].reshape(modes.shape).astype(BF16)
     for at in range(chunks):
         for fetch in fetches[at]:
             fetch.wait()
         if at + ahead < chunks:
             start(at + ahead)
-        point = [matmul(mixer_ref[...], grads[at, part]) for part in range(PARTS)]
-        field[at] = (
-            matmul(modes[...], table[at]) + jnp.concatenate(point, axis=0)
-        ).astype(BF16)
+        field[at] = (matmul(modes[...], table[at]) + mixed[at].astype(F32)).astype(BF16)
         sends[at].start()
     for send in sends:
         send.wait()
 
 
-def last(packed, grads, table, mixer, xl, tl):
+def last(packed, mixed, table, xl, tl):
     rows = xl * tl * CHANS
-    part = rows // PARTS
     chunks = CELLS // WIDTH
     apart = pl.BlockSpec(memory_space=pltpu.HBM)
     return pl.pallas_call(
         functools.partial(last_kernel, xl, tl),
-        in_specs=[
-            pl.BlockSpec(memory_space=pltpu.VMEM),
-            pl.BlockSpec(memory_space=pl.ANY),
-        ]
-        + [apart] * (1 + PARTS),
+        in_specs=[pl.BlockSpec(memory_space=pltpu.VMEM), apart, apart],
         out_specs=apart,
         out_shape=jax.ShapeDtypeStruct((rows, CELLS), BF16),
         scratch_shapes=[
-            pltpu.VMEM(packed.shape, BF16),
             pltpu.VMEM((xl, tl, CHANS, KQ), F32),
             pltpu.VMEM((rows, KQ), BF16),
             pltpu.VMEM((chunks, KQ, WIDTH), BF16),
-            pltpu.VMEM((chunks, PARTS, part, WIDTH), BF16),
             pltpu.VMEM((chunks, rows, WIDTH), BF16),
-            pltpu.SemaphoreType.DMA,
+            pltpu.VMEM((chunks, rows, WIDTH), BF16),
             pltpu.SemaphoreType.DMA((chunks,)),
-            pltpu.SemaphoreType.DMA((chunks, PARTS)),
+            pltpu.SemaphoreType.DMA((chunks,)),
             pltpu.SemaphoreType.DMA((chunks,)),
         ],
-        compiler_params=vmem_params(60),
+        compiler_params=vmem_params(44),
         cost_estimate=pl.CostEstimate(
             flops=2 * rows * CELLS * KQ, bytes_accessed=18 << 20, transcendentals=0
         ),
         name="last",
-    )(mixer, packed, table, *grads)
+    )(packed, table, mixed)
 
 
 def swap(blocks):
     return lax.all_to_all(blocks, ("gx", "ta"), split_axis=0, concat_axis=0, tiled=True)
 
 
-def sum_pairs(values, devices, step, end):
-    while step < end:
+def sum_everywhere(values, devices):
+    step = 1
+    while step < devices:
         pairs = [(at, at ^ step) for at in range(devices)]
         values = values + lax.ppermute(values, ("gx", "ta"), pairs)
         step *= 2
@@ -625,13 +642,12 @@
     part_shape = (gx, ta, xl * CHANS, LANES)
     whole_shape = (gx, ta, xl_all * CHANS, LANES)
     packed_weight = pack_weight(spec_weight)
-    sums = jnp.zeros((CHANS, LANES), F32)
 
     spread_in = swap(analyse(field, table, xl_all, tl, devices)).reshape(whole_shape)
     spectrum, *mixed = mix(
         [spread_in], packed_weight, (mixer, mixer_back, bias), (x_in[0], t_in, x_out[1], t_out), False
     )
-    output = None
+    output, sums = None, None
     grads, spread_grad = [], []
     for part in range(PARTS):
         returned = swap(mixed[part].reshape(devices, xl * CHANS, LANES))
@@ -640,14 +656,14 @@
         )
         grads.append(grad)
         spread_grad.append(swap(sent).reshape(part_shape))
-    partly = sum_pairs(sums, devices, 1, 8)
+    summed = sum_everywhere(sums, devices)
     grad_modes, mixed_back = mix(
-        spread_grad, packed_weight, (partly,), (x_in[1], t_in, x_out[0], t_out), True
+        spread_grad, packed_weight, (summed,), (x_in[1], t_in, x_out[0], t_out), True
     )
     grad_back = swap(mixed_back.reshape(devices, xl_all * CHANS, LANES))
     grad_spec = outer(spectrum, grad_modes, own)
-    grad_field = last(grad_back, grads, table, mixer_back, xl_all, tl)
-    summed = sum_pairs(partly, devices, 8, devices) * norm_scale
+    grad_field = last(grad_back, point(grads, mixer_back), table, xl_all, tl)
+    summed = summed * norm_scale
     return (
         output.reshape(features.shape),
         grad_field.reshape(features.shape),

time: 193 us -> 185 us (0.959)
  waiting for transfers between devices: 44 us -> 32.7 us
    ppermute x5, waiting for transfers between devices: 24.8 us -> 8.17 us  [sum_everywhere(): values = values + lax.ppermute(values, ('gx', 'ta'), pairs)]
    pallas_call x0 -> x1, Pallas kernels: none -> 5.52 us  [point(): pl.pallas_call(point_kernel, grid=(chunks // per,), in_specs=[pl.BlockSpe...]
    all_to_all x5, waiting for transfers between devices: 19.2 us -> 24.6 us  [swap(): lax.all_to_all(blocks, ('gx', 'ta'), split_axis=0, concat_axis=0, tiled=T...]
    pallas_call x1, Pallas kernels: 12.6 us -> 8.09 us  [last(): pl.pallas_call(functools.partial(last_kernel, xl, tl), in_specs=[pl.Block...]
    all_to_all x5, starting transfers between devices: 25.1 us -> 27.9 us  [swap(): lax.all_to_all(blocks, ('gx', 'ta'), split_axis=0, concat_axis=0, tiled=T...]
    unnamed x26 -> x24, local copies, waits for them, and re-layouts: 2.84 us -> 4.01 us
  transfers between devices with their start and end apart: 10 -> 10, of which waited for: 7 -> 7; matrix products, arithmetic and copies ran while one was open for 3% -> 3% of each run, Pallas kernels for 27% -> 32%
where the time goes in v7:
time: 185 us; the launch traced here: 183 us
  Pallas kernels  85.1 us (46%)
  starting transfers between devices  36.5 us (20%)
  waiting for transfers between devices  32.7 us (18%)
  blocking collectives  19.3 us (10%)
  local copies, waits for them, and re-layouts  4.7 us (3%)
  matrix products  2.84 us (2%)
    pallas_call x2, Pallas kernels, middle(): pl.pallas_call(kernel, grid=(chunks // per,), in_specs=specs, out_specs=[...  33.5 us
    all_to_all x5, starting transfers between devices, swap(): lax.all_to_all(blocks, ('gx', 'ta'), split_axis=0, concat_axis=0, tiled=T...  27.9 us
    all_to_all x5, waiting for transfers between devices, swap(): lax.all_to_all(blocks, ('gx', 'ta'), split_axis=0, concat_axis=0, tiled=T...  24.6 us
    all_to_all x1, blocking collectives, swap(): lax.all_to_all(blocks, ('gx', 'ta'), split_axis=0, concat_axis=0, tiled=T...  19.3 us
    pallas_call x2, Pallas kernels, mix(): pl.pallas_call(functools.partial(mix_kernel, backward, len(after)), out_s...  10.7 us
    pallas_call x1, Pallas kernels, pack_weight(): pl.pallas_call(weight_kernel, grid=(KX // per,), in_specs=[pl.BlockSpec((...  9.74 us
    pallas_call x1, Pallas kernels, outer(): pl.pallas_call(outer_kernel, grid=(KX // per,), in_specs=[pl.BlockSpec((p...  9.06 us
    ppermute x5, starting transfers between devices, sum_everywhere(): values = values + lax.ppermute(values, ('gx', 'ta'), pairs)  8.63 us
  transfers between devices with their start and end apart: 10, of which 7 were waited for; matrix products, arithmetic and copies ran while one was open for 3% of the time, Pallas kernels for 32%

profile of v7, /device:TPU:0, one launch (start us, length us, event | category | flops | bytes accessed | tf_op | source)
XLA Modules:
  0.0 183.4 jit_solution(5057843215138806548)
XLA Ops:
  0.6 8.4 %analyse.1 = bf16[32,128,128]{2,1,0:T(8,128)(2,1)} custom-call(bf16[512,4096]{1,0:T(8,128)(2,1)} %bitcast.20, bf16[8,1024,512]{2,1,0:T(8,128)(2,1)} %constant.22.clone.table_ref.refs_3_), custom_call_target="tpu_custom_call" | custom-call | flops 4294967296 | bytes 13631488 | tf_op jit(solution)/shard_map/analyse/pallas_call | solution.py:145
  9.0 7.3 %all-to-all-start = ((bf16[32,128,128]{2,1,0:T(8,128)(2,1)}), bf16[32,128,128]{2,1,0:T(8,128)(2,1)S(1)}, u32[]{:S(2)}, u32[]{:S(2)}) async-start(bf16[32,128,128]{2,1,0:T(8,128)(2,1)} %analyse.1), calls=%async_computation | async-start | bytes 2097152 | tf_op jit(solution)/shard_map/all_to_all | solution.py:588
  16.4 9.7 %pack_weight.1.weight_ref = bf16[32,64,512]{2,1,0:T(8,128)(2,1)} custom-call(f32[32,16,8,8,32]{4,3,2,1,0:T(8,128)} %weight_ref.1), custom_call_target="tpu_custom_call" | custom-call | flops 1048576 | bytes 20971520 | tf_op jit(solution)/shard_map/pack_weight/pallas_call | solution.py:178
  26.1 1.0 fusion.2.refs_2_.refs_5_.bias_ref
  27.1 0.9 fusion.refs_0_.refs_4_.mixer_ref
  28.1 0.9 fusion.1.refs_1_.mixer_ref
  29.0 13.6 %all-to-all-done = bf16[32,128,128]{2,1,0:T(8,128)(2,1)S(1)} async-done(((bf16[32,128,128]{2,1,0:T(8,128)(2,1)}), bf16[32,128,128]{2,1,0:T(8,128)(2,1)S(1)}, u32[]{:S(2)}, u32[]{:S(2)}) %all-to-all-start) | async-done | bytes 1048608 | tf_op jit(solution)/shard_map/all_to_all | solution.py:588
  42.6 1.0 copy-done.3
  43.6 4.9 %mix.1 = (f32[256,512]{1,0:T(8,128)}, bf16[8,4,64,128]{3,2,1,0:T(8,128)(2,1)}, bf16[8,4,64,128]{3,2,1,0:T(8,128)(2,1)}) custom-call(bf16[32,64,512]{2,1,0:T(8,128)(2,1)} %pack_weight.1.weight_ref, bf16[256,256]{1,0:T(8,128)(2,1)} %fusion.refs_0_.refs_4_.mixer_ref, bf16[256,256]{1,0:T(8,128)(2,1)} %fusion.1.refs_1_.mixer_ref, ...), custom_call_target="tpu_custom_call" | custom-call | flops 1073741824 | bytes 9437184 | tf_op jit(solution)/shard_map/mix/pallas_call | solution.py:289
  48.5 19.3 %all_to_all.30.refs_0_ = bf16[32,64,128]{2,1,0:T(8,128)(2,1)} all-to-all(bf16[32,64,128]{2,1,0:T(8,128)(2,1)} %bitcast.30), channel_id=1, replica_groups=mesh['gx'=8,'ta'=4] {'gx','ta'}, dimensions={0} | all-to-all | bytes 1048576 | tf_op jit(solution)/shard_map/all_to_all | solution.py:588
  67.8 3.1 %all-to-all-start.1 = ((bf16[32,64,128]{2,1,0:T(8,128)(2,1)}), bf16[32,64,128]{2,1,0:T(8,128)(2,1)S(1)}, u32[]{:S(2)}, u32[]{:S(2)}) async-start(bf16[32,64,128]{2,1,0:T(8,128)(2,1)} %bitcast.29), calls=%async_computation.1 | async-start | bytes 1048576 | tf_op jit(solution)/shard_map/all_to_all | solution.py:588
  70.9 16.7 %middle.2 = (bf16[512,4096]{1,0:T(8,128)(2,1)}, bf16[8,256,512]{2,1,0:T(8,128)(2,1)}, bf16[32,64,128]{2,1,0:T(8,128)(2,1)}, f32[8,128]{1,0:T(8,128)}) custom-call(bf16[32,64,128]{2,1,0:T(8,128)(2,1)} %all_to_all.30.refs_0_, bf16[512,4096]{1,0:T(8,128)(2,1)} %bitcast.21, bf16[512,4096]{1,0:T(8,128)(2,1)} %bitcast.23, ...), custom_call_target="tpu_custom_call" | custom-call | flops 5368709120 | bytes 18874368 | tf_op jit(solution)/shard_map/middle/pallas_call | solution.py:492
  87.6 6.0 %all-to-all-start.3 = ((bf16[32,64,128]{2,1,0:T(8,128)(2,1)}), bf16[32,64,128]{2,1,0:T(8,128)(2,1)S(1)}, u32[]{:S(2)}, u32[]{:S(2)}) async-start(bf16[32,64,128]{2,1,0:T(8,128)(2,1)} %get-tuple-element.24), calls=%async_computation.3 | async-start | bytes 1048576 | tf_op jit(solution)/shard_map/all_to_all | solution.py:588
  93.7 16.8 %middle.3 = (bf16[512,4096]{1,0:T(8,128)(2,1)}, bf16[8,256,512]{2,1,0:T(8,128)(2,1)}, bf16[32,64,128]{2,1,0:T(8,128)(2,1)}, f32[8,128]{1,0:T(8,128)}) custom-call(bf16[32,64,128]{2,1,0:T(8,128)(2,1)} %copy-done.6, bf16[512,4096]{1,0:T(8,128)(2,1)} %bitcast.22, bf16[512,4096]{1,0:T(8,128)(2,1)} %bitcast.24, ...), custom_call_target="tpu_custom_call", output_to_operand_aliasing={{0}: (7, {})} | custom-call | flops 5368709120 | bytes 18874368 | tf_op jit(solution)/shard_map/middle/pallas_call | solution.py:492
  110.5 5.7 %all-to-all-start.4 = ((bf16[32,64,128]{2,1,0:T(8,128)(2,1)}), bf16[32,64,128]{2,1,0:T(8,128)(2,1)S(1)}, u32[]{:S(2)}, u32[]{:S(2)}) async-start(bf16[32,64,128]{2,1,0:T(8,128)(2,1)} %get-tuple-element.25), calls=%async_computation.4 | async-start | bytes 1048576 | tf_op jit(solution)/shard_map/all_to_all | solution.py:588
  116.5 1.1 collective-permute-done
  118.3 1.8 collective-permute-start.1
  120.1 1.9 %collective-permute-done.1 = f32[8,128]{1,0:T(8,128)S(1)} collective-permute-done((f32[8,128]{1,0:T(8,128)S(1)}, f32[8,128]{1,0:T(8,128)S(1)}, u32[]{:S(2)}, u32[]{:S(2)}) %collective-permute-start.1) | collective-permute-done | bytes 4128 | tf_op jit(solution)/shard_map/ppermute | solution.py:595
  121.9 1.9 %collective-permute-start.2 = (f32[8,128]{1,0:T(8,128)S(1)}, f32[8,128]{1,0:T(8,128)S(1)}, u32[]{:S(2)}, u32[]{:S(2)}) collective-permute-start(f32[8,128]{1,0:T(8,128)S(1)} %add.16), channel_id=1, source_target_pairs={{0,4},{1,5},{2,6},{3,7},{4,0},{5,1},{6,2},{7,3},{8,12},{9,13},{10,... | collective-permute-start | bytes 12296 | tf_op jit(solution)/shard_map/ppermute | solution.py:595
  123.9 1.7 collective-permute-done.2
  125.5 1.8 collective-permute-start.3
  127.3 1.8 collective-permute-done.3
  129.2 2.8 %collective-permute-start.4 = (f32[8,128]{1,0:T(8,128)S(1)}, f32[8,128]{1,0:T(8,128)S(1)}, u32[]{:S(2)}, u32[]{:S(2)}) collective-permute-start(f32[8,128]{1,0:T(8,128)S(1)} %add.18), channel_id=1, source_target_pairs={{0,16},{1,17},{2,18},{3,19},{4,20},{5,21},{6,22},{7,23},{8,24},{9,... | collective-permute-start | bytes 12296 | tf_op jit(solution)/shard_map/ppermute | solution.py:595
  132.0 1.7 collective-permute-done.4
  134.3 0.8 copy-done.5
  135.1 5.8 %mix_back.1 = (f32[256,512]{1,0:T(8,128)}, bf16[8,4,128,128]{3,2,1,0:T(8,128)(2,1)}) custom-call(bf16[32,64,512]{2,1,0:T(8,128)(2,1)} %pack_weight.1.weight_ref, f32[8,128]{1,0:T(8,128)} %get-tuple-element.32.refs_0_, bf16[2,256,512]{2,1,0:T(8,128)(2,1)} %constant.24.clone.refs_1_, bf16[512,512]{1,0:T(8,128)(2,1)} %constant.27.clone.refs_4_.refs_2_, ...), custom_call_target="tpu_custom_call" | custom-call | flops 1073741824 | bytes 9437184 | tf_op jit(solution)/shard_map/mix_back/pallas_call | solution.py:289
  140.9 5.9 %all-to-all-start.5 = ((bf16[32,128,128]{2,1,0:T(8,128)(2,1)}), bf16[32,128,128]{2,1,0:T(8,128)(2,1)S(1)}, u32[]{:S(2)}, u32[]{:S(2)}) async-start(bf16[32,128,128]{2,1,0:T(8,128)(2,1)} %bitcast.28), calls=%async_computation.5 | async-start | bytes 2097152 | tf_op jit(solution)/shard_map/all_to_all | solution.py:588
  146.7 5.5 %point.1.mixed_ref = bf16[8,512,512]{2,1,0:T(8,128)(2,1)} custom-call(bf16[256,256]{1,0:T(8,128)(2,1)} %fusion.1.refs_1_.mixer_ref, bf16[8,256,512]{2,1,0:T(8,128)(2,1)} %get-tuple-element.27.refs_0_, bf16[8,256,512]{2,1,0:T(8,128)(2,1)} %get-tuple-element.28.refs_1_), custom_call_target="tpu_custom_call" | custom-call | flops 1073741824 | bytes 8388608 | tf_op jit(solution)/shard_map/point/pallas_call | solution.py:366
  152.9 9.1 %outer.1 = f32[32,16,8,8,32]{4,3,2,1,0:T(8,128)} custom-call(f32[256,512]{1,0:T(8,128)} %get-tuple-element.29.spectrum_ref, f32[256,512]{1,0:T(8,128)} %get-tuple-element.30.grad_ref), custom_call_target="tpu_custom_call" | custom-call | flops 1048576 | bytes 17825792 | tf_op jit(solution)/shard_map/outer/pallas_call | solution.py:329
  162.0 11.0 %all-to-all-done.5.packed_ref = bf16[32,128,128]{2,1,0:T(8,128)(2,1)S(1)} async-done(((bf16[32,128,128]{2,1,0:T(8,128)(2,1)}), bf16[32,128,128]{2,1,0:T(8,128)(2,1)S(1)}, u32[]{:S(2)}, u32[]{:S(2)}) %all-to-all-start.5) | async-done | bytes 1048608 | tf_op jit(solution)/shard_map/all_to_all | solution.py:588
  173.0 2.2 %copy-done.2 = bf16[8,512,512]{2,1,0:T(8,128)(2,1)S(1)} copy-done((bf16[8,512,512]{2,1,0:T(8,128)(2,1)S(1)}, bf16[8,512,512]{2,1,0:T(8,128)(2,1)}, u32[]{:S(2)}) %copy-start.2) | copy-done | bytes 4194328
  175.2 8.1 %last.1 = bf16[512,4096]{1,0:T(8,128)(2,1)} custom-call(bf16[32,128,128]{2,1,0:T(8,128)(2,1)S(1)} %all-to-all-done.5.packed_ref, bf16[8,1024,512]{2,1,0:T(8,128)(2,1)} %constant.22.clone.table_ref.refs_3_, bf16[8,512,512]{2,1,0:T(8,128)(2,1)S(1)} %copy-done.2), custom_call_target="tpu_custom_call" | custom-call | flops 4294967296 | bytes 18874368 | tf_op jit(solution)/shard_map/last/pallas_call | solution.py:564
  (31 shorter events, 2.4 us)
Async XLA Ops:
  0.6 26.5 %copy-start = (bf16[8,8]{1,0:T(8,128)(2,1)S(1)}, bf16[8,8]{1,0:T(8,128)(2,1)}, u32[]{:S(2)}) copy-start(bf16[8,8]{1,0:T(8,128)(2,1)} %param.18) | copy-start | bytes 388
  9.0 33.5 %all-to-all-start = ((bf16[32,128,128]{2,1,0:T(8,128)(2,1)}), bf16[32,128,128]{2,1,0:T(8,128)(2,1)S(1)}, u32[]{:S(2)}, u32[]{:S(2)}) async-start(bf16[32,128,128]{2,1,0:T(8,128)(2,1)} %analyse.1), calls=%async_computation | async-start | bytes 2097152 | tf_op jit(solution)/shard_map/all_to_all | solution.py:588
  16.4 9.8 %copy-start.9 = (f32[256,8]{1,0:T(8,128)S(1)}, f32[256,8]{1,0:T(8,128)}, u32[]{:S(2)}) copy-start(f32[256,8]{1,0:T(8,128)} %constant.31.clone) | copy-start | bytes 24580
  16.4 9.8 %copy-start.11 = (f32[8]{0:T(128)S(1)}, f32[8]{0:T(128)}, u32[]{:S(2)}) copy-start(f32[8]{0:T(128)} %param.19) | copy-start | bytes 100
  16.4 10.7 %copy-start.7 = (f32[256,256]{1,0:T(8,128)S(1)}, f32[256,256]{1,0:T(8,128)}, u32[]{:S(2)}) copy-start(f32[256,256]{1,0:T(8,128)} %constant.30.clone) | copy-start | bytes 786436
  16.4 10.7 %copy-start.8 = (bf16[256,8]{1,0:T(8,128)(2,1)S(1)}, bf16[256,8]{1,0:T(8,128)(2,1)}, u32[]{:S(2)}) copy-start(bf16[256,8]{1,0:T(8,128)(2,1)} %constant.29.clone) | copy-start | bytes 12292
  42.6 1.0 copy-start.3
  67.8 19.8 %all-to-all-start.1 = ((bf16[32,64,128]{2,1,0:T(8,128)(2,1)}), bf16[32,64,128]{2,1,0:T(8,128)(2,1)S(1)}, u32[]{:S(2)}, u32[]{:S(2)}) async-start(bf16[32,64,128]{2,1,0:T(8,128)(2,1)} %bitcast.29), calls=%async_computation.1 | async-start | bytes 1048576 | tf_op jit(solution)/shard_map/all_to_all | solution.py:588
  87.6 6.0 %copy-start.6 = (bf16[32,64,128]{2,1,0:T(8,128)(2,1)}, bf16[32,64,128]{2,1,0:T(8,128)(2,1)S(1)}, u32[]{:S(2)}) copy-start(bf16[32,64,128]{2,1,0:T(8,128)(2,1)S(1)} %all-to-all-done.1.packed_ref) | copy-start | bytes 1572868
  87.6 22.8 %all-to-all-start.3 = ((bf16[32,64,128]{2,1,0:T(8,128)(2,1)}), bf16[32,64,128]{2,1,0:T(8,128)(2,1)S(1)}, u32[]{:S(2)}, u32[]{:S(2)}) async-start(bf16[32,64,128]{2,1,0:T(8,128)(2,1)} %get-tuple-element.24), calls=%async_computation.3 | async-start | bytes 1048576 | tf_op jit(solution)/shard_map/all_to_all | solution.py:588
  110.5 23.8 %copy-start.4 = (bf16[32,64,128]{2,1,0:T(8,128)(2,1)}, bf16[32,64,128]{2,1,0:T(8,128)(2,1)S(1)}, u32[]{:S(2)}) copy-start(bf16[32,64,128]{2,1,0:T(8,128)(2,1)S(1)} %all-to-all-done.3) | copy-start | bytes 1572868
  110.5 23.8 %all-to-all-start.4 = ((bf16[32,64,128]{2,1,0:T(8,128)(2,1)}), bf16[32,64,128]{2,1,0:T(8,128)(2,1)S(1)}, u32[]{:S(2)}, u32[]{:S(2)}) async-start(bf16[32,64,128]{2,1,0:T(8,128)(2,1)} %get-tuple-element.25), calls=%async_computation.4 | async-start | bytes 1048576 | tf_op jit(solution)/shard_map/all_to_all | solution.py:588
  116.2 1.4 collective-permute-start
  118.3 3.6 %collective-permute-start.1 = (f32[8,128]{1,0:T(8,128)S(1)}, f32[8,128]{1,0:T(8,128)S(1)}, u32[]{:S(2)}, u32[]{:S(2)}) collective-permute-start(f32[8,128]{1,0:T(8,128)S(1)} %add.15), channel_id=1, source_target_pairs={{0,2},{1,3},{2,0},{3,1},{4,6},{5,7},{6,4},{7,5},{8,10},{9,11},{10,... | collective-permute-start | bytes 12296 | tf_op jit(solution)/shard_map/ppermute | solution.py:595
  121.9 3.6 %collective-permute-start.2 = (f32[8,128]{1,0:T(8,128)S(1)}, f32[8,128]{1,0:T(8,128)S(1)}, u32[]{:S(2)}, u32[]{:S(2)}) collective-permute-start(f32[8,128]{1,0:T(8,128)S(1)} %add.16), channel_id=1, source_target_pairs={{0,4},{1,5},{2,6},{3,7},{4,0},{5,1},{6,2},{7,3},{8,12},{9,13},{10,... | collective-permute-start | bytes 12296 | tf_op jit(solution)/shard_map/ppermute | solution.py:595
  125.5 3.6 %collective-permute-start.3 = (f32[8,128]{1,0:T(8,128)S(1)}, f32[8,128]{1,0:T(8,128)S(1)}, u32[]{:S(2)}, u32[]{:S(2)}) collective-permute-start(f32[8,128]{1,0:T(8,128)S(1)} %add.17), channel_id=1, source_target_pairs={{0,8},{1,9},{2,10},{3,11},{4,12},{5,13},{6,14},{7,15},{8,0},{9,1},... | collective-permute-start | bytes 12296 | tf_op jit(solution)/shard_map/ppermute | solution.py:595
  129.2 4.5 %collective-permute-start.4 = (f32[8,128]{1,0:T(8,128)S(1)}, f32[8,128]{1,0:T(8,128)S(1)}, u32[]{:S(2)}, u32[]{:S(2)}) collective-permute-start(f32[8,128]{1,0:T(8,128)S(1)} %add.18), channel_id=1, source_target_pairs={{0,16},{1,17},{2,18},{3,19},{4,20},{5,21},{6,22},{7,23},{8,24},{9,... | collective-permute-start | bytes 12296 | tf_op jit(solution)/shard_map/ppermute | solution.py:595
  134.3 18.0 %copy-start.10 = (f32[8,128]{1,0:T(8,128)}, f32[8,128]{1,0:T(8,128)S(1)}, u32[]{:S(2)}) copy-start(f32[8,128]{1,0:T(8,128)S(1)} %get-tuple-element.31) | copy-start | bytes 12292
  134.3 0.8 copy-start.5
  140.9 32.1 %all-to-all-start.5 = ((bf16[32,128,128]{2,1,0:T(8,128)(2,1)}), bf16[32,128,128]{2,1,0:T(8,128)(2,1)S(1)}, u32[]{:S(2)}, u32[]{:S(2)}) async-start(bf16[32,128,128]{2,1,0:T(8,128)(2,1)} %bitcast.28), calls=%async_computation.5 | async-start | bytes 2097152 | tf_op jit(solution)/shard_map/all_to_all | solution.py:588
  173.0 2.2 %copy-start.2 = (bf16[8,512,512]{2,1,0:T(8,128)(2,1)S(1)}, bf16[8,512,512]{2,1,0:T(8,128)(2,1)}, u32[]{:S(2)}) copy-start(bf16[8,512,512]{2,1,0:T(8,128)(2,1)} %point.1.mixed_ref) | copy-start | bytes 12582916
  175.2 8.1 %copy-start.1 = (bf16[8,8]{1,0:T(8,128)(2,1)S(1)}, bf16[8,8]{1,0:T(8,128)(2,1)}, u32[]{:S(2)}) copy-start(bf16[8,8]{1,0:T(8,128)(2,1)} %param.18) | copy-start | bytes 388

commit v8 on v7

--- a/solution.py
+++ b/solution.py
@@ -164,12 +164,13 @@
     )(field, table)
 
 
-def weight_kernel(weight_ref, packed_ref):
+def weight_kernel(weight_ref, packed_ref, later_ref):
     for kx in range(weight_ref.shape[0]):
         for group in range(KT // 4):
             parts = [weight_ref[kx, 4 * group + k] for k in range(4)]
             joined = jnp.concatenate(parts, axis=-1).reshape(CHANS * CHANS, LANES)
             packed_ref[kx, :, group * LANES : (group + 1) * LANES] = joined.astype(BF16)
+            later_ref[kx, :, group * LANES : (group + 1) * LANES] = joined.astype(BF16)
 
 
 def pack_weight(weight):
@@ -179,9 +180,9 @@
         weight_kernel,
         grid=(KX // per,),
         in_specs=[pl.BlockSpec((per, KT, CHANS, CHANS, own), lambda n: (n, 0, 0, 0, 0))],
-        out_specs=pl.BlockSpec((per, CHANS * CHANS, KT * own), lambda n: (n, 0, 0)),
-        out_shape=jax.ShapeDtypeStruct((KX, CHANS * CHANS, KT * own), BF16),
-        compiler_params=vmem_params(60),
+        out_specs=[pl.BlockSpec((per, CHANS * CHANS, KT * own), lambda n: (n, 0, 0))] * 2,
+        out_shape=[jax.ShapeDtypeStruct((KX, CHANS * CHANS, KT * own), BF16)] * 2,
+        compiler_params=vmem_params(24),
         cost_estimate=pl.CostEstimate(flops=1 << 20, bytes_accessed=20 << 20, transcendentals=0),
         name="pack_weight",
     )(weight)
@@ -303,7 +304,7 @@
             pltpu.SemaphoreType.DMA((len(spreads),)),
             pltpu.SemaphoreType.DMA((outs, 4 // outs)),
         ],
-        compiler_params=vmem_params(60),
+        compiler_params=vmem_params(60 if backward else 40),
         cost_estimate=pl.CostEstimate(flops=1 << 30, bytes_accessed=9 << 20, transcendentals=0),
         name="mix_back" if backward else "mix",
     )(weight, *after, *tables, *spreads)
@@ -332,7 +333,7 @@
         in_specs=[pl.BlockSpec((per * CHANS, width), lambda n: (n, 0))] * 2,
         out_specs=pl.BlockSpec((per, KT, CHANS, CHANS, own), lambda n: (n, 0, 0, 0, 0)),
         out_shape=jax.ShapeDtypeStruct((KX, KT, CHANS, CHANS, own), F32),
-        compiler_params=vmem_params(60),
+        compiler_params=vmem_params(24),
         cost_estimate=pl.CostEstimate(flops=1 << 20, bytes_accessed=17 << 20, transcendentals=0),
         name="outer",
     )(spectrum, grad)
@@ -370,7 +371,7 @@
         + [pl.BlockSpec((per, rows, WIDTH), lambda n: (n, 0, 0))] * PARTS,
         out_specs=pl.BlockSpec((per, PARTS * rows, WIDTH), lambda n: (n, 0, 0)),
         out_shape=jax.ShapeDtypeStruct((chunks, PARTS * rows, WIDTH), BF16),
-        compiler_params=vmem_params(60),
+        compiler_params=vmem_params(24),
         cost_estimate=pl.CostEstimate(
             flops=2 * PARTS * rows * CELLS * rows, bytes_accessed=8 << 20, transcendentals=0
         ),
@@ -591,9 +592,15 @@
 def sum_everywhere(values, devices):
     step = 1
     while step < devices:
-        pairs = [(at, at ^ step) for at in range(devices)]
-        values = values + lax.ppermute(values, ("gx", "ta"), pairs)
-        step *= 2
+        others = 3 if 2 * step < devices else 1
+        got = [
+            lax.ppermute(values, ("gx", "ta"), [(at, at ^ (k * step)) for at in range(devices)])
+            for k in range(1, others + 1)
+        ]
+        values = values + got[0]
+        if others == 3:
+            values = values + (got[1] + got[2])
+        step *= others + 1
     return values
 
 
@@ -641,7 +648,7 @@
     )
     part_shape = (gx, ta, xl * CHANS, LANES)
     whole_shape = (gx, ta, xl_all * CHANS, LANES)
-    packed_weight = pack_weight(spec_weight)
+    packed_weight, later_weight = pack_weight(spec_weight)
 
     spread_in = swap(analyse(field, table, xl_all, tl, devices)).reshape(whole_shape)
     spectrum, *mixed = mix(
@@ -658,7 +665,7 @@
         spread_grad.append(swap(sent).reshape(part_shape))
     summed = sum_everywhere(sums, devices)
     grad_modes, mixed_back = mix(
-        spread_grad, packed_weight, (summed,), (x_in[1], t_in, x_out[0], t_out), True
+        spread_grad, later_weight, (summed,), (x_in[1], t_in, x_out[0], t_out), True
     )
     grad_back = swap(mixed_back.reshape(devices, xl_all * CHANS, LANES))
     grad_spec = outer(spectrum, grad_modes, own)

time: 185 us -> 185 us (level)
  local copies, waits for them, and re-layouts: 4.7 us -> 19.4 us
  Pallas kernels: 85.1 us -> 70.6 us
    unnamed x24 -> x50, local copies, waits for them, and re-layouts: 4.01 us -> 18.7 us
    pallas_call x1, Pallas kernels: 9.74 us -> 2.25 us  [pack_weight(): pl.pallas_call(weight_kernel, grid=(KX // per,), in_specs=[pl.BlockSpec((...]
    pallas_call x1, Pallas kernels: 5.52 us -> 1.78 us  [point(): pl.pallas_call(point_kernel, grid=(chunks // per,), in_specs=[pl.BlockSpe...]
    pallas_call x2, Pallas kernels: 10.7 us -> 8.68 us  [mix(): pl.pallas_call(functools.partial(mix_kernel, backward, len(after)), out_s...]
    ppermute x5 -> x7, starting transfers between devices: 8.63 us -> 9.2 us  [sum_everywhere(): lax.ppermute(values, ('gx', 'ta'), [(at, at ^ k * step) for at in range(d...]
    ppermute x5 -> x7, waiting for transfers between devices: 8.17 us -> 7.61 us  [sum_everywhere(): lax.ppermute(values, ('gx', 'ta'), [(at, at ^ k * step) for at in range(d...]
  transfers between devices with their start and end apart: 10 -> 12, of which waited for: 7 -> 8; matrix products, arithmetic and copies ran while one was open for 3% -> 3% of each run, Pallas kernels for 32% -> 25%
where the time goes in v8:
time: 185 us; the launch traced here: 184 us
  Pallas kernels  70.6 us (38%)
  starting transfers between devices  36.2 us (20%)
  waiting for transfers between devices  33.5 us (18%)
  local copies, waits for them, and re-layouts  19.4 us (10%)
  blocking collectives  19.1 us (10%)
  matrix products  2.94 us (2%)
    pallas_call x2, Pallas kernels, middle(): pl.pallas_call(kernel, grid=(chunks // per,), in_specs=specs, out_specs=[...  33.5 us
    all_to_all x5, starting transfers between devices, swap(): lax.all_to_all(blocks, ('gx', 'ta'), split_axis=0, concat_axis=0, tiled=T...  27 us
    all_to_all x5, waiting for transfers between devices, swap(): lax.all_to_all(blocks, ('gx', 'ta'), split_axis=0, concat_axis=0, tiled=T...  25.9 us
    all_to_all x1, blocking collectives, swap(): lax.all_to_all(blocks, ('gx', 'ta'), split_axis=0, concat_axis=0, tiled=T...  19.1 us
    unnamed x50, local copies, waits for them, and re-layouts  18.7 us
    ppermute x7, starting transfers between devices, sum_everywhere(): lax.ppermute(values, ('gx', 'ta'), [(at, at ^ k * step) for at in range(d...  9.2 us
    pallas_call x2, Pallas kernels, mix(): pl.pallas_call(functools.partial(mix_kernel, backward, len(after)), out_s...  8.68 us
    pallas_call x1, Pallas kernels, analyse(): pl.pallas_call(functools.partial(analyse_kernel, xl, tl), in_specs=[pl.Bl...  8.39 us
  transfers between devices with their start and end apart: 12, of which 8 were waited for; matrix products, arithmetic and copies ran while one was open for 3% of the time, Pallas kernels for 25%

profile of v8, /device:TPU:0, one launch (start us, length us, event | category | flops | bytes accessed | tf_op | source)
XLA Modules:
  0.0 184.1 jit_solution(16056997293731982249)
XLA Ops:
  0.6 8.4 %analyse.1 = bf16[32,128,128]{2,1,0:T(8,128)(2,1)} custom-call(bf16[512,4096]{1,0:T(8,128)(2,1)} %bitcast.22, bf16[8,1024,512]{2,1,0:T(8,128)(2,1)} %constant.22.clone.table_ref.refs_3_), custom_call_target="tpu_custom_call" | custom-call | flops 4294967296 | bytes 13631488 | tf_op jit(solution)/shard_map/analyse/pallas_call | solution.py:145
  9.0 7.3 %all-to-all-start = ((bf16[32,128,128]{2,1,0:T(8,128)(2,1)}), bf16[32,128,128]{2,1,0:T(8,128)(2,1)S(1)}, u32[]{:S(2)}, u32[]{:S(2)}) async-start(bf16[32,128,128]{2,1,0:T(8,128)(2,1)} %analyse.1), calls=%async_computation | async-start | bytes 2097152 | tf_op jit(solution)/shard_map/all_to_all | solution.py:589
  16.4 5.8 %copy-done.4 = f32[32,16,8,8,32]{4,3,2,1,0:T(8,128)S(1)} copy-done((f32[32,16,8,8,32]{4,3,2,1,0:T(8,128)S(1)}, f32[32,16,8,8,32]{4,3,2,1,0:T(8,128)}, u32[]{:S(2)}) %copy-start.4) | copy-done | bytes 4194328
  22.1 2.3 %pack_weight.1 = (bf16[32,64,512]{2,1,0:T(8,128)(2,1)S(1)}, bf16[32,64,512]{2,1,0:T(8,128)(2,1)S(1)}) custom-call(f32[32,16,8,8,32]{4,3,2,1,0:T(8,128)S(1)} %copy-done.4), custom_call_target="tpu_custom_call" | custom-call | flops 1048576 | bytes 20971520 | tf_op jit(solution)/shard_map/pack_weight/pallas_call | solution.py:179
  24.4 1.3 copy-done.5
  26.1 1.3 fusion.refs_0_.refs_4_.mixer_ref
  27.4 1.4 fusion.1.refs_1_.mixer_ref
  28.8 13.8 %all-to-all-done = bf16[32,128,128]{2,1,0:T(8,128)(2,1)S(1)} async-done(((bf16[32,128,128]{2,1,0:T(8,128)(2,1)}), bf16[32,128,128]{2,1,0:T(8,128)(2,1)S(1)}, u32[]{:S(2)}, u32[]{:S(2)}) %all-to-all-start) | async-done | bytes 1048608 | tf_op jit(solution)/shard_map/all_to_all | solution.py:589
  42.6 1.0 copy-done.8
  46.8 2.9 %mix.1 = (f32[256,512]{1,0:T(8,128)S(1)}, bf16[8,4,64,128]{3,2,1,0:T(8,128)(2,1)S(1)}, bf16[8,4,64,128]{3,2,1,0:T(8,128)(2,1)S(1)}) custom-call(bf16[32,64,512]{2,1,0:T(8,128)(2,1)S(1)} %get-tuple-element.20.weight_ref, bf16[256,256]{1,0:T(8,128)(2,1)S(1)} %fusion.refs_0_.refs_4_.mixer_ref, bf16[256,256]{1,0:T(8,128)(2,1)S(1)} %fusion.1.refs_1_.mixer_ref, ...), custom_call_target="tpu_custom_call" | custom-call | flops 1073741824 | bytes 9437184 | tf_op jit(solution)/shard_map/mix/pallas_call | solution.py:290
  50.4 19.1 %all_to_all.30.refs_0_ = bf16[32,64,128]{2,1,0:T(8,128)(2,1)} all-to-all(bf16[32,64,128]{2,1,0:T(8,128)(2,1)S(1)} %bitcast.20), channel_id=1, replica_groups=mesh['gx'=8,'ta'=4] {'gx','ta'}, dimensions={0} | all-to-all | bytes 1048576 | tf_op jit(solution)/shard_map/all_to_all | solution.py:589
  69.5 3.1 %all-to-all-start.1 = ((bf16[32,64,128]{2,1,0:T(8,128)(2,1)}), bf16[32,64,128]{2,1,0:T(8,128)(2,1)S(1)}, u32[]{:S(2)}, u32[]{:S(2)}) async-start(bf16[32,64,128]{2,1,0:T(8,128)(2,1)} %bitcast.19), calls=%async_computation.1 | async-start | bytes 1048576 | tf_op jit(solution)/shard_map/all_to_all | solution.py:589
  72.6 16.7 %middle.2 = (bf16[512,4096]{1,0:T(8,128)(2,1)}, bf16[8,256,512]{2,1,0:T(8,128)(2,1)}, bf16[32,64,128]{2,1,0:T(8,128)(2,1)}, f32[8,128]{1,0:T(8,128)}) custom-call(bf16[32,64,128]{2,1,0:T(8,128)(2,1)} %all_to_all.30.refs_0_, bf16[512,4096]{1,0:T(8,128)(2,1)} %bitcast.23, bf16[512,4096]{1,0:T(8,128)(2,1)} %bitcast.25, ...), custom_call_target="tpu_custom_call" | custom-call | flops 5368709120 | bytes 18874368 | tf_op jit(solution)/shard_map/middle/pallas_call | solution.py:493
  89.4 6.0 %all-to-all-start.3 = ((bf16[32,64,128]{2,1,0:T(8,128)(2,1)}), bf16[32,64,128]{2,1,0:T(8,128)(2,1)S(1)}, u32[]{:S(2)}, u32[]{:S(2)}) async-start(bf16[32,64,128]{2,1,0:T(8,128)(2,1)} %get-tuple-element.28), calls=%async_computation.3 | async-start | bytes 1048576 | tf_op jit(solution)/shard_map/all_to_all | solution.py:589
  95.4 16.8 %middle.3 = (bf16[512,4096]{1,0:T(8,128)(2,1)}, bf16[8,256,512]{2,1,0:T(8,128)(2,1)}, bf16[32,64,128]{2,1,0:T(8,128)(2,1)}, f32[8,128]{1,0:T(8,128)}) custom-call(bf16[32,64,128]{2,1,0:T(8,128)(2,1)} %copy-done.20, bf16[512,4096]{1,0:T(8,128)(2,1)} %bitcast.24, bf16[512,4096]{1,0:T(8,128)(2,1)} %bitcast.26, ...), custom_call_target="tpu_custom_call", output_to_operand_aliasing={{0}: (7, {})} | custom-call | flops 5368709120 | bytes 18874368 | tf_op jit(solution)/shard_map/middle/pallas_call | solution.py:493
  112.2 5.7 %all-to-all-start.4 = ((bf16[32,64,128]{2,1,0:T(8,128)(2,1)}), bf16[32,64,128]{2,1,0:T(8,128)(2,1)S(1)}, u32[]{:S(2)}, u32[]{:S(2)}) async-start(bf16[32,64,128]{2,1,0:T(8,128)(2,1)} %get-tuple-element.29), calls=%async_computation.4 | async-start | bytes 1048576 | tf_op jit(solution)/shard_map/all_to_all | solution.py:589
  117.9 1.8 collective-permute-start.1
  120.1 2.5 %collective-permute-done.1 = f32[8,128]{1,0:T(8,128)S(1)} collective-permute-done((f32[8,128]{1,0:T(8,128)}, f32[8,128]{1,0:T(8,128)S(1)}, u32[]{:S(2)}, u32[]{:S(2)}) %collective-permute-start.1) | collective-permute-done | bytes 4128 | tf_op jit(solution)/shard_map/ppermute | solution.py:597
  123.7 1.6 collective-permute-start.4
  125.3 1.4 collective-permute-start.5
  127.3 2.5 %collective-permute-done.5 = f32[8,128]{1,0:T(8,128)S(1)} collective-permute-done((f32[8,128]{1,0:T(8,128)S(1)}, f32[8,128]{1,0:T(8,128)S(1)}, u32[]{:S(2)}, u32[]{:S(2)}) %collective-permute-start.5) | collective-permute-done | bytes 4128 | tf_op jit(solution)/shard_map/ppermute | solution.py:597
  130.3 3.5 %collective-permute-start.6 = (f32[8,128]{1,0:T(8,128)S(1)}, f32[8,128]{1,0:T(8,128)S(1)}, u32[]{:S(2)}, u32[]{:S(2)}) collective-permute-start(f32[8,128]{1,0:T(8,128)S(1)} %add_add_fusion), channel_id=1, source_target_pairs={{0,16},{1,17},{2,18},{3,19},{4,20},{5,21},{6,22},{7,23},{8,24},{9,... | collective-permute-start | bytes 12296 | tf_op jit(solution)/shard_map/ppermute | solution.py:597
  133.8 1.6 collective-permute-done.6
  136.9 5.8 %mix_back.1 = (f32[256,512]{1,0:T(8,128)}, bf16[8,4,128,128]{3,2,1,0:T(8,128)(2,1)}) custom-call(bf16[32,64,512]{2,1,0:T(8,128)(2,1)} %copy-done.5, f32[8,128]{1,0:T(8,128)} %get-tuple-element.36.refs_0_, bf16[2,256,512]{2,1,0:T(8,128)(2,1)} %constant.24.clone.refs_1_, bf16[512,512]{1,0:T(8,128)(2,1)} %constant.27.clone.refs_4_.refs_2_, ...), custom_call_target="tpu_custom_call" | custom-call | flops 1073741824 | bytes 9437184 | tf_op jit(solution)/shard_map/mix_back/pallas_call | solution.py:290
  142.7 4.9 %all-to-all-start.5 = ((bf16[32,128,128]{2,1,0:T(8,128)(2,1)}), bf16[32,128,128]{2,1,0:T(8,128)(2,1)S(1)}, u32[]{:S(2)}, u32[]{:S(2)}) async-start(bf16[32,128,128]{2,1,0:T(8,128)(2,1)} %bitcast.30), calls=%async_computation.5 | async-start | bytes 2097152 | tf_op jit(solution)/shard_map/all_to_all | solution.py:589
  147.6 1.6 copy-done.7
  149.2 1.8 point.1.mixed_ref
  151.0 2.0 %copy-done.2 = bf16[8,512,512]{2,1,0:T(8,128)(2,1)} copy-done((bf16[8,512,512]{2,1,0:T(8,128)(2,1)}, bf16[8,512,512]{2,1,0:T(8,128)(2,1)S(1)}, u32[]{:S(2)}) %copy-start.2) | copy-done | bytes 4194328
  153.7 7.9 %outer.1 = f32[32,16,8,8,32]{4,3,2,1,0:T(8,128)} custom-call(f32[256,512]{1,0:T(8,128)S(1)} %copy-done.13, f32[256,512]{1,0:T(8,128)S(1)} %copy-done.14), custom_call_target="tpu_custom_call" | custom-call | flops 1048576 | bytes 17825792 | tf_op jit(solution)/shard_map/outer/pallas_call | solution.py:330
  161.6 12.1 %all-to-all-done.5.packed_ref = bf16[32,128,128]{2,1,0:T(8,128)(2,1)S(1)} async-done(((bf16[32,128,128]{2,1,0:T(8,128)(2,1)}), bf16[32,128,128]{2,1,0:T(8,128)(2,1)S(1)}, u32[]{:S(2)}, u32[]{:S(2)}) %all-to-all-start.5) | async-done | bytes 1048608 | tf_op jit(solution)/shard_map/all_to_all | solution.py:589
  173.6 2.2 %copy-done.3 = bf16[8,512,512]{2,1,0:T(8,128)(2,1)S(1)} copy-done((bf16[8,512,512]{2,1,0:T(8,128)(2,1)S(1)}, bf16[8,512,512]{2,1,0:T(8,128)(2,1)}, u32[]{:S(2)}) %copy-start.3) | copy-done | bytes 4194328
  175.8 8.1 %last.1 = bf16[512,4096]{1,0:T(8,128)(2,1)} custom-call(bf16[32,128,128]{2,1,0:T(8,128)(2,1)S(1)} %all-to-all-done.5.packed_ref, bf16[8,1024,512]{2,1,0:T(8,128)(2,1)} %constant.22.clone.table_ref.refs_3_, bf16[8,512,512]{2,1,0:T(8,128)(2,1)S(1)} %copy-done.3), custom_call_target="tpu_custom_call" | custom-call | flops 4294967296 | bytes 18874368 | tf_op jit(solution)/shard_map/last/pallas_call | solution.py:565
  (59 shorter events, 9.0 us)
Async XLA Ops:
  0.6 25.4 %copy-start = (bf16[8,8]{1,0:T(8,128)(2,1)S(1)}, bf16[8,8]{1,0:T(8,128)(2,1)}, u32[]{:S(2)}) copy-start(bf16[8,8]{1,0:T(8,128)(2,1)} %param.18) | copy-start | bytes 388
  9.0 33.5 %all-to-all-start = ((bf16[32,128,128]{2,1,0:T(8,128)(2,1)}), bf16[32,128,128]{2,1,0:T(8,128)(2,1)S(1)}, u32[]{:S(2)}, u32[]{:S(2)}) async-start(bf16[32,128,128]{2,1,0:T(8,128)(2,1)} %analyse.1), calls=%async_computation | async-start | bytes 2097152 | tf_op jit(solution)/shard_map/all_to_all | solution.py:589
  16.4 5.8 %copy-start.4 = (f32[32,16,8,8,32]{4,3,2,1,0:T(8,128)S(1)}, f32[32,16,8,8,32]{4,3,2,1,0:T(8,128)}, u32[]{:S(2)}) copy-start(f32[32,16,8,8,32]{4,3,2,1,0:T(8,128)} %weight_ref.1) | copy-start | bytes 12582916
  22.1 3.6 %copy-start.22 = (f32[256,8]{1,0:T(8,128)S(1)}, f32[256,8]{1,0:T(8,128)}, u32[]{:S(2)}) copy-start(f32[256,8]{1,0:T(8,128)} %constant.31.clone) | copy-start | bytes 24580
  22.1 3.6 %copy-start.24 = (f32[8]{0:T(128)S(1)}, f32[8]{0:T(128)}, u32[]{:S(2)}) copy-start(f32[8]{0:T(128)} %param.19) | copy-start | bytes 100
  22.1 4.0 %copy-start.21 = (bf16[256,8]{1,0:T(8,128)(2,1)S(1)}, bf16[256,8]{1,0:T(8,128)(2,1)}, u32[]{:S(2)}) copy-start(bf16[256,8]{1,0:T(8,128)(2,1)} %constant.29.clone) | copy-start | bytes 12292
  24.4 1.4 copy-start.5
  26.1 43.4 %copy-start.10 = (f32[256,128]{1,0:T(8,128)}, f32[256,128]{1,0:T(8,128)S(1)}, u32[]{:S(2)}) copy-start(f32[256,128]{1,0:T(8,128)S(1)} %fusion.2.refs_2_.refs_5_.bias_ref) | copy-start | bytes 393220
  27.4 45.2 %copy-start.11 = (bf16[256,256]{1,0:T(8,128)(2,1)}, bf16[256,256]{1,0:T(8,128)(2,1)S(1)}, u32[]{:S(2)}) copy-start(bf16[256,256]{1,0:T(8,128)(2,1)S(1)} %fusion.refs_0_.refs_4_.mixer_ref) | copy-start | bytes 393220
  42.6 1.0 copy-start.8
  50.4 19.1 %copy-start.15 = (bf16[8,4,64,128]{3,2,1,0:T(8,128)(2,1)}, bf16[8,4,64,128]{3,2,1,0:T(8,128)(2,1)S(1)}, u32[]{:S(2)}) copy-start(bf16[8,4,64,128]{3,2,1,0:T(8,128)(2,1)S(1)} %get-tuple-element.21) | copy-start | bytes 1572868
  69.5 19.8 %all-to-all-start.1 = ((bf16[32,64,128]{2,1,0:T(8,128)(2,1)}), bf16[32,64,128]{2,1,0:T(8,128)(2,1)S(1)}, u32[]{:S(2)}, u32[]{:S(2)}) async-start(bf16[32,64,128]{2,1,0:T(8,128)(2,1)} %bitcast.19), calls=%async_computation.1 | async-start | bytes 1048576 | tf_op jit(solution)/shard_map/all_to_all | solution.py:589
  89.4 6.0 %copy-start.20 = (bf16[32,64,128]{2,1,0:T(8,128)(2,1)}, bf16[32,64,128]{2,1,0:T(8,128)(2,1)S(1)}, u32[]{:S(2)}) copy-start(bf16[32,64,128]{2,1,0:T(8,128)(2,1)S(1)} %all-to-all-done.1.packed_ref) | copy-start | bytes 1572868
  89.4 22.8 %all-to-all-start.3 = ((bf16[32,64,128]{2,1,0:T(8,128)(2,1)}), bf16[32,64,128]{2,1,0:T(8,128)(2,1)S(1)}, u32[]{:S(2)}, u32[]{:S(2)}) async-start(bf16[32,64,128]{2,1,0:T(8,128)(2,1)} %get-tuple-element.28), calls=%async_computation.3 | async-start | bytes 1048576 | tf_op jit(solution)/shard_map/all_to_all | solution.py:589
  112.2 23.8 %copy-start.18 = (bf16[32,64,128]{2,1,0:T(8,128)(2,1)}, bf16[32,64,128]{2,1,0:T(8,128)(2,1)S(1)}, u32[]{:S(2)}) copy-start(bf16[32,64,128]{2,1,0:T(8,128)(2,1)S(1)} %all-to-all-done.3) | copy-start | bytes 1572868
  112.2 35.4 %copy-start.6 = (bf16[8,256,512]{2,1,0:T(8,128)(2,1)S(1)}, bf16[8,256,512]{2,1,0:T(8,128)(2,1)}, u32[]{:S(2)}) copy-start(bf16[8,256,512]{2,1,0:T(8,128)(2,1)} %get-tuple-element.31.refs_0_) | copy-start | bytes 6291460
  112.2 23.8 %all-to-all-start.4 = ((bf16[32,64,128]{2,1,0:T(8,128)(2,1)}), bf16[32,64,128]{2,1,0:T(8,128)(2,1)S(1)}, u32[]{:S(2)}, u32[]{:S(2)}) async-start(bf16[32,64,128]{2,1,0:T(8,128)(2,1)} %get-tuple-element.29), calls=%async_computation.4 | async-start | bytes 1048576 | tf_op jit(solution)/shard_map/all_to_all | solution.py:589
  117.9 4.7 %collective-permute-start.1 = (f32[8,128]{1,0:T(8,128)}, f32[8,128]{1,0:T(8,128)S(1)}, u32[]{:S(2)}, u32[]{:S(2)}) collective-permute-start(f32[8,128]{1,0:T(8,128)} %get-tuple-element.27), channel_id=1, source_target_pairs={{0,2},{1,3},{2,0},{3,1},{4,6},{5,7},{6,4},{7,5},{8,10},{9,11},{10,... | collective-permute-start | bytes 12296 | tf_op jit(solution)/shard_map/ppermute | solution.py:597
  119.8 3.2 %collective-permute-start.2 = (f32[8,128]{1,0:T(8,128)}, f32[8,128]{1,0:T(8,128)S(1)}, u32[]{:S(2)}, u32[]{:S(2)}) collective-permute-start(f32[8,128]{1,0:T(8,128)} %get-tuple-element.27), channel_id=1, source_target_pairs={{0,3},{1,2},{2,1},{3,0},{4,7},{5,6},{6,5},{7,4},{8,11},{9,10},{10,... | collective-permute-start | bytes 12296 | tf_op jit(solution)/shard_map/ppermute | solution.py:597
  119.8 3.2 %collective-permute-start = (f32[8,128]{1,0:T(8,128)}, f32[8,128]{1,0:T(8,128)S(1)}, u32[]{:S(2)}, u32[]{:S(2)}) collective-permute-start(f32[8,128]{1,0:T(8,128)} %get-tuple-element.27), channel_id=1, source_target_pairs={{0,1},{1,0},{2,3},{3,2},{4,5},{5,4},{6,7},{7,6},{8,9},{9,8},{10,11... | collective-permute-start | bytes 12296 | tf_op jit(solution)/shard_map/ppermute | solution.py:597
  123.7 3.6 %collective-permute-start.4 = (f32[8,128]{1,0:T(8,128)S(1)}, f32[8,128]{1,0:T(8,128)S(1)}, u32[]{:S(2)}, u32[]{:S(2)}) collective-permute-start(f32[8,128]{1,0:T(8,128)S(1)} %add_add_fusion.1), channel_id=1, source_target_pairs={{0,8},{1,9},{2,10},{3,11},{4,12},{5,13},{6,14},{7,15},{8,0},{9,1},... | collective-permute-start | bytes 12296 | tf_op jit(solution)/shard_map/ppermute | solution.py:597
  125.3 4.5 %collective-permute-start.5 = (f32[8,128]{1,0:T(8,128)S(1)}, f32[8,128]{1,0:T(8,128)S(1)}, u32[]{:S(2)}, u32[]{:S(2)}) collective-permute-start(f32[8,128]{1,0:T(8,128)S(1)} %add_add_fusion.1), channel_id=1, source_target_pairs={{0,12},{1,13},{2,14},{3,15},{4,8},{5,9},{6,10},{7,11},{8,4},{9,5},... | collective-permute-start | bytes 12296 | tf_op jit(solution)/shard_map/ppermute | solution.py:597
  126.7 3.6 %collective-permute-start.3 = (f32[8,128]{1,0:T(8,128)S(1)}, f32[8,128]{1,0:T(8,128)S(1)}, u32[]{:S(2)}, u32[]{:S(2)}) collective-permute-start(f32[8,128]{1,0:T(8,128)S(1)} %add_add_fusion.1), channel_id=1, source_target_pairs={{0,4},{1,5},{2,6},{3,7},{4,0},{5,1},{6,2},{7,3},{8,12},{9,13},{10,... | collective-permute-start | bytes 12296 | tf_op jit(solution)/shard_map/ppermute | solution.py:597
  130.3 5.1 %collective-permute-start.6 = (f32[8,128]{1,0:T(8,128)S(1)}, f32[8,128]{1,0:T(8,128)S(1)}, u32[]{:S(2)}, u32[]{:S(2)}) collective-permute-start(f32[8,128]{1,0:T(8,128)S(1)} %add_add_fusion), channel_id=1, source_target_pairs={{0,16},{1,17},{2,18},{3,19},{4,20},{5,21},{6,22},{7,23},{8,24},{9,... | collective-permute-start | bytes 12296 | tf_op jit(solution)/shard_map/ppermute | solution.py:597
  136.0 17.0 %copy-start.23 = (f32[8,128]{1,0:T(8,128)}, f32[8,128]{1,0:T(8,128)S(1)}, u32[]{:S(2)}) copy-start(f32[8,128]{1,0:T(8,128)S(1)} %get-tuple-element.35) | copy-start | bytes 12292
  142.7 31.0 %all-to-all-start.5 = ((bf16[32,128,128]{2,1,0:T(8,128)(2,1)}), bf16[32,128,128]{2,1,0:T(8,128)(2,1)S(1)}, u32[]{:S(2)}, u32[]{:S(2)}) async-start(bf16[32,128,128]{2,1,0:T(8,128)(2,1)} %bitcast.30), calls=%async_computation.5 | async-start | bytes 2097152 | tf_op jit(solution)/shard_map/all_to_all | solution.py:589
  147.6 1.6 copy-start.7
  149.2 4.5 %copy-start.13 = (f32[256,512]{1,0:T(8,128)S(1)}, f32[256,512]{1,0:T(8,128)}, u32[]{:S(2)}) copy-start(f32[256,512]{1,0:T(8,128)} %copy-done.12) | copy-start | bytes 1572868
  149.2 4.5 %copy-start.14 = (f32[256,512]{1,0:T(8,128)S(1)}, f32[256,512]{1,0:T(8,128)}, u32[]{:S(2)}) copy-start(f32[256,512]{1,0:T(8,128)} %get-tuple-element.34.grad_ref) | copy-start | bytes 1572868
  151.0 2.0 %copy-start.2 = (bf16[8,512,512]{2,1,0:T(8,128)(2,1)}, bf16[8,512,512]{2,1,0:T(8,128)(2,1)S(1)}, u32[]{:S(2)}) copy-start(bf16[8,512,512]{2,1,0:T(8,128)(2,1)S(1)} %point.1.mixed_ref) | copy-start | bytes 12582916
  173.6 2.2 %copy-start.3 = (bf16[8,512,512]{2,1,0:T(8,128)(2,1)S(1)}, bf16[8,512,512]{2,1,0:T(8,128)(2,1)}, u32[]{:S(2)}) copy-start(bf16[8,512,512]{2,1,0:T(8,128)(2,1)} %copy-done.2) | copy-start | bytes 12582916
  175.8 8.1 %copy-start.1 = (bf16[8,8]{1,0:T(8,128)(2,1)S(1)}, bf16[8,8]{1,0:T(8,128)(2,1)}, u32[]{:S(2)}) copy-start(bf16[8,8]{1,0:T(8,128)(2,1)} %param.18) | copy-start | bytes 388
  (5 other events, 4.8 us)

commit v9 on v7

--- a/solution.py
+++ b/solution.py
@@ -351,48 +351,139 @@
     return jnp.where(values >= 0.0, 1.0 - tail, tail), decay
 
 
-def point_kernel(mixer_ref, *refs):
-    grad_refs, mixed_ref = refs[:PARTS], refs[PARTS]
+def point_field_kernel(mixer_ref, bias_ref, field_ref, mixed_ref):
+    rows = mixer_ref.shape[0]
+    bias = jnp.concatenate([bias_ref[...]] * (WIDTH // LANES), axis=1)
+    for at in range(mixed_ref.shape[0]):
+        for first in range(0, field_ref.shape[0], rows):
+            part = slice(first, first + rows)
+            field = field_ref[part, at * WIDTH : (at + 1) * WIDTH]
+            mixed_ref[at, part, :] = (matmul(mixer_ref[...], field) + bias).astype(BF16)
+
+
+def point_field(field, mixer, bias):
+    rows = field.shape[0]
+    group = mixer.shape[0]
+    per = 2
+    return pl.pallas_call(
+        point_field_kernel,
+        grid=(CELLS // (per * WIDTH),),
+        in_specs=[
+            pl.BlockSpec((group, group), lambda n: (0, 0)),
+            pl.BlockSpec((group, LANES), lambda n: (0, 0)),
+            pl.BlockSpec((rows, per * WIDTH), lambda n: (0, n)),
+        ],
+        out_specs=pl.BlockSpec((per, rows, WIDTH), lambda n: (n, 0, 0)),
+        out_shape=jax.ShapeDtypeStruct((CELLS // WIDTH, rows, WIDTH), BF16),
+        compiler_params=vmem_params(60),
+        cost_estimate=pl.CostEstimate(
+            flops=2 * rows * CELLS * group, bytes_accessed=8 << 20, transcendentals=0
+        ),
+        name="point_field",
+    )(mixer, bias, field)
+
+
+def point_grad_kernel(mixer_ref, grad_ref, mixed_ref):
     rows = mixer_ref.shape[0]
     for at in range(mixed_ref.shape[0]):
-        for part, grad_ref in enumerate(grad_refs):
-            mixed = matmul(mixer_ref[...], grad_ref[at])
-            mixed_ref[at, part * rows : (part + 1) * rows, :] = mixed.astype(BF16)
-
-
-def point(grads, mixer):
-    chunks, rows, _ = grads[0].shape
+        for first in range(0, grad_ref.shape[1], rows):
+            part = slice(first, first + rows)
+            mixed_ref[at, part, :] = matmul(mixer_ref[...], grad_ref[at, part, :]).astype(BF16)
+
+
+def point_grad(grad, mixer):
+    chunks, rows, _ = grad.shape
+    group = mixer.shape[0]
     per = 2
-    return pl.pallas_call(
-        point_kernel,
+    blocks = pl.BlockSpec((per, rows, WIDTH), lambda n: (n, 0, 0))
+    return pl.pallas_call(
+        point_grad_kernel,
         grid=(chunks // per,),
-        in_specs=[pl.BlockSpec((rows, rows), lambda n: (0, 0))]
-        + [pl.BlockSpec((per, rows, WIDTH), lambda n: (n, 0, 0))] * PARTS,
-        out_specs=pl.BlockSpec((per, PARTS * rows, WIDTH), lambda n: (n, 0, 0)),
-        out_shape=jax.ShapeDtypeStruct((chunks, PARTS * rows, WIDTH), BF16),
+        in_specs=[pl.BlockSpec((group, group), lambda n: (0, 0)), blocks],
+        out_specs=blocks,
+        out_shape=jax.ShapeDtypeStruct(grad.shape, BF16),
         compiler_params=vmem_params(60),
         cost_estimate=pl.CostEstimate(
-            flops=2 * PARTS * rows * CELLS * rows, bytes_accessed=8 << 20, transcendentals=0
+            flops=2 * rows * CELLS * group, bytes_accessed=8 << 20, transcendentals=0
         ),
-        name="point",
-    )(mixer, *grads)
+        name="point_grad",
+    )(mixer, grad)
+
+
+def sums_kernel(group, field_ref, grad_ref, sums_ref, total):
+    step = pl.program_id(0)
+    rows, width = field_ref.shape
+    blocks = grad_ref.shape[0]
+    ones = jnp.ones((16, width), BF16)
+    part = 0.0
+    for first in range(0, rows, group):
+        at = slice(first, first + group)
+        passing = jnp.concatenate([field_ref[at, :], ones], axis=0)
+        grads = jnp.concatenate([grad_ref[block, at, :] for block in range(blocks)], axis=1)
+        part = part + matmul_turned(passing, grads)
+
+    @pl.when(step == 0)
+    def _():
+        total[...] = part
+
+    @pl.when(step > 0)
+    def _():
+        total[...] += part
+
+    @pl.when(step == pl.num_programs(0) - 1)
+    def _():
+        row = lax.broadcasted_iota(jnp.int32, (group, group), 0)
+        column = lax.broadcasted_iota(jnp.int32, (group, group), 1)
+        gram = total[:group, :].T
+        bias = total[group : group + CHANS, :]
+        same = jnp.where(row // CHANS == column // CHANS, gram, 0.0)
+        folded = jnp.sum(same.reshape(group // CHANS, CHANS, group), axis=0)
+        source = lax.broadcasted_iota(jnp.int32, (group, LANES), 0)
+        target = lax.broadcasted_iota(jnp.int32, (group, LANES), 1)
+        select = jnp.where(source % CHANS == target, 1.0, 0.0)
+        chan = lax.broadcasted_iota(jnp.int32, (CHANS, group), 0)
+        place = lax.broadcasted_iota(jnp.int32, (CHANS, group), 1)
+        own_bias = jnp.sum(
+            jnp.where(place % CHANS == chan, bias, 0.0), axis=1, keepdims=True
+        )
+        point = jnp.dot(
+            folded, select, precision=lax.Precision.HIGHEST, preferred_element_type=F32
+        )
+        lane = lax.broadcasted_iota(jnp.int32, (CHANS, LANES), 1)
+        sums_ref[...] = jnp.where(lane == CHANS, own_bias, point)
+
+
+def own_sums(field, grad, group):
+    chunks, rows, _ = grad.shape
+    per = 2
+    return pl.pallas_call(
+        functools.partial(sums_kernel, group),
+        grid=(chunks // per,),
+        in_specs=[
+            pl.BlockSpec((rows, per * WIDTH), lambda n: (0, n)),
+            pl.BlockSpec((per, rows, WIDTH), lambda n: (n, 0, 0)),
+        ],
+        out_specs=pl.BlockSpec((CHANS, LANES), lambda n: (0, 0)),
+        out_shape=jax.ShapeDtypeStruct((CHANS, LANES), F32),
+        scratch_shapes=[pltpu.VMEM((group + 16, group), F32)],
+        compiler_params=vmem_params(60),
+        cost_estimate=pl.CostEstimate(
+            flops=2 * rows * CELLS * group, bytes_accessed=8 << 20, transcendentals=0
+        ),
+        name="own_sums",
+    )(field, grad)
 
 
 def middle_kernel(
     xl,
     tl,
     packed_ref,
-    field_ref,
     cotangent_ref,
+    mixed_ref,
     table_ref,
-    mixer_ref,
-    bias_ref,
-    sums_in_ref,
-    _,
     output_ref,
     grad_ref,
     sent_ref,
-    sums_ref,
     wide,
     modes,
     total,
@@ -400,10 +491,9 @@
     sems,
 ):
     step = pl.program_id(0)
-    rows, width = field_ref.shape
+    rows, width = cotangent_ref.shape
     tile = 256
     chunk = 32
-    ones = 16
 
     @pl.when(step == 0)
     def _():
@@ -411,22 +501,17 @@
         modes[...] = wide[...].reshape(rows, KQ).astype(BF16)
         total[...] = jnp.zeros_like(total)
 
-    blocks = table_ref.shape[0]
-
     def build(at):
-        block, first = divmod(at.start, WIDTH)
-        spatial = matmul(modes[...], table_ref[block, :, first : first + tile])
-        return spatial + matmul(mixer_ref[...], field_ref[:, at])
+        return matmul(modes[...], table_ref[0, :, at])
 
     def pointwise(pre, at):
         for first in range(0, rows, chunk):
             part = slice(first, first + chunk)
-            values = pre[part, :] + jnp.concatenate([bias_ref[part, :]] * (tile // LANES), axis=1)
+            values = pre[part, :] + mixed_ref[0, part, at].astype(F32)
             integral, decay = normal_parts(values)
             output_ref[part, at] = (values * integral).astype(BF16)
             slope = integral + (values * DENSITY) * decay
-            grad = (cotangent_ref[part, at].astype(F32) * slope).astype(BF16)
-            grad_ref[at.start // WIDTH, part, at.start % WIDTH : at.start % WIDTH + tile] = grad
+            grad_ref[0, part, at] = (cotangent_ref[part, at].astype(F32) * slope).astype(BF16)
 
     tiles = [slice(first, first + tile) for first in range(0, width, tile)]
     ready = build(tiles[0])
@@ -435,90 +520,46 @@
         if index + 1 < len(tiles):
             ready = build(tiles[index + 1])
         pointwise(pre, at)
-    passing = jnp.concatenate([table_ref[at] for at in range(blocks)], axis=1)
-    passing = jnp.concatenate([passing, field_ref[...], jnp.ones((ones, width), BF16)], axis=0)
-    grads = jnp.concatenate([grad_ref[at] for at in range(blocks)], axis=1)
-    total[...] += matmul_turned(passing, grads)
+    total[...] += matmul_turned(table_ref[0], grad_ref[0])
 
     @pl.when(step == pl.num_programs(0) - 1)
     def _():
         pack_modes(total, held, sent_ref, sems, xl, tl)
-        row = lax.broadcasted_iota(jnp.int32, (rows, rows), 0)
-        column = lax.broadcasted_iota(jnp.int32, (rows, rows), 1)
-        gram = total[KQ : KQ + rows, :].T
-        bias = total[KQ + rows : KQ + rows + CHANS, :]
-        same = jnp.where(row // CHANS == column // CHANS, gram, 0.0)
-        folded = jnp.sum(same.reshape(rows // CHANS, CHANS, rows), axis=0)
-        source = lax.broadcasted_iota(jnp.int32, (rows, LANES), 0)
-        target = lax.broadcasted_iota(jnp.int32, (rows, LANES), 1)
-        select = jnp.where(source % CHANS == target, 1.0, 0.0)
-        chan = lax.broadcasted_iota(jnp.int32, (CHANS, rows), 0)
-        place = lax.broadcasted_iota(jnp.int32, (CHANS, rows), 1)
-        own_bias = jnp.sum(
-            jnp.where(place % CHANS == chan, bias, 0.0), axis=1, keepdims=True
-        )
-        sums = jnp.dot(
-            folded, select, precision=lax.Precision.HIGHEST, preferred_element_type=F32
-        )
-        lane = lax.broadcasted_iota(jnp.int32, (CHANS, LANES), 1)
-        sums = jnp.where(lane == CHANS, own_bias, sums)
-        sums_ref[...] = sums if sums_in_ref is None else sums_in_ref[...] + sums
-
-
-def middle(packed, field, cotangent, table, mixer, bias, sums, output, part, xl, tl):
+
+
+def middle(packed, cotangent, mixed, table, xl, tl):
     rows = xl * tl * CHANS
-    per = 2
     chunks = CELLS // WIDTH
-    whole = lambda *shape: pl.BlockSpec(shape, lambda n: (0,) * len(shape))
-    tile = pl.BlockSpec((rows, per * WIDTH), lambda n: (part, n))
-    kernel = functools.partial(middle_kernel, xl, tl)
-    operands = (packed, field, cotangent, table, mixer, bias)
-    specs = [
-        whole(*packed.shape),
-        tile,
-        tile,
-        pl.BlockSpec((per, KQ, WIDTH), lambda n: (n, 0, 0)),
-        whole(rows, rows),
-        whole(rows, LANES),
-    ]
-    aliases = {}
-    if output is None:
-        inner = kernel
-        kernel = lambda *refs: inner(*refs[:6], None, None, *refs[6:])
-    else:
-        operands += (sums, output)
-        aliases = {len(operands) - 1: 0}
-        specs += [whole(CHANS, LANES), pl.BlockSpec(memory_space=pltpu.HBM)]
-    return pl.pallas_call(
-        kernel,
-        grid=(chunks // per,),
-        in_specs=specs,
-        out_specs=[
+    tile = pl.BlockSpec((rows, WIDTH), lambda n: (0, n))
+    block = pl.BlockSpec((1, rows, WIDTH), lambda n: (n, 0, 0))
+    return pl.pallas_call(
+        functools.partial(middle_kernel, xl, tl),
+        grid=(chunks,),
+        in_specs=[
+            pl.BlockSpec(packed.shape, lambda n: (0, 0, 0)),
             tile,
-            pl.BlockSpec((per, rows, WIDTH), lambda n: (n, 0, 0)),
-            pl.BlockSpec(memory_space=pl.ANY),
-            whole(CHANS, LANES),
+            block,
+            pl.BlockSpec((1, KQ, WIDTH), lambda n: (n, 0, 0)),
         ],
+        out_specs=[tile, block, pl.BlockSpec(memory_space=pl.ANY)],
         out_shape=(
-            jax.ShapeDtypeStruct(field.shape, BF16),
+            jax.ShapeDtypeStruct((rows, CELLS), BF16),
             jax.ShapeDtypeStruct((chunks, rows, WIDTH), BF16),
             jax.ShapeDtypeStruct(packed.shape, BF16),
-            jax.ShapeDtypeStruct((CHANS, LANES), F32),
         ),
         scratch_shapes=[
             pltpu.VMEM((xl, tl, CHANS, KQ), F32),
             pltpu.VMEM((rows, KQ), BF16),
-            pltpu.VMEM((KQ + rows + 16, rows), F32),
+            pltpu.VMEM((KQ, rows), F32),
             pltpu.VMEM(packed.shape, BF16),
             pltpu.SemaphoreType.DMA((KQ // LANES,)),
         ],
-        input_output_aliases=aliases,
         compiler_params=vmem_params(60),
         cost_estimate=pl.CostEstimate(
-            flops=5 * rows * CELLS * KQ, bytes_accessed=18 << 20, transcendentals=rows * CELLS
+            flops=4 * rows * CELLS * KQ, bytes_accessed=26 << 20, transcendentals=rows * CELLS
         ),
         name="middle",
-    )(*operands)
+    )(packed, cotangent, mixed, table)
 
 
 def last_kernel(xl, tl, packed_ref, table_ref, mixed_ref, field_ref, *scratch):
@@ -598,37 +639,26 @@
 
 
 def fast_body(gx, ta, features, cotangent, spec_weight, point_weight, bias_vector):
-    _, xl_all, tl, _, cells = features.shape
+    _, xl, tl, _, cells = features.shape
     own = spec_weight.shape[4]
     devices = gx * ta
-    xl = xl_all // PARTS
     rows = xl * tl * CHANS
+    group = rows // PARTS
     yz = np.kron(
         narrow(basis(NY, MY)).astype(np.float32), narrow(basis(NZ, MZ)).astype(np.float32)
     )
     blocks = yz.reshape(KQ, CELLS // WIDTH, WIDTH).transpose(1, 0, 2)
     table = jnp.asarray(narrow(blocks))
-    x_whole = basis(NX, MX).reshape(KX, gx, 1, xl_all)
-    x_split = basis(NX, MX).reshape(KX, gx, PARTS, xl)
-    x_tables = [
-        np.stack(
-            [
-                np.kron(split[:, :, part].reshape(KX, -1), np.eye(CHANS))
-                for part in range(split.shape[2])
-            ]
-        )
-        for split in (x_whole, x_split)
-    ]
-    x_in = [jnp.asarray(narrow(x_table)) for x_table in x_tables]
-    x_out = [jnp.asarray(narrow(x_table.transpose(0, 2, 1))) for x_table in x_tables]
+    x_wide = np.kron(basis(NX, MX), np.eye(CHANS))[None]
+    x_in, x_out = jnp.asarray(narrow(x_wide)), jnp.asarray(narrow(x_wide.transpose(0, 2, 1)))
     t_wide = np.kron(basis(NT, MT), np.eye(own))
     t_in, t_out = jnp.asarray(narrow(t_wide.T)), jnp.asarray(narrow(t_wide))
     norm_scale = float(BATCH * NX * NT * NY * NZ) ** (-0.5)
 
-    field = features.reshape(PARTS * rows, cells)
-    cot = cotangent.reshape(PARTS * rows, cells)
-    pick = np.tile(np.eye(CHANS, dtype=np.float32), (rows // CHANS, 1))
-    same = np.kron(np.eye(rows // CHANS, dtype=np.float32), np.ones((CHANS, CHANS), np.float32))
+    field = features.reshape(rows, cells)
+    cot = cotangent.reshape(rows, cells)
+    pick = np.tile(np.eye(CHANS, dtype=np.float32), (group // CHANS, 1))
+    same = np.kron(np.eye(group // CHANS, dtype=np.float32), np.ones((CHANS, CHANS), np.float32))
     picked = jnp.asarray(narrow(pick))
     spread_point = matmul(matmul(picked, point_weight).astype(BF16), picked.T)
     spread_back = matmul(matmul(picked, point_weight.T).astype(BF16), picked.T)
@@ -639,30 +669,22 @@
         jnp.broadcast_to(bias_vector[:, None], (CHANS, LANES)),
         precision=lax.Precision.HIGHEST,
     )
-    part_shape = (gx, ta, xl * CHANS, LANES)
-    whole_shape = (gx, ta, xl_all * CHANS, LANES)
+    spread_shape = (gx, ta, xl * CHANS, LANES)
+    block_shape = (devices, xl * CHANS, LANES)
     packed_weight = pack_weight(spec_weight)
-
-    spread_in = swap(analyse(field, table, xl_all, tl, devices)).reshape(whole_shape)
-    spectrum, *mixed = mix(
-        [spread_in], packed_weight, (mixer, mixer_back, bias), (x_in[0], t_in, x_out[1], t_out), False
-    )
-    output, sums = None, None
-    grads, spread_grad = [], []
-    for part in range(PARTS):
-        returned = swap(mixed[part].reshape(devices, xl * CHANS, LANES))
-        output, grad, sent, sums = middle(
-            returned, field, cot, table, mixer, bias, sums, output, part, xl, tl
-        )
-        grads.append(grad)
-        spread_grad.append(swap(sent).reshape(part_shape))
-    summed = sum_everywhere(sums, devices)
-    grad_modes, mixed_back = mix(
-        spread_grad, packed_weight, (summed,), (x_in[1], t_in, x_out[0], t_out), True
-    )
-    grad_back = swap(mixed_back.reshape(devices, xl_all * CHANS, LANES))
+    tables = (x_in, t_in, x_out, t_out)
+
+    spread_in = swap(analyse(field, table, xl, tl, devices)).reshape(spread_shape)
+    spectrum, mixed = mix([spread_in], packed_weight, (mixer, mixer_back, bias), tables, False)
+    returned = swap(mixed.reshape(block_shape))
+    mixed_field = point_field(field, mixer, bias)
+    output, grad, sent = middle(returned, cot, mixed_field, table, xl, tl)
+    spread_grad = swap(sent).reshape(spread_shape)
+    summed = sum_everywhere(own_sums(field, grad, group), devices)
+    grad_modes, mixed_back = mix([spread_grad], packed_weight, (summed,), tables, True)
+    grad_back = swap(mixed_back.reshape(block_shape))
     grad_spec = outer(spectrum, grad_modes, own)
-    grad_field = last(grad_back, point(grads, mixer_back), table, xl_all, tl)
+    grad_field = last(grad_back, point_grad(grad, mixer_back), table, xl, tl)
     summed = summed * norm_scale
     return (
         output.reshape(features.shape),

time: 185 us -> 184 us (level)
  waiting for transfers between devices: 32.7 us -> 57.1 us
  blocking collectives: 19.3 us -> 0 us
  starting transfers between devices: 36.5 us -> 26.1 us
  Pallas kernels: 85.1 us -> 88.6 us
    all_to_all x5 -> x4, waiting for transfers between devices: 24.6 us -> 45.2 us  [swap(): lax.all_to_all(blocks, ('gx', 'ta'), split_axis=0, concat_axis=0, tiled=T...]
    all_to_all x1 -> x0, blocking collectives: 19.3 us -> none  [swap(): lax.all_to_all(blocks, ('gx', 'ta'), split_axis=0, concat_axis=0, tiled=T...]
    all_to_all x5 -> x4, starting transfers between devices: 27.9 us -> 18.4 us  [swap(): lax.all_to_all(blocks, ('gx', 'ta'), split_axis=0, concat_axis=0, tiled=T...]
    ppermute x5, waiting for transfers between devices: 8.17 us -> 11.9 us  [sum_everywhere(): values = values + lax.ppermute(values, ('gx', 'ta'), pairs)]
    pallas_call x3 -> x4, Pallas kernels: 39 us -> 42.5 us  [the longest x1 25.6 us: middle(): pl.pallas_call(functools.partial(middle_kernel, xl, tl), grid=(chunks,),...]
    unnamed x24 -> x22, local copies, waits for them, and re-layouts: 4.01 us -> 5.14 us
  transfers between devices with their start and end apart: 10 -> 9, of which waited for: 7 -> 8; matrix products, arithmetic and copies ran while one was open for 3% -> 3% of each run, Pallas kernels for 32% -> 20%
where the time goes in v9:
time: 184 us; the launch traced here: 183 us
  Pallas kernels  88.6 us (48%)
  waiting for transfers between devices  57.1 us (31%)
  starting transfers between devices  26.1 us (14%)
  local copies, waits for them, and re-layouts  5.83 us (3%)
  matrix products  2.84 us (2%)
    all_to_all x4, waiting for transfers between devices, swap(): lax.all_to_all(blocks, ('gx', 'ta'), split_axis=0, concat_axis=0, tiled=T...  45.2 us
    pallas_call x1, Pallas kernels, middle(): pl.pallas_call(functools.partial(middle_kernel, xl, tl), grid=(chunks,),...  25.6 us
    all_to_all x4, starting transfers between devices, swap(): lax.all_to_all(blocks, ('gx', 'ta'), split_axis=0, concat_axis=0, tiled=T...  18.4 us
    ppermute x5, waiting for transfers between devices, sum_everywhere(): values = values + lax.ppermute(values, ('gx', 'ta'), pairs)  11.9 us
    pallas_call x2, Pallas kernels, mix(): pl.pallas_call(functools.partial(mix_kernel, backward, len(after)), out_s...  10.8 us
    pallas_call x1, Pallas kernels, pack_weight(): pl.pallas_call(weight_kernel, grid=(KX // per,), in_specs=[pl.BlockSpec((...  9.73 us
    pallas_call x1, Pallas kernels, outer(): pl.pallas_call(outer_kernel, grid=(KX // per,), in_specs=[pl.BlockSpec((p...  9.06 us
    pallas_call x1, Pallas kernels, analyse(): pl.pallas_call(functools.partial(analyse_kernel, xl, tl), in_specs=[pl.Bl...  8.39 us
  transfers between devices with their start and end apart: 9, of which 8 were waited for; matrix products, arithmetic and copies ran while one was open for 3% of the time, Pallas kernels for 20%

profile of v9, /device:TPU:0, one launch (start us, length us, event | category | flops | bytes accessed | tf_op | source)
XLA Modules:
  0.0 182.7 jit_solution(15876115483406315401)
XLA Ops:
  0.6 8.4 %analyse.1 = bf16[32,128,128]{2,1,0:T(8,128)(2,1)} custom-call(bf16[512,4096]{1,0:T(8,128)(2,1)} %bitcast.16, bf16[8,1024,512]{2,1,0:T(8,128)(2,1)} %constant.18.clone.table_ref), custom_call_target="tpu_custom_call" | custom-call | flops 4294967296 | bytes 13631488 | tf_op jit(solution)/shard_map/analyse/pallas_call | solution.py:145
  9.0 7.3 %all-to-all-start = ((bf16[32,128,128]{2,1,0:T(8,128)(2,1)}), bf16[32,128,128]{2,1,0:T(8,128)(2,1)S(1)}, u32[]{:S(2)}, u32[]{:S(2)}) async-start(bf16[32,128,128]{2,1,0:T(8,128)(2,1)} %analyse.1), calls=%async_computation | async-start | bytes 2097152 | tf_op jit(solution)/shard_map/all_to_all | solution.py:629
  16.4 9.7 %pack_weight.1.weight_ref = bf16[32,64,512]{2,1,0:T(8,128)(2,1)} custom-call(f32[32,16,8,8,32]{4,3,2,1,0:T(8,128)} %weight_ref.1), custom_call_target="tpu_custom_call" | custom-call | flops 1048576 | bytes 20971520 | tf_op jit(solution)/shard_map/pack_weight/pallas_call | solution.py:178
  26.1 1.0 fusion.2.refs_2_.bias_ref
  27.1 0.9 fusion.refs_0_.mixer_ref
  29.0 13.6 %all-to-all-done = bf16[32,128,128]{2,1,0:T(8,128)(2,1)S(1)} async-done(((bf16[32,128,128]{2,1,0:T(8,128)(2,1)}), bf16[32,128,128]{2,1,0:T(8,128)(2,1)S(1)}, u32[]{:S(2)}, u32[]{:S(2)}) %all-to-all-start) | async-done | bytes 1048608 | tf_op jit(solution)/shard_map/all_to_all | solution.py:629
  42.6 1.0 copy-done.4
  43.6 4.9 %mix.1 = (f32[256,512]{1,0:T(8,128)}, bf16[8,4,128,128]{3,2,1,0:T(8,128)(2,1)}) custom-call(bf16[32,64,512]{2,1,0:T(8,128)(2,1)} %pack_weight.1.weight_ref, bf16[256,256]{1,0:T(8,128)(2,1)} %fusion.refs_0_.mixer_ref, bf16[256,256]{1,0:T(8,128)(2,1)} %fusion.1.refs_1_.mixer_ref, f32[256,128]{1,0:T(8,128)} %fusion.2.refs_2_.bias_ref, ...), custom_call_target="tpu_custom_call" | custom-call | flops 1073741824 | bytes 9437184 | tf_op jit(solution)/shard_map/mix/pallas_call | solution.py:289
  48.5 3.6 %all-to-all-start.1 = ((bf16[32,128,128]{2,1,0:T(8,128)(2,1)}), bf16[32,128,128]{2,1,0:T(8,128)(2,1)S(1)}, u32[]{:S(2)}, u32[]{:S(2)}) async-start(bf16[32,128,128]{2,1,0:T(8,128)(2,1)} %bitcast.23), calls=%async_computation.1 | async-start | bytes 2097152 | tf_op jit(solution)/shard_map/all_to_all | solution.py:629
  52.1 5.6 %point_field.1.mixed_ref = bf16[8,512,512]{2,1,0:T(8,128)(2,1)} custom-call(bf16[256,256]{1,0:T(8,128)(2,1)} %fusion.refs_0_.mixer_ref, f32[256,128]{1,0:T(8,128)} %fusion.2.refs_2_.bias_ref, bf16[512,4096]{1,0:T(8,128)(2,1)} %bitcast.17), custom_call_target="tpu_custom_call" | custom-call | flops 1073741824 | bytes 8388608 | tf_op jit(solution)/shard_map/point_field/pallas_call | solution.py:368
  57.7 20.6 %all-to-all-done.1.packed_ref = bf16[32,128,128]{2,1,0:T(8,128)(2,1)S(1)} async-done(((bf16[32,128,128]{2,1,0:T(8,128)(2,1)}), bf16[32,128,128]{2,1,0:T(8,128)(2,1)S(1)}, u32[]{:S(2)}, u32[]{:S(2)}) %all-to-all-start.1) | async-done | bytes 1048608 | tf_op jit(solution)/shard_map/all_to_all | solution.py:629
  78.4 1.0 copy-done.5
  79.3 25.6 %middle.1 = (bf16[512,4096]{1,0:T(8,128)(2,1)}, bf16[8,512,512]{2,1,0:T(8,128)(2,1)}, bf16[32,128,128]{2,1,0:T(8,128)(2,1)}) custom-call(bf16[32,128,128]{2,1,0:T(8,128)(2,1)} %copy-done.5, bf16[512,4096]{1,0:T(8,128)(2,1)} %bitcast.25, bf16[8,512,512]{2,1,0:T(8,128)(2,1)} %point_field.1.mixed_ref, bf16[8,1024,512]{2,1,0:T(8,128)(2,1)} %constant.18.clone.table_ref), custom_call_target="tpu_custom_call" | custom-call | flops 8589934592 | bytes 27262976 | tf_op jit(solution)/shard_map/middle/pallas_call | solution.py:535
  104.9 3.8 %all-to-all-start.2 = ((bf16[32,128,128]{2,1,0:T(8,128)(2,1)}), bf16[32,128,128]{2,1,0:T(8,128)(2,1)S(1)}, u32[]{:S(2)}, u32[]{:S(2)}) async-start(bf16[32,128,128]{2,1,0:T(8,128)(2,1)} %get-tuple-element.15), calls=%async_computation.2 | async-start | bytes 2097152 | tf_op jit(solution)/shard_map/all_to_all | solution.py:629
  108.7 5.8 %own_sums.1 = f32[8,128]{1,0:T(8,128)} custom-call(bf16[512,4096]{1,0:T(8,128)(2,1)} %bitcast.18, bf16[8,512,512]{2,1,0:T(8,128)(2,1)} %get-tuple-element.14.grad_ref), custom_call_target="tpu_custom_call" | custom-call | flops 1073741824 | bytes 8388608 | tf_op jit(solution)/shard_map/own_sums/pallas_call | solution.py:459
  114.6 1.3 collective-permute-done
  116.6 1.6 collective-permute-start.1
  118.2 2.0 %collective-permute-done.1 = f32[8,128]{1,0:T(8,128)S(1)} collective-permute-done((f32[8,128]{1,0:T(8,128)S(1)}, f32[8,128]{1,0:T(8,128)S(1)}, u32[]{:S(2)}, u32[]{:S(2)}) %collective-permute-start.1) | collective-permute-done | bytes 4128 | tf_op jit(solution)/shard_map/ppermute | solution.py:636
  120.2 1.6 collective-permute-start.2
  121.8 2.0 %collective-permute-done.2 = f32[8,128]{1,0:T(8,128)S(1)} collective-permute-done((f32[8,128]{1,0:T(8,128)S(1)}, f32[8,128]{1,0:T(8,128)S(1)}, u32[]{:S(2)}, u32[]{:S(2)}) %collective-permute-start.2) | collective-permute-done | bytes 4128 | tf_op jit(solution)/shard_map/ppermute | solution.py:636
  123.9 1.6 collective-permute-start.3
  125.5 2.4 %collective-permute-done.3 = f32[8,128]{1,0:T(8,128)S(1)} collective-permute-done((f32[8,128]{1,0:T(8,128)S(1)}, f32[8,128]{1,0:T(8,128)S(1)}, u32[]{:S(2)}, u32[]{:S(2)}) %collective-permute-start.3) | collective-permute-done | bytes 4128 | tf_op jit(solution)/shard_map/ppermute | solution.py:636
  127.9 2.9 %collective-permute-start.4 = (f32[8,128]{1,0:T(8,128)S(1)}, f32[8,128]{1,0:T(8,128)S(1)}, u32[]{:S(2)}, u32[]{:S(2)}) collective-permute-start(f32[8,128]{1,0:T(8,128)S(1)} %add.18), channel_id=1, source_target_pairs={{0,16},{1,17},{2,18},{3,19},{4,20},{5,21},{6,22},{7,23},{8,24},{9,... | collective-permute-start | bytes 12296 | tf_op jit(solution)/shard_map/ppermute | solution.py:636
  130.8 4.2 %collective-permute-done.4 = f32[8,128]{1,0:T(8,128)S(1)} collective-permute-done((f32[8,128]{1,0:T(8,128)S(1)}, f32[8,128]{1,0:T(8,128)S(1)}, u32[]{:S(2)}, u32[]{:S(2)}) %collective-permute-start.4) | collective-permute-done | bytes 4128 | tf_op jit(solution)/shard_map/ppermute | solution.py:636
  135.6 1.0 copy-done.3
  136.6 5.8 %mix_back.1 = (f32[256,512]{1,0:T(8,128)}, bf16[8,4,128,128]{3,2,1,0:T(8,128)(2,1)}) custom-call(bf16[32,64,512]{2,1,0:T(8,128)(2,1)} %pack_weight.1.weight_ref, f32[8,128]{1,0:T(8,128)} %get-tuple-element.20.refs_0_, bf16[1,256,1024]{2,1,0:T(8,128)(2,1)} %constant.19.clone.refs_3_.refs_1_, bf16[512,512]{1,0:T(8,128)(2,1)} %constant.21.clone.refs_4_.refs_2_, ...), custom_call_target="tpu_custom_call" | custom-call | flops 1073741824 | bytes 9437184 | tf_op jit(solution)/shard_map/mix_back/pallas_call | solution.py:289
  142.4 3.6 %all-to-all-start.3 = ((bf16[32,128,128]{2,1,0:T(8,128)(2,1)}), bf16[32,128,128]{2,1,0:T(8,128)(2,1)S(1)}, u32[]{:S(2)}, u32[]{:S(2)}) async-start(bf16[32,128,128]{2,1,0:T(8,128)(2,1)} %bitcast.22), calls=%async_computation.3 | async-start | bytes 2097152 | tf_op jit(solution)/shard_map/all_to_all | solution.py:629
  146.0 5.5 %point_grad.1.mixed_ref = bf16[8,512,512]{2,1,0:T(8,128)(2,1)} custom-call(bf16[256,256]{1,0:T(8,128)(2,1)} %fusion.1.refs_1_.mixer_ref, bf16[8,512,512]{2,1,0:T(8,128)(2,1)} %get-tuple-element.14.grad_ref), custom_call_target="tpu_custom_call" | custom-call | flops 1073741824 | bytes 8388608 | tf_op jit(solution)/shard_map/point_grad/pallas_call | solution.py:399
  152.2 9.1 %outer.1 = f32[32,16,8,8,32]{4,3,2,1,0:T(8,128)} custom-call(f32[256,512]{1,0:T(8,128)} %get-tuple-element.17.spectrum_ref, f32[256,512]{1,0:T(8,128)} %get-tuple-element.18.grad_ref), custom_call_target="tpu_custom_call" | custom-call | flops 1048576 | bytes 17825792 | tf_op jit(solution)/shard_map/outer/pallas_call | solution.py:329
  161.3 10.9 %all-to-all-done.3.packed_ref = bf16[32,128,128]{2,1,0:T(8,128)(2,1)S(1)} async-done(((bf16[32,128,128]{2,1,0:T(8,128)(2,1)}), bf16[32,128,128]{2,1,0:T(8,128)(2,1)S(1)}, u32[]{:S(2)}, u32[]{:S(2)}) %all-to-all-start.3) | async-done | bytes 1048608 | tf_op jit(solution)/shard_map/all_to_all | solution.py:629
  172.3 2.2 %copy-done.2 = bf16[8,512,512]{2,1,0:T(8,128)(2,1)S(1)} copy-done((bf16[8,512,512]{2,1,0:T(8,128)(2,1)S(1)}, bf16[8,512,512]{2,1,0:T(8,128)(2,1)}, u32[]{:S(2)}) %copy-start.2) | copy-done | bytes 4194328
  174.4 8.1 %last.1 = bf16[512,4096]{1,0:T(8,128)(2,1)} custom-call(bf16[32,128,128]{2,1,0:T(8,128)(2,1)S(1)} %all-to-all-done.3.packed_ref, bf16[8,1024,512]{2,1,0:T(8,128)(2,1)} %constant.18.clone.table_ref, bf16[8,512,512]{2,1,0:T(8,128)(2,1)S(1)} %copy-done.2), custom_call_target="tpu_custom_call" | custom-call | flops 4294967296 | bytes 18874368 | tf_op jit(solution)/shard_map/last/pallas_call | solution.py:605
  (27 shorter events, 3.0 us)
Async XLA Ops:
  0.6 26.5 %copy-start = (bf16[8,8]{1,0:T(8,128)(2,1)S(1)}, bf16[8,8]{1,0:T(8,128)(2,1)}, u32[]{:S(2)}) copy-start(bf16[8,8]{1,0:T(8,128)(2,1)} %param.16) | copy-start | bytes 388
  9.0 33.5 %all-to-all-start = ((bf16[32,128,128]{2,1,0:T(8,128)(2,1)}), bf16[32,128,128]{2,1,0:T(8,128)(2,1)S(1)}, u32[]{:S(2)}, u32[]{:S(2)}) async-start(bf16[32,128,128]{2,1,0:T(8,128)(2,1)} %analyse.1), calls=%async_computation | async-start | bytes 2097152 | tf_op jit(solution)/shard_map/all_to_all | solution.py:629
  16.4 9.8 %copy-start.8 = (f32[256,8]{1,0:T(8,128)S(1)}, f32[256,8]{1,0:T(8,128)}, u32[]{:S(2)}) copy-start(f32[256,8]{1,0:T(8,128)} %constant.25.clone) | copy-start | bytes 24580
  16.4 9.8 %copy-start.10 = (f32[8]{0:T(128)S(1)}, f32[8]{0:T(128)}, u32[]{:S(2)}) copy-start(f32[8]{0:T(128)} %param.17) | copy-start | bytes 100
  16.4 10.7 %copy-start.6 = (f32[256,256]{1,0:T(8,128)S(1)}, f32[256,256]{1,0:T(8,128)}, u32[]{:S(2)}) copy-start(f32[256,256]{1,0:T(8,128)} %constant.24.clone) | copy-start | bytes 786436
  16.4 10.7 %copy-start.7 = (bf16[256,8]{1,0:T(8,128)(2,1)S(1)}, bf16[256,8]{1,0:T(8,128)(2,1)}, u32[]{:S(2)}) copy-start(bf16[256,8]{1,0:T(8,128)(2,1)} %constant.23.clone) | copy-start | bytes 12292
  42.6 1.0 copy-start.4
  48.5 29.9 %all-to-all-start.1 = ((bf16[32,128,128]{2,1,0:T(8,128)(2,1)}), bf16[32,128,128]{2,1,0:T(8,128)(2,1)S(1)}, u32[]{:S(2)}, u32[]{:S(2)}) async-start(bf16[32,128,128]{2,1,0:T(8,128)(2,1)} %bitcast.23), calls=%async_computation.1 | async-start | bytes 2097152 | tf_op jit(solution)/shard_map/all_to_all | solution.py:629
  78.4 1.0 copy-start.5
  104.9 30.7 %all-to-all-start.2 = ((bf16[32,128,128]{2,1,0:T(8,128)(2,1)}), bf16[32,128,128]{2,1,0:T(8,128)(2,1)S(1)}, u32[]{:S(2)}, u32[]{:S(2)}) async-start(bf16[32,128,128]{2,1,0:T(8,128)(2,1)} %get-tuple-element.15), calls=%async_computation.2 | async-start | bytes 2097152 | tf_op jit(solution)/shard_map/all_to_all | solution.py:629
  114.6 1.4 collective-permute-start
  116.6 3.6 %collective-permute-start.1 = (f32[8,128]{1,0:T(8,128)S(1)}, f32[8,128]{1,0:T(8,128)S(1)}, u32[]{:S(2)}, u32[]{:S(2)}) collective-permute-start(f32[8,128]{1,0:T(8,128)S(1)} %add.15), channel_id=1, source_target_pairs={{0,2},{1,3},{2,0},{3,1},{4,6},{5,7},{6,4},{7,5},{8,10},{9,11},{10,... | collective-permute-start | bytes 12296 | tf_op jit(solution)/shard_map/ppermute | solution.py:636
  120.2 3.6 %collective-permute-start.2 = (f32[8,128]{1,0:T(8,128)S(1)}, f32[8,128]{1,0:T(8,128)S(1)}, u32[]{:S(2)}, u32[]{:S(2)}) collective-permute-start(f32[8,128]{1,0:T(8,128)S(1)} %add.16), channel_id=1, source_target_pairs={{0,4},{1,5},{2,6},{3,7},{4,0},{5,1},{6,2},{7,3},{8,12},{9,13},{10,... | collective-permute-start | bytes 12296 | tf_op jit(solution)/shard_map/ppermute | solution.py:636
  123.9 4.0 %collective-permute-start.3 = (f32[8,128]{1,0:T(8,128)S(1)}, f32[8,128]{1,0:T(8,128)S(1)}, u32[]{:S(2)}, u32[]{:S(2)}) collective-permute-start(f32[8,128]{1,0:T(8,128)S(1)} %add.17), channel_id=1, source_target_pairs={{0,8},{1,9},{2,10},{3,11},{4,12},{5,13},{6,14},{7,15},{8,0},{9,1},... | collective-permute-start | bytes 12296 | tf_op jit(solution)/shard_map/ppermute | solution.py:636
  127.9 7.1 %collective-permute-start.4 = (f32[8,128]{1,0:T(8,128)S(1)}, f32[8,128]{1,0:T(8,128)S(1)}, u32[]{:S(2)}, u32[]{:S(2)}) collective-permute-start(f32[8,128]{1,0:T(8,128)S(1)} %add.18), channel_id=1, source_target_pairs={{0,16},{1,17},{2,18},{3,19},{4,20},{5,21},{6,22},{7,23},{8,24},{9,... | collective-permute-start | bytes 12296 | tf_op jit(solution)/shard_map/ppermute | solution.py:636
  135.6 25.7 %copy-start.9 = (f32[8,128]{1,0:T(8,128)}, f32[8,128]{1,0:T(8,128)S(1)}, u32[]{:S(2)}) copy-start(f32[8,128]{1,0:T(8,128)S(1)} %get-tuple-element.19) | copy-start | bytes 12292
  135.6 1.0 copy-start.3
  142.4 29.9 %all-to-all-start.3 = ((bf16[32,128,128]{2,1,0:T(8,128)(2,1)}), bf16[32,128,128]{2,1,0:T(8,128)(2,1)S(1)}, u32[]{:S(2)}, u32[]{:S(2)}) async-start(bf16[32,128,128]{2,1,0:T(8,128)(2,1)} %bitcast.22), calls=%async_computation.3 | async-start | bytes 2097152 | tf_op jit(solution)/shard_map/all_to_all | solution.py:629
  172.3 2.2 %copy-start.2 = (bf16[8,512,512]{2,1,0:T(8,128)(2,1)S(1)}, bf16[8,512,512]{2,1,0:T(8,128)(2,1)}, u32[]{:S(2)}) copy-start(bf16[8,512,512]{2,1,0:T(8,128)(2,1)} %point_grad.1.mixed_ref) | copy-start | bytes 12582916
  174.4 8.1 %copy-start.1 = (bf16[8,8]{1,0:T(8,128)(2,1)S(1)}, bf16[8,8]{1,0:T(8,128)(2,1)}, u32[]{:S(2)}) copy-start(bf16[8,8]{1,0:T(8,128)(2,1)} %param.16) | copy-start | bytes 388

commit v10 on v9

--- a/solution.py
+++ b/solution.py
@@ -383,7 +383,7 @@
     )(mixer, bias, field)
 
 
-def point_grad_kernel(mixer_ref, grad_ref, mixed_ref):
+def point_grad_kernel(mixer_ref, grad_ref, _, mixed_ref):
     rows = mixer_ref.shape[0]
     for at in range(mixed_ref.shape[0]):
         for first in range(0, grad_ref.shape[1], rows):
@@ -391,7 +391,7 @@
             mixed_ref[at, part, :] = matmul(mixer_ref[...], grad_ref[at, part, :]).astype(BF16)
 
 
-def point_grad(grad, mixer):
+def point_grad(grad, mixer, after):
     chunks, rows, _ = grad.shape
     group = mixer.shape[0]
     per = 2
@@ -399,15 +399,19 @@
     return pl.pallas_call(
         point_grad_kernel,
         grid=(chunks // per,),
-        in_specs=[pl.BlockSpec((group, group), lambda n: (0, 0)), blocks],
+        in_specs=[
+            pl.BlockSpec((group, group), lambda n: (0, 0)),
+            blocks,
+            pl.BlockSpec(memory_space=pltpu.HBM),
+        ],
         out_specs=blocks,
         out_shape=jax.ShapeDtypeStruct(grad.shape, BF16),
-        compiler_params=vmem_params(60),
+        compiler_params=vmem_params(16),
         cost_estimate=pl.CostEstimate(
             flops=2 * rows * CELLS * group, bytes_accessed=8 << 20, transcendentals=0
         ),
         name="point_grad",
-    )(mixer, grad)
+    )(mixer, grad, after)
 
 
 def sums_kernel(group, field_ref, grad_ref, sums_ref, total):
@@ -502,25 +506,31 @@
         total[...] = jnp.zeros_like(total)
 
     def build(at):
-        return matmul(modes[...], table_ref[0, :, at])
+        block, first = divmod(at, WIDTH)
+        return matmul(modes[...], table_ref[block, :, first : first + tile])
 
     def pointwise(pre, at):
-        for first in range(0, rows, chunk):
-            part = slice(first, first + chunk)
-            values = pre[part, :] + mixed_ref[0, part, at].astype(F32)
+        block, first = divmod(at, WIDTH)
+        for top in range(0, rows, chunk):
+            part = slice(top, top + chunk)
+            inner, outer = slice(first, first + tile), slice(at, at + tile)
+            values = pre[part, :] + mixed_ref[block, part, inner].astype(F32)
             integral, decay = normal_parts(values)
-            output_ref[part, at] = (values * integral).astype(BF16)
+            output_ref[part, outer] = (values * integral).astype(BF16)
             slope = integral + (values * DENSITY) * decay
-            grad_ref[0, part, at] = (cotangent_ref[part, at].astype(F32) * slope).astype(BF16)
-
-    tiles = [slice(first, first + tile) for first in range(0, width, tile)]
-    ready = build(tiles[0])
-    for index, at in enumerate(tiles):
+            grad = (cotangent_ref[part, outer].astype(F32) * slope).astype(BF16)
+            grad_ref[block, part, inner] = grad
+
+    firsts = range(0, width, tile)
+    ready = build(0)
+    for at in firsts:
         pre = ready
-        if index + 1 < len(tiles):
-            ready = build(tiles[index + 1])
+        if at + tile < width:
+            ready = build(at + tile)
         pointwise(pre, at)
-    total[...] += matmul_turned(table_ref[0], grad_ref[0])
+        block, first = divmod(at + tile, WIDTH)
+        if first == 0:
+            total[...] += matmul_turned(table_ref[block - 1], grad_ref[block - 1])
 
     @pl.when(step == pl.num_programs(0) - 1)
     def _():
@@ -530,16 +540,17 @@
 def middle(packed, cotangent, mixed, table, xl, tl):
     rows = xl * tl * CHANS
     chunks = CELLS // WIDTH
-    tile = pl.BlockSpec((rows, WIDTH), lambda n: (0, n))
-    block = pl.BlockSpec((1, rows, WIDTH), lambda n: (n, 0, 0))
+    per = 2
+    tile = pl.BlockSpec((rows, per * WIDTH), lambda n: (0, n))
+    block = pl.BlockSpec((per, rows, WIDTH), lambda n: (n, 0, 0))
     return pl.pallas_call(
         functools.partial(middle_kernel, xl, tl),
-        grid=(chunks,),
+        grid=(chunks // per,),
         in_specs=[
             pl.BlockSpec(packed.shape, lambda n: (0, 0, 0)),
             tile,
             block,
-            pl.BlockSpec((1, KQ, WIDTH), lambda n: (n, 0, 0)),
+            pl.BlockSpec((per, KQ, WIDTH), lambda n: (n, 0, 0)),
         ],
         out_specs=[tile, block, pl.BlockSpec(memory_space=pl.ANY)],
         out_shape=(
@@ -684,7 +695,7 @@
     grad_modes, mixed_back = mix([spread_grad], packed_weight, (summed,), tables, True)
     grad_back = swap(mixed_back.reshape(block_shape))
     grad_spec = outer(spectrum, grad_modes, own)
-    grad_field = last(grad_back, point_grad(grad, mixer_back), table, xl, tl)
+    grad_field = last(grad_back, point_grad(grad, mixer_back, grad_spec), table, xl, tl)
     summed = summed * norm_scale
     return (
         output.reshape(features.shape),

time: 184 us -> 182 us (0.989)
  local copies, waits for them, and re-layouts: 5.83 us -> 15.8 us
  waiting for transfers between devices: 57.1 us -> 49.3 us
  Pallas kernels: 88.6 us -> 83.4 us
    unnamed x22 -> x30, local copies, waits for them, and re-layouts: 5.14 us -> 15.1 us
    all_to_all x4, waiting for transfers between devices: 45.2 us -> 38.5 us  [swap(): lax.all_to_all(blocks, ('gx', 'ta'), split_axis=0, concat_axis=0, tiled=T...]
    pallas_call x1, Pallas kernels: 5.53 us -> 1.78 us  [point_grad(): pl.pallas_call(point_grad_kernel, grid=(chunks // per,), in_specs=[pl.Blo...]
  transfers between devices with their start and end apart: 9 -> 9, of which waited for: 8 -> 8; matrix products, arithmetic and copies ran while one was open for 3% -> 3% of each run, Pallas kernels for 20% -> 18%
where the time goes in v10:
time: 182 us; the launch traced here: 181 us
  Pallas kernels  83.4 us (46%)
  waiting for transfers between devices  49.3 us (27%)
  starting transfers between devices  27.7 us (15%)
  local copies, waits for them, and re-layouts  15.8 us (9%)
  matrix products  2.83 us (2%)
    all_to_all x4, waiting for transfers between devices, swap(): lax.all_to_all(blocks, ('gx', 'ta'), split_axis=0, concat_axis=0, tiled=T...  38.5 us
    pallas_call x1, Pallas kernels, middle(): pl.pallas_call(functools.partial(middle_kernel, xl, tl), grid=(chunks //...  24.2 us
    all_to_all x4, starting transfers between devices, swap(): lax.all_to_all(blocks, ('gx', 'ta'), split_axis=0, concat_axis=0, tiled=T...  18.6 us
    unnamed x30, local copies, waits for them, and re-layouts  15.1 us
    ppermute x5, waiting for transfers between devices, sum_everywhere(): values = values + lax.ppermute(values, ('gx', 'ta'), pairs)  10.8 us
    pallas_call x2, Pallas kernels, mix(): pl.pallas_call(functools.partial(mix_kernel, backward, len(after)), out_s...  10.8 us
    pallas_call x1, Pallas kernels, pack_weight(): pl.pallas_call(weight_kernel, grid=(KX // per,), in_specs=[pl.BlockSpec((...  9.74 us
    pallas_call x1, Pallas kernels, outer(): pl.pallas_call(outer_kernel, grid=(KX // per,), in_specs=[pl.BlockSpec((p...  9.1 us
  transfers between devices with their start and end apart: 9, of which 8 were waited for; matrix products, arithmetic and copies ran while one was open for 3% of the time, Pallas kernels for 18%

profile of v10, /device:TPU:0, one launch (start us, length us, event | category | flops | bytes accessed | tf_op | source)
XLA Modules:
  0.0 181.4 jit_solution(15832782697737850806)
XLA Ops:
  0.6 8.4 %analyse.1 = bf16[32,128,128]{2,1,0:T(8,128)(2,1)} custom-call(bf16[512,4096]{1,0:T(8,128)(2,1)} %bitcast.16, bf16[8,1024,512]{2,1,0:T(8,128)(2,1)} %constant.18.clone.table_ref), custom_call_target="tpu_custom_call" | custom-call | flops 4294967296 | bytes 13631488 | tf_op jit(solution)/shard_map/analyse/pallas_call | solution.py:145
  9.0 7.3 %all-to-all-start = ((bf16[32,128,128]{2,1,0:T(8,128)(2,1)}), bf16[32,128,128]{2,1,0:T(8,128)(2,1)S(1)}, u32[]{:S(2)}, u32[]{:S(2)}) async-start(bf16[32,128,128]{2,1,0:T(8,128)(2,1)} %analyse.1), calls=%async_computation | async-start | bytes 2097152 | tf_op jit(solution)/shard_map/all_to_all | solution.py:640
  16.4 9.7 %pack_weight.1.weight_ref = bf16[32,64,512]{2,1,0:T(8,128)(2,1)} custom-call(f32[32,16,8,8,32]{4,3,2,1,0:T(8,128)} %weight_ref.1), custom_call_target="tpu_custom_call" | custom-call | flops 1048576 | bytes 20971520 | tf_op jit(solution)/shard_map/pack_weight/pallas_call | solution.py:178
  29.0 13.6 %all-to-all-done = bf16[32,128,128]{2,1,0:T(8,128)(2,1)S(1)} async-done(((bf16[32,128,128]{2,1,0:T(8,128)(2,1)}), bf16[32,128,128]{2,1,0:T(8,128)(2,1)S(1)}, u32[]{:S(2)}, u32[]{:S(2)}) %all-to-all-start) | async-done | bytes 1048608 | tf_op jit(solution)/shard_map/all_to_all | solution.py:640
  43.6 4.9 %mix.1 = (f32[256,512]{1,0:T(8,128)}, bf16[8,4,128,128]{3,2,1,0:T(8,128)(2,1)}) custom-call(bf16[32,64,512]{2,1,0:T(8,128)(2,1)} %pack_weight.1.weight_ref, bf16[256,256]{1,0:T(8,128)(2,1)} %fusion.refs_0_.mixer_ref, bf16[256,256]{1,0:T(8,128)(2,1)} %fusion.1.refs_1_.mixer_ref, f32[256,128]{1,0:T(8,128)} %fusion.2.refs_2_.bias_ref, ...), custom_call_target="tpu_custom_call" | custom-call | flops 1073741824 | bytes 9437184 | tf_op jit(solution)/shard_map/mix/pallas_call | solution.py:289
  48.5 3.8 %all-to-all-start.1 = ((bf16[32,128,128]{2,1,0:T(8,128)(2,1)}), bf16[32,128,128]{2,1,0:T(8,128)(2,1)S(1)}, u32[]{:S(2)}, u32[]{:S(2)}) async-start(bf16[32,128,128]{2,1,0:T(8,128)(2,1)} %bitcast.23), calls=%async_computation.1 | async-start | bytes 2097152 | tf_op jit(solution)/shard_map/all_to_all | solution.py:640
  52.3 5.6 %point_field.1.mixed_ref = bf16[8,512,512]{2,1,0:T(8,128)(2,1)} custom-call(bf16[256,256]{1,0:T(8,128)(2,1)} %fusion.refs_0_.mixer_ref, f32[256,128]{1,0:T(8,128)} %fusion.2.refs_2_.bias_ref, bf16[512,4096]{1,0:T(8,128)(2,1)} %bitcast.17), custom_call_target="tpu_custom_call" | custom-call | flops 1073741824 | bytes 8388608 | tf_op jit(solution)/shard_map/point_field/pallas_call | solution.py:368
  57.9 20.4 %all-to-all-done.1.packed_ref = bf16[32,128,128]{2,1,0:T(8,128)(2,1)S(1)} async-done(((bf16[32,128,128]{2,1,0:T(8,128)(2,1)}), bf16[32,128,128]{2,1,0:T(8,128)(2,1)S(1)}, u32[]{:S(2)}, u32[]{:S(2)}) %all-to-all-start.1) | async-done | bytes 1048608 | tf_op jit(solution)/shard_map/all_to_all | solution.py:640
  78.4 1.0 copy-done.9
  79.4 24.2 %middle.1 = (bf16[512,4096]{1,0:T(8,128)(2,1)}, bf16[8,512,512]{2,1,0:T(8,128)(2,1)}, bf16[32,128,128]{2,1,0:T(8,128)(2,1)}) custom-call(bf16[32,128,128]{2,1,0:T(8,128)(2,1)} %copy-done.9, bf16[512,4096]{1,0:T(8,128)(2,1)} %bitcast.25, bf16[8,512,512]{2,1,0:T(8,128)(2,1)} %point_field.1.mixed_ref, bf16[8,1024,512]{2,1,0:T(8,128)(2,1)} %constant.18.clone.table_ref), custom_call_target="tpu_custom_call" | custom-call | flops 8589934592 | bytes 27262976 | tf_op jit(solution)/shard_map/middle/pallas_call | solution.py:546
  103.5 3.6 %all-to-all-start.2 = ((bf16[32,128,128]{2,1,0:T(8,128)(2,1)}), bf16[32,128,128]{2,1,0:T(8,128)(2,1)S(1)}, u32[]{:S(2)}, u32[]{:S(2)}) async-start(bf16[32,128,128]{2,1,0:T(8,128)(2,1)} %get-tuple-element.15), calls=%async_computation.2 | async-start | bytes 2097152 | tf_op jit(solution)/shard_map/all_to_all | solution.py:640
  107.2 5.8 %own_sums.1 = f32[8,128]{1,0:T(8,128)} custom-call(bf16[512,4096]{1,0:T(8,128)(2,1)} %bitcast.18, bf16[8,512,512]{2,1,0:T(8,128)(2,1)} %get-tuple-element.14.grad_ref), custom_call_target="tpu_custom_call" | custom-call | flops 1073741824 | bytes 8388608 | tf_op jit(solution)/shard_map/own_sums/pallas_call | solution.py:463
  113.2 1.1 collective-permute-done
  115.1 1.8 collective-permute-start.1
  116.8 1.9 %collective-permute-done.1 = f32[8,128]{1,0:T(8,128)S(1)} collective-permute-done((f32[8,128]{1,0:T(8,128)S(1)}, f32[8,128]{1,0:T(8,128)S(1)}, u32[]{:S(2)}, u32[]{:S(2)}) %collective-permute-start.1) | collective-permute-done | bytes 4128 | tf_op jit(solution)/shard_map/ppermute | solution.py:647
  118.7 1.8 collective-permute-start.2
  120.4 1.8 %collective-permute-done.2 = f32[8,128]{1,0:T(8,128)S(1)} collective-permute-done((f32[8,128]{1,0:T(8,128)S(1)}, f32[8,128]{1,0:T(8,128)S(1)}, u32[]{:S(2)}, u32[]{:S(2)}) %collective-permute-start.2) | collective-permute-done | bytes 4128 | tf_op jit(solution)/shard_map/ppermute | solution.py:647
  122.3 1.8 collective-permute-start.3
  124.1 1.8 collective-permute-done.3
  125.9 3.5 %collective-permute-start.4 = (f32[8,128]{1,0:T(8,128)S(1)}, f32[8,128]{1,0:T(8,128)S(1)}, u32[]{:S(2)}, u32[]{:S(2)}) collective-permute-start(f32[8,128]{1,0:T(8,128)S(1)} %add.18), channel_id=1, source_target_pairs={{0,16},{1,17},{2,18},{3,19},{4,20},{5,21},{6,22},{7,23},{8,24},{9,... | collective-permute-start | bytes 12296 | tf_op jit(solution)/shard_map/ppermute | solution.py:647
  129.4 4.2 %collective-permute-done.4 = f32[8,128]{1,0:T(8,128)S(1)} collective-permute-done((f32[8,128]{1,0:T(8,128)S(1)}, f32[8,128]{1,0:T(8,128)S(1)}, u32[]{:S(2)}, u32[]{:S(2)}) %collective-permute-start.4) | collective-permute-done | bytes 4128 | tf_op jit(solution)/shard_map/ppermute | solution.py:647
  134.2 1.0 copy-done.7
  135.2 5.8 %mix_back.1 = (f32[256,512]{1,0:T(8,128)}, bf16[8,4,128,128]{3,2,1,0:T(8,128)(2,1)}) custom-call(bf16[32,64,512]{2,1,0:T(8,128)(2,1)} %pack_weight.1.weight_ref, f32[8,128]{1,0:T(8,128)} %get-tuple-element.20.refs_0_, bf16[1,256,1024]{2,1,0:T(8,128)(2,1)} %constant.19.clone.refs_3_.refs_1_, bf16[512,512]{1,0:T(8,128)(2,1)} %constant.21.clone.refs_4_.refs_2_, ...), custom_call_target="tpu_custom_call" | custom-call | flops 1073741824 | bytes 9437184 | tf_op jit(solution)/shard_map/mix_back/pallas_call | solution.py:289
  141.0 3.8 %all-to-all-start.3 = ((bf16[32,128,128]{2,1,0:T(8,128)(2,1)}), bf16[32,128,128]{2,1,0:T(8,128)(2,1)S(1)}, u32[]{:S(2)}, u32[]{:S(2)}) async-start(bf16[32,128,128]{2,1,0:T(8,128)(2,1)} %bitcast.22), calls=%async_computation.3 | async-start | bytes 2097152 | tf_op jit(solution)/shard_map/all_to_all | solution.py:640
  145.6 9.1 %outer.1._ = f32[32,16,8,8,32]{4,3,2,1,0:T(8,128)} custom-call(f32[256,512]{1,0:T(8,128)} %get-tuple-element.17.spectrum_ref, f32[256,512]{1,0:T(8,128)} %get-tuple-element.18.grad_ref), custom_call_target="tpu_custom_call" | custom-call | flops 1048576 | bytes 17825792 | tf_op jit(solution)/shard_map/outer/pallas_call | solution.py:329
  154.7 5.8 %copy-done.2 = f32[32,16,8,8,32]{4,3,2,1,0:T(8,128)S(1)} copy-done((f32[32,16,8,8,32]{4,3,2,1,0:T(8,128)S(1)}, f32[32,16,8,8,32]{4,3,2,1,0:T(8,128)}, u32[]{:S(2)}) %copy-start.2) | copy-done | bytes 4194328
  160.4 2.2 %copy-done.5 = bf16[8,512,512]{2,1,0:T(8,128)(2,1)S(1)} copy-done((bf16[8,512,512]{2,1,0:T(8,128)(2,1)S(1)}, bf16[8,512,512]{2,1,0:T(8,128)(2,1)}, u32[]{:S(2)}) %copy-start.5) | copy-done | bytes 4194328
  162.6 1.8 point_grad.1.mixed_ref
  164.4 2.0 %copy-done.3 = bf16[8,512,512]{2,1,0:T(8,128)(2,1)} copy-done((bf16[8,512,512]{2,1,0:T(8,128)(2,1)}, bf16[8,512,512]{2,1,0:T(8,128)(2,1)S(1)}, u32[]{:S(2)}) %copy-start.3) | copy-done | bytes 4194328
  166.4 4.5 %all-to-all-done.3.packed_ref = bf16[32,128,128]{2,1,0:T(8,128)(2,1)S(1)} async-done(((bf16[32,128,128]{2,1,0:T(8,128)(2,1)}), bf16[32,128,128]{2,1,0:T(8,128)(2,1)S(1)}, u32[]{:S(2)}, u32[]{:S(2)}) %all-to-all-start.3) | async-done | bytes 1048608 | tf_op jit(solution)/shard_map/all_to_all | solution.py:640
  170.9 2.2 %copy-done.4 = bf16[8,512,512]{2,1,0:T(8,128)(2,1)S(1)} copy-done((bf16[8,512,512]{2,1,0:T(8,128)(2,1)S(1)}, bf16[8,512,512]{2,1,0:T(8,128)(2,1)}, u32[]{:S(2)}) %copy-start.4) | copy-done | bytes 4194328
  173.1 8.1 %last.1 = bf16[512,4096]{1,0:T(8,128)(2,1)} custom-call(bf16[32,128,128]{2,1,0:T(8,128)(2,1)S(1)} %all-to-all-done.3.packed_ref, bf16[8,1024,512]{2,1,0:T(8,128)(2,1)} %constant.18.clone.table_ref, bf16[8,512,512]{2,1,0:T(8,128)(2,1)S(1)} %copy-done.4), custom_call_target="tpu_custom_call" | custom-call | flops 4294967296 | bytes 18874368 | tf_op jit(solution)/shard_map/last/pallas_call | solution.py:616
  (35 shorter events, 6.1 us)
Async XLA Ops:
  0.6 26.5 %copy-start = (bf16[8,8]{1,0:T(8,128)(2,1)S(1)}, bf16[8,8]{1,0:T(8,128)(2,1)}, u32[]{:S(2)}) copy-start(bf16[8,8]{1,0:T(8,128)(2,1)} %param.16) | copy-start | bytes 388
  9.0 33.5 %all-to-all-start = ((bf16[32,128,128]{2,1,0:T(8,128)(2,1)}), bf16[32,128,128]{2,1,0:T(8,128)(2,1)S(1)}, u32[]{:S(2)}, u32[]{:S(2)}) async-start(bf16[32,128,128]{2,1,0:T(8,128)(2,1)} %analyse.1), calls=%async_computation | async-start | bytes 2097152 | tf_op jit(solution)/shard_map/all_to_all | solution.py:640
  16.4 9.8 %copy-start.12 = (f32[256,8]{1,0:T(8,128)S(1)}, f32[256,8]{1,0:T(8,128)}, u32[]{:S(2)}) copy-start(f32[256,8]{1,0:T(8,128)} %constant.25.clone) | copy-start | bytes 24580
  16.4 9.8 %copy-start.14 = (f32[8]{0:T(128)S(1)}, f32[8]{0:T(128)}, u32[]{:S(2)}) copy-start(f32[8]{0:T(128)} %param.17) | copy-start | bytes 100
  16.4 10.7 %copy-start.10 = (f32[256,256]{1,0:T(8,128)S(1)}, f32[256,256]{1,0:T(8,128)}, u32[]{:S(2)}) copy-start(f32[256,256]{1,0:T(8,128)} %constant.24.clone) | copy-start | bytes 786436
  16.4 10.7 %copy-start.11 = (bf16[256,8]{1,0:T(8,128)(2,1)S(1)}, bf16[256,8]{1,0:T(8,128)(2,1)}, u32[]{:S(2)}) copy-start(bf16[256,8]{1,0:T(8,128)(2,1)} %constant.23.clone) | copy-start | bytes 12292
  42.6 1.0 copy-start.8
  48.5 29.9 %all-to-all-start.1 = ((bf16[32,128,128]{2,1,0:T(8,128)(2,1)}), bf16[32,128,128]{2,1,0:T(8,128)(2,1)S(1)}, u32[]{:S(2)}, u32[]{:S(2)}) async-start(bf16[32,128,128]{2,1,0:T(8,128)(2,1)} %bitcast.23), calls=%async_computation.1 | async-start | bytes 2097152 | tf_op jit(solution)/shard_map/all_to_all | solution.py:640
  78.4 1.0 copy-start.9
  103.5 30.7 %all-to-all-start.2 = ((bf16[32,128,128]{2,1,0:T(8,128)(2,1)}), bf16[32,128,128]{2,1,0:T(8,128)(2,1)S(1)}, u32[]{:S(2)}, u32[]{:S(2)}) async-start(bf16[32,128,128]{2,1,0:T(8,128)(2,1)} %get-tuple-element.15), calls=%async_computation.2 | async-start | bytes 2097152 | tf_op jit(solution)/shard_map/all_to_all | solution.py:640
  113.0 1.4 collective-permute-start
  115.1 3.6 %collective-permute-start.1 = (f32[8,128]{1,0:T(8,128)S(1)}, f32[8,128]{1,0:T(8,128)S(1)}, u32[]{:S(2)}, u32[]{:S(2)}) collective-permute-start(f32[8,128]{1,0:T(8,128)S(1)} %add.15), channel_id=1, source_target_pairs={{0,2},{1,3},{2,0},{3,1},{4,6},{5,7},{6,4},{7,5},{8,10},{9,11},{10,... | collective-permute-start | bytes 12296 | tf_op jit(solution)/shard_map/ppermute | solution.py:647
  118.7 3.6 %collective-permute-start.2 = (f32[8,128]{1,0:T(8,128)S(1)}, f32[8,128]{1,0:T(8,128)S(1)}, u32[]{:S(2)}, u32[]{:S(2)}) collective-permute-start(f32[8,128]{1,0:T(8,128)S(1)} %add.16), channel_id=1, source_target_pairs={{0,4},{1,5},{2,6},{3,7},{4,0},{5,1},{6,2},{7,3},{8,12},{9,13},{10,... | collective-permute-start | bytes 12296 | tf_op jit(solution)/shard_map/ppermute | solution.py:647
  122.3 3.6 %collective-permute-start.3 = (f32[8,128]{1,0:T(8,128)S(1)}, f32[8,128]{1,0:T(8,128)S(1)}, u32[]{:S(2)}, u32[]{:S(2)}) collective-permute-start(f32[8,128]{1,0:T(8,128)S(1)} %add.17), channel_id=1, source_target_pairs={{0,8},{1,9},{2,10},{3,11},{4,12},{5,13},{6,14},{7,15},{8,0},{9,1},... | collective-permute-start | bytes 12296 | tf_op jit(solution)/shard_map/ppermute | solution.py:647
  125.9 7.7 %collective-permute-start.4 = (f32[8,128]{1,0:T(8,128)S(1)}, f32[8,128]{1,0:T(8,128)S(1)}, u32[]{:S(2)}, u32[]{:S(2)}) collective-permute-start(f32[8,128]{1,0:T(8,128)S(1)} %add.18), channel_id=1, source_target_pairs={{0,16},{1,17},{2,18},{3,19},{4,20},{5,21},{6,22},{7,23},{8,24},{9,... | collective-permute-start | bytes 12296 | tf_op jit(solution)/shard_map/ppermute | solution.py:647
  134.2 20.5 %copy-start.13 = (f32[8,128]{1,0:T(8,128)}, f32[8,128]{1,0:T(8,128)S(1)}, u32[]{:S(2)}) copy-start(f32[8,128]{1,0:T(8,128)S(1)} %get-tuple-element.19) | copy-start | bytes 12292
  134.2 1.0 copy-start.7
  141.0 29.9 %all-to-all-start.3 = ((bf16[32,128,128]{2,1,0:T(8,128)(2,1)}), bf16[32,128,128]{2,1,0:T(8,128)(2,1)S(1)}, u32[]{:S(2)}, u32[]{:S(2)}) async-start(bf16[32,128,128]{2,1,0:T(8,128)(2,1)} %bitcast.22), calls=%async_computation.3 | async-start | bytes 2097152 | tf_op jit(solution)/shard_map/all_to_all | solution.py:640
  145.6 9.1 %copy-start.6 = (bf16[256,256]{1,0:T(8,128)(2,1)S(1)}, bf16[256,256]{1,0:T(8,128)(2,1)}, u32[]{:S(2)}) copy-start(bf16[256,256]{1,0:T(8,128)(2,1)} %fusion.1.refs_1_.mixer_ref) | copy-start | bytes 393220
  154.7 5.8 %copy-start.2 = (f32[32,16,8,8,32]{4,3,2,1,0:T(8,128)S(1)}, f32[32,16,8,8,32]{4,3,2,1,0:T(8,128)}, u32[]{:S(2)}) copy-start(f32[32,16,8,8,32]{4,3,2,1,0:T(8,128)} %outer.1._) | copy-start | bytes 12582916
  160.4 2.2 %copy-start.5 = (bf16[8,512,512]{2,1,0:T(8,128)(2,1)S(1)}, bf16[8,512,512]{2,1,0:T(8,128)(2,1)}, u32[]{:S(2)}) copy-start(bf16[8,512,512]{2,1,0:T(8,128)(2,1)} %get-tuple-element.14.grad_ref) | copy-start | bytes 12582916
  164.4 2.0 %copy-start.3 = (bf16[8,512,512]{2,1,0:T(8,128)(2,1)}, bf16[8,512,512]{2,1,0:T(8,128)(2,1)S(1)}, u32[]{:S(2)}) copy-start(bf16[8,512,512]{2,1,0:T(8,128)(2,1)S(1)} %point_grad.1.mixed_ref) | copy-start | bytes 12582916
  170.9 2.2 %copy-start.4 = (bf16[8,512,512]{2,1,0:T(8,128)(2,1)S(1)}, bf16[8,512,512]{2,1,0:T(8,128)(2,1)}, u32[]{:S(2)}) copy-start(bf16[8,512,512]{2,1,0:T(8,128)(2,1)} %copy-done.3) | copy-start | bytes 12582916
  173.1 8.1 %copy-start.1 = (bf16[8,8]{1,0:T(8,128)(2,1)S(1)}, bf16[8,8]{1,0:T(8,128)(2,1)}, u32[]{:S(2)}) copy-start(bf16[8,8]{1,0:T(8,128)(2,1)} %param.16) | copy-start | bytes 388

commit v11 on v10

--- a/solution.py
+++ b/solution.py
@@ -383,7 +383,7 @@
     )(mixer, bias, field)
 
 
-def point_grad_kernel(mixer_ref, grad_ref, _, mixed_ref):
+def point_grad_kernel(mixer_ref, grad_ref, mixed_ref):
     rows = mixer_ref.shape[0]
     for at in range(mixed_ref.shape[0]):
         for first in range(0, grad_ref.shape[1], rows):
@@ -391,7 +391,7 @@
             mixed_ref[at, part, :] = matmul(mixer_ref[...], grad_ref[at, part, :]).astype(BF16)
 
 
-def point_grad(grad, mixer, after):
+def point_grad(grad, mixer):
     chunks, rows, _ = grad.shape
     group = mixer.shape[0]
     per = 2
@@ -399,19 +399,15 @@
     return pl.pallas_call(
         point_grad_kernel,
         grid=(chunks // per,),
-        in_specs=[
-            pl.BlockSpec((group, group), lambda n: (0, 0)),
-            blocks,
-            pl.BlockSpec(memory_space=pltpu.HBM),
-        ],
+        in_specs=[pl.BlockSpec((group, group), lambda n: (0, 0)), blocks],
         out_specs=blocks,
         out_shape=jax.ShapeDtypeStruct(grad.shape, BF16),
-        compiler_params=vmem_params(16),
+        compiler_params=vmem_params(60),
         cost_estimate=pl.CostEstimate(
             flops=2 * rows * CELLS * group, bytes_accessed=8 << 20, transcendentals=0
         ),
         name="point_grad",
-    )(mixer, grad, after)
+    )(mixer, grad)
 
 
 def sums_kernel(group, field_ref, grad_ref, sums_ref, total):
@@ -565,7 +561,7 @@
             pltpu.VMEM(packed.shape, BF16),
             pltpu.SemaphoreType.DMA((KQ // LANES,)),
         ],
-        compiler_params=vmem_params(60),
+        compiler_params=vmem_params(50),
         cost_estimate=pl.CostEstimate(
             flops=4 * rows * CELLS * KQ, bytes_accessed=26 << 20, transcendentals=rows * CELLS
         ),
@@ -628,7 +624,7 @@
             pltpu.SemaphoreType.DMA((chunks,)),
             pltpu.SemaphoreType.DMA((chunks,)),
         ],
-        compiler_params=vmem_params(44),
+        compiler_params=vmem_params(50),
         cost_estimate=pl.CostEstimate(
             flops=2 * rows * CELLS * KQ, bytes_accessed=18 << 20, transcendentals=0
         ),
@@ -695,7 +691,7 @@
     grad_modes, mixed_back = mix([spread_grad], packed_weight, (summed,), tables, True)
     grad_back = swap(mixed_back.reshape(block_shape))
     grad_spec = outer(spectrum, grad_modes, own)
-    grad_field = last(grad_back, point_grad(grad, mixer_back, grad_spec), table, xl, tl)
+    grad_field = last(grad_back, point_grad(grad, mixer_back), table, xl, tl)
     summed = summed * norm_scale
     return (
         output.reshape(features.shape),

time: 182 us -> 180 us (0.989)
  local copies, waits for them, and re-layouts: 15.8 us -> 2.68 us
  waiting for transfers between devices: 49.3 us -> 55.6 us
  Pallas kernels: 83.4 us -> 88.1 us
    unnamed x30 -> x18, local copies, waits for them, and re-layouts: 15.1 us -> 1.99 us
    all_to_all x4, waiting for transfers between devices: 38.5 us -> 44.8 us  [swap(): lax.all_to_all(blocks, ('gx', 'ta'), split_axis=0, concat_axis=0, tiled=T...]
    pallas_call x1, Pallas kernels: 1.78 us -> 5.52 us  [point_grad(): pl.pallas_call(point_grad_kernel, grid=(chunks // per,), in_specs=[pl.Blo...]
  transfers between devices with their start and end apart: 9 -> 9, of which waited for: 8 -> 8; matrix products, arithmetic and copies ran while one was open for 3% -> 3% of each run, Pallas kernels for 18% -> 20%
where the time goes in v11:
time: 180 us; the launch traced here: 179 us
  Pallas kernels  88.1 us (49%)
  waiting for transfers between devices  55.6 us (31%)
  starting transfers between devices  27.7 us (15%)
  matrix products  2.84 us (2%)
  local copies, waits for them, and re-layouts  2.68 us (1%)
    all_to_all x4, waiting for transfers between devices, swap(): lax.all_to_all(blocks, ('gx', 'ta'), split_axis=0, concat_axis=0, tiled=T...  44.8 us
    pallas_call x1, Pallas kernels, middle(): pl.pallas_call(functools.partial(middle_kernel, xl, tl), grid=(chunks //...  23.6 us
    all_to_all x4, starting transfers between devices, swap(): lax.all_to_all(blocks, ('gx', 'ta'), split_axis=0, concat_axis=0, tiled=T...  18.6 us
    ppermute x5, waiting for transfers between devices, sum_everywhere(): values = values + lax.ppermute(values, ('gx', 'ta'), pairs)  10.8 us
    pallas_call x2, Pallas kernels, mix(): pl.pallas_call(functools.partial(mix_kernel, backward, len(after)), out_s...  10.8 us
    pallas_call x1, Pallas kernels, pack_weight(): pl.pallas_call(weight_kernel, grid=(KX // per,), in_specs=[pl.BlockSpec((...  9.72 us
    pallas_call x1, Pallas kernels, last(): pl.pallas_call(functools.partial(last_kernel, xl, tl), in_specs=[pl.Block...  9.57 us
    ppermute x5, starting transfers between devices, sum_everywhere(): values = values + lax.ppermute(values, ('gx', 'ta'), pairs)  9.08 us
  transfers between devices with their start and end apart: 9, of which 8 were waited for; matrix products, arithmetic and copies ran while one was open for 3% of the time, Pallas kernels for 20%

profile of v11, /device:TPU:0, one launch (start us, length us, event | category | flops | bytes accessed | tf_op | source)
XLA Modules:
  0.0 179.1 jit_solution(4656311752742084596)
XLA Ops:
  0.6 8.4 %analyse.1 = bf16[32,128,128]{2,1,0:T(8,128)(2,1)} custom-call(bf16[512,4096]{1,0:T(8,128)(2,1)} %bitcast.16, bf16[8,1024,512]{2,1,0:T(8,128)(2,1)} %constant.18.clone.table_ref), custom_call_target="tpu_custom_call" | custom-call | flops 4294967296 | bytes 13631488 | tf_op jit(solution)/shard_map/analyse/pallas_call | solution.py:145
  9.0 7.3 %all-to-all-start = ((bf16[32,128,128]{2,1,0:T(8,128)(2,1)}), bf16[32,128,128]{2,1,0:T(8,128)(2,1)S(1)}, u32[]{:S(2)}, u32[]{:S(2)}) async-start(bf16[32,128,128]{2,1,0:T(8,128)(2,1)} %analyse.1), calls=%async_computation | async-start | bytes 2097152 | tf_op jit(solution)/shard_map/all_to_all | solution.py:636
  16.4 9.7 %pack_weight.1.weight_ref = bf16[32,64,512]{2,1,0:T(8,128)(2,1)} custom-call(f32[32,16,8,8,32]{4,3,2,1,0:T(8,128)} %weight_ref.1), custom_call_target="tpu_custom_call" | custom-call | flops 1048576 | bytes 20971520 | tf_op jit(solution)/shard_map/pack_weight/pallas_call | solution.py:178
  26.1 1.0 fusion.2.refs_2_.bias_ref
  27.1 0.9 fusion.refs_0_.mixer_ref
  28.0 0.9 fusion.1.refs_1_.mixer_ref
  29.0 13.6 %all-to-all-done = bf16[32,128,128]{2,1,0:T(8,128)(2,1)S(1)} async-done(((bf16[32,128,128]{2,1,0:T(8,128)(2,1)}), bf16[32,128,128]{2,1,0:T(8,128)(2,1)S(1)}, u32[]{:S(2)}, u32[]{:S(2)}) %all-to-all-start) | async-done | bytes 1048608 | tf_op jit(solution)/shard_map/all_to_all | solution.py:636
  42.6 1.0 copy-done.3
  43.6 4.9 %mix.1 = (f32[256,512]{1,0:T(8,128)}, bf16[8,4,128,128]{3,2,1,0:T(8,128)(2,1)}) custom-call(bf16[32,64,512]{2,1,0:T(8,128)(2,1)} %pack_weight.1.weight_ref, bf16[256,256]{1,0:T(8,128)(2,1)} %fusion.refs_0_.mixer_ref, bf16[256,256]{1,0:T(8,128)(2,1)} %fusion.1.refs_1_.mixer_ref, f32[256,128]{1,0:T(8,128)} %fusion.2.refs_2_.bias_ref, ...), custom_call_target="tpu_custom_call" | custom-call | flops 1073741824 | bytes 9437184 | tf_op jit(solution)/shard_map/mix/pallas_call | solution.py:289
  48.5 3.8 %all-to-all-start.1 = ((bf16[32,128,128]{2,1,0:T(8,128)(2,1)}), bf16[32,128,128]{2,1,0:T(8,128)(2,1)S(1)}, u32[]{:S(2)}, u32[]{:S(2)}) async-start(bf16[32,128,128]{2,1,0:T(8,128)(2,1)} %bitcast.23), calls=%async_computation.1 | async-start | bytes 2097152 | tf_op jit(solution)/shard_map/all_to_all | solution.py:636
  52.3 5.6 %point_field.1.mixed_ref = bf16[8,512,512]{2,1,0:T(8,128)(2,1)} custom-call(bf16[256,256]{1,0:T(8,128)(2,1)} %fusion.refs_0_.mixer_ref, f32[256,128]{1,0:T(8,128)} %fusion.2.refs_2_.bias_ref, bf16[512,4096]{1,0:T(8,128)(2,1)} %bitcast.17), custom_call_target="tpu_custom_call" | custom-call | flops 1073741824 | bytes 8388608 | tf_op jit(solution)/shard_map/point_field/pallas_call | solution.py:368
  57.9 20.4 %all-to-all-done.1.packed_ref = bf16[32,128,128]{2,1,0:T(8,128)(2,1)S(1)} async-done(((bf16[32,128,128]{2,1,0:T(8,128)(2,1)}), bf16[32,128,128]{2,1,0:T(8,128)(2,1)S(1)}, u32[]{:S(2)}, u32[]{:S(2)}) %all-to-all-start.1) | async-done | bytes 1048608 | tf_op jit(solution)/shard_map/all_to_all | solution.py:636
  78.4 23.6 %middle.1 = (bf16[512,4096]{1,0:T(8,128)(2,1)}, bf16[8,512,512]{2,1,0:T(8,128)(2,1)}, bf16[32,128,128]{2,1,0:T(8,128)(2,1)}) custom-call(bf16[32,128,128]{2,1,0:T(8,128)(2,1)S(1)} %all-to-all-done.1.packed_ref, bf16[512,4096]{1,0:T(8,128)(2,1)} %bitcast.25, bf16[8,512,512]{2,1,0:T(8,128)(2,1)} %point_field.1.mixed_ref, ...), custom_call_target="tpu_custom_call" | custom-call | flops 8589934592 | bytes 27262976 | tf_op jit(solution)/shard_map/middle/pallas_call | solution.py:542
  102.0 3.6 %all-to-all-start.2 = ((bf16[32,128,128]{2,1,0:T(8,128)(2,1)}), bf16[32,128,128]{2,1,0:T(8,128)(2,1)S(1)}, u32[]{:S(2)}, u32[]{:S(2)}) async-start(bf16[32,128,128]{2,1,0:T(8,128)(2,1)} %get-tuple-element.15), calls=%async_computation.2 | async-start | bytes 2097152 | tf_op jit(solution)/shard_map/all_to_all | solution.py:636
  105.6 5.8 %own_sums.1 = f32[8,128]{1,0:T(8,128)} custom-call(bf16[512,4096]{1,0:T(8,128)(2,1)} %bitcast.18, bf16[8,512,512]{2,1,0:T(8,128)(2,1)} %get-tuple-element.14.grad_ref), custom_call_target="tpu_custom_call" | custom-call | flops 1073741824 | bytes 8388608 | tf_op jit(solution)/shard_map/own_sums/pallas_call | solution.py:459
  111.7 1.1 collective-permute-done
  113.5 1.8 collective-permute-start.1
  115.3 1.8 %collective-permute-done.1 = f32[8,128]{1,0:T(8,128)S(1)} collective-permute-done((f32[8,128]{1,0:T(8,128)S(1)}, f32[8,128]{1,0:T(8,128)S(1)}, u32[]{:S(2)}, u32[]{:S(2)}) %collective-permute-start.1) | collective-permute-done | bytes 4128 | tf_op jit(solution)/shard_map/ppermute | solution.py:643
  117.1 1.8 collective-permute-start.2
  118.9 1.8 %collective-permute-done.2 = f32[8,128]{1,0:T(8,128)S(1)} collective-permute-done((f32[8,128]{1,0:T(8,128)S(1)}, f32[8,128]{1,0:T(8,128)S(1)}, u32[]{:S(2)}, u32[]{:S(2)}) %collective-permute-start.2) | collective-permute-done | bytes 4128 | tf_op jit(solution)/shard_map/ppermute | solution.py:643
  120.8 1.8 %collective-permute-start.3 = (f32[8,128]{1,0:T(8,128)S(1)}, f32[8,128]{1,0:T(8,128)S(1)}, u32[]{:S(2)}, u32[]{:S(2)}) collective-permute-start(f32[8,128]{1,0:T(8,128)S(1)} %add.17), channel_id=1, source_target_pairs={{0,8},{1,9},{2,10},{3,11},{4,12},{5,13},{6,14},{7,15},{8,0},{9,1},... | collective-permute-start | bytes 12296 | tf_op jit(solution)/shard_map/ppermute | solution.py:643
  122.6 1.8 %collective-permute-done.3 = f32[8,128]{1,0:T(8,128)S(1)} collective-permute-done((f32[8,128]{1,0:T(8,128)S(1)}, f32[8,128]{1,0:T(8,128)S(1)}, u32[]{:S(2)}, u32[]{:S(2)}) %collective-permute-start.3) | collective-permute-done | bytes 4128 | tf_op jit(solution)/shard_map/ppermute | solution.py:643
  124.4 3.5 %collective-permute-start.4 = (f32[8,128]{1,0:T(8,128)S(1)}, f32[8,128]{1,0:T(8,128)S(1)}, u32[]{:S(2)}, u32[]{:S(2)}) collective-permute-start(f32[8,128]{1,0:T(8,128)S(1)} %add.18), channel_id=1, source_target_pairs={{0,16},{1,17},{2,18},{3,19},{4,20},{5,21},{6,22},{7,23},{8,24},{9,... | collective-permute-start | bytes 12296 | tf_op jit(solution)/shard_map/ppermute | solution.py:643
  127.9 4.2 %collective-permute-done.4 = f32[8,128]{1,0:T(8,128)S(1)} collective-permute-done((f32[8,128]{1,0:T(8,128)S(1)}, f32[8,128]{1,0:T(8,128)S(1)}, u32[]{:S(2)}, u32[]{:S(2)}) %collective-permute-start.4) | collective-permute-done | bytes 4128 | tf_op jit(solution)/shard_map/ppermute | solution.py:643
  132.7 1.0 copy-done.2
  133.6 5.8 %mix_back.1 = (f32[256,512]{1,0:T(8,128)}, bf16[8,4,128,128]{3,2,1,0:T(8,128)(2,1)}) custom-call(bf16[32,64,512]{2,1,0:T(8,128)(2,1)} %pack_weight.1.weight_ref, f32[8,128]{1,0:T(8,128)} %get-tuple-element.20.refs_0_, bf16[1,256,1024]{2,1,0:T(8,128)(2,1)} %constant.19.clone.refs_3_.refs_1_, bf16[512,512]{1,0:T(8,128)(2,1)} %constant.21.clone.refs_4_.refs_2_, ...), custom_call_target="tpu_custom_call" | custom-call | flops 1073741824 | bytes 9437184 | tf_op jit(solution)/shard_map/mix_back/pallas_call | solution.py:289
  139.5 3.8 %all-to-all-start.3 = ((bf16[32,128,128]{2,1,0:T(8,128)(2,1)}), bf16[32,128,128]{2,1,0:T(8,128)(2,1)S(1)}, u32[]{:S(2)}, u32[]{:S(2)}) async-start(bf16[32,128,128]{2,1,0:T(8,128)(2,1)} %bitcast.22), calls=%async_computation.3 | async-start | bytes 2097152 | tf_op jit(solution)/shard_map/all_to_all | solution.py:636
  143.3 5.5 %point_grad.1.mixed_ref = bf16[8,512,512]{2,1,0:T(8,128)(2,1)} custom-call(bf16[256,256]{1,0:T(8,128)(2,1)} %fusion.1.refs_1_.mixer_ref, bf16[8,512,512]{2,1,0:T(8,128)(2,1)} %get-tuple-element.14.grad_ref), custom_call_target="tpu_custom_call" | custom-call | flops 1073741824 | bytes 8388608 | tf_op jit(solution)/shard_map/point_grad/pallas_call | solution.py:399
  148.8 0.7 slice_reduce_fusion
  149.5 9.1 %outer.1 = f32[32,16,8,8,32]{4,3,2,1,0:T(8,128)} custom-call(f32[256,512]{1,0:T(8,128)} %get-tuple-element.17.spectrum_ref, f32[256,512]{1,0:T(8,128)} %get-tuple-element.18.grad_ref), custom_call_target="tpu_custom_call" | custom-call | flops 1048576 | bytes 17825792 | tf_op jit(solution)/shard_map/outer/pallas_call | solution.py:329
  158.6 10.7 %all-to-all-done.3.packed_ref = bf16[32,128,128]{2,1,0:T(8,128)(2,1)S(1)} async-done(((bf16[32,128,128]{2,1,0:T(8,128)(2,1)}), bf16[32,128,128]{2,1,0:T(8,128)(2,1)S(1)}, u32[]{:S(2)}, u32[]{:S(2)}) %all-to-all-start.3) | async-done | bytes 1048608 | tf_op jit(solution)/shard_map/all_to_all | solution.py:636
  169.3 9.6 %last.1 = bf16[512,4096]{1,0:T(8,128)(2,1)} custom-call(bf16[32,128,128]{2,1,0:T(8,128)(2,1)S(1)} %all-to-all-done.3.packed_ref, bf16[8,1024,512]{2,1,0:T(8,128)(2,1)} %constant.18.clone.table_ref, bf16[8,512,512]{2,1,0:T(8,128)(2,1)} %point_grad.1.mixed_ref), custom_call_target="tpu_custom_call" | custom-call | flops 4294967296 | bytes 18874368 | tf_op jit(solution)/shard_map/last/pallas_call | solution.py:612
  (23 shorter events, 1.6 us)
Async XLA Ops:
  0.6 26.5 %copy-start = (bf16[8,8]{1,0:T(8,128)(2,1)S(1)}, bf16[8,8]{1,0:T(8,128)(2,1)}, u32[]{:S(2)}) copy-start(bf16[8,8]{1,0:T(8,128)(2,1)} %param.16) | copy-start | bytes 388
  9.0 33.5 %all-to-all-start = ((bf16[32,128,128]{2,1,0:T(8,128)(2,1)}), bf16[32,128,128]{2,1,0:T(8,128)(2,1)S(1)}, u32[]{:S(2)}, u32[]{:S(2)}) async-start(bf16[32,128,128]{2,1,0:T(8,128)(2,1)} %analyse.1), calls=%async_computation | async-start | bytes 2097152 | tf_op jit(solution)/shard_map/all_to_all | solution.py:636
  16.4 9.8 %copy-start.6 = (f32[256,8]{1,0:T(8,128)S(1)}, f32[256,8]{1,0:T(8,128)}, u32[]{:S(2)}) copy-start(f32[256,8]{1,0:T(8,128)} %constant.25.clone) | copy-start | bytes 24580
  16.4 9.8 %copy-start.8 = (f32[8]{0:T(128)S(1)}, f32[8]{0:T(128)}, u32[]{:S(2)}) copy-start(f32[8]{0:T(128)} %param.17) | copy-start | bytes 100
  16.4 10.7 %copy-start.4 = (f32[256,256]{1,0:T(8,128)S(1)}, f32[256,256]{1,0:T(8,128)}, u32[]{:S(2)}) copy-start(f32[256,256]{1,0:T(8,128)} %constant.24.clone) | copy-start | bytes 786436
  16.4 10.7 %copy-start.5 = (bf16[256,8]{1,0:T(8,128)(2,1)S(1)}, bf16[256,8]{1,0:T(8,128)(2,1)}, u32[]{:S(2)}) copy-start(bf16[256,8]{1,0:T(8,128)(2,1)} %constant.23.clone) | copy-start | bytes 12292
  42.6 1.0 copy-start.3
  48.5 29.9 %all-to-all-start.1 = ((bf16[32,128,128]{2,1,0:T(8,128)(2,1)}), bf16[32,128,128]{2,1,0:T(8,128)(2,1)S(1)}, u32[]{:S(2)}, u32[]{:S(2)}) async-start(bf16[32,128,128]{2,1,0:T(8,128)(2,1)} %bitcast.23), calls=%async_computation.1 | async-start | bytes 2097152 | tf_op jit(solution)/shard_map/all_to_all | solution.py:636
  102.0 30.6 %all-to-all-start.2 = ((bf16[32,128,128]{2,1,0:T(8,128)(2,1)}), bf16[32,128,128]{2,1,0:T(8,128)(2,1)S(1)}, u32[]{:S(2)}, u32[]{:S(2)}) async-start(bf16[32,128,128]{2,1,0:T(8,128)(2,1)} %get-tuple-element.15), calls=%async_computation.2 | async-start | bytes 2097152 | tf_op jit(solution)/shard_map/all_to_all | solution.py:636
  111.5 1.4 collective-permute-start
  113.5 3.6 %collective-permute-start.1 = (f32[8,128]{1,0:T(8,128)S(1)}, f32[8,128]{1,0:T(8,128)S(1)}, u32[]{:S(2)}, u32[]{:S(2)}) collective-permute-start(f32[8,128]{1,0:T(8,128)S(1)} %add.15), channel_id=1, source_target_pairs={{0,2},{1,3},{2,0},{3,1},{4,6},{5,7},{6,4},{7,5},{8,10},{9,11},{10,... | collective-permute-start | bytes 12296 | tf_op jit(solution)/shard_map/ppermute | solution.py:643
  117.1 3.6 %collective-permute-start.2 = (f32[8,128]{1,0:T(8,128)S(1)}, f32[8,128]{1,0:T(8,128)S(1)}, u32[]{:S(2)}, u32[]{:S(2)}) collective-permute-start(f32[8,128]{1,0:T(8,128)S(1)} %add.16), channel_id=1, source_target_pairs={{0,4},{1,5},{2,6},{3,7},{4,0},{5,1},{6,2},{7,3},{8,12},{9,13},{10,... | collective-permute-start | bytes 12296 | tf_op jit(solution)/shard_map/ppermute | solution.py:643
  120.8 3.6 %collective-permute-start.3 = (f32[8,128]{1,0:T(8,128)S(1)}, f32[8,128]{1,0:T(8,128)S(1)}, u32[]{:S(2)}, u32[]{:S(2)}) collective-permute-start(f32[8,128]{1,0:T(8,128)S(1)} %add.17), channel_id=1, source_target_pairs={{0,8},{1,9},{2,10},{3,11},{4,12},{5,13},{6,14},{7,15},{8,0},{9,1},... | collective-permute-start | bytes 12296 | tf_op jit(solution)/shard_map/ppermute | solution.py:643
  124.4 7.7 %collective-permute-start.4 = (f32[8,128]{1,0:T(8,128)S(1)}, f32[8,128]{1,0:T(8,128)S(1)}, u32[]{:S(2)}, u32[]{:S(2)}) collective-permute-start(f32[8,128]{1,0:T(8,128)S(1)} %add.18), channel_id=1, source_target_pairs={{0,16},{1,17},{2,18},{3,19},{4,20},{5,21},{6,22},{7,23},{8,24},{9,... | collective-permute-start | bytes 12296 | tf_op jit(solution)/shard_map/ppermute | solution.py:643
  132.6 25.9 %copy-start.7 = (f32[8,128]{1,0:T(8,128)}, f32[8,128]{1,0:T(8,128)S(1)}, u32[]{:S(2)}) copy-start(f32[8,128]{1,0:T(8,128)S(1)} %get-tuple-element.19) | copy-start | bytes 12292
  132.6 1.0 copy-start.2
  139.5 29.9 %all-to-all-start.3 = ((bf16[32,128,128]{2,1,0:T(8,128)(2,1)}), bf16[32,128,128]{2,1,0:T(8,128)(2,1)S(1)}, u32[]{:S(2)}, u32[]{:S(2)}) async-start(bf16[32,128,128]{2,1,0:T(8,128)(2,1)} %bitcast.22), calls=%async_computation.3 | async-start | bytes 2097152 | tf_op jit(solution)/shard_map/all_to_all | solution.py:636
  169.3 9.6 %copy-start.1 = (bf16[8,8]{1,0:T(8,128)(2,1)S(1)}, bf16[8,8]{1,0:T(8,128)(2,1)}, u32[]{:S(2)}) copy-start(bf16[8,8]{1,0:T(8,128)(2,1)} %param.16) | copy-start | bytes 388

commit v12 on v11

--- a/solution.py
+++ b/solution.py
@@ -303,7 +303,7 @@
             pltpu.SemaphoreType.DMA((len(spreads),)),
             pltpu.SemaphoreType.DMA((outs, 4 // outs)),
         ],
-        compiler_params=vmem_params(60),
+        compiler_params=vmem_params(50),
         cost_estimate=pl.CostEstimate(flops=1 << 30, bytes_accessed=9 << 20, transcendentals=0),
         name="mix_back" if backward else "mix",
     )(weight, *after, *tables, *spreads)

time: 180 us -> 180 us (level)
  local copies, waits for them, and re-layouts: 2.68 us -> 5.27 us
  Pallas kernels: 88.1 us -> 86 us
    unnamed x18 -> x36, local copies, waits for them, and re-layouts: 1.99 us -> 4.57 us
    pallas_call x2, Pallas kernels: 10.8 us -> 8.61 us  [mix(): pl.pallas_call(functools.partial(mix_kernel, backward, len(after)), out_s...]
  transfers between devices with their start and end apart: 9 -> 9, of which waited for: 8 -> 8; matrix products, arithmetic and copies ran while one was open for 3% -> 2% of each run, Pallas kernels for 20% -> 20%
where the time goes in v12:
time: 180 us; the launch traced here: 179 us
  Pallas kernels  86 us (48%)
  waiting for transfers between devices  55.3 us (31%)
  starting transfers between devices  27.6 us (15%)
  local copies, waits for them, and re-layouts  5.27 us (3%)
  matrix products  2.94 us (2%)
    all_to_all x4, waiting for transfers between devices, swap(): lax.all_to_all(blocks, ('gx', 'ta'), split_axis=0, concat_axis=0, tiled=T...  44.5 us
    pallas_call x1, Pallas kernels, middle(): pl.pallas_call(functools.partial(middle_kernel, xl, tl), grid=(chunks //...  23.6 us
    all_to_all x4, starting transfers between devices, swap(): lax.all_to_all(blocks, ('gx', 'ta'), split_axis=0, concat_axis=0, tiled=T...  18.6 us
    ppermute x5, waiting for transfers between devices, sum_everywhere(): values = values + lax.ppermute(values, ('gx', 'ta'), pairs)  10.8 us
    pallas_call x1, Pallas kernels, pack_weight(): pl.pallas_call(weight_kernel, grid=(KX // per,), in_specs=[pl.BlockSpec((...  9.83 us
    pallas_call x1, Pallas kernels, last(): pl.pallas_call(functools.partial(last_kernel, xl, tl), in_specs=[pl.Block...  9.58 us
    ppermute x5, starting transfers between devices, sum_everywhere(): values = values + lax.ppermute(values, ('gx', 'ta'), pairs)  9.08 us
    pallas_call x1, Pallas kernels, outer(): pl.pallas_call(outer_kernel, grid=(KX // per,), in_specs=[pl.BlockSpec((p...  9.06 us
  transfers between devices with their start and end apart: 9, of which 8 were waited for; matrix products, arithmetic and copies ran while one was open for 2% of the time, Pallas kernels for 20%

profile of v12, /device:TPU:0, one launch (start us, length us, event | category | flops | bytes accessed | tf_op | source)
XLA Modules:
  0.0 178.9 jit_solution(6753722467016834898)
XLA Ops:
  0.6 8.4 %analyse.1 = bf16[32,128,128]{2,1,0:T(8,128)(2,1)} custom-call(bf16[512,4096]{1,0:T(8,128)(2,1)} %bitcast.17, bf16[8,1024,512]{2,1,0:T(8,128)(2,1)} %constant.18.clone.table_ref), custom_call_target="tpu_custom_call" | custom-call | flops 4294967296 | bytes 13631488 | tf_op jit(solution)/shard_map/analyse/pallas_call | solution.py:145
  9.0 7.3 %all-to-all-start = ((bf16[32,128,128]{2,1,0:T(8,128)(2,1)}), bf16[32,128,128]{2,1,0:T(8,128)(2,1)S(1)}, u32[]{:S(2)}, u32[]{:S(2)}) async-start(bf16[32,128,128]{2,1,0:T(8,128)(2,1)} %analyse.1), calls=%async_computation | async-start | bytes 2097152 | tf_op jit(solution)/shard_map/all_to_all | solution.py:636
  16.4 9.8 %pack_weight.1.weight_ref = bf16[32,64,512]{2,1,0:T(8,128)(2,1)} custom-call(f32[32,16,8,8,32]{4,3,2,1,0:T(8,128)} %weight_ref.1), custom_call_target="tpu_custom_call" | custom-call | flops 1048576 | bytes 20971520 | tf_op jit(solution)/shard_map/pack_weight/pallas_call | solution.py:178
  26.6 1.3 fusion.refs_0_.mixer_ref
  27.9 1.4 fusion.1.refs_1_.mixer_ref
  29.3 13.3 %all-to-all-done = bf16[32,128,128]{2,1,0:T(8,128)(2,1)S(1)} async-done(((bf16[32,128,128]{2,1,0:T(8,128)(2,1)}), bf16[32,128,128]{2,1,0:T(8,128)(2,1)S(1)}, u32[]{:S(2)}, u32[]{:S(2)}) %all-to-all-start) | async-done | bytes 1048608 | tf_op jit(solution)/shard_map/all_to_all | solution.py:636
  42.6 1.0 copy-done.13
  43.6 3.8 %mix.1 = (f32[256,512]{1,0:T(8,128)S(1)}, bf16[8,4,128,128]{3,2,1,0:T(8,128)(2,1)S(1)}) custom-call(bf16[32,64,512]{2,1,0:T(8,128)(2,1)} %pack_weight.1.weight_ref, bf16[256,256]{1,0:T(8,128)(2,1)S(1)} %fusion.refs_0_.mixer_ref, bf16[256,256]{1,0:T(8,128)(2,1)S(1)} %fusion.1.refs_1_.mixer_ref, f32[256,128]{1,0:T(8,128)S(1)} %fusion.2.refs_2_.bias_ref, ...), custom_call_target="tpu_custom_call" | custom-call | flops 1073741824 | bytes 9437184 | tf_op jit(solution)/shard_map/mix/pallas_call | solution.py:289
  47.4 1.0 copy-done.9
  48.3 0.8 copy-done.10
  49.1 3.8 %all-to-all-start.1 = ((bf16[32,128,128]{2,1,0:T(8,128)(2,1)}), bf16[32,128,128]{2,1,0:T(8,128)(2,1)S(1)}, u32[]{:S(2)}, u32[]{:S(2)}) async-start(bf16[32,128,128]{2,1,0:T(8,128)(2,1)} %bitcast.16), calls=%async_computation.1 | async-start | bytes 2097152 | tf_op jit(solution)/shard_map/all_to_all | solution.py:636
  52.9 5.6 %point_field.1.mixed_ref = bf16[8,512,512]{2,1,0:T(8,128)(2,1)} custom-call(bf16[256,256]{1,0:T(8,128)(2,1)} %copy-done.8, f32[256,128]{1,0:T(8,128)} %copy-done.6, bf16[512,4096]{1,0:T(8,128)(2,1)} %bitcast.18), custom_call_target="tpu_custom_call" | custom-call | flops 1073741824 | bytes 8388608 | tf_op jit(solution)/shard_map/point_field/pallas_call | solution.py:368
  58.5 20.4 %all-to-all-done.1.packed_ref = bf16[32,128,128]{2,1,0:T(8,128)(2,1)S(1)} async-done(((bf16[32,128,128]{2,1,0:T(8,128)(2,1)}), bf16[32,128,128]{2,1,0:T(8,128)(2,1)S(1)}, u32[]{:S(2)}, u32[]{:S(2)}) %all-to-all-start.1) | async-done | bytes 1048608 | tf_op jit(solution)/shard_map/all_to_all | solution.py:636
  79.0 23.6 %middle.1 = (bf16[512,4096]{1,0:T(8,128)(2,1)}, bf16[8,512,512]{2,1,0:T(8,128)(2,1)}, bf16[32,128,128]{2,1,0:T(8,128)(2,1)}) custom-call(bf16[32,128,128]{2,1,0:T(8,128)(2,1)S(1)} %all-to-all-done.1.packed_ref, bf16[512,4096]{1,0:T(8,128)(2,1)} %bitcast.24, bf16[8,512,512]{2,1,0:T(8,128)(2,1)} %point_field.1.mixed_ref, ...), custom_call_target="tpu_custom_call" | custom-call | flops 8589934592 | bytes 27262976 | tf_op jit(solution)/shard_map/middle/pallas_call | solution.py:542
  102.6 3.6 %all-to-all-start.2 = ((bf16[32,128,128]{2,1,0:T(8,128)(2,1)}), bf16[32,128,128]{2,1,0:T(8,128)(2,1)S(1)}, u32[]{:S(2)}, u32[]{:S(2)}) async-start(bf16[32,128,128]{2,1,0:T(8,128)(2,1)} %get-tuple-element.15), calls=%async_computation.2 | async-start | bytes 2097152 | tf_op jit(solution)/shard_map/all_to_all | solution.py:636
  106.2 5.8 %own_sums.1 = f32[8,128]{1,0:T(8,128)} custom-call(bf16[512,4096]{1,0:T(8,128)(2,1)} %bitcast.19, bf16[8,512,512]{2,1,0:T(8,128)(2,1)} %get-tuple-element.14.grad_ref), custom_call_target="tpu_custom_call" | custom-call | flops 1073741824 | bytes 8388608 | tf_op jit(solution)/shard_map/own_sums/pallas_call | solution.py:459
  112.3 1.1 collective-permute-done
  114.1 1.8 collective-permute-start.1
  115.9 1.9 %collective-permute-done.1 = f32[8,128]{1,0:T(8,128)S(1)} collective-permute-done((f32[8,128]{1,0:T(8,128)S(1)}, f32[8,128]{1,0:T(8,128)S(1)}, u32[]{:S(2)}, u32[]{:S(2)}) %collective-permute-start.1) | collective-permute-done | bytes 4128 | tf_op jit(solution)/shard_map/ppermute | solution.py:643
  117.7 1.8 collective-permute-start.2
  119.5 1.8 %collective-permute-done.2 = f32[8,128]{1,0:T(8,128)S(1)} collective-permute-done((f32[8,128]{1,0:T(8,128)S(1)}, f32[8,128]{1,0:T(8,128)S(1)}, u32[]{:S(2)}, u32[]{:S(2)}) %collective-permute-start.2) | collective-permute-done | bytes 4128 | tf_op jit(solution)/shard_map/ppermute | solution.py:643
  121.3 1.8 %collective-permute-start.3 = (f32[8,128]{1,0:T(8,128)S(1)}, f32[8,128]{1,0:T(8,128)S(1)}, u32[]{:S(2)}, u32[]{:S(2)}) collective-permute-start(f32[8,128]{1,0:T(8,128)S(1)} %add.17), channel_id=1, source_target_pairs={{0,8},{1,9},{2,10},{3,11},{4,12},{5,13},{6,14},{7,15},{8,0},{9,1},... | collective-permute-start | bytes 12296 | tf_op jit(solution)/shard_map/ppermute | solution.py:643
  123.2 1.8 %collective-permute-done.3 = f32[8,128]{1,0:T(8,128)S(1)} collective-permute-done((f32[8,128]{1,0:T(8,128)S(1)}, f32[8,128]{1,0:T(8,128)S(1)}, u32[]{:S(2)}, u32[]{:S(2)}) %collective-permute-start.3) | collective-permute-done | bytes 4128 | tf_op jit(solution)/shard_map/ppermute | solution.py:643
  125.0 3.5 %collective-permute-start.4 = (f32[8,128]{1,0:T(8,128)S(1)}, f32[8,128]{1,0:T(8,128)S(1)}, u32[]{:S(2)}, u32[]{:S(2)}) collective-permute-start(f32[8,128]{1,0:T(8,128)S(1)} %add.18), channel_id=1, source_target_pairs={{0,16},{1,17},{2,18},{3,19},{4,20},{5,21},{6,22},{7,23},{8,24},{9,... | collective-permute-start | bytes 12296 | tf_op jit(solution)/shard_map/ppermute | solution.py:643
  128.4 4.2 %collective-permute-done.4 = f32[8,128]{1,0:T(8,128)S(1)} collective-permute-done((f32[8,128]{1,0:T(8,128)S(1)}, f32[8,128]{1,0:T(8,128)S(1)}, u32[]{:S(2)}, u32[]{:S(2)}) %collective-permute-start.4) | collective-permute-done | bytes 4128 | tf_op jit(solution)/shard_map/ppermute | solution.py:643
  132.7 1.0 copy-done.12
  133.6 4.9 %mix_back.1 = (f32[256,512]{1,0:T(8,128)S(1)}, bf16[8,4,128,128]{3,2,1,0:T(8,128)(2,1)}) custom-call(bf16[32,64,512]{2,1,0:T(8,128)(2,1)} %pack_weight.1.weight_ref, f32[8,128]{1,0:T(8,128)S(1)} %get-tuple-element.20.refs_0_, bf16[1,256,1024]{2,1,0:T(8,128)(2,1)S(1)} %copy-done.2, bf16[512,512]{1,0:T(8,128)(2,1)S(1)} %copy-done.3, ...), custom_call_target="tpu_custom_call" | custom-call | flops 1073741824 | bytes 9437184 | tf_op jit(solution)/shard_map/mix_back/pallas_call | solution.py:289
  139.3 3.8 %all-to-all-start.3 = ((bf16[32,128,128]{2,1,0:T(8,128)(2,1)}), bf16[32,128,128]{2,1,0:T(8,128)(2,1)S(1)}, u32[]{:S(2)}, u32[]{:S(2)}) async-start(bf16[32,128,128]{2,1,0:T(8,128)(2,1)} %bitcast.6), calls=%async_computation.3 | async-start | bytes 2097152 | tf_op jit(solution)/shard_map/all_to_all | solution.py:636
  143.1 5.5 %point_grad.1.mixed_ref = bf16[8,512,512]{2,1,0:T(8,128)(2,1)} custom-call(bf16[256,256]{1,0:T(8,128)(2,1)} %copy-done.7, bf16[8,512,512]{2,1,0:T(8,128)(2,1)} %get-tuple-element.14.grad_ref), custom_call_target="tpu_custom_call" | custom-call | flops 1073741824 | bytes 8388608 | tf_op jit(solution)/shard_map/point_grad/pallas_call | solution.py:399
  149.4 9.1 %outer.1 = f32[32,16,8,8,32]{4,3,2,1,0:T(8,128)} custom-call(f32[256,512]{1,0:T(8,128)} %copy-done.10, f32[256,512]{1,0:T(8,128)} %copy-done.11), custom_call_target="tpu_custom_call" | custom-call | flops 1048576 | bytes 17825792 | tf_op jit(solution)/shard_map/outer/pallas_call | solution.py:329
  158.4 10.7 %all-to-all-done.3.packed_ref = bf16[32,128,128]{2,1,0:T(8,128)(2,1)S(1)} async-done(((bf16[32,128,128]{2,1,0:T(8,128)(2,1)}), bf16[32,128,128]{2,1,0:T(8,128)(2,1)S(1)}, u32[]{:S(2)}, u32[]{:S(2)}) %all-to-all-start.3) | async-done | bytes 1048608 | tf_op jit(solution)/shard_map/all_to_all | solution.py:636
  169.2 9.6 %last.1 = bf16[512,4096]{1,0:T(8,128)(2,1)} custom-call(bf16[32,128,128]{2,1,0:T(8,128)(2,1)S(1)} %all-to-all-done.3.packed_ref, bf16[8,1024,512]{2,1,0:T(8,128)(2,1)} %constant.18.clone.table_ref, bf16[8,512,512]{2,1,0:T(8,128)(2,1)} %point_grad.1.mixed_ref), custom_call_target="tpu_custom_call" | custom-call | flops 4294967296 | bytes 18874368 | tf_op jit(solution)/shard_map/last/pallas_call | solution.py:612
  (41 shorter events, 2.8 us)
Async XLA Ops:
  0.6 26.0 %copy-start = (bf16[8,8]{1,0:T(8,128)(2,1)S(1)}, bf16[8,8]{1,0:T(8,128)(2,1)}, u32[]{:S(2)}) copy-start(bf16[8,8]{1,0:T(8,128)(2,1)} %param.16) | copy-start | bytes 388
  9.0 33.5 %all-to-all-start = ((bf16[32,128,128]{2,1,0:T(8,128)(2,1)}), bf16[32,128,128]{2,1,0:T(8,128)(2,1)S(1)}, u32[]{:S(2)}, u32[]{:S(2)}) async-start(bf16[32,128,128]{2,1,0:T(8,128)(2,1)} %analyse.1), calls=%async_computation | async-start | bytes 2097152 | tf_op jit(solution)/shard_map/all_to_all | solution.py:636
  16.4 9.9 %copy-start.15 = (f32[256,8]{1,0:T(8,128)S(1)}, f32[256,8]{1,0:T(8,128)}, u32[]{:S(2)}) copy-start(f32[256,8]{1,0:T(8,128)} %constant.25.clone) | copy-start | bytes 24580
  16.4 9.9 %copy-start.17 = (f32[8]{0:T(128)S(1)}, f32[8]{0:T(128)}, u32[]{:S(2)}) copy-start(f32[8]{0:T(128)} %param.17) | copy-start | bytes 100
  16.4 10.2 %copy-start.14 = (bf16[256,8]{1,0:T(8,128)(2,1)S(1)}, bf16[256,8]{1,0:T(8,128)(2,1)}, u32[]{:S(2)}) copy-start(bf16[256,8]{1,0:T(8,128)(2,1)} %constant.23.clone) | copy-start | bytes 12292
  16.4 27.2 %copy-start.2 = (bf16[1,256,1024]{2,1,0:T(8,128)(2,1)S(1)}, bf16[1,256,1024]{2,1,0:T(8,128)(2,1)}, u32[]{:S(2)}) copy-start(bf16[1,256,1024]{2,1,0:T(8,128)(2,1)} %constant.19.clone.refs_3_.refs_1_) | copy-start | bytes 1572868
  16.4 27.2 %copy-start.3 = (bf16[512,512]{1,0:T(8,128)(2,1)S(1)}, bf16[512,512]{1,0:T(8,128)(2,1)}, u32[]{:S(2)}) copy-start(bf16[512,512]{1,0:T(8,128)(2,1)} %constant.21.clone.refs_4_.refs_2_) | copy-start | bytes 1572868
  16.4 27.2 %copy-start.4 = (bf16[1,1024,256]{2,1,0:T(8,128)(2,1)S(1)}, bf16[1,1024,256]{2,1,0:T(8,128)(2,1)}, u32[]{:S(2)}) copy-start(bf16[1,1024,256]{2,1,0:T(8,128)(2,1)} %constant.20.clone.refs_5_.refs_3_) | copy-start | bytes 1572868
  16.4 27.1 %copy-start.5 = (bf16[512,512]{1,0:T(8,128)(2,1)S(1)}, bf16[512,512]{1,0:T(8,128)(2,1)}, u32[]{:S(2)}) copy-start(bf16[512,512]{1,0:T(8,128)(2,1)} %constant.22.clone.refs_6_.refs_4_) | copy-start | bytes 1572868
  26.6 22.5 %copy-start.6 = (f32[256,128]{1,0:T(8,128)}, f32[256,128]{1,0:T(8,128)S(1)}, u32[]{:S(2)}) copy-start(f32[256,128]{1,0:T(8,128)S(1)} %fusion.2.refs_2_.bias_ref) | copy-start | bytes 393220
  27.9 25.0 %copy-start.8 = (bf16[256,256]{1,0:T(8,128)(2,1)}, bf16[256,256]{1,0:T(8,128)(2,1)S(1)}, u32[]{:S(2)}) copy-start(bf16[256,256]{1,0:T(8,128)(2,1)S(1)} %fusion.refs_0_.mixer_ref) | copy-start | bytes 393220
  29.3 29.3 %copy-start.7 = (bf16[256,256]{1,0:T(8,128)(2,1)}, bf16[256,256]{1,0:T(8,128)(2,1)S(1)}, u32[]{:S(2)}) copy-start(bf16[256,256]{1,0:T(8,128)(2,1)S(1)} %fusion.1.refs_1_.mixer_ref) | copy-start | bytes 393220
  42.6 1.0 copy-start.13
  47.3 1.0 copy-start.9
  48.3 0.8 copy-start.10
  49.1 29.9 %all-to-all-start.1 = ((bf16[32,128,128]{2,1,0:T(8,128)(2,1)}), bf16[32,128,128]{2,1,0:T(8,128)(2,1)S(1)}, u32[]{:S(2)}, u32[]{:S(2)}) async-start(bf16[32,128,128]{2,1,0:T(8,128)(2,1)} %bitcast.16), calls=%async_computation.1 | async-start | bytes 2097152 | tf_op jit(solution)/shard_map/all_to_all | solution.py:636
  102.6 30.1 %all-to-all-start.2 = ((bf16[32,128,128]{2,1,0:T(8,128)(2,1)}), bf16[32,128,128]{2,1,0:T(8,128)(2,1)S(1)}, u32[]{:S(2)}, u32[]{:S(2)}) async-start(bf16[32,128,128]{2,1,0:T(8,128)(2,1)} %get-tuple-element.15), calls=%async_computation.2 | async-start | bytes 2097152 | tf_op jit(solution)/shard_map/all_to_all | solution.py:636
  112.0 1.4 collective-permute-start
  114.1 3.6 %collective-permute-start.1 = (f32[8,128]{1,0:T(8,128)S(1)}, f32[8,128]{1,0:T(8,128)S(1)}, u32[]{:S(2)}, u32[]{:S(2)}) collective-permute-start(f32[8,128]{1,0:T(8,128)S(1)} %add.15), channel_id=1, source_target_pairs={{0,2},{1,3},{2,0},{3,1},{4,6},{5,7},{6,4},{7,5},{8,10},{9,11},{10,... | collective-permute-start | bytes 12296 | tf_op jit(solution)/shard_map/ppermute | solution.py:643
  117.7 3.6 %collective-permute-start.2 = (f32[8,128]{1,0:T(8,128)S(1)}, f32[8,128]{1,0:T(8,128)S(1)}, u32[]{:S(2)}, u32[]{:S(2)}) collective-permute-start(f32[8,128]{1,0:T(8,128)S(1)} %add.16), channel_id=1, source_target_pairs={{0,4},{1,5},{2,6},{3,7},{4,0},{5,1},{6,2},{7,3},{8,12},{9,13},{10,... | collective-permute-start | bytes 12296 | tf_op jit(solution)/shard_map/ppermute | solution.py:643
  121.3 3.6 %collective-permute-start.3 = (f32[8,128]{1,0:T(8,128)S(1)}, f32[8,128]{1,0:T(8,128)S(1)}, u32[]{:S(2)}, u32[]{:S(2)}) collective-permute-start(f32[8,128]{1,0:T(8,128)S(1)} %add.17), channel_id=1, source_target_pairs={{0,8},{1,9},{2,10},{3,11},{4,12},{5,13},{6,14},{7,15},{8,0},{9,1},... | collective-permute-start | bytes 12296 | tf_op jit(solution)/shard_map/ppermute | solution.py:643
  125.0 7.7 %collective-permute-start.4 = (f32[8,128]{1,0:T(8,128)S(1)}, f32[8,128]{1,0:T(8,128)S(1)}, u32[]{:S(2)}, u32[]{:S(2)}) collective-permute-start(f32[8,128]{1,0:T(8,128)S(1)} %add.18), channel_id=1, source_target_pairs={{0,16},{1,17},{2,18},{3,19},{4,20},{5,21},{6,22},{7,23},{8,24},{9,... | collective-permute-start | bytes 12296 | tf_op jit(solution)/shard_map/ppermute | solution.py:643
  132.6 25.8 %copy-start.16 = (f32[8,128]{1,0:T(8,128)}, f32[8,128]{1,0:T(8,128)S(1)}, u32[]{:S(2)}) copy-start(f32[8,128]{1,0:T(8,128)S(1)} %get-tuple-element.19) | copy-start | bytes 12292
  132.7 1.0 copy-start.12
  138.5 0.8 copy-start.11
  139.3 29.9 %all-to-all-start.3 = ((bf16[32,128,128]{2,1,0:T(8,128)(2,1)}), bf16[32,128,128]{2,1,0:T(8,128)(2,1)S(1)}, u32[]{:S(2)}, u32[]{:S(2)}) async-start(bf16[32,128,128]{2,1,0:T(8,128)(2,1)} %bitcast.6), calls=%async_computation.3 | async-start | bytes 2097152 | tf_op jit(solution)/shard_map/all_to_all | solution.py:636
  169.1 9.6 %copy-start.1 = (bf16[8,8]{1,0:T(8,128)(2,1)S(1)}, bf16[8,8]{1,0:T(8,128)(2,1)}, u32[]{:S(2)}) copy-start(bf16[8,8]{1,0:T(8,128)(2,1)} %param.16) | copy-start | bytes 388

commit v13 on v11

--- a/solution.py
+++ b/solution.py
@@ -107,7 +107,7 @@
     xl, tl, field_ref, table_ref, packed_ref, field, table, total, held, field_sems, table_sems, sems
 ):
     chunks = table.shape[0]
-    ahead = 4
+    ahead = 8
     fetches = []
     for at in range(chunks):
         lanes = slice(at * WIDTH, (at + 1) * WIDTH)
@@ -572,7 +572,7 @@
 def last_kernel(xl, tl, packed_ref, table_ref, mixed_ref, field_ref, *scratch):
     wide, modes, table, mixed, field, table_sems, mixed_sems, field_sems = scratch
     chunks = table.shape[0]
-    ahead = 4
+    ahead = 8
     fetches, sends = [], []
     for at in range(chunks):
         lanes = slice(at * WIDTH, (at + 1) * WIDTH)

time: 180 us -> 180 us (level)
  no operation moved by 1% of the time
where the time goes in v13:
time: 180 us; the launch traced here: 179 us
  Pallas kernels  88.1 us (49%)
  waiting for transfers between devices  55.6 us (31%)
  starting transfers between devices  27.7 us (15%)
  matrix products  2.84 us (2%)
  local copies, waits for them, and re-layouts  2.68 us (1%)
    all_to_all x4, waiting for transfers between devices, swap(): lax.all_to_all(blocks, ('gx', 'ta'), split_axis=0, concat_axis=0, tiled=T...  44.8 us
    pallas_call x1, Pallas kernels, middle(): pl.pallas_call(functools.partial(middle_kernel, xl, tl), grid=(chunks //...  23.6 us
    all_to_all x4, starting transfers between devices, swap(): lax.all_to_all(blocks, ('gx', 'ta'), split_axis=0, concat_axis=0, tiled=T...  18.6 us
    ppermute x5, waiting for transfers between devices, sum_everywhere(): values = values + lax.ppermute(values, ('gx', 'ta'), pairs)  10.8 us
    pallas_call x2, Pallas kernels, mix(): pl.pallas_call(functools.partial(mix_kernel, backward, len(after)), out_s...  10.8 us
    pallas_call x1, Pallas kernels, pack_weight(): pl.pallas_call(weight_kernel, grid=(KX // per,), in_specs=[pl.BlockSpec((...  9.72 us
    pallas_call x1, Pallas kernels, last(): pl.pallas_call(functools.partial(last_kernel, xl, tl), in_specs=[pl.Block...  9.58 us
    ppermute x5, starting transfers between devices, sum_everywhere(): values = values + lax.ppermute(values, ('gx', 'ta'), pairs)  9.08 us
  transfers between devices with their start and end apart: 9, of which 8 were waited for; matrix products, arithmetic and copies ran while one was open for 3% of the time, Pallas kernels for 20%

profile of v13, /device:TPU:0, one launch (start us, length us, event | category | flops | bytes accessed | tf_op | source)
XLA Modules:
  0.0 179.1 jit_solution(3819337708760016446)
XLA Ops:
  0.6 8.4 %analyse.1 = bf16[32,128,128]{2,1,0:T(8,128)(2,1)} custom-call(bf16[512,4096]{1,0:T(8,128)(2,1)} %bitcast.16, bf16[8,1024,512]{2,1,0:T(8,128)(2,1)} %constant.18.clone.table_ref), custom_call_target="tpu_custom_call" | custom-call | flops 4294967296 | bytes 13631488 | tf_op jit(solution)/shard_map/analyse/pallas_call | solution.py:145
  9.0 7.3 %all-to-all-start = ((bf16[32,128,128]{2,1,0:T(8,128)(2,1)}), bf16[32,128,128]{2,1,0:T(8,128)(2,1)S(1)}, u32[]{:S(2)}, u32[]{:S(2)}) async-start(bf16[32,128,128]{2,1,0:T(8,128)(2,1)} %analyse.1), calls=%async_computation | async-start | bytes 2097152 | tf_op jit(solution)/shard_map/all_to_all | solution.py:636
  16.4 9.7 %pack_weight.1.weight_ref = bf16[32,64,512]{2,1,0:T(8,128)(2,1)} custom-call(f32[32,16,8,8,32]{4,3,2,1,0:T(8,128)} %weight_ref.1), custom_call_target="tpu_custom_call" | custom-call | flops 1048576 | bytes 20971520 | tf_op jit(solution)/shard_map/pack_weight/pallas_call | solution.py:178
  26.1 1.0 fusion.2.refs_2_.bias_ref
  27.1 0.9 fusion.refs_0_.mixer_ref
  28.0 0.9 fusion.1.refs_1_.mixer_ref
  29.0 13.6 %all-to-all-done = bf16[32,128,128]{2,1,0:T(8,128)(2,1)S(1)} async-done(((bf16[32,128,128]{2,1,0:T(8,128)(2,1)}), bf16[32,128,128]{2,1,0:T(8,128)(2,1)S(1)}, u32[]{:S(2)}, u32[]{:S(2)}) %all-to-all-start) | async-done | bytes 1048608 | tf_op jit(solution)/shard_map/all_to_all | solution.py:636
  42.6 1.0 copy-done.3
  43.6 4.9 %mix.1 = (f32[256,512]{1,0:T(8,128)}, bf16[8,4,128,128]{3,2,1,0:T(8,128)(2,1)}) custom-call(bf16[32,64,512]{2,1,0:T(8,128)(2,1)} %pack_weight.1.weight_ref, bf16[256,256]{1,0:T(8,128)(2,1)} %fusion.refs_0_.mixer_ref, bf16[256,256]{1,0:T(8,128)(2,1)} %fusion.1.refs_1_.mixer_ref, f32[256,128]{1,0:T(8,128)} %fusion.2.refs_2_.bias_ref, ...), custom_call_target="tpu_custom_call" | custom-call | flops 1073741824 | bytes 9437184 | tf_op jit(solution)/shard_map/mix/pallas_call | solution.py:289
  48.5 3.8 %all-to-all-start.1 = ((bf16[32,128,128]{2,1,0:T(8,128)(2,1)}), bf16[32,128,128]{2,1,0:T(8,128)(2,1)S(1)}, u32[]{:S(2)}, u32[]{:S(2)}) async-start(bf16[32,128,128]{2,1,0:T(8,128)(2,1)} %bitcast.23), calls=%async_computation.1 | async-start | bytes 2097152 | tf_op jit(solution)/shard_map/all_to_all | solution.py:636
  52.3 5.6 %point_field.1.mixed_ref = bf16[8,512,512]{2,1,0:T(8,128)(2,1)} custom-call(bf16[256,256]{1,0:T(8,128)(2,1)} %fusion.refs_0_.mixer_ref, f32[256,128]{1,0:T(8,128)} %fusion.2.refs_2_.bias_ref, bf16[512,4096]{1,0:T(8,128)(2,1)} %bitcast.17), custom_call_target="tpu_custom_call" | custom-call | flops 1073741824 | bytes 8388608 | tf_op jit(solution)/shard_map/point_field/pallas_call | solution.py:368
  57.9 20.4 %all-to-all-done.1.packed_ref = bf16[32,128,128]{2,1,0:T(8,128)(2,1)S(1)} async-done(((bf16[32,128,128]{2,1,0:T(8,128)(2,1)}), bf16[32,128,128]{2,1,0:T(8,128)(2,1)S(1)}, u32[]{:S(2)}, u32[]{:S(2)}) %all-to-all-start.1) | async-done | bytes 1048608 | tf_op jit(solution)/shard_map/all_to_all | solution.py:636
  78.4 23.6 %middle.1 = (bf16[512,4096]{1,0:T(8,128)(2,1)}, bf16[8,512,512]{2,1,0:T(8,128)(2,1)}, bf16[32,128,128]{2,1,0:T(8,128)(2,1)}) custom-call(bf16[32,128,128]{2,1,0:T(8,128)(2,1)S(1)} %all-to-all-done.1.packed_ref, bf16[512,4096]{1,0:T(8,128)(2,1)} %bitcast.25, bf16[8,512,512]{2,1,0:T(8,128)(2,1)} %point_field.1.mixed_ref, ...), custom_call_target="tpu_custom_call" | custom-call | flops 8589934592 | bytes 27262976 | tf_op jit(solution)/shard_map/middle/pallas_call | solution.py:542
  102.0 3.6 %all-to-all-start.2 = ((bf16[32,128,128]{2,1,0:T(8,128)(2,1)}), bf16[32,128,128]{2,1,0:T(8,128)(2,1)S(1)}, u32[]{:S(2)}, u32[]{:S(2)}) async-start(bf16[32,128,128]{2,1,0:T(8,128)(2,1)} %get-tuple-element.15), calls=%async_computation.2 | async-start | bytes 2097152 | tf_op jit(solution)/shard_map/all_to_all | solution.py:636
  105.6 5.8 %own_sums.1 = f32[8,128]{1,0:T(8,128)} custom-call(bf16[512,4096]{1,0:T(8,128)(2,1)} %bitcast.18, bf16[8,512,512]{2,1,0:T(8,128)(2,1)} %get-tuple-element.14.grad_ref), custom_call_target="tpu_custom_call" | custom-call | flops 1073741824 | bytes 8388608 | tf_op jit(solution)/shard_map/own_sums/pallas_call | solution.py:459
  111.7 1.1 collective-permute-done
  113.5 1.8 collective-permute-start.1
  115.3 1.8 %collective-permute-done.1 = f32[8,128]{1,0:T(8,128)S(1)} collective-permute-done((f32[8,128]{1,0:T(8,128)S(1)}, f32[8,128]{1,0:T(8,128)S(1)}, u32[]{:S(2)}, u32[]{:S(2)}) %collective-permute-start.1) | collective-permute-done | bytes 4128 | tf_op jit(solution)/shard_map/ppermute | solution.py:643
  117.1 1.8 collective-permute-start.2
  118.9 1.8 %collective-permute-done.2 = f32[8,128]{1,0:T(8,128)S(1)} collective-permute-done((f32[8,128]{1,0:T(8,128)S(1)}, f32[8,128]{1,0:T(8,128)S(1)}, u32[]{:S(2)}, u32[]{:S(2)}) %collective-permute-start.2) | collective-permute-done | bytes 4128 | tf_op jit(solution)/shard_map/ppermute | solution.py:643
  120.8 1.8 %collective-permute-start.3 = (f32[8,128]{1,0:T(8,128)S(1)}, f32[8,128]{1,0:T(8,128)S(1)}, u32[]{:S(2)}, u32[]{:S(2)}) collective-permute-start(f32[8,128]{1,0:T(8,128)S(1)} %add.17), channel_id=1, source_target_pairs={{0,8},{1,9},{2,10},{3,11},{4,12},{5,13},{6,14},{7,15},{8,0},{9,1},... | collective-permute-start | bytes 12296 | tf_op jit(solution)/shard_map/ppermute | solution.py:643
  122.6 1.8 %collective-permute-done.3 = f32[8,128]{1,0:T(8,128)S(1)} collective-permute-done((f32[8,128]{1,0:T(8,128)S(1)}, f32[8,128]{1,0:T(8,128)S(1)}, u32[]{:S(2)}, u32[]{:S(2)}) %collective-permute-start.3) | collective-permute-done | bytes 4128 | tf_op jit(solution)/shard_map/ppermute | solution.py:643
  124.4 3.5 %collective-permute-start.4 = (f32[8,128]{1,0:T(8,128)S(1)}, f32[8,128]{1,0:T(8,128)S(1)}, u32[]{:S(2)}, u32[]{:S(2)}) collective-permute-start(f32[8,128]{1,0:T(8,128)S(1)} %add.18), channel_id=1, source_target_pairs={{0,16},{1,17},{2,18},{3,19},{4,20},{5,21},{6,22},{7,23},{8,24},{9,... | collective-permute-start | bytes 12296 | tf_op jit(solution)/shard_map/ppermute | solution.py:643
  127.9 4.2 %collective-permute-done.4 = f32[8,128]{1,0:T(8,128)S(1)} collective-permute-done((f32[8,128]{1,0:T(8,128)S(1)}, f32[8,128]{1,0:T(8,128)S(1)}, u32[]{:S(2)}, u32[]{:S(2)}) %collective-permute-start.4) | collective-permute-done | bytes 4128 | tf_op jit(solution)/shard_map/ppermute | solution.py:643
  132.7 1.0 copy-done.2
  133.6 5.8 %mix_back.1 = (f32[256,512]{1,0:T(8,128)}, bf16[8,4,128,128]{3,2,1,0:T(8,128)(2,1)}) custom-call(bf16[32,64,512]{2,1,0:T(8,128)(2,1)} %pack_weight.1.weight_ref, f32[8,128]{1,0:T(8,128)} %get-tuple-element.20.refs_0_, bf16[1,256,1024]{2,1,0:T(8,128)(2,1)} %constant.19.clone.refs_3_.refs_1_, bf16[512,512]{1,0:T(8,128)(2,1)} %constant.21.clone.refs_4_.refs_2_, ...), custom_call_target="tpu_custom_call" | custom-call | flops 1073741824 | bytes 9437184 | tf_op jit(solution)/shard_map/mix_back/pallas_call | solution.py:289
  139.5 3.8 %all-to-all-start.3 = ((bf16[32,128,128]{2,1,0:T(8,128)(2,1)}), bf16[32,128,128]{2,1,0:T(8,128)(2,1)S(1)}, u32[]{:S(2)}, u32[]{:S(2)}) async-start(bf16[32,128,128]{2,1,0:T(8,128)(2,1)} %bitcast.22), calls=%async_computation.3 | async-start | bytes 2097152 | tf_op jit(solution)/shard_map/all_to_all | solution.py:636
  143.3 5.5 %point_grad.1.mixed_ref = bf16[8,512,512]{2,1,0:T(8,128)(2,1)} custom-call(bf16[256,256]{1,0:T(8,128)(2,1)} %fusion.1.refs_1_.mixer_ref, bf16[8,512,512]{2,1,0:T(8,128)(2,1)} %get-tuple-element.14.grad_ref), custom_call_target="tpu_custom_call" | custom-call | flops 1073741824 | bytes 8388608 | tf_op jit(solution)/shard_map/point_grad/pallas_call | solution.py:399
  148.8 0.7 slice_reduce_fusion
  149.5 9.1 %outer.1 = f32[32,16,8,8,32]{4,3,2,1,0:T(8,128)} custom-call(f32[256,512]{1,0:T(8,128)} %get-tuple-element.17.spectrum_ref, f32[256,512]{1,0:T(8,128)} %get-tuple-element.18.grad_ref), custom_call_target="tpu_custom_call" | custom-call | flops 1048576 | bytes 17825792 | tf_op jit(solution)/shard_map/outer/pallas_call | solution.py:329
  158.6 10.7 %all-to-all-done.3.packed_ref = bf16[32,128,128]{2,1,0:T(8,128)(2,1)S(1)} async-done(((bf16[32,128,128]{2,1,0:T(8,128)(2,1)}), bf16[32,128,128]{2,1,0:T(8,128)(2,1)S(1)}, u32[]{:S(2)}, u32[]{:S(2)}) %all-to-all-start.3) | async-done | bytes 1048608 | tf_op jit(solution)/shard_map/all_to_all | solution.py:636
  169.3 9.6 %last.1 = bf16[512,4096]{1,0:T(8,128)(2,1)} custom-call(bf16[32,128,128]{2,1,0:T(8,128)(2,1)S(1)} %all-to-all-done.3.packed_ref, bf16[8,1024,512]{2,1,0:T(8,128)(2,1)} %constant.18.clone.table_ref, bf16[8,512,512]{2,1,0:T(8,128)(2,1)} %point_grad.1.mixed_ref), custom_call_target="tpu_custom_call" | custom-call | flops 4294967296 | bytes 18874368 | tf_op jit(solution)/shard_map/last/pallas_call | solution.py:612
  (23 shorter events, 1.6 us)
Async XLA Ops:
  0.6 26.5 %copy-start = (bf16[8,8]{1,0:T(8,128)(2,1)S(1)}, bf16[8,8]{1,0:T(8,128)(2,1)}, u32[]{:S(2)}) copy-start(bf16[8,8]{1,0:T(8,128)(2,1)} %param.16) | copy-start | bytes 388
  9.0 33.6 %all-to-all-start = ((bf16[32,128,128]{2,1,0:T(8,128)(2,1)}), bf16[32,128,128]{2,1,0:T(8,128)(2,1)S(1)}, u32[]{:S(2)}, u32[]{:S(2)}) async-start(bf16[32,128,128]{2,1,0:T(8,128)(2,1)} %analyse.1), calls=%async_computation | async-start | bytes 2097152 | tf_op jit(solution)/shard_map/all_to_all | solution.py:636
  16.4 9.8 %copy-start.6 = (f32[256,8]{1,0:T(8,128)S(1)}, f32[256,8]{1,0:T(8,128)}, u32[]{:S(2)}) copy-start(f32[256,8]{1,0:T(8,128)} %constant.25.clone) | copy-start | bytes 24580
  16.4 9.8 %copy-start.8 = (f32[8]{0:T(128)S(1)}, f32[8]{0:T(128)}, u32[]{:S(2)}) copy-start(f32[8]{0:T(128)} %param.17) | copy-start | bytes 100
  16.4 10.7 %copy-start.4 = (f32[256,256]{1,0:T(8,128)S(1)}, f32[256,256]{1,0:T(8,128)}, u32[]{:S(2)}) copy-start(f32[256,256]{1,0:T(8,128)} %constant.24.clone) | copy-start | bytes 786436
  16.4 10.7 %copy-start.5 = (bf16[256,8]{1,0:T(8,128)(2,1)S(1)}, bf16[256,8]{1,0:T(8,128)(2,1)}, u32[]{:S(2)}) copy-start(bf16[256,8]{1,0:T(8,128)(2,1)} %constant.23.clone) | copy-start | bytes 12292
  42.6 1.0 copy-start.3
  48.5 29.9 %all-to-all-start.1 = ((bf16[32,128,128]{2,1,0:T(8,128)(2,1)}), bf16[32,128,128]{2,1,0:T(8,128)(2,1)S(1)}, u32[]{:S(2)}, u32[]{:S(2)}) async-start(bf16[32,128,128]{2,1,0:T(8,128)(2,1)} %bitcast.23), calls=%async_computation.1 | async-start | bytes 2097152 | tf_op jit(solution)/shard_map/all_to_all | solution.py:636
  102.0 30.6 %all-to-all-start.2 = ((bf16[32,128,128]{2,1,0:T(8,128)(2,1)}), bf16[32,128,128]{2,1,0:T(8,128)(2,1)S(1)}, u32[]{:S(2)}, u32[]{:S(2)}) async-start(bf16[32,128,128]{2,1,0:T(8,128)(2,1)} %get-tuple-element.15), calls=%async_computation.2 | async-start | bytes 2097152 | tf_op jit(solution)/shard_map/all_to_all | solution.py:636
  111.5 1.4 collective-permute-start
  113.5 3.6 %collective-permute-start.1 = (f32[8,128]{1,0:T(8,128)S(1)}, f32[8,128]{1,0:T(8,128)S(1)}, u32[]{:S(2)}, u32[]{:S(2)}) collective-permute-start(f32[8,128]{1,0:T(8,128)S(1)} %add.15), channel_id=1, source_target_pairs={{0,2},{1,3},{2,0},{3,1},{4,6},{5,7},{6,4},{7,5},{8,10},{9,11},{10,... | collective-permute-start | bytes 12296 | tf_op jit(solution)/shard_map/ppermute | solution.py:643
  117.1 3.6 %collective-permute-start.2 = (f32[8,128]{1,0:T(8,128)S(1)}, f32[8,128]{1,0:T(8,128)S(1)}, u32[]{:S(2)}, u32[]{:S(2)}) collective-permute-start(f32[8,128]{1,0:T(8,128)S(1)} %add.16), channel_id=1, source_target_pairs={{0,4},{1,5},{2,6},{3,7},{4,0},{5,1},{6,2},{7,3},{8,12},{9,13},{10,... | collective-permute-start | bytes 12296 | tf_op jit(solution)/shard_map/ppermute | solution.py:643
  120.8 3.6 %collective-permute-start.3 = (f32[8,128]{1,0:T(8,128)S(1)}, f32[8,128]{1,0:T(8,128)S(1)}, u32[]{:S(2)}, u32[]{:S(2)}) collective-permute-start(f32[8,128]{1,0:T(8,128)S(1)} %add.17), channel_id=1, source_target_pairs={{0,8},{1,9},{2,10},{3,11},{4,12},{5,13},{6,14},{7,15},{8,0},{9,1},... | collective-permute-start | bytes 12296 | tf_op jit(solution)/shard_map/ppermute | solution.py:643
  124.4 7.7 %collective-permute-start.4 = (f32[8,128]{1,0:T(8,128)S(1)}, f32[8,128]{1,0:T(8,128)S(1)}, u32[]{:S(2)}, u32[]{:S(2)}) collective-permute-start(f32[8,128]{1,0:T(8,128)S(1)} %add.18), channel_id=1, source_target_pairs={{0,16},{1,17},{2,18},{3,19},{4,20},{5,21},{6,22},{7,23},{8,24},{9,... | collective-permute-start | bytes 12296 | tf_op jit(solution)/shard_map/ppermute | solution.py:643
  132.6 25.9 %copy-start.7 = (f32[8,128]{1,0:T(8,128)}, f32[8,128]{1,0:T(8,128)S(1)}, u32[]{:S(2)}) copy-start(f32[8,128]{1,0:T(8,128)S(1)} %get-tuple-element.19) | copy-start | bytes 12292
  132.6 1.0 copy-start.2
  139.5 29.9 %all-to-all-start.3 = ((bf16[32,128,128]{2,1,0:T(8,128)(2,1)}), bf16[32,128,128]{2,1,0:T(8,128)(2,1)S(1)}, u32[]{:S(2)}, u32[]{:S(2)}) async-start(bf16[32,128,128]{2,1,0:T(8,128)(2,1)} %bitcast.22), calls=%async_computation.3 | async-start | bytes 2097152 | tf_op jit(solution)/shard_map/all_to_all | solution.py:636
  169.3 9.6 %copy-start.1 = (bf16[8,8]{1,0:T(8,128)(2,1)S(1)}, bf16[8,8]{1,0:T(8,128)(2,1)}, u32[]{:S(2)}) copy-start(bf16[8,8]{1,0:T(8,128)(2,1)} %param.16) | copy-start | bytes 388
